TPU v7x, 32 devices: a whole 2x2x4 slice. The times are simulated.
32 devices in a mesh: chain: 2 (over x), tile: 16 (over z, y, core).
Axes of the slice: x: 2, y: 2, z: 4, core: 2. Of those that a mesh axis runs over, the one named last changes fastest.
Arguments:
- right_side: float32 [3, 2, 32, 8192], P(None, None, None, ('chain', 'tile')), may hold values from -6 to 6
- diag_inverse: float32 [2, 8192, 4096], P(None, ('chain', 'tile'))
- coupling: float32 [2, 8192, 4096], P(None, ('chain', 'tile')), may hold values from -0.0390625 to 0.0390625
- updates: float32 [8192, 192], P(('chain', 'tile')), may hold values from -2.4 to 2.4
- update_rows: int32 [8192], P(('chain', 'tile')), may hold values from 0 to 4095, as said below
- tile_counts: int32 [64], P(('chain', 'tile')), may hold values from 32 to 128, as said below
Outputs:
- solution: float32 [3, 2, 32, 8192], P(None, None, None, ('chain', 'tile'))
Inputs may be any that keep to these rules, and one draw needn't show every extreme that they name: `update_rows`: rows are counted within the supernode of the group that holds the entry. In each aligned block of 256 entries (the update rows of one device) at most 32 entries fall in any one aligned range of 256 rows, and in each run of 16 aligned blocks one such range receives exactly 32 entries from every block of the run. Padding rows carry entries too. `tile_counts`: one tile has all 128 rows live.
All inputs are finite; a program needn't handle non-finite values.
Results may differ from a plain program's by a relative error of at most 0.0001.
Values sent between devices are 32-bit elements; how exact they have to be, the bound alone decides.
No kernel may reach another device: no remote copies, remote signals or barrier semaphores. Data moves between devices by JAX's collectives and lax.ppermute only.
A program may use at most 64 MiB of HBM per device.

v0:
```python
import jax
import jax.numpy as jnp
from jax import lax
from jax.sharding import PartitionSpec as P

highest = lax.Precision.HIGHEST


def shifted(value, axis, by):
    peers = lax.axis_size(axis)
    pairs = [(i, i + by) for i in range(peers) if 0 <= i + by < peers]
    return lax.ppermute(value, axis, pairs)


def combine_parts(products):
    return jnp.stack([products[0, 0] - products[1, 1], products[0, 1] + products[1, 0]], axis=0)


def body(right_side, diag_inverse, coupling, updates, update_rows, tile_counts):
    batches, halves, sources, own_rows = right_side.shape
    chain_size = lax.axis_size("chain")
    full_rows = diag_inverse.shape[2]
    row_count = updates.shape[0]
    tile_rows = row_count // tile_counts.shape[0]
    limits = jnp.broadcast_to(tile_counts[:, None], (tile_counts.shape[0], tile_rows)).reshape(-1)
    is_live = jnp.arange(row_count, dtype=jnp.int32) % tile_rows < limits
    live_updates = jnp.where(is_live[:, None], updates, 0.0)
    dense_sum = jax.ops.segment_sum(live_updates, update_rows, num_segments=full_rows)
    accumulated = lax.psum_scatter(dense_sum, "tile", scatter_dimension=0, tiled=True)
    arranged = accumulated.reshape(own_rows, batches, halves, sources).transpose(1, 2, 3, 0)
    reduced_all = right_side - arranged
    chain_index = lax.axis_index("chain")
    section_count = chain_size + batches - 1

    def accumulate(columns):
        diag_part = jnp.einsum("jrs,kis->kjri", columns, diag_inverse, precision=highest)
        couple_part = jnp.einsum("jrs,kis->kjri", columns, coupling, precision=highest)
        return (diag_part, couple_part)

    def advance(section_index, loop_state):
        carried, solution = loop_state
        incoming = shifted(carried, "chain", 1)
        batch_index = section_index - chain_index
        active = (batch_index >= 0) & (batch_index < batches)
        clamped = jnp.clip(batch_index, 0, batches - 1)
        reduced = lax.dynamic_index_in_dim(reduced_all, clamped, 0, keepdims=False) - incoming
        diag_sum, couple_sum = accumulate(lax.all_gather(reduced, "tile", axis=2, tiled=True))
        updated = lax.dynamic_update_index_in_dim(solution, combine_parts(diag_sum), clamped, 0)
        return (combine_parts(couple_sum), jnp.where(active, updated, solution))

    start_state = (jnp.zeros((2, sources, own_rows), jnp.float32), jnp.zeros_like(right_side))
    final_carry, solution = lax.fori_loop(0, section_count, advance, start_state)
    return solution


def solution(mesh):
    in_specs = (
        P(None, None, None, ("chain", "tile")),
        P(None, ("chain", "tile"), None),
        P(None, ("chain", "tile"), None),
        P(("chain", "tile"), None),
        P(("chain", "tile")),
        P(("chain", "tile")),
    )
    out_specs = P(None, None, None, ("chain", "tile"))
    return jax.shard_map(body, mesh=mesh, in_specs=in_specs, out_specs=out_specs, check_vma=False)
```

profile of v0, /device:TPU:0, one launch (start us, length us, event | category | flops | bytes accessed | tf_op | source)
XLA Modules:
  0.0 344.7 jit_solution(7960716470185932587)
XLA Ops:
  6.5 0.0 copy-start.3
  6.5 0.0 reduce-scatter.2.cloned.1.call-start
  6.5 0.8 fusion.22
  7.3 0.9 broadcast_select_fusion
  8.3 0.1 copy.21
  8.4 4.2 %scatter_custom_fusion = f32[4096,192]{1,0:T(8,128)} fusion(s32[256]{0:T(256)} %param.12, f32[256,192]{1,0:T(8,128)S(1)} %copy.21, f32[]{:T(128)} %constant.60.clone.1), kind=kCustom, calls=%fused_computation.26 | custom fusion | flops 49152 | bytes 3146240 | tf_op jit(solution)/shard_map/scatter-add | solution.py:28
  12.6 0.0 reduce-scatter.2.cloned.1.call-update
  12.7 75.5 %reduce-scatter.2.cloned.1.call-done = f32[256,192]{1,0:T(8,128)} async-done(((f32[4096,192]{1,0:T(8,128)}), f32[256,192]{1,0:T(8,128)}) %reduce-scatter.2.cloned.1.call-update) | async-done | bytes 196624 | tf_op jit(solution)/shard_map/reduce_scatter | solution.py:29
  88.2 1.1 copy.22
  89.2 0.0 copy-done.3
  89.3 248.1 %while.15 = (s32[]{:T(128)}, f32[2,32,256]{2,1,0:T(8,128)S(1)}, f32[3,2,32,256]{3,2,1,0:T(8,128)S(1)}, s32[]{:T(128)}, f32[3,2,32,256]{3,2,1,0:T(8,128)S(1)}, /*...) while((s32[]{:T(128)}, f32[2,32,256]{2,1,0:T(8,128)S(1)}, ...), condition=%wide.region_3.4_spmd, body=%wide.region_2.3_spmd.sunk | while | flops 3221323776 | bytes 61407540 | solution.py:52
  89.3 0.0 all-gather.2.cloned.1.call-start
  89.4 3.4 collective-permute-start
  92.8 1.9 collective-permute-done
  94.6 0.6 bitcast_subtract_fusion.2
  95.3 0.0 all-gather.2.cloned.1.call-update
  95.3 37.0 %all-gather.2.cloned.1.call-done = f32[2,32,4096]{2,1,0:T(8,128)} async-done(((f32[2,32,256]{2,1,0:T(8,128)}), f32[2,32,4096]{2,1,0:T(8,128)}) %all-gather.2.cloned.1.call-update) | async-done | bytes 1048592 | tf_op jit(solution)/shard_map/while/body/eval_jaxpr/all_gather | solution.py:47
  132.3 0.0 copy-start
  132.3 0.0 copy-start.1
  132.3 10.5 %fusion.41 = f32[2,2,32,256]{3,2,0,1:T(8,128)S(1)} fusion(f32[2,256,4096]{2,1,0:T(8,128)} %get-tuple-element.215, f32[2,32,4096]{2,1,0:T(8,128)} %all-gather.2.cloned.1.call-done), kind=kOutput, calls=%fused_computation.6.clone.1 | convolution fusion | flops 1610612736 | bytes 9568256 | tf_op jit(solution)/shard_map/while/body/eval_jaxpr/jrs,kis->kjri/dot_general | solution.py:36
  142.9 0.0 copy-done
  142.9 0.0 copy-done.1
  142.9 8.1 %fusion.38 = f32[2,2,32,256]{3,2,0,1:T(8,128)S(1)} fusion(f32[2,256,4096]{2,1,0:T(8,128)S(1)} %copy-done, f32[2,32,4096]{2,1,0:T(8,128)S(1)} %copy-done.1), kind=kOutput, calls=%fused_computation.5.clone.1 | convolution fusion | flops 1610612736 | bytes 9568256 | tf_op jit(solution)/shard_map/while/body/eval_jaxpr/jrs,kis->kjri/dot_general | solution.py:37
  151.1 0.0 all-gather.2.cloned.1.call-start
  151.1 3.3 collective-permute-start
  154.4 1.9 collective-permute-done
  156.3 0.6 bitcast_subtract_fusion.2
  156.9 0.0 all-gather.2.cloned.1.call-update
  157.0 37.4 %all-gather.2.cloned.1.call-done = f32[2,32,4096]{2,1,0:T(8,128)} async-done(((f32[2,32,256]{2,1,0:T(8,128)}), f32[2,32,4096]{2,1,0:T(8,128)}) %all-gather.2.cloned.1.call-update) | async-done | bytes 1048592 | tf_op jit(solution)/shard_map/while/body/eval_jaxpr/all_gather | solution.py:47
  194.4 0.0 copy-start
  194.4 0.0 copy-start.1
  194.4 10.5 %fusion.41 = f32[2,2,32,256]{3,2,0,1:T(8,128)S(1)} fusion(f32[2,256,4096]{2,1,0:T(8,128)} %get-tuple-element.215, f32[2,32,4096]{2,1,0:T(8,128)} %all-gather.2.cloned.1.call-done), kind=kOutput, calls=%fused_computation.6.clone.1 | convolution fusion | flops 1610612736 | bytes 9568256 | tf_op jit(solution)/shard_map/while/body/eval_jaxpr/jrs,kis->kjri/dot_general | solution.py:36
  205.0 0.0 copy-done
  205.0 0.0 copy-done.1
  205.0 8.1 %fusion.38 = f32[2,2,32,256]{3,2,0,1:T(8,128)S(1)} fusion(f32[2,256,4096]{2,1,0:T(8,128)S(1)} %copy-done, f32[2,32,4096]{2,1,0:T(8,128)S(1)} %copy-done.1), kind=kOutput, calls=%fused_computation.5.clone.1 | convolution fusion | flops 1610612736 | bytes 9568256 | tf_op jit(solution)/shard_map/while/body/eval_jaxpr/jrs,kis->kjri/dot_general | solution.py:37
  213.2 0.0 all-gather.2.cloned.1.call-start
  213.3 3.3 collective-permute-start
  216.6 1.9 collective-permute-done
  218.4 0.6 bitcast_subtract_fusion.2
  219.1 0.0 all-gather.2.cloned.1.call-update
  219.1 37.4 %all-gather.2.cloned.1.call-done = f32[2,32,4096]{2,1,0:T(8,128)} async-done(((f32[2,32,256]{2,1,0:T(8,128)}), f32[2,32,4096]{2,1,0:T(8,128)}) %all-gather.2.cloned.1.call-update) | async-done | bytes 1048592 | tf_op jit(solution)/shard_map/while/body/eval_jaxpr/all_gather | solution.py:47
  256.5 0.0 copy-start
  256.5 0.0 copy-start.1
  256.5 10.5 %fusion.41 = f32[2,2,32,256]{3,2,0,1:T(8,128)S(1)} fusion(f32[2,256,4096]{2,1,0:T(8,128)} %get-tuple-element.215, f32[2,32,4096]{2,1,0:T(8,128)} %all-gather.2.cloned.1.call-done), kind=kOutput, calls=%fused_computation.6.clone.1 | convolution fusion | flops 1610612736 | bytes 9568256 | tf_op jit(solution)/shard_map/while/body/eval_jaxpr/jrs,kis->kjri/dot_general | solution.py:36
  267.1 0.0 copy-done
  267.1 0.0 copy-done.1
  267.1 8.1 %fusion.38 = f32[2,2,32,256]{3,2,0,1:T(8,128)S(1)} fusion(f32[2,256,4096]{2,1,0:T(8,128)S(1)} %copy-done, f32[2,32,4096]{2,1,0:T(8,128)S(1)} %copy-done.1), kind=kOutput, calls=%fused_computation.5.clone.1 | convolution fusion | flops 1610612736 | bytes 9568256 | tf_op jit(solution)/shard_map/while/body/eval_jaxpr/jrs,kis->kjri/dot_general | solution.py:37
  275.3 0.0 all-gather.2.cloned.1.call-start
  275.4 3.3 collective-permute-start
  278.7 1.9 collective-permute-done
  280.6 0.6 bitcast_subtract_fusion.2
  281.2 0.0 all-gather.2.cloned.1.call-update
  281.2 37.4 %all-gather.2.cloned.1.call-done = f32[2,32,4096]{2,1,0:T(8,128)} async-done(((f32[2,32,256]{2,1,0:T(8,128)}), f32[2,32,4096]{2,1,0:T(8,128)}) %all-gather.2.cloned.1.call-update) | async-done | bytes 1048592 | tf_op jit(solution)/shard_map/while/body/eval_jaxpr/all_gather | solution.py:47
  318.7 0.0 copy-start
  318.7 0.0 copy-start.1
  318.7 10.5 %fusion.41 = f32[2,2,32,256]{3,2,0,1:T(8,128)S(1)} fusion(f32[2,256,4096]{2,1,0:T(8,128)} %get-tuple-element.215, f32[2,32,4096]{2,1,0:T(8,128)} %all-gather.2.cloned.1.call-done), kind=kOutput, calls=%fused_computation.6.clone.1 | convolution fusion | flops 1610612736 | bytes 9568256 | tf_op jit(solution)/shard_map/while/body/eval_jaxpr/jrs,kis->kjri/dot_general | solution.py:36
  329.3 0.0 copy-done
  329.3 0.0 copy-done.1
  329.3 8.1 %fusion.38 = f32[2,2,32,256]{3,2,0,1:T(8,128)S(1)} fusion(f32[2,256,4096]{2,1,0:T(8,128)S(1)} %copy-done, f32[2,32,4096]{2,1,0:T(8,128)S(1)} %copy-done.1), kind=kOutput, calls=%fused_computation.5.clone.1 | convolution fusion | flops 1610612736 | bytes 9568256 | tf_op jit(solution)/shard_map/while/body/eval_jaxpr/jrs,kis->kjri/dot_general | solution.py:37
  337.5 0.0 copy-start.2
  337.5 0.7 copy-done.2
  (27 shorter events, 0.2 us)
Async XLA Ops:
  6.5 82.7 %copy-start.3 = (f32[3,2,32,256]{3,2,1,0:T(8,128)S(1)}, f32[3,2,32,256]{3,2,1,0:T(8,128)}, u32[]{:S(2)}) copy-start(f32[3,2,32,256]{3,2,1,0:T(8,128)} %param.8) | copy-start | bytes 589828
  6.5 81.6 %reduce-scatter.2.cloned.1.call-start = ((), (), s32[]{:S(2)}) async-start(), calls=%async_computation.1 | async-start | bytes 4456448 | tf_op jit(solution)/shard_map/reduce_scatter | solution.py:29
  89.3 42.9 %all-gather.2.cloned.1.call-start = ((), (), s32[]{:S(2)}) async-start(), calls=%async_computation.2 | async-start | bytes 1114112 | tf_op jit(solution)/shard_map/while/body/eval_jaxpr/all_gather | solution.py:47
  89.4 5.3 %collective-permute-start = (f32[2,32,256]{2,1,0:T(8,128)S(1)}, f32[2,32,256]{2,1,0:T(8,128)S(1)}, u32[]{:S(2)}, u32[]{:S(2)}) collective-permute-start(f32[2,32,256]{2,1,0:T(8,128)S(1)} %get-tuple-element.199), channel_id=1, source_target_pairs={{0,16},{1,17},{2,18},{3,19},{4,20},{5,21},{6,22},{7,23},{8,24},{9,... | collective-permute-start | bytes 196616 | tf_op jit(solution)/shard_map/while/body/eval_jaxpr/ppermute | solution.py:12
  132.3 10.6 %copy-start = (f32[2,256,4096]{2,1,0:T(8,128)S(1)}, f32[2,256,4096]{2,1,0:T(8,128)}, u32[]{:S(2)}) copy-start(f32[2,256,4096]{2,1,0:T(8,128)} %get-tuple-element.214) | copy-start | bytes 25165828 | tf_op jit(solution)/shard_map/while
  132.3 10.6 %copy-start.1 = (f32[2,32,4096]{2,1,0:T(8,128)S(1)}, f32[2,32,4096]{2,1,0:T(8,128)}, u32[]{:S(2)}) copy-start(f32[2,32,4096]{2,1,0:T(8,128)} %all-gather.2.cloned.1.call-done) | copy-start | bytes 3145732 | tf_op jit(solution)/shard_map/while
  151.1 43.3 %all-gather.2.cloned.1.call-start = ((), (), s32[]{:S(2)}) async-start(), calls=%async_computation.2 | async-start | bytes 1114112 | tf_op jit(solution)/shard_map/while/body/eval_jaxpr/all_gather | solution.py:47
  151.1 5.2 %collective-permute-start = (f32[2,32,256]{2,1,0:T(8,128)S(1)}, f32[2,32,256]{2,1,0:T(8,128)S(1)}, u32[]{:S(2)}, u32[]{:S(2)}) collective-permute-start(f32[2,32,256]{2,1,0:T(8,128)S(1)} %get-tuple-element.199), channel_id=1, source_target_pairs={{0,16},{1,17},{2,18},{3,19},{4,20},{5,21},{6,22},{7,23},{8,24},{9,... | collective-permute-start | bytes 196616 | tf_op jit(solution)/shard_map/while/body/eval_jaxpr/ppermute | solution.py:12
  194.4 10.6 %copy-start = (f32[2,256,4096]{2,1,0:T(8,128)S(1)}, f32[2,256,4096]{2,1,0:T(8,128)}, u32[]{:S(2)}) copy-start(f32[2,256,4096]{2,1,0:T(8,128)} %get-tuple-element.214) | copy-start | bytes 25165828 | tf_op jit(solution)/shard_map/while
  194.4 10.6 %copy-start.1 = (f32[2,32,4096]{2,1,0:T(8,128)S(1)}, f32[2,32,4096]{2,1,0:T(8,128)}, u32[]{:S(2)}) copy-start(f32[2,32,4096]{2,1,0:T(8,128)} %all-gather.2.cloned.1.call-done) | copy-start | bytes 3145732 | tf_op jit(solution)/shard_map/while
  213.2 43.3 %all-gather.2.cloned.1.call-start = ((), (), s32[]{:S(2)}) async-start(), calls=%async_computation.2 | async-start | bytes 1114112 | tf_op jit(solution)/shard_map/while/body/eval_jaxpr/all_gather | solution.py:47
  213.3 5.2 %collective-permute-start = (f32[2,32,256]{2,1,0:T(8,128)S(1)}, f32[2,32,256]{2,1,0:T(8,128)S(1)}, u32[]{:S(2)}, u32[]{:S(2)}) collective-permute-start(f32[2,32,256]{2,1,0:T(8,128)S(1)} %get-tuple-element.199), channel_id=1, source_target_pairs={{0,16},{1,17},{2,18},{3,19},{4,20},{5,21},{6,22},{7,23},{8,24},{9,... | collective-permute-start | bytes 196616 | tf_op jit(solution)/shard_map/while/body/eval_jaxpr/ppermute | solution.py:12
  256.5 10.6 %copy-start = (f32[2,256,4096]{2,1,0:T(8,128)S(1)}, f32[2,256,4096]{2,1,0:T(8,128)}, u32[]{:S(2)}) copy-start(f32[2,256,4096]{2,1,0:T(8,128)} %get-tuple-element.214) | copy-start | bytes 25165828 | tf_op jit(solution)/shard_map/while
  256.5 10.6 %copy-start.1 = (f32[2,32,4096]{2,1,0:T(8,128)S(1)}, f32[2,32,4096]{2,1,0:T(8,128)}, u32[]{:S(2)}) copy-start(f32[2,32,4096]{2,1,0:T(8,128)} %all-gather.2.cloned.1.call-done) | copy-start | bytes 3145732 | tf_op jit(solution)/shard_map/while
  275.3 43.3 %all-gather.2.cloned.1.call-start = ((), (), s32[]{:S(2)}) async-start(), calls=%async_computation.2 | async-start | bytes 1114112 | tf_op jit(solution)/shard_map/while/body/eval_jaxpr/all_gather | solution.py:47
  275.4 5.2 %collective-permute-start = (f32[2,32,256]{2,1,0:T(8,128)S(1)}, f32[2,32,256]{2,1,0:T(8,128)S(1)}, u32[]{:S(2)}, u32[]{:S(2)}) collective-permute-start(f32[2,32,256]{2,1,0:T(8,128)S(1)} %get-tuple-element.199), channel_id=1, source_target_pairs={{0,16},{1,17},{2,18},{3,19},{4,20},{5,21},{6,22},{7,23},{8,24},{9,... | collective-permute-start | bytes 196616 | tf_op jit(solution)/shard_map/while/body/eval_jaxpr/ppermute | solution.py:12
  318.7 10.6 %copy-start = (f32[2,256,4096]{2,1,0:T(8,128)S(1)}, f32[2,256,4096]{2,1,0:T(8,128)}, u32[]{:S(2)}) copy-start(f32[2,256,4096]{2,1,0:T(8,128)} %get-tuple-element.214) | copy-start | bytes 25165828 | tf_op jit(solution)/shard_map/while
  318.7 10.6 %copy-start.1 = (f32[2,32,4096]{2,1,0:T(8,128)S(1)}, f32[2,32,4096]{2,1,0:T(8,128)}, u32[]{:S(2)}) copy-start(f32[2,32,4096]{2,1,0:T(8,128)} %all-gather.2.cloned.1.call-done) | copy-start | bytes 3145732 | tf_op jit(solution)/shard_map/while
  337.5 0.7 copy-start.2
Sparse Core Ops, SparseCore 0:
  12.8 75.3 reduce-scatter.1
  95.4 36.8 all-gather.1
  157.1 37.2 all-gather.1
  219.2 37.2 all-gather.1
  281.3 37.2 all-gather.1
where the time goes:
time: 345 us
  waiting for transfers between devices  232 us (67%)
  matrix products  74.6 us (22%)
  starting transfers between devices  13.4 us (4%)
  between operations  13.1 us (4%)
  other arithmetic  8.73 us (3%)
    all_gather x4, waiting for transfers between devices, advance(): lax.all_gather(reduced, 'tile', axis=2, tiled=True)  149 us
    reduce_scatter x1, waiting for transfers between devices, body(): lax.psum_scatter(dense_sum, 'tile', scatter_dimension=0, tiled=True)  75.5 us
    dot_general x4, matrix products, accumulate(): jnp.einsum('jrs,kis->kjri', columns, diag_inverse, precision=highest)  42.2 us
    dot_general x4, matrix products, accumulate(): jnp.einsum('jrs,kis->kjri', columns, coupling, precision=highest)  32.5 us
    ppermute x4, starting transfers between devices, shifted(): return lax.ppermute(value, axis, pairs)  13.2 us
    ppermute x4, waiting for transfers between devices, shifted(): return lax.ppermute(value, axis, pairs)  7.5 us
  transfers between devices with their start and end apart: 9, of which 9 were waited for; matrix products, arithmetic and copies ran while one was open for 0% of the time, Pallas kernels for 0%

commit v1 on v0

v1 whole, which is shorter than its diff:
```python
import functools

import jax
import jax.numpy as jnp
from jax import lax
from jax.experimental import pallas as pl
from jax.experimental.pallas import tpu as pltpu
from jax.sharding import PartitionSpec as P

MIB = 1 << 20
f32 = jnp.float32
bf16 = jnp.bfloat16


def halves_of(value):
    high = value.astype(bf16)
    return high, (value - high.astype(f32)).astype(bf16)


def thirds_of(value):
    high = value.astype(bf16)
    rest = value - high.astype(f32)
    middle = rest.astype(bf16)
    return high, middle, (rest - middle.astype(f32)).astype(bf16)


def pack_kernel(own_rows, cap, columns, tile_rows, counts_ref, lane_rows_ref, column_rows_ref, updates_ref, packed_ref):
    entries = updates_ref.shape[0]
    slots, width = packed_ref.shape
    entry = lax.broadcasted_iota(jnp.int32, (entries, 1), 0)
    live = jnp.zeros((entries, 1), jnp.bool_)
    for tile in range(entries // tile_rows):
        start = tile * tile_rows
        live = live | ((entry >= start) & (entry < start + counts_ref[tile]))
    column_rows = column_rows_ref[...]
    lane_rows = lane_rows_ref[...]
    column_owner = column_rows // own_rows
    lane_owner = lane_rows // own_rows
    earlier = lax.broadcasted_iota(jnp.int32, (entries, entries), 0) < lax.broadcasted_iota(jnp.int32, (entries, entries), 1)
    rank = jnp.sum(jnp.where(earlier & (column_owner == lane_owner), 1, 0), axis=0, keepdims=True)
    slot = lane_owner * cap + rank
    choose = jnp.where(lax.broadcasted_iota(jnp.int32, (slots, entries), 0) == slot, 1.0, 0.0).astype(bf16)
    data = jnp.where(live, updates_ref[...], 0.0)
    local_row = (column_rows - column_owner * own_rows).astype(f32)
    tail = jnp.where(lax.broadcasted_iota(jnp.int32, (entries, width - columns), 1) == 0, local_row, 0.0)
    data = jnp.concatenate([data, tail], axis=1)
    packed = jnp.zeros((slots, width), f32)
    for piece in thirds_of(data):
        packed += jnp.dot(choose, piece, preferred_element_type=f32)
    packed_ref[...] = packed


def reduce_kernel(columns, received_ref, right_ref, reduced_ref):
    slots = received_ref.shape[0]
    own_rows = reduced_ref.shape[1]
    received = received_ref[...]
    local_row = received[:, columns:columns + 1].astype(jnp.int32)
    place = jnp.where(lax.broadcasted_iota(jnp.int32, (slots, own_rows), 1) == local_row, 1.0, 0.0).astype(bf16)
    total = jnp.zeros(reduced_ref.shape, f32)
    for piece in thirds_of(received[:, :columns].T):
        total += jnp.dot(piece, place, preferred_element_type=f32)
    reduced_ref[...] = right_ref[...] - total


def product_kernel(halves, sources, x_ref, k_ref, out_ref, total_ref):
    step = pl.program_id(0)
    parts, own_rows, width = k_ref.shape
    columns = x_ref.shape[1]
    x = jnp.concatenate([x_ref[i] for i in range(x_ref.shape[0])], axis=1)
    k = k_ref[...].reshape(parts * own_rows, width)
    x_high, x_low = halves_of(x)
    k_high, k_low = halves_of(k)
    contract = (((1,), (1,)), ((), ()))
    both = lax.dot_general(jnp.concatenate([x_high, x_low], axis=0), k_high, contract, preferred_element_type=f32)
    part = both[:columns] + both[columns:] + lax.dot_general(x_high, k_low, contract, preferred_element_type=f32)

    @pl.when(step == 0)
    def _():
        total_ref[...] = part

    @pl.when(step > 0)
    def _():
        total_ref[...] += part

    @pl.when(step == pl.num_programs(0) - 1)
    def _():
        group = halves * sources
        for batch in range(columns // group):
            real = pl.ds(batch * group, sources)
            imag = pl.ds(batch * group + sources, sources)
            out_ref[real, :] = total_ref[real, :own_rows] - total_ref[imag, own_rows:]
            out_ref[imag, :] = total_ref[imag, :own_rows] + total_ref[real, own_rows:]


def complex_apply(matrix, blocks, halves, sources):
    parts, own_rows, full_rows = matrix.shape
    count, columns, block = blocks.shape
    per_step = min(count, max(1, 1024 // block))
    width = per_step * block
    return pl.pallas_call(
        functools.partial(product_kernel, halves, sources),
        grid=(full_rows // width,),
        in_specs=[
            pl.BlockSpec((per_step, columns, block), lambda i: (i, 0, 0)),
            pl.BlockSpec((parts, own_rows, width), lambda i: (0, 0, i)),
        ],
        out_specs=pl.BlockSpec((columns, own_rows), lambda i: (0, 0)),
        out_shape=jax.ShapeDtypeStruct((columns, own_rows), f32),
        scratch_shapes=[pltpu.VMEM((columns, parts * own_rows), f32)],
        compiler_params=pltpu.CompilerParams(vmem_limit_bytes=32 * MIB),
        cost_estimate=pl.CostEstimate(flops=6 * columns * parts * own_rows * full_rows, bytes_accessed=4 * matrix.size, transcendentals=0),
    )(blocks, matrix)


def gather_blocks(reduced):
    columns, own_rows = reduced.shape
    gathered = lax.all_gather(reduced, "tile", axis=0, tiled=False)
    if own_rows % 128 == 0:
        return gathered
    block = 256
    whole = gathered.transpose(1, 0, 2).reshape(columns, -1, block)
    return whole.transpose(1, 0, 2)


def body(right_side, diag_inverse, coupling, updates, update_rows, tile_counts):
    batches, halves, sources, own_rows = right_side.shape
    chain_size = lax.axis_size("chain")
    tile_size = lax.axis_size("tile")
    entries, columns = updates.shape
    tile_rows = entries // tile_counts.shape[0]
    cap = 2 * entries // tile_size
    slots = tile_size * cap
    width = -(-(columns + 1) // 128) * 128
    vmem = pl.BlockSpec(memory_space=pltpu.VMEM)
    smem = pl.BlockSpec(memory_space=pltpu.SMEM)
    packed = pl.pallas_call(
        functools.partial(pack_kernel, own_rows, cap, columns, tile_rows),
        in_specs=[smem, vmem, vmem, vmem],
        out_specs=vmem,
        out_shape=jax.ShapeDtypeStruct((slots, width), f32),
        compiler_params=pltpu.CompilerParams(vmem_limit_bytes=32 * MIB),
    )(tile_counts, update_rows[None, :], update_rows[:, None], updates)
    received = lax.all_to_all(packed.reshape(tile_size, cap, width), "tile", 0, 0, tiled=False).reshape(slots, width)
    reduced_all = pl.pallas_call(
        functools.partial(reduce_kernel, columns),
        in_specs=[vmem, vmem],
        out_specs=vmem,
        out_shape=jax.ShapeDtypeStruct((columns, own_rows), f32),
        compiler_params=pltpu.CompilerParams(vmem_limit_bytes=32 * MIB),
    )(received, right_side.reshape(columns, own_rows))
    onward = [(i, i + 1) for i in range(chain_size - 1)]
    reduced = reduced_all
    for _ in range(chain_size - 1):
        carried = complex_apply(coupling, gather_blocks(reduced), halves, sources)
        reduced = reduced_all - lax.ppermute(carried, "chain", onward)
    solution = complex_apply(diag_inverse, gather_blocks(reduced), halves, sources)
    return solution.reshape(right_side.shape)


def solution(mesh):
    in_specs = (
        P(None, None, None, ("chain", "tile")),
        P(None, ("chain", "tile"), None),
        P(None, ("chain", "tile"), None),
        P(("chain", "tile"), None),
        P(("chain", "tile")),
        P(("chain", "tile")),
    )
    out_specs = P(None, None, None, ("chain", "tile"))
    return jax.shard_map(body, mesh=mesh, in_specs=in_specs, out_specs=out_specs, check_vma=False)
```

time: 345 us -> 162 us (0.47)
  waiting for transfers between devices: 232 us -> 94.5 us
  matrix products: 74.6 us -> 0 us
  blocking collectives: 0 us -> 21.7 us
  local copies, waits for them, and re-layouts: 1.91 us -> 14.7 us
  Pallas kernels: 0 us -> 11.8 us
  starting transfers between devices: 13.4 us -> 3.42 us
  other arithmetic: 8.73 us -> 1.63 us
    reduce_scatter x1 -> x0, waiting for transfers between devices: 75.5 us -> none  [body(): lax.psum_scatter(dense_sum, 'tile', scatter_dimension=0, tiled=True)]
    dot_general x8 -> x0, matrix products: 74.6 us -> none  [the longest x4 42.2 us: accumulate(): jnp.einsum('jrs,kis->kjri', columns, diag_inverse, precision=highest)]
    all_gather x4 -> x2, waiting for transfers between devices: 149 us -> 89.9 us  [gather_blocks(): gathered = lax.all_gather(reduced, 'tile', axis=0, tiled=False)]
    all_to_all x0 -> x1, blocking collectives: none -> 21.7 us  [body(): lax.all_to_all(packed.reshape(tile_size, cap, width), 'tile', 0, 0, tiled...]
    unnamed x4 -> x15, local copies, waits for them, and re-layouts: 0.68 us -> 13.9 us
    pallas_call x0 -> x4, Pallas kernels: none -> 11.8 us  [the longest x2 9.51 us: complex_apply(): pl.pallas_call(functools.partial(product_kernel, halves, sources), grid=(...]
    ppermute x4 -> x1, starting transfers between devices: 13.2 us -> 3.38 us  [body(): reduced = reduced_all - lax.ppermute(carried, 'chain', onward)]
    scatter-add x1 -> x0, other arithmetic: 4.25 us -> none  [body(): jax.ops.segment_sum(live_updates, update_rows, num_segments=full_rows)]
  transfers between devices with their start and end apart: 9 -> 3, of which waited for: 9 -> 3; matrix products, arithmetic and copies ran while one was open for 0% -> 0% of each run, Pallas kernels for 0% -> 0%
where the time goes in v1:
time: 162 us; the launch traced here: 161 us
  waiting for transfers between devices  94.5 us (58%)
  blocking collectives  21.7 us (13%)
  local copies, waits for them, and re-layouts  14.7 us (9%)
  between operations  13.5 us (8%)
  Pallas kernels  11.8 us (7%)
  starting transfers between devices  3.42 us (2%)
  other arithmetic  1.63 us (1%)
    all_gather x2, waiting for transfers between devices, gather_blocks(): gathered = lax.all_gather(reduced, 'tile', axis=0, tiled=False)  89.9 us
    all_to_all x1, blocking collectives, body(): lax.all_to_all(packed.reshape(tile_size, cap, width), 'tile', 0, 0, tiled...  21.7 us
    unnamed x15, local copies, waits for them, and re-layouts  13.9 us
    pallas_call x2, Pallas kernels, complex_apply(): pl.pallas_call(functools.partial(product_kernel, halves, sources), grid=(...  9.51 us
    ppermute x1, waiting for transfers between devices, body(): reduced = reduced_all - lax.ppermute(carried, 'chain', onward)  4.54 us
    ppermute x1, starting transfers between devices, body(): reduced = reduced_all - lax.ppermute(carried, 'chain', onward)  3.38 us
  transfers between devices with their start and end apart: 3, of which 3 were waited for; matrix products, arithmetic and copies ran while one was open for 0% of the time, Pallas kernels for 0%

profile of v1, /device:TPU:0, one launch (start us, length us, event | category | flops | bytes accessed | tf_op | source)
XLA Modules:
  0.0 161.1 jit_solution(2170596865775437724)
XLA Ops:
  6.5 0.0 all-gather.5.cloned.1.call-start
  6.5 0.8 copy.8.column_rows_ref
  7.3 1.1 copy.9.updates_ref
  8.4 0.0 copy-start.5
  8.4 0.7 copy-done.5
  9.1 0.0 copy-start.6
  9.1 0.7 copy-done.6
  9.8 1.1 shard_map.64
  10.9 21.7 %all_to_all.5 = f32[16,32,256]{2,1,0:T(8,128)S(1)} all-to-all(f32[16,32,256]{2,1,0:T(8,128)S(1)} %bitcast.11), channel_id=1, replica_groups=mesh['chain'=2,'tile'=16] {'tile'}, dimensions={0} | all-to-all | bytes 1048576 | tf_op jit(solution)/shard_map/all_to_all | solution.py:143
  32.6 0.0 copy-start.4
  32.6 0.9 copy-done.4
  33.5 1.2 shard_map.65
  34.7 0.0 all-gather.5.cloned.1.call-update
  34.7 0.0 all-gather.7.cloned.1.call-start
  34.7 44.7 %all-gather.5.cloned.1.call-done = f32[3072,256]{1,0:T(8,128)} async-done(((f32[192,256]{1,0:T(8,128)}), f32[3072,256]{1,0:T(8,128)}) %all-gather.5.cloned.1.call-update) | async-done | bytes 3145744 | tf_op jit(solution)/shard_map/all_gather | solution.py:117
  79.4 0.0 copy-start
  79.4 3.4 %copy-done = f32[2,256,4096]{2,1,0:T(8,128)S(1)} copy-done((f32[2,256,4096]{2,1,0:T(8,128)S(1)}, f32[2,256,4096]{2,1,0:T(8,128)}, u32[]{:S(2)}) %copy-start) | copy-done | bytes 8388632
  82.8 0.0 copy-start.2
  82.8 1.9 %copy-done.2 = f32[3072,256]{1,0:T(8,128)S(1)} copy-done((f32[3072,256]{1,0:T(8,128)S(1)}, f32[3072,256]{1,0:T(8,128)}, u32[]{:S(2)}) %copy-start.2) | copy-done | bytes 3145752
  84.7 4.4 %shard_map.66 = f32[192,256]{1,0:T(8,128)S(1)} custom-call(f32[16,192,256]{2,1,0:T(8,128)S(1)} %bitcast.8, f32[2,256,4096]{2,1,0:T(8,128)S(1)} %copy-done), custom_call_target="tpu_custom_call" | custom-call | flops 2415919104 | bytes 8388608 | tf_op jit(solution)/shard_map/pallas_call | solution.py:100
  89.2 3.4 %collective-permute-start = (f32[192,256]{1,0:T(8,128)S(1)}, f32[192,256]{1,0:T(8,128)S(1)}, u32[]{:S(2)}, u32[]{:S(2)}) collective-permute-start(f32[192,256]{1,0:T(8,128)S(1)} %shard_map.66), channel_id=1, source_target_pairs={{0,16},{1,17},{2,18},{3,19},{4,20},{5,21},{6,22},{7,23},{8,24},{9,... | collective-permute-start | bytes 589832 | tf_op jit(solution)/shard_map/ppermute | solution.py:155
  92.5 4.5 %collective-permute-done = f32[192,256]{1,0:T(8,128)S(1)} collective-permute-done((f32[192,256]{1,0:T(8,128)S(1)}, f32[192,256]{1,0:T(8,128)S(1)}, u32[]{:S(2)}, u32[]{:S(2)}) %collective-permute-start) | collective-permute-done | bytes 196640 | tf_op jit(solution)/shard_map/ppermute | solution.py:155
  97.1 1.6 %sub.3 = f32[192,256]{1,0:T(8,128)} subtract(f32[192,256]{1,0:T(8,128)} %shard_map.65, f32[192,256]{1,0:T(8,128)S(1)} %collective-permute-done) | non-fusion elementwise | flops 49152 | bytes 589824 | tf_op jit(solution)/shard_map/sub | solution.py:155
  98.7 0.0 all-gather.7.cloned.1.call-update
  98.7 45.2 %all-gather.7.cloned.1.call-done = f32[3072,256]{1,0:T(8,128)} async-done(((f32[192,256]{1,0:T(8,128)}), f32[3072,256]{1,0:T(8,128)}) %all-gather.7.cloned.1.call-update) | async-done | bytes 3145744 | tf_op jit(solution)/shard_map/all_gather | solution.py:117
  143.9 0.0 copy-start.1
  143.9 3.4 %copy-done.1 = f32[2,256,4096]{2,1,0:T(8,128)S(1)} copy-done((f32[2,256,4096]{2,1,0:T(8,128)S(1)}, f32[2,256,4096]{2,1,0:T(8,128)}, u32[]{:S(2)}) %copy-start.1) | copy-done | bytes 8388632
  147.3 0.0 copy-start.3
  147.3 1.9 %copy-done.3 = f32[3072,256]{1,0:T(8,128)S(1)} copy-done((f32[3072,256]{1,0:T(8,128)S(1)}, f32[3072,256]{1,0:T(8,128)}, u32[]{:S(2)}) %copy-start.3) | copy-done | bytes 3145752
  149.2 5.1 %shard_map.67 = f32[192,256]{1,0:T(8,128)} custom-call(f32[16,192,256]{2,1,0:T(8,128)S(1)} %bitcast.9, f32[2,256,4096]{2,1,0:T(8,128)S(1)} %copy-done.1), custom_call_target="tpu_custom_call" | custom-call | flops 2415919104 | bytes 8388608 | tf_op jit(solution)/shard_map/pallas_call | solution.py:100
Async XLA Ops:
  6.5 72.9 %all-gather.5.cloned.1.call-start = ((), (), s32[]{:S(2)}) async-start(), calls=%async_computation.1 | async-start | bytes 3342336 | tf_op jit(solution)/shard_map/all_gather | solution.py:117
  8.4 0.7 copy-start.5
  9.1 0.7 copy-start.6
  32.6 0.9 copy-start.4
  34.7 109.2 %all-gather.7.cloned.1.call-start = ((), (), s32[]{:S(2)}) async-start(), calls=%async_computation.2 | async-start | bytes 3342336 | tf_op jit(solution)/shard_map/all_gather | solution.py:117
  79.4 3.4 %copy-start = (f32[2,256,4096]{2,1,0:T(8,128)S(1)}, f32[2,256,4096]{2,1,0:T(8,128)}, u32[]{:S(2)}) copy-start(f32[2,256,4096]{2,1,0:T(8,128)} %k_ref.2) | copy-start | bytes 25165828
  82.8 1.9 %copy-start.2 = (f32[3072,256]{1,0:T(8,128)S(1)}, f32[3072,256]{1,0:T(8,128)}, u32[]{:S(2)}) copy-start(f32[3072,256]{1,0:T(8,128)} %all-gather.5.cloned.1.call-done) | copy-start | bytes 9437188
  89.2 7.9 %collective-permute-start = (f32[192,256]{1,0:T(8,128)S(1)}, f32[192,256]{1,0:T(8,128)S(1)}, u32[]{:S(2)}, u32[]{:S(2)}) collective-permute-start(f32[192,256]{1,0:T(8,128)S(1)} %shard_map.66), channel_id=1, source_target_pairs={{0,16},{1,17},{2,18},{3,19},{4,20},{5,21},{6,22},{7,23},{8,24},{9,... | collective-permute-start | bytes 589832 | tf_op jit(solution)/shard_map/ppermute | solution.py:155
  143.9 3.4 %copy-start.1 = (f32[2,256,4096]{2,1,0:T(8,128)S(1)}, f32[2,256,4096]{2,1,0:T(8,128)}, u32[]{:S(2)}) copy-start(f32[2,256,4096]{2,1,0:T(8,128)} %k_ref.3) | copy-start | bytes 25165828
  147.3 1.9 %copy-start.3 = (f32[3072,256]{1,0:T(8,128)S(1)}, f32[3072,256]{1,0:T(8,128)}, u32[]{:S(2)}) copy-start(f32[3072,256]{1,0:T(8,128)} %all-gather.7.cloned.1.call-done) | copy-start | bytes 9437188
Sparse Core Ops, SparseCore 0:
  34.8 44.5 all-gather.4
  98.9 45.0 all-gather.6

commit v2 on v1

v2 whole, which is shorter than its diff:
```python
import functools

import jax
import jax.numpy as jnp
from jax import lax
from jax.experimental import pallas as pl
from jax.experimental.pallas import tpu as pltpu
from jax.sharding import PartitionSpec as P

MIB = 1 << 20
CHUNKS = 2
f32 = jnp.float32
bf16 = jnp.bfloat16
lanes_contract = (((1,), (1,)), ((), ()))


def halves_of(value):
    high = value.astype(bf16)
    return high, (value - high.astype(f32)).astype(bf16)


def thirds_of(value):
    high = value.astype(bf16)
    rest = value - high.astype(f32)
    middle = rest.astype(bf16)
    return high, middle, (rest - middle.astype(f32)).astype(bf16)


def kernel_params():
    return pltpu.CompilerParams(vmem_limit_bytes=56 * MIB)


def pack_kernel(own_rows, cap, tile_rows, counts_ref, rows_ref, updates_ref, packed_ref):
    columns, entries = updates_ref.shape
    slots, width = packed_ref.shape
    entry = lax.broadcasted_iota(jnp.int32, (1, entries), 1)
    live = jnp.zeros((1, entries), jnp.bool_)
    for tile in range(entries // tile_rows):
        start = tile * tile_rows
        live = live | ((entry >= start) & (entry < start + counts_ref[tile]))
    rows = rows_ref[...]
    owner = rows // own_rows
    lane_owner = jnp.broadcast_to(owner.astype(f32), (entries, entries))
    earlier = lax.broadcasted_iota(jnp.int32, (entries, entries), 0) < lax.broadcasted_iota(jnp.int32, (entries, entries), 1)
    rank = jnp.sum(jnp.where(earlier & (lane_owner.T == lane_owner), 1, 0), axis=0, keepdims=True)
    slot = owner * cap + rank
    choose = jnp.where(lax.broadcasted_iota(jnp.int32, (slots, entries), 0) == slot, 1.0, 0.0).astype(bf16)
    data = jnp.where(live, updates_ref[...], 0.0)
    local_row = (rows - owner * own_rows).astype(f32)
    tail = jnp.where(lax.broadcasted_iota(jnp.int32, (width - columns, entries), 0) == 0, local_row, 0.0)
    data = jnp.concatenate([data, tail], axis=0)
    packed = jnp.zeros((slots, width), f32)
    for piece in thirds_of(data):
        packed += lax.dot_general(choose, piece, lanes_contract, preferred_element_type=f32)
    packed_ref[...] = packed


def reduce_kernel(received_ref, right_ref, *reduced_refs):
    slots = received_ref.shape[0]
    batches, halves, sources, own_rows = right_ref.shape
    columns = batches * halves * sources
    received = received_ref[...]
    local_row = received[:, columns:columns + 1].astype(jnp.int32)
    place = jnp.where(lax.broadcasted_iota(jnp.int32, (slots, own_rows), 1) == local_row, 1.0, 0.0).astype(bf16)
    total = jnp.zeros((columns, own_rows), f32)
    for piece in thirds_of(received[:, :columns].T):
        total += jnp.dot(piece, place, preferred_element_type=f32)
    reduced = right_ref[...].reshape(columns, own_rows) - total
    share = sources // len(reduced_refs)
    for group in range(batches * halves):
        for chunk, reduced_ref in enumerate(reduced_refs):
            start = group * sources + chunk * share
            reduced_ref[group * share:(group + 1) * share, :] = reduced[start:start + share]


def product_kernel(sources, blocks_count, *refs):
    x_refs = refs[:blocks_count]
    k_ref, out_ref, total_ref = refs[blocks_count:]
    step = pl.program_id(0)
    parts, own_rows, width = k_ref.shape
    columns = out_ref.shape[0]
    x = jnp.concatenate([x_refs[0][i] for i in range(x_refs[0].shape[0])], axis=1)
    for x_ref in x_refs[1:]:
        x -= jnp.concatenate([x_ref[i] for i in range(x_ref.shape[0])], axis=1)
    k = k_ref[...].reshape(parts * own_rows, width)
    x_high, x_low = halves_of(x)
    k_high, k_low = halves_of(k)
    both = lax.dot_general(jnp.concatenate([x_high, x_low], axis=0), k_high, lanes_contract, preferred_element_type=f32)
    part = both[:columns] + both[columns:] + lax.dot_general(x_high, k_low, lanes_contract, preferred_element_type=f32)

    @pl.when(step == 0)
    def _():
        total_ref[...] = part

    @pl.when(step > 0)
    def _():
        total_ref[...] += part

    @pl.when(step == pl.num_programs(0) - 1)
    def _():
        for batch in range(columns // (2 * sources)):
            real = pl.ds(batch * 2 * sources, sources)
            imag = pl.ds((batch * 2 + 1) * sources, sources)
            out_ref[real, :] = total_ref[real, :own_rows] - total_ref[imag, own_rows:]
            out_ref[imag, :] = total_ref[imag, :own_rows] + total_ref[real, own_rows:]


def complex_apply(matrix, blocks, sources):
    parts, own_rows, full_rows = matrix.shape
    count, columns, block = blocks[0].shape
    per_step = min(count, max(1, 512 // block))
    width = per_step * block
    return pl.pallas_call(
        functools.partial(product_kernel, sources, len(blocks)),
        grid=(full_rows // width,),
        in_specs=[pl.BlockSpec((per_step, columns, block), lambda i: (i, 0, 0)) for _ in blocks]
        + [pl.BlockSpec((parts, own_rows, width), lambda i: (0, 0, i))],
        out_specs=pl.BlockSpec((columns, own_rows), lambda i: (0, 0)),
        out_shape=jax.ShapeDtypeStruct((columns, own_rows), f32),
        scratch_shapes=[pltpu.VMEM((columns, parts * own_rows), f32)],
        compiler_params=kernel_params(),
        cost_estimate=pl.CostEstimate(flops=6 * columns * parts * own_rows * full_rows, bytes_accessed=4 * matrix.size, transcendentals=0),
    )(*blocks, matrix)


def gather_blocks(reduced):
    columns, own_rows = reduced.shape
    gathered = lax.all_gather(reduced, "tile", axis=0, tiled=False)
    if own_rows % 128 == 0:
        return gathered
    block = 256
    whole = gathered.transpose(1, 0, 2).reshape(columns, -1, block)
    return whole.transpose(1, 0, 2)


def body(right_side, diag_inverse, coupling, updates, update_rows, tile_counts):
    batches, halves, sources, own_rows = right_side.shape
    chain_size = lax.axis_size("chain")
    tile_size = lax.axis_size("tile")
    entries, columns = updates.shape
    tile_rows = entries // tile_counts.shape[0]
    cap = 2 * entries // tile_size
    slots = tile_size * cap
    width = -(-(columns + 1) // 128) * 128
    share = sources // CHUNKS
    vmem = pl.BlockSpec(memory_space=pltpu.VMEM)
    smem = pl.BlockSpec(memory_space=pltpu.SMEM)
    packed = pl.pallas_call(
        functools.partial(pack_kernel, own_rows, cap, tile_rows),
        in_specs=[smem, vmem, vmem],
        out_specs=vmem,
        out_shape=jax.ShapeDtypeStruct((slots, width), f32),
        compiler_params=kernel_params(),
    )(tile_counts, update_rows[None, :], updates.T)
    received = lax.all_to_all(packed.reshape(tile_size, cap, width), "tile", 0, 0, tiled=False).reshape(slots, width)
    reduced = pl.pallas_call(
        reduce_kernel,
        in_specs=[vmem, vmem],
        out_specs=[vmem] * CHUNKS,
        out_shape=[jax.ShapeDtypeStruct((columns // CHUNKS, own_rows), f32)] * CHUNKS,
        compiler_params=kernel_params(),
    )(received, right_side)
    onward = [(i, i + 1) for i in range(chain_size - 1)]
    own = [gather_blocks(chunk) for chunk in reduced]
    state = [[blocks] for blocks in own]
    for _ in range(chain_size - 1):
        for chunk in range(CHUNKS):
            carried = complex_apply(coupling, state[chunk], share)
            state[chunk] = [own[chunk], gather_blocks(lax.ppermute(carried, "chain", onward))]
    pieces = [complex_apply(diag_inverse, blocks, share).reshape(batches, halves, share, own_rows) for blocks in state]
    return jnp.concatenate(pieces, axis=2)


def solution(mesh):
    in_specs = (
        P(None, None, None, ("chain", "tile")),
        P(None, ("chain", "tile"), None),
        P(None, ("chain", "tile"), None),
        P(("chain", "tile"), None),
        P(("chain", "tile")),
        P(("chain", "tile")),
    )
    out_specs = P(None, None, None, ("chain", "tile"))
    return jax.shard_map(body, mesh=mesh, in_specs=in_specs, out_specs=out_specs, check_vma=False)
```

time: 162 us -> 213 us (1.31)
  waiting for transfers between devices: 94.5 us -> 127 us
  Pallas kernels: 11.8 us -> 39.6 us
  local copies, waits for them, and re-layouts: 14.7 us -> 1.28 us
  starting transfers between devices: 3.42 us -> 6.85 us
    all_gather x2 -> x4, waiting for transfers between devices: 89.9 us -> 121 us  [gather_blocks(): gathered = lax.all_gather(reduced, 'tile', axis=0, tiled=False)]
    pallas_call x4 -> x6, Pallas kernels: 11.8 us -> 39.6 us  [the longest x4 35.1 us: complex_apply(): pl.pallas_call(functools.partial(product_kernel, sources, len(blocks)), g...]
    unnamed x15 -> x6, local copies, waits for them, and re-layouts: 13.9 us -> 1.28 us
    ppermute x1 -> x2, starting transfers between devices: 3.38 us -> 6.73 us  [body(): lax.ppermute(carried, 'chain', onward)]
    ppermute x1 -> x2, waiting for transfers between devices: 4.54 us -> 5.55 us  [body(): lax.ppermute(carried, 'chain', onward)]
  transfers between devices with their start and end apart: 3 -> 6, of which waited for: 3 -> 6; matrix products, arithmetic and copies ran while one was open for 0% -> 0% of each run, Pallas kernels for 0% -> 12%
where the time goes in v2:
time: 213 us; the launch traced here: 212 us
  waiting for transfers between devices  127 us (60%)
  Pallas kernels  39.6 us (19%)
  blocking collectives  22 us (10%)
  between operations  13.1 us (6%)
  starting transfers between devices  6.85 us (3%)
    all_gather x4, waiting for transfers between devices, gather_blocks(): gathered = lax.all_gather(reduced, 'tile', axis=0, tiled=False)  121 us
    pallas_call x4, Pallas kernels, complex_apply(): pl.pallas_call(functools.partial(product_kernel, sources, len(blocks)), g...  35.1 us
    all_to_all x1, blocking collectives, body(): lax.all_to_all(packed.reshape(tile_size, cap, width), 'tile', 0, 0, tiled...  22 us
    ppermute x2, starting transfers between devices, body(): lax.ppermute(carried, 'chain', onward)  6.73 us
    ppermute x2, waiting for transfers between devices, body(): lax.ppermute(carried, 'chain', onward)  5.55 us
  transfers between devices with their start and end apart: 6, of which 6 were waited for; matrix products, arithmetic and copies ran while one was open for 0% of the time, Pallas kernels for 12%

profile of v2, /device:TPU:0, one launch (start us, length us, event | category | flops | bytes accessed | tf_op | source)
XLA Modules:
  0.0 211.8 jit_solution(3719411702748032353)
XLA Ops:
  6.5 0.0 all-gather.9.cloned.1.call-start
  6.5 2.2 %shard_map.64 = f32[512,256]{1,0:T(8,128)} custom-call(s32[2]{0:T(128)} %counts_ref.1, s32[1,256]{1,0:T(1,128)} %bitcast.21, f32[192,256]{1,0:T(8,128)} %bitcast.20), custom_call_target="tpu_custom_call" | custom-call | tf_op jit(solution)/shard_map/pallas_call | solution.py:148
  8.8 22.0 %all_to_all.5 = f32[16,32,256]{2,1,0:T(8,128)} all-to-all(f32[16,32,256]{2,1,0:T(8,128)} %bitcast.15), channel_id=1, replica_groups=mesh['chain'=2,'tile'=16] {'tile'}, dimensions={0} | all-to-all | bytes 1048576 | tf_op jit(solution)/shard_map/all_to_all | solution.py:155
  30.7 2.3 %shard_map.65 = (f32[96,256]{1,0:T(8,128)}, f32[96,256]{1,0:T(8,128)}) custom-call(f32[512,256]{1,0:T(8,128)} %bitcast.14, f32[3,2,32,256]{3,2,1,0:T(8,128)} %right_ref.1), custom_call_target="tpu_custom_call" | custom-call | tf_op jit(solution)/shard_map/pallas_call | solution.py:156
  33.0 0.0 all-gather.9.cloned.1.call-update
  33.0 0.0 all-gather.13.cloned.1.call-start
  33.1 0.7 all-gather.13.cloned.1.call-update
  33.8 0.0 all-gather.11.cloned.1.call-start
  33.8 38.4 %all-gather.9.cloned.1.call-done = f32[1536,256]{1,0:T(8,128)} async-done(((f32[96,256]{1,0:T(8,128)}), f32[1536,256]{1,0:T(8,128)}) %all-gather.9.cloned.1.call-update) | async-done | bytes 1572880 | tf_op jit(solution)/shard_map/all_gather | solution.py:128
  72.3 8.6 %shard_map.66 = f32[96,256]{1,0:T(8,128)} custom-call(f32[16,96,256]{2,1,0:T(8,128)} %bitcast.10, f32[2,256,4096]{2,1,0:T(8,128)} %refs_1_.3), custom_call_target="tpu_custom_call" | custom-call | flops 1207959552 | bytes 8388608 | tf_op jit(solution)/shard_map/pallas_call | solution.py:113
  80.9 3.4 %collective-permute-start = (f32[96,256]{1,0:T(8,128)}, f32[96,256]{1,0:T(8,128)S(1)}, u32[]{:S(2)}, u32[]{:S(2)}) collective-permute-start(f32[96,256]{1,0:T(8,128)} %shard_map.66), channel_id=1, source_target_pairs={{0,16},{1,17},{2,18},{3,19},{4,20},{5,21},{6,22},{7,23},{8,24},{9,... | collective-permute-start | bytes 294920 | tf_op jit(solution)/shard_map/ppermute | solution.py:169
  84.2 2.8 %collective-permute-done = f32[96,256]{1,0:T(8,128)S(1)} collective-permute-done((f32[96,256]{1,0:T(8,128)}, f32[96,256]{1,0:T(8,128)S(1)}, u32[]{:S(2)}, u32[]{:S(2)}) %collective-permute-start) | collective-permute-done | bytes 98336 | tf_op jit(solution)/shard_map/ppermute | solution.py:169
  87.0 0.0 copy-start.1
  87.0 0.6 copy-done.1
  87.6 0.0 all-gather.11.cloned.1.call-update
  87.7 0.0 all-gather.15.cloned.1.call-start
  87.7 25.4 %all-gather.13.cloned.1.call-done = f32[1536,256]{1,0:T(8,128)} async-done(((f32[96,256]{1,0:T(8,128)}), f32[1536,256]{1,0:T(8,128)}) %all-gather.13.cloned.1.call-update) | async-done | bytes 1572880 | tf_op jit(solution)/shard_map/all_gather | solution.py:128
  113.1 8.6 %shard_map.68 = f32[96,256]{1,0:T(8,128)} custom-call(f32[16,96,256]{2,1,0:T(8,128)} %bitcast.12, f32[2,256,4096]{2,1,0:T(8,128)} %refs_1_.3), custom_call_target="tpu_custom_call" | custom-call | flops 1207959552 | bytes 8388608 | tf_op jit(solution)/shard_map/pallas_call | solution.py:113
  121.7 3.4 %collective-permute-start.1 = (f32[96,256]{1,0:T(8,128)}, f32[96,256]{1,0:T(8,128)S(1)}, u32[]{:S(2)}, u32[]{:S(2)}) collective-permute-start(f32[96,256]{1,0:T(8,128)} %shard_map.68), channel_id=1, source_target_pairs={{0,16},{1,17},{2,18},{3,19},{4,20},{5,21},{6,22},{7,23},{8,24},{9,... | collective-permute-start | bytes 294920 | tf_op jit(solution)/shard_map/ppermute | solution.py:169
  125.1 2.8 %collective-permute-done.1 = f32[96,256]{1,0:T(8,128)S(1)} collective-permute-done((f32[96,256]{1,0:T(8,128)}, f32[96,256]{1,0:T(8,128)S(1)}, u32[]{:S(2)}, u32[]{:S(2)}) %collective-permute-start.1) | collective-permute-done | bytes 98336 | tf_op jit(solution)/shard_map/ppermute | solution.py:169
  127.8 0.0 copy-start.2
  127.9 0.6 copy-done.2
  128.5 0.0 all-gather.15.cloned.1.call-update
  128.5 25.4 %all-gather.11.cloned.1.call-done = f32[1536,256]{1,0:T(8,128)} async-done(((f32[96,256]{1,0:T(8,128)}), f32[1536,256]{1,0:T(8,128)}) %all-gather.11.cloned.1.call-update) | async-done | bytes 1572880 | tf_op jit(solution)/shard_map/all_gather | solution.py:128
  153.9 8.9 %shard_map.67 = f32[96,256]{1,0:T(8,128)} custom-call(f32[16,96,256]{2,1,0:T(8,128)} %bitcast.11, f32[16,96,256]{2,1,0:T(8,128)} %bitcast.16, f32[2,256,4096]{2,1,0:T(8,128)} %refs_2_.3), custom_call_target="tpu_custom_call" | custom-call | flops 1207959552 | bytes 8388608 | tf_op jit(solution)/shard_map/pallas_call | solution.py:113
  162.9 31.8 %all-gather.15.cloned.1.call-done = f32[1536,256]{1,0:T(8,128)} async-done(((f32[96,256]{1,0:T(8,128)}), f32[1536,256]{1,0:T(8,128)}) %all-gather.15.cloned.1.call-update) | async-done | bytes 1572880 | tf_op jit(solution)/shard_map/all_gather | solution.py:128
  194.7 0.0 copy-start
  194.7 9.0 %shard_map.69 = f32[96,256]{1,0:T(8,128)} custom-call(f32[16,96,256]{2,1,0:T(8,128)} %bitcast.13, f32[16,96,256]{2,1,0:T(8,128)} %bitcast.17, f32[2,256,4096]{2,1,0:T(8,128)} %refs_2_.3), custom_call_target="tpu_custom_call" | custom-call | flops 1207959552 | bytes 8388608 | tf_op jit(solution)/shard_map/pallas_call | solution.py:113
  203.6 0.0 copy-done
  203.6 1.6 pad_maximum_fusion
Async XLA Ops:
  6.5 65.7 %all-gather.9.cloned.1.call-start = ((), (), s32[]{:S(2)}) async-start(), calls=%async_computation.1 | async-start | bytes 1671168 | tf_op jit(solution)/shard_map/all_gather | solution.py:128
  33.0 80.1 %all-gather.13.cloned.1.call-start = ((), (), s32[]{:S(2)}) async-start(), calls=%async_computation.3 | async-start | bytes 1671168 | tf_op jit(solution)/shard_map/all_gather | solution.py:128
  33.8 120.2 %all-gather.11.cloned.1.call-start = ((), (), s32[]{:S(2)}) async-start(), calls=%async_computation.2 | async-start | bytes 1671168 | tf_op jit(solution)/shard_map/all_gather | solution.py:128
  80.9 6.1 %collective-permute-start = (f32[96,256]{1,0:T(8,128)}, f32[96,256]{1,0:T(8,128)S(1)}, u32[]{:S(2)}, u32[]{:S(2)}) collective-permute-start(f32[96,256]{1,0:T(8,128)} %shard_map.66), channel_id=1, source_target_pairs={{0,16},{1,17},{2,18},{3,19},{4,20},{5,21},{6,22},{7,23},{8,24},{9,... | collective-permute-start | bytes 294920 | tf_op jit(solution)/shard_map/ppermute | solution.py:169
  87.0 0.6 copy-start.1
  87.7 107.0 %all-gather.15.cloned.1.call-start = ((), (), s32[]{:S(2)}) async-start(), calls=%async_computation.4 | async-start | bytes 1671168 | tf_op jit(solution)/shard_map/all_gather | solution.py:128
  121.7 6.1 %collective-permute-start.1 = (f32[96,256]{1,0:T(8,128)}, f32[96,256]{1,0:T(8,128)S(1)}, u32[]{:S(2)}, u32[]{:S(2)}) collective-permute-start(f32[96,256]{1,0:T(8,128)} %shard_map.68), channel_id=1, source_target_pairs={{0,16},{1,17},{2,18},{3,19},{4,20},{5,21},{6,22},{7,23},{8,24},{9,... | collective-permute-start | bytes 294920 | tf_op jit(solution)/shard_map/ppermute | solution.py:169
  127.8 0.6 copy-start.2
  194.7 9.0 %copy-start = (f32[96,256]{1,0:T(8,128)S(1)}, f32[96,256]{1,0:T(8,128)}, u32[]{:S(2)}) copy-start(f32[96,256]{1,0:T(8,128)} %shard_map.67) | copy-start | bytes 294916
Sparse Core Ops, SparseCore 0:
  33.1 39.0 all-gather.8
  74.5 38.5 all-gather.12
  115.4 38.5 all-gather.10
  156.1 38.5 all-gather.14

commit v3 on v2

v3 whole, which is shorter than its diff:
```python
import functools

import jax
import jax.numpy as jnp
from jax import lax
from jax.experimental import pallas as pl
from jax.experimental.pallas import tpu as pltpu
from jax.sharding import PartitionSpec as P

MIB = 1 << 20
AHEAD = 3
f32 = jnp.float32
bf16 = jnp.bfloat16
lanes_contract = (((1,), (1,)), ((), ()))


def halves_of(value):
    high = value.astype(bf16)
    return high, (value - high.astype(f32)).astype(bf16)


def thirds_of(value):
    high = value.astype(bf16)
    rest = value - high.astype(f32)
    middle = rest.astype(bf16)
    return high, middle, (rest - middle.astype(f32)).astype(bf16)


def kernel_params():
    return pltpu.CompilerParams(vmem_limit_bytes=56 * MIB)


def pack_kernel(own_rows, cap, tile_rows, counts_ref, rows_ref, updates_ref, packed_ref):
    columns, entries = updates_ref.shape
    slots, width = packed_ref.shape
    entry = lax.broadcasted_iota(jnp.int32, (1, entries), 1)
    live = jnp.zeros((1, entries), jnp.bool_)
    for tile in range(entries // tile_rows):
        start = tile * tile_rows
        live = live | ((entry >= start) & (entry < start + counts_ref[tile]))
    rows = rows_ref[...]
    owner = rows // own_rows
    lane_owner = jnp.broadcast_to(owner.astype(f32), (entries, entries))
    earlier = lax.broadcasted_iota(jnp.int32, (entries, entries), 0) < lax.broadcasted_iota(jnp.int32, (entries, entries), 1)
    rank = jnp.sum(jnp.where(earlier & (lane_owner.T == lane_owner), 1, 0), axis=0, keepdims=True)
    slot = owner * cap + rank
    choose = jnp.where(lax.broadcasted_iota(jnp.int32, (slots, entries), 0) == slot, 1.0, 0.0).astype(bf16)
    data = jnp.where(live, updates_ref[...], 0.0)
    local_row = (rows - owner * own_rows).astype(f32)
    tail = jnp.where(lax.broadcasted_iota(jnp.int32, (width - columns, entries), 0) == 0, local_row, 0.0)
    data = jnp.concatenate([data, tail], axis=0)
    packed = jnp.zeros((slots, width), f32)
    for piece in thirds_of(data):
        packed += lax.dot_general(choose, piece, lanes_contract, preferred_element_type=f32)
    packed_ref[...] = packed


def reduce_kernel(received_ref, right_ref, reduced_ref):
    slots = received_ref.shape[0]
    columns, own_rows = reduced_ref.shape
    received = received_ref[...]
    local_row = received[:, columns:columns + 1].astype(jnp.int32)
    place = jnp.where(lax.broadcasted_iota(jnp.int32, (slots, own_rows), 1) == local_row, 1.0, 0.0).astype(bf16)
    total = jnp.zeros((columns, own_rows), f32)
    for piece in thirds_of(received[:, :columns].T):
        total += jnp.dot(piece, place, preferred_element_type=f32)
    reduced_ref[...] = right_ref[...] - total


def product_kernel(sources, plain, counts, order_ref, *refs):
    sets = 1 if plain else 2
    x_refs = refs[:len(counts)]
    own_refs = refs[len(counts):-6]
    k_ref, out_ref, x_buf, k_buf, total_ref, sems = refs[-6:]
    parts, own_rows, block = k_buf.shape[1:]
    columns = out_ref.shape[0]
    count = sum(counts)
    place = [(i, j) for i in range(len(counts)) for j in range(counts[i])]

    def copies(q):
        i, j = place[q]
        tile = order_ref[q]
        made = [
            (x_refs[i].at[j], x_buf.at[0, q], sems.at[0, q]),
            (k_ref.at[:, :, pl.ds(pl.multiple_of(tile * block, block), block)], k_buf.at[q], sems.at[1, q]),
        ]
        if not plain:
            made.append((own_refs[i * len(own_refs) // len(counts)].at[tile // 2], x_buf.at[1, q], sems.at[2, q]))
        return [pltpu.make_async_copy(*each) for each in made]

    for q in range(min(count, 2 * AHEAD)):
        for copy in copies(q):
            copy.start()
    total = None
    for first in range(0, count, 2):
        pair = range(first, min(first + 2, count))
        for q in pair:
            if q + 2 * AHEAD < count:
                for copy in copies(q + 2 * AHEAD):
                    copy.start()
        for q in pair:
            for copy in copies(q):
                copy.wait()
        x = jnp.concatenate([x_buf[0, q] if plain else x_buf[1, q] - x_buf[0, q] for q in pair], axis=1)
        k = jnp.concatenate([k_buf[q].reshape(parts * own_rows, block) for q in pair], axis=1)
        x_high, x_low = halves_of(x)
        k_high, k_low = halves_of(k)
        both = lax.dot_general(jnp.concatenate([x_high, x_low], axis=0), k_high, lanes_contract, preferred_element_type=f32)
        part = both[:columns] + both[columns:] + lax.dot_general(x_high, k_low, lanes_contract, preferred_element_type=f32)
        if first == 0:
            total_ref[...] = part
        else:
            total_ref[...] += part
    for batch in range(columns // (2 * sources)):
        real = pl.ds(batch * 2 * sources, sources)
        imag = pl.ds((batch * 2 + 1) * sources, sources)
        out_ref[real, :] = total_ref[real, :own_rows] - total_ref[imag, own_rows:]
        out_ref[imag, :] = total_ref[imag, :own_rows] + total_ref[real, own_rows:]


def complex_apply(matrix, order, blocks, own, sources):
    parts, own_rows, full_rows = matrix.shape
    columns, block = blocks[0].shape[1:]
    counts = [each.shape[0] for each in blocks]
    plain = len(own) == 0
    anywhere = pl.BlockSpec(memory_space=pl.ANY)
    count = sum(counts)
    return pl.pallas_call(
        functools.partial(product_kernel, sources, plain, counts),
        in_specs=[pl.BlockSpec(memory_space=pltpu.SMEM)] + [anywhere] * (len(blocks) + len(own) + 1),
        out_specs=pl.BlockSpec(memory_space=pltpu.VMEM),
        out_shape=jax.ShapeDtypeStruct((columns, own_rows), f32),
        scratch_shapes=[
            pltpu.VMEM((1 if plain else 2, count, columns, block), f32),
            pltpu.VMEM((count, parts, own_rows, block), f32),
            pltpu.VMEM((columns, parts * own_rows), f32),
            pltpu.SemaphoreType.DMA((3, count)),
        ],
        compiler_params=kernel_params(),
        cost_estimate=pl.CostEstimate(flops=6 * columns * parts * own_rows * full_rows, bytes_accessed=4 * matrix.size, transcendentals=0),
    )(order, *blocks, *own, matrix)


def swap(value, distance, size):
    return lax.ppermute(value, "tile", [(i, i ^ distance) for i in range(size)])


def solve_paired(reduced, diag_inverse, coupling, sources):
    chain_size = lax.axis_size("chain")
    tile_size = lax.axis_size("tile")
    layers = tile_size // 4
    me = lax.axis_index("tile")
    core, row, layer = me % 2, me // 2 % 2, me // 4
    chips = tile_size // 2
    groups = [[2 * chip + side for chip in range(chips)] for side in range(2)]
    mine = lax.all_gather(reduced, "tile", axis=0, tiled=False, axis_index_groups=groups)
    own = [mine, swap(mine, 1, tile_size)]
    chip_order = 2 * jnp.arange(chips, dtype=jnp.int32)
    order = jnp.concatenate([chip_order + core, chip_order + 1 - core])
    blocks, others = own, []
    layer_order = (layer - jnp.arange(layers, dtype=jnp.int32)) % layers * 4
    near = layer_order + row * 2
    far = layer_order + (1 - row) * 2
    hop_order = jnp.concatenate([near + core, far + core, near + 1 - core, far + 1 - core])
    for _ in range(chain_size - 1):
        carried = complex_apply(coupling, order, blocks, others, sources)
        arrived = []
        for by in range(layers):
            pairs = [
                (c * tile_size + t, (c + 1) * tile_size + (t + 4 * by) % tile_size)
                for c in range(chain_size - 1)
                for t in range(tile_size)
            ]
            arrived.append(lax.ppermute(carried, ("chain", "tile"), pairs))
        line = jnp.stack(arrived)
        across = swap(line, 2, tile_size)
        blocks = [line, across, swap(line, 1, tile_size), swap(across, 1, tile_size)]
        order, others = hop_order, own
    return complex_apply(diag_inverse, order, blocks, others, sources)


def solve_flat(reduced, diag_inverse, coupling, sources):
    chain_size = lax.axis_size("chain")
    columns = reduced.shape[0]
    full_rows = diag_inverse.shape[2]
    block = min(256, full_rows)
    order = jnp.arange(full_rows // block, dtype=jnp.int32)
    onward = [(i, i + 1) for i in range(chain_size - 1)]

    def gathered(value):
        whole = lax.all_gather(value, "tile", axis=1, tiled=True)
        return [whole.reshape(columns, -1, block).transpose(1, 0, 2)]

    current = reduced
    for _ in range(chain_size - 1):
        carried = complex_apply(coupling, order, gathered(current), [], sources)
        current = reduced - lax.ppermute(carried, "chain", onward)
    return complex_apply(diag_inverse, order, gathered(current), [], sources)


def body(right_side, diag_inverse, coupling, updates, update_rows, tile_counts):
    batches, halves, sources, own_rows = right_side.shape
    tile_size = lax.axis_size("tile")
    entries, columns = updates.shape
    tile_rows = entries // tile_counts.shape[0]
    cap = 2 * entries // tile_size
    slots = tile_size * cap
    width = -(-(columns + 1) // 128) * 128
    vmem = pl.BlockSpec(memory_space=pltpu.VMEM)
    smem = pl.BlockSpec(memory_space=pltpu.SMEM)
    packed = pl.pallas_call(
        functools.partial(pack_kernel, own_rows, cap, tile_rows),
        in_specs=[smem, vmem, vmem],
        out_specs=vmem,
        out_shape=jax.ShapeDtypeStruct((slots, width), f32),
        compiler_params=kernel_params(),
    )(tile_counts, update_rows[None, :], updates.T)
    received = lax.all_to_all(packed.reshape(tile_size, cap, width), "tile", 0, 0, tiled=False).reshape(slots, width)
    reduced = pl.pallas_call(
        reduce_kernel,
        in_specs=[vmem, vmem],
        out_specs=vmem,
        out_shape=jax.ShapeDtypeStruct((columns, own_rows), f32),
        compiler_params=kernel_params(),
    )(received, right_side.reshape(columns, own_rows))
    paired = own_rows % 128 == 0 and tile_size % 8 == 0
    solve = solve_paired if paired else solve_flat
    return solve(reduced, diag_inverse, coupling, sources).reshape(right_side.shape)


def solution(mesh):
    in_specs = (
        P(None, None, None, ("chain", "tile")),
        P(None, ("chain", "tile"), None),
        P(None, ("chain", "tile"), None),
        P(("chain", "tile"), None),
        P(("chain", "tile")),
        P(("chain", "tile")),
    )
    out_specs = P(None, None, None, ("chain", "tile"))
    return jax.shard_map(body, mesh=mesh, in_specs=in_specs, out_specs=out_specs, check_vma=False)
```

time: 213 us -> 150 us (0.70)
  the two profiles are of different devices: /device:TPU:0 before, /device:TPU:3 now
where the time goes in v3:
time: 150 us
  waiting for transfers between devices  80.8 us (54%)
  Pallas kernels  21.2 us (14%)
  blocking collectives  20.7 us (14%)
  between operations  13.5 us (9%)
  starting transfers between devices  10.4 us (7%)
  local copies, waits for them, and re-layouts  2.05 us (1%)
    all_gather x1, waiting for transfers between devices, solve_paired(): lax.all_gather(reduced, 'tile', axis=0, tiled=False, axis_index_groups=gr...  42.9 us
    all_to_all x1, blocking collectives, body(): lax.all_to_all(packed.reshape(tile_size, cap, width), 'tile', 0, 0, tiled...  20.7 us
    ppermute x4, waiting for transfers between devices, swap(): return lax.ppermute(value, 'tile', [(i, i ^ distance) for i in range(size)])  19.9 us
    ppermute x4, waiting for transfers between devices, solve_paired(): arrived.append(lax.ppermute(carried, ('chain', 'tile'), pairs))  17.9 us
    pallas_call x2, Pallas kernels, complex_apply(): pl.pallas_call(functools.partial(product_kernel, sources, plain, counts),...  16.7 us
    ppermute x4, starting transfers between devices, swap(): return lax.ppermute(value, 'tile', [(i, i ^ distance) for i in range(size)])  5.24 us
    ppermute x4, starting transfers between devices, solve_paired(): arrived.append(lax.ppermute(carried, ('chain', 'tile'), pairs))  5.17 us
  transfers between devices with their start and end apart: 9, of which 6 were waited for; matrix products, arithmetic and copies ran while one was open for 1% of the time, Pallas kernels for 0%

profile of v3, /device:TPU:3, one launch (start us, length us, event | category | flops | bytes accessed | tf_op | source)
XLA Modules:
  0.0 149.9 jit_solution(4482537984910132897)
XLA Ops:
  6.5 0.0 all-gather.3.cloned.1.call-start
  6.5 2.2 %shard_map.64 = f32[512,256]{1,0:T(8,128)} custom-call(s32[2]{0:T(128)} %counts_ref.1, s32[1,256]{1,0:T(1,128)} %bitcast.22, f32[192,256]{1,0:T(8,128)} %bitcast.21), custom_call_target="tpu_custom_call" | custom-call | tf_op jit(solution)/shard_map/pallas_call | solution.py:211
  8.8 20.7 %all_to_all.5 = f32[16,32,256]{2,1,0:T(8,128)} all-to-all(f32[16,32,256]{2,1,0:T(8,128)} %bitcast.15), channel_id=1, replica_groups=mesh['chain'=2,'tile'=16] {'tile'}, dimensions={0} | all-to-all | bytes 1048576 | tf_op jit(solution)/shard_map/all_to_all | solution.py:218
  29.5 2.3 %shard_map.65 = f32[192,256]{1,0:T(8,128)} custom-call(f32[512,256]{1,0:T(8,128)} %bitcast.14, f32[192,256]{1,0:T(8,128)} %bitcast.16), custom_call_target="tpu_custom_call" | custom-call | tf_op jit(solution)/shard_map/pallas_call | solution.py:219
  31.7 0.0 all-gather.3.cloned.1.call-update
  31.7 42.9 %all-gather.3.cloned.1.call-done = f32[1536,256]{1,0:T(8,128)} async-done(((f32[192,256]{1,0:T(8,128)}), f32[1536,256]{1,0:T(8,128)}) %all-gather.3.cloned.1.call-update) | async-done | bytes 1572880 | tf_op jit(solution)/shard_map/all_gather | solution.py:156
  74.7 1.3 collective-permute-start
  76.0 0.7 pad_add_fusion.1.order_ref
  76.6 2.6 %collective-permute-done.refs_1_.refs_5_ = f32[8,192,256]{2,1,0:T(8,128)S(1)} collective-permute-done((f32[8,192,256]{2,1,0:T(8,128)}, f32[8,192,256]{2,1,0:T(8,128)S(1)}, u32[]{:S(2)}, u32[]{:S(2)}) %collective-permute-start) | collective-permute-done | bytes 1572896 | tf_op jit(solution)/shard_map/ppermute | solution.py:145
  79.2 0.0 copy-start
  79.2 1.1 copy-done
  80.4 8.3 %shard_map.66 = f32[192,256]{1,0:T(8,128)} custom-call(s32[16]{0:T(128)} %pad_add_fusion.1.order_ref, f32[8,192,256]{2,1,0:T(8,128)} %bitcast.12, f32[8,192,256]{2,1,0:T(8,128)} %copy-done, f32[2,256,4096]{2,1,0:T(8,128)} %refs_2_.1), custom_call_target="tpu_custom_call" | custom-call | flops 2415919104 | bytes 8388608 | tf_op jit(solution)/shard_map/pallas_call | solution.py:128
  88.6 1.3 collective-permute-start.4
  89.9 1.3 collective-permute-start.3
  91.2 1.3 collective-permute-start.2
  92.5 1.3 collective-permute-start.1
  93.8 3.9 %collective-permute-done.4 = f32[192,256]{1,0:T(8,128)S(1)} collective-permute-done((f32[192,256]{1,0:T(8,128)}, f32[192,256]{1,0:T(8,128)S(1)}, u32[]{:S(2)}, u32[]{:S(2)}) %collective-permute-start.4) | collective-permute-done | bytes 196640 | tf_op jit(solution)/shard_map/ppermute | solution.py:174
  97.8 14.0 %collective-permute-done.3 = f32[192,256]{1,0:T(8,128)S(1)} collective-permute-done((f32[192,256]{1,0:T(8,128)}, f32[192,256]{1,0:T(8,128)S(1)}, u32[]{:S(2)}, u32[]{:S(2)}) %collective-permute-start.3) | collective-permute-done | bytes 196640 | tf_op jit(solution)/shard_map/ppermute | solution.py:174
  111.7 0.0 collective-permute-done.2
  111.7 0.0 collective-permute-done.1
  111.7 0.1 pad_maximum_fusion.refs_0_
  111.8 0.0 copy-start.1
  111.8 0.3 collective-permute-start.5
  112.1 1.5 collective-permute-start.6
  113.6 16.1 %collective-permute-done.5.refs_1_ = f32[4,192,256]{2,1,0:T(8,128)S(1)} collective-permute-done((f32[4,192,256]{2,1,0:T(8,128)S(1)}, f32[4,192,256]{2,1,0:T(8,128)S(1)}, u32[]{:S(2)}, u32[]{:S(2)}) %collective-permute-start.5) | collective-permute-done | bytes 786464 | tf_op jit(solution)/shard_map/ppermute | solution.py:145
  129.7 0.0 copy-start.2
  129.7 2.1 %collective-permute-start.7 = (f32[4,192,256]{2,1,0:T(8,128)S(1)}, f32[4,192,256]{2,1,0:T(8,128)S(1)}, u32[]{:S(2)}, u32[]{:S(2)}) collective-permute-start(f32[4,192,256]{2,1,0:T(8,128)S(1)} %collective-permute-done.5.refs_1_), channel_id=1, source_target_pairs={{0,1},{1,0},{2,3},{3,2},{4,5},{5,4},{6,7},{7,6},{8,9},{9,8},{10,11... | collective-permute-start | bytes 2359304 | tf_op jit(solution)/shard_map/ppermute | solution.py:145
  131.9 0.6 pad_add_fusion.order_ref
  132.5 0.0 collective-permute-done.6.refs_2_
  132.5 0.0 copy-start.3
  132.5 1.3 collective-permute-done.7.refs_3_
  133.7 0.0 copy-done.1
  133.7 0.0 copy-done.2
  133.7 0.0 copy-done.3
  133.7 0.0 copy-start.4
  133.7 0.9 copy-done.4
  134.6 8.4 %shard_map.67 = f32[192,256]{1,0:T(8,128)} custom-call(s32[16]{0:T(128)} %pad_add_fusion.order_ref, f32[4,192,256]{2,1,0:T(8,128)} %copy-done.1, f32[4,192,256]{2,1,0:T(8,128)} %copy-done.2, f32[4,192,256]{2,1,0:T(8,128)} %copy-done.3, f32[4,192,256]{2,1,0:T(8,128)} %copy-done.4, f32[8,192,256]{2,1,0:T(8,128)} %bitcast.13, f32[8,192,256]{2,1,0:T(8,128)} %copy-done, ...), custom_call_target="tpu_custom_call" | custom-call | flops 2415919104 | bytes 8388608 | tf_op jit(solution)/shard_map/pallas_call | solution.py:128
  (3 shorter events, 0.0 us)
Async XLA Ops:
  6.5 68.1 %all-gather.3.cloned.1.call-start = ((), (), s32[]{:S(2)}) async-start(), calls=%async_computation.1 | async-start | bytes 1769472 | tf_op jit(solution)/shard_map/all_gather | solution.py:156
  74.7 4.5 %collective-permute-start = (f32[8,192,256]{2,1,0:T(8,128)}, f32[8,192,256]{2,1,0:T(8,128)S(1)}, u32[]{:S(2)}, u32[]{:S(2)}) collective-permute-start(f32[8,192,256]{2,1,0:T(8,128)} %bitcast.11), channel_id=1, source_target_pairs={{0,1},{1,0},{2,3},{3,2},{4,5},{5,4},{6,7},{7,6},{8,9},{9,8},{10,11... | collective-permute-start | bytes 4718600 | tf_op jit(solution)/shard_map/ppermute | solution.py:145
  79.2 1.1 copy-start
  88.6 9.1 %collective-permute-start.4 = (f32[192,256]{1,0:T(8,128)}, f32[192,256]{1,0:T(8,128)S(1)}, u32[]{:S(2)}, u32[]{:S(2)}) collective-permute-start(f32[192,256]{1,0:T(8,128)} %shard_map.66), channel_id=1, source_target_pairs={{0,28},{1,29},{2,30},{3,31},{4,16},{5,17},{6,18},{7,19},{8,20},{9,... | collective-permute-start | bytes 589832 | tf_op jit(solution)/shard_map/ppermute | solution.py:174
  89.9 21.8 %collective-permute-start.3 = (f32[192,256]{1,0:T(8,128)}, f32[192,256]{1,0:T(8,128)S(1)}, u32[]{:S(2)}, u32[]{:S(2)}) collective-permute-start(f32[192,256]{1,0:T(8,128)} %shard_map.66), channel_id=1, source_target_pairs={{0,24},{1,25},{2,26},{3,27},{4,28},{5,29},{6,30},{7,31},{8,16},{9,... | collective-permute-start | bytes 589832 | tf_op jit(solution)/shard_map/ppermute | solution.py:174
  91.2 20.5 %collective-permute-start.2 = (f32[192,256]{1,0:T(8,128)}, f32[192,256]{1,0:T(8,128)S(1)}, u32[]{:S(2)}, u32[]{:S(2)}) collective-permute-start(f32[192,256]{1,0:T(8,128)} %shard_map.66), channel_id=1, source_target_pairs={{0,20},{1,21},{2,22},{3,23},{4,24},{5,25},{6,26},{7,27},{8,28},{9,... | collective-permute-start | bytes 589832 | tf_op jit(solution)/shard_map/ppermute | solution.py:174
  92.5 19.2 %collective-permute-start.1 = (f32[192,256]{1,0:T(8,128)}, f32[192,256]{1,0:T(8,128)S(1)}, u32[]{:S(2)}, u32[]{:S(2)}) collective-permute-start(f32[192,256]{1,0:T(8,128)} %shard_map.66), channel_id=1, source_target_pairs={{0,16},{1,17},{2,18},{3,19},{4,20},{5,21},{6,22},{7,23},{8,24},{9,... | collective-permute-start | bytes 589832 | tf_op jit(solution)/shard_map/ppermute | solution.py:174
  111.8 21.9 %copy-start.1 = (f32[4,192,256]{2,1,0:T(8,128)}, f32[4,192,256]{2,1,0:T(8,128)S(1)}, u32[]{:S(2)}) copy-start(f32[4,192,256]{2,1,0:T(8,128)S(1)} %pad_maximum_fusion.refs_0_) | copy-start | bytes 2359300
  111.8 17.9 %collective-permute-start.5 = (f32[4,192,256]{2,1,0:T(8,128)S(1)}, f32[4,192,256]{2,1,0:T(8,128)S(1)}, u32[]{:S(2)}, u32[]{:S(2)}) collective-permute-start(f32[4,192,256]{2,1,0:T(8,128)S(1)} %pad_maximum_fusion.refs_0_), channel_id=1, source_target_pairs={{0,2},{1,3},{2,0},{3,1},{4,6},{5,7},{6,4},{7,5},{8,10},{9,11},{10,... | collective-permute-start | bytes 2359304 | tf_op jit(solution)/shard_map/ppermute | solution.py:145
  112.1 20.3 %collective-permute-start.6 = (f32[4,192,256]{2,1,0:T(8,128)S(1)}, f32[4,192,256]{2,1,0:T(8,128)S(1)}, u32[]{:S(2)}, u32[]{:S(2)}) collective-permute-start(f32[4,192,256]{2,1,0:T(8,128)S(1)} %pad_maximum_fusion.refs_0_), channel_id=1, source_target_pairs={{0,1},{1,0},{2,3},{3,2},{4,5},{5,4},{6,7},{7,6},{8,9},{9,8},{10,11... | collective-permute-start | bytes 2359304 | tf_op jit(solution)/shard_map/ppermute | solution.py:145
  129.7 4.0 %copy-start.2 = (f32[4,192,256]{2,1,0:T(8,128)}, f32[4,192,256]{2,1,0:T(8,128)S(1)}, u32[]{:S(2)}) copy-start(f32[4,192,256]{2,1,0:T(8,128)S(1)} %collective-permute-done.5.refs_1_) | copy-start | bytes 2359300
  129.7 4.0 %collective-permute-start.7 = (f32[4,192,256]{2,1,0:T(8,128)S(1)}, f32[4,192,256]{2,1,0:T(8,128)S(1)}, u32[]{:S(2)}, u32[]{:S(2)}) collective-permute-start(f32[4,192,256]{2,1,0:T(8,128)S(1)} %collective-permute-done.5.refs_1_), channel_id=1, source_target_pairs={{0,1},{1,0},{2,3},{3,2},{4,5},{5,4},{6,7},{7,6},{8,9},{9,8},{10,11... | collective-permute-start | bytes 2359304 | tf_op jit(solution)/shard_map/ppermute | solution.py:145
  132.5 1.3 copy-start.3
  133.7 0.9 copy-start.4
Sparse Core Ops, SparseCore 0:
  31.9 42.7 all-gather.2

commit v4 on v2

v4 whole, which is shorter than its diff:
```python
import functools

import jax
import jax.numpy as jnp
from jax import lax
from jax.experimental import pallas as pl
from jax.experimental.pallas import tpu as pltpu
from jax.sharding import PartitionSpec as P

MIB = 1 << 20
f32 = jnp.float32
bf16 = jnp.bfloat16
lanes_contract = (((1,), (1,)), ((), ()))


def halves_of(value):
    high = value.astype(bf16)
    return high, (value - high.astype(f32)).astype(bf16)


def thirds_of(value):
    high = value.astype(bf16)
    rest = value - high.astype(f32)
    middle = rest.astype(bf16)
    return high, middle, (rest - middle.astype(f32)).astype(bf16)


def kernel_params():
    return pltpu.CompilerParams(vmem_limit_bytes=56 * MIB)


def pack_kernel(own_rows, cap, tile_rows, counts_ref, rows_ref, updates_ref, packed_ref):
    columns, entries = updates_ref.shape
    slots, width = packed_ref.shape
    entry = lax.broadcasted_iota(jnp.int32, (1, entries), 1)
    live = jnp.zeros((1, entries), jnp.bool_)
    for tile in range(entries // tile_rows):
        start = tile * tile_rows
        live = live | ((entry >= start) & (entry < start + counts_ref[tile]))
    rows = rows_ref[...]
    owner = rows // own_rows
    lane_owner = jnp.broadcast_to(owner.astype(f32), (entries, entries))
    earlier = lax.broadcasted_iota(jnp.int32, (entries, entries), 0) < lax.broadcasted_iota(jnp.int32, (entries, entries), 1)
    rank = jnp.sum(jnp.where(earlier & (lane_owner.T == lane_owner), 1, 0), axis=0, keepdims=True)
    slot = owner * cap + rank
    choose = jnp.where(lax.broadcasted_iota(jnp.int32, (slots, entries), 0) == slot, 1.0, 0.0).astype(bf16)
    data = jnp.where(live, updates_ref[...], 0.0)
    local_row = (rows - owner * own_rows).astype(f32)
    tail = jnp.where(lax.broadcasted_iota(jnp.int32, (width - columns, entries), 0) == 0, local_row, 0.0)
    data = jnp.concatenate([data, tail], axis=0)
    packed = jnp.zeros((slots, width), f32)
    for piece in thirds_of(data):
        packed += lax.dot_general(choose, piece, lanes_contract, preferred_element_type=f32)
    packed_ref[...] = packed


def reduce_kernel(received_ref, right_ref, *reduced_refs):
    slots = received_ref.shape[0]
    columns, own_rows = right_ref.shape
    received = received_ref[...]
    local_row = received[:, columns:columns + 1].astype(jnp.int32)
    place = jnp.where(lax.broadcasted_iota(jnp.int32, (slots, own_rows), 1) == local_row, 1.0, 0.0).astype(bf16)
    total = jnp.zeros((columns, own_rows), f32)
    for piece in thirds_of(received[:, :columns].T):
        total += jnp.dot(piece, place, preferred_element_type=f32)
    reduced = right_ref[...] - total
    start = 0
    for reduced_ref in reduced_refs:
        reduced_ref[...] = reduced[start:start + reduced_ref.shape[0]]
        start += reduced_ref.shape[0]


def split_kernel(k_ref, high_ref, low_ref):
    blocks, rows, block = high_ref.shape
    for i in range(blocks):
        high, low = halves_of(k_ref[:, :, i * block:(i + 1) * block].reshape(rows, block))
        high_ref[i] = high
        low_ref[i] = low


def split_blocks(matrix, block):
    parts, own_rows, full_rows = matrix.shape
    count = full_rows // block
    per_step = 4 if count % 4 == 0 else 1
    shape = jax.ShapeDtypeStruct((count, parts * own_rows, block), bf16)
    out_spec = pl.BlockSpec((per_step, parts * own_rows, block), lambda i: (i, 0, 0))
    return pl.pallas_call(
        split_kernel,
        grid=(count // per_step,),
        in_specs=[pl.BlockSpec((parts, own_rows, per_step * block), lambda i: (0, 0, i))],
        out_specs=[out_spec, out_spec],
        out_shape=[shape, shape],
        compiler_params=pltpu.CompilerParams(vmem_limit_bytes=12 * MIB),
        cost_estimate=pl.CostEstimate(flops=3 * matrix.size, bytes_accessed=8 * matrix.size, transcendentals=0),
    )(matrix)


def product_kernel(sources, layout, inputs, sets, order_ref, *refs):
    high_ref, low_ref = refs[inputs * sets:inputs * sets + 2]
    out_refs, total_ref = refs[inputs * sets + 2:-1], refs[-1]
    count, both_rows, block = high_ref.shape
    columns, own_rows = total_ref.shape[0], both_rows // 2
    per_step = 4 if count % 4 == 0 else 1

    def block_of(q):
        pieces = []
        for group in layout:
            which, place = group[q]
            value = refs[which][place]
            if sets == 2:
                value = refs[inputs + which][place] - value
            pieces.append(value)
        return jnp.concatenate(pieces, axis=0)

    for first in range(0, count, per_step):
        tiles = [order_ref[q] for q in range(first, first + per_step)]
        x_high, x_low = halves_of(jnp.concatenate([block_of(q) for q in range(first, first + per_step)], axis=1))
        k_high = jnp.concatenate([high_ref[tile] for tile in tiles], axis=1)
        k_low = jnp.concatenate([low_ref[tile] for tile in tiles], axis=1)
        both = lax.dot_general(jnp.concatenate([x_high, x_low], axis=0), k_high, lanes_contract, preferred_element_type=f32)
        part = both[:columns] + both[columns:] + lax.dot_general(x_high, k_low, lanes_contract, preferred_element_type=f32)
        if first == 0:
            total_ref[...] = part
        else:
            total_ref[...] += part
    start = 0
    for out_ref in out_refs:
        for first in range(0, out_ref.shape[0], 2 * sources):
            real = pl.ds(start + first, sources)
            imag = pl.ds(start + first + sources, sources)
            out_ref[first:first + sources, :] = total_ref[real, :own_rows] - total_ref[imag, own_rows:]
            out_ref[first + sources:first + 2 * sources, :] = total_ref[imag, :own_rows] + total_ref[real, own_rows:]
        start += out_ref.shape[0]


def complex_apply(split, order, layout, blocks, own, sources, shares):
    count, both_rows, block = split[0].shape
    vmem = pl.BlockSpec(memory_space=pltpu.VMEM)
    sets = 2 if own else 1
    arrays = list(blocks) + list(own)
    return pl.pallas_call(
        functools.partial(product_kernel, sources, layout, len(blocks), sets),
        in_specs=[pl.BlockSpec(memory_space=pltpu.SMEM)] + [vmem] * (len(arrays) + 2),
        out_specs=[vmem] * len(shares),
        out_shape=[jax.ShapeDtypeStruct((rows, both_rows // 2), f32) for rows in shares],
        scratch_shapes=[pltpu.VMEM((sum(shares), both_rows), f32)],
        compiler_params=pltpu.CompilerParams(vmem_limit_bytes=32 * MIB),
        cost_estimate=pl.CostEstimate(flops=6 * sum(shares) * both_rows * block * count, bytes_accessed=MIB, transcendentals=0),
    )(order, *arrays, *split)


def tied(value, to):
    return lax.optimization_barrier((value, to))[0]


def solve_paired(reduced, diag_inverse, coupling, sources):
    chain_size = lax.axis_size("chain")
    tile_size = lax.axis_size("tile")
    own_rows = reduced[0].shape[1]
    shares = [each.shape[0] for each in reduced]
    layers = tile_size // 4
    me = lax.axis_index("tile")
    core, row, layer = lax.rem(me, 2), lax.rem(lax.div(me, 2), 2), lax.div(me, 4)
    order = []
    for side in range(2):
        for across in range(2):
            for by in range(layers):
                from_layer = lax.rem(layer + layers - by, layers)
                from_row = row + across - 2 * row * across
                from_core = core + side - 2 * core * side
                order.append(from_layer * 4 + from_row * 2 + from_core)
    order = jnp.stack(order).astype(jnp.int32)
    places = [(side, across, by) for side in range(2) for across in range(2) for by in range(layers)]
    layout = [
        [(2 * side + across, (by,)) for side, across, by in places],
        [(4 + side, (by, across)) for side, across, by in places],
    ]

    def send(value, hop, target):
        if not hop:
            return lax.ppermute(value, "tile", [(t, target(t)) for t in range(tile_size)])
        pairs = [(c * tile_size + t, (c + 1) * tile_size + target(t)) for c in range(chain_size - 1) for t in range(tile_size)]
        return lax.ppermute(value, ("chain", "tile"), pairs)

    def gathered(first, second, hop, matrix):
        pair = [second if across == 0 and not hop else send(second, hop, lambda t: t ^ (2 * across)) for across in range(2)]
        line = [first if by == 0 and not hop else send(first, hop, lambda t: (t + 4 * by) % tile_size) for by in range(layers)]
        split = split_blocks(tied(matrix, first), own_rows)
        pair, line, split = lax.optimization_barrier((jnp.stack(pair), jnp.stack(line), split))
        far = send(line, False, lambda t: t ^ 2)
        rest = [pair if by == 0 else send(pair, False, lambda t: (t + 4 * by) % tile_size) for by in range(layers)]
        rest = jnp.stack(rest)
        held = [line, far]
        return held + [send(each, False, lambda t: t ^ 1) for each in held] + [rest, send(rest, False, lambda t: t ^ 1)], split

    own, split = gathered(*reduced, False, coupling if chain_size > 1 else diag_inverse)
    state, others = own, []
    coupling_split = split
    for step in range(chain_size - 1):
        carried = complex_apply(coupling_split, order, layout, state, others, sources, shares)
        state, split = gathered(*carried, True, diag_inverse if step == chain_size - 2 else coupling)
        others = own
    return complex_apply(split, order, layout, state, others, sources, [sum(shares)])[0]


def solve_flat(reduced, diag_inverse, coupling, sources):
    chain_size = lax.axis_size("chain")
    reduced = reduced[0]
    columns = reduced.shape[0]
    full_rows = diag_inverse.shape[2]
    block = min(256, full_rows)
    count = full_rows // block
    order = jnp.arange(count, dtype=jnp.int32)
    layout = [[(0, (q,)) for q in range(count)]]
    onward = [(i, i + 1) for i in range(chain_size - 1)]
    diag_split = split_blocks(diag_inverse, block)
    coupling_split = split_blocks(coupling, block)

    def gathered(value):
        whole = lax.all_gather(value, "tile", axis=1, tiled=True)
        return [whole.reshape(columns, count, block).transpose(1, 0, 2)]

    current = reduced
    for _ in range(chain_size - 1):
        carried = complex_apply(coupling_split, order, layout, gathered(current), [], sources, [columns])[0]
        current = reduced - lax.ppermute(carried, "chain", onward)
    return complex_apply(diag_split, order, layout, gathered(current), [], sources, [columns])[0]


def body(right_side, diag_inverse, coupling, updates, update_rows, tile_counts):
    batches, halves, sources, own_rows = right_side.shape
    tile_size = lax.axis_size("tile")
    entries, columns = updates.shape
    tile_rows = entries // tile_counts.shape[0]
    cap = 2 * entries // tile_size
    slots = tile_size * cap
    width = -(-(columns + 1) // 128) * 128
    vmem = pl.BlockSpec(memory_space=pltpu.VMEM)
    smem = pl.BlockSpec(memory_space=pltpu.SMEM)
    packed = pl.pallas_call(
        functools.partial(pack_kernel, own_rows, cap, tile_rows),
        in_specs=[smem, vmem, vmem],
        out_specs=vmem,
        out_shape=jax.ShapeDtypeStruct((slots, width), f32),
        compiler_params=kernel_params(),
    )(tile_counts, update_rows[None, :], updates.T)
    received = lax.all_to_all(packed.reshape(tile_size, cap, width), "tile", 0, 0, tiled=False).reshape(slots, width)
    paired = own_rows % 128 == 0 and tile_size % 8 == 0 and batches > 1
    early = batches * 2 // 3 * halves * sources
    shares = [early, columns - early] if paired else [columns]
    reduced = pl.pallas_call(
        reduce_kernel,
        in_specs=[vmem, vmem],
        out_specs=[vmem] * len(shares),
        out_shape=[jax.ShapeDtypeStruct((rows, own_rows), f32) for rows in shares],
        compiler_params=kernel_params(),
    )(received, right_side.reshape(columns, own_rows))
    solve = solve_paired if paired else solve_flat
    return solve(reduced, diag_inverse, coupling, sources).reshape(right_side.shape)


def solution(mesh):
    in_specs = (
        P(None, None, None, ("chain", "tile")),
        P(None, ("chain", "tile"), None),
        P(None, ("chain", "tile"), None),
        P(("chain", "tile"), None),
        P(("chain", "tile")),
        P(("chain", "tile")),
    )
    out_specs = P(None, None, None, ("chain", "tile"))
    return jax.shard_map(body, mesh=mesh, in_specs=in_specs, out_specs=out_specs, check_vma=False)
```

time: 213 us -> 109 us (0.51)
  waiting for transfers between devices: 127 us -> 27.8 us
  Pallas kernels: 39.6 us -> 16.6 us
  starting transfers between devices: 6.85 us -> 26.7 us
  local copies, waits for them, and re-layouts: 1.28 us -> 15.2 us
  between operations: 13.1 us -> 0.23 us
    all_gather x4 -> x0, waiting for transfers between devices: 121 us -> none  [gather_blocks(): gathered = lax.all_gather(reduced, 'tile', axis=0, tiled=False)]
    pallas_call x5, Pallas kernels: 37.4 us -> 14.4 us  [the longest x2 7.87 us: complex_apply(): pl.pallas_call(functools.partial(product_kernel, sources, layout, len(blo...]
    ppermute x2 -> x24, waiting for transfers between devices: 5.55 us -> 27.8 us  [the longest x18 27 us: send(): lax.ppermute(value, 'tile', [(t, target(t)) for t in range(tile_size)])]
    ppermute x2 -> x24, starting transfers between devices: 6.73 us -> 26.7 us  [the longest x18 16 us: send(): lax.ppermute(value, 'tile', [(t, target(t)) for t in range(tile_size)])]
    unnamed x6 -> x16, local copies, waits for them, and re-layouts: 1.28 us -> 15.1 us
  transfers between devices with their start and end apart: 6 -> 24, of which waited for: 6 -> 10; matrix products, arithmetic and copies ran while one was open for 0% -> 0% of each run, Pallas kernels for 12% -> 4%
where the time goes in v4:
time: 109 us
  waiting for transfers between devices  27.8 us (26%)
  starting transfers between devices  26.7 us (24%)
  blocking collectives  22 us (20%)
  Pallas kernels  16.6 us (15%)
  local copies, waits for them, and re-layouts  15.2 us (14%)
    ppermute x18, waiting for transfers between devices, send(): lax.ppermute(value, 'tile', [(t, target(t)) for t in range(tile_size)])  27 us
    all_to_all x1, blocking collectives, body(): lax.all_to_all(packed.reshape(tile_size, cap, width), 'tile', 0, 0, tiled...  22 us
    ppermute x18, starting transfers between devices, send(): lax.ppermute(value, 'tile', [(t, target(t)) for t in range(tile_size)])  16 us
    unnamed x16, local copies, waits for them, and re-layouts  15.1 us
    ppermute x6, starting transfers between devices, send(): return lax.ppermute(value, ('chain', 'tile'), pairs)  10.8 us
    pallas_call x2, Pallas kernels, complex_apply(): pl.pallas_call(functools.partial(product_kernel, sources, layout, len(blo...  7.87 us
    pallas_call x2, Pallas kernels, split_blocks(): pl.pallas_call(split_kernel, grid=(count // per_step,), in_specs=[pl.Bloc...  4.25 us
    pallas_call x1, Pallas kernels, body(): pl.pallas_call(functools.partial(pack_kernel, own_rows, cap, tile_rows),...  2.23 us
  transfers between devices with their start and end apart: 24, of which 10 were waited for; matrix products, arithmetic and copies ran while one was open for 0% of the time, Pallas kernels for 4%

profile of v4, /device:TPU:0, one launch (start us, length us, event | category | flops | bytes accessed | tf_op | source)
XLA Modules:
  0.0 108.6 jit_solution(17934796504873073573)
XLA Ops:
  0.0 2.2 %shard_map.64 = f32[512,256]{1,0:T(8,128)} custom-call(s32[2]{0:T(128)} %counts_ref.1, s32[1,256]{1,0:T(1,128)} %bitcast.66, f32[192,256]{1,0:T(8,128)} %bitcast.46), custom_call_target="tpu_custom_call" | custom-call | tf_op jit(solution)/shard_map/pallas_call | solution.py:240
  2.2 22.0 %all_to_all.5 = f32[16,32,256]{2,1,0:T(8,128)} all-to-all(f32[16,32,256]{2,1,0:T(8,128)} %bitcast.43), channel_id=1, replica_groups=mesh['chain'=2,'tile'=16] {'tile'}, dimensions={0} | all-to-all | bytes 1048576 | tf_op jit(solution)/shard_map/all_to_all | solution.py:247
  24.2 2.2 %shard_map.65 = (f32[128,256]{1,0:T(8,128)}, f32[64,256]{1,0:T(8,128)}) custom-call(f32[512,256]{1,0:T(8,128)} %bitcast.42, f32[192,256]{1,0:T(8,128)} %bitcast.47), custom_call_target="tpu_custom_call" | custom-call | tf_op jit(solution)/shard_map/pallas_call | solution.py:251
  26.4 0.4 collective-permute-start
  26.8 2.9 %collective-permute-start.3 = (f32[128,256]{1,0:T(8,128)}, f32[128,256]{1,0:T(8,128)S(1)}, u32[]{:S(2)}, u32[]{:S(2)}) collective-permute-start(f32[128,256]{1,0:T(8,128)} %get-tuple-element.24), channel_id=1, source_target_pairs={{0,12},{1,13},{2,14},{3,15},{4,0},{5,1},{6,2},{7,3},{8,4},{9,5},{1... | collective-permute-start | bytes 393224 | tf_op jit(solution)/shard_map/ppermute | solution.py:181
  29.7 0.5 collective-permute-start.2
  30.3 0.5 collective-permute-start.1
  30.7 3.4 %copy-done = f32[2,256,4096]{2,1,0:T(8,128)S(1)} copy-done((f32[2,256,4096]{2,1,0:T(8,128)S(1)}, f32[2,256,4096]{2,1,0:T(8,128)}, u32[]{:S(2)}) %copy-start) | copy-done | bytes 8388632
  34.1 2.1 %shard_map.66 = (bf16[16,512,256]{2,1,0:T(8,128)(2,1)S(1)}, bf16[16,512,256]{2,1,0:T(8,128)(2,1)S(1)}) custom-call(f32[2,256,4096]{2,1,0:T(8,128)S(1)} %copy-done), custom_call_target="tpu_custom_call" | custom-call | flops 6291456 | bytes 16777216 | tf_op jit(solution)/shard_map/pallas_call | solution.py:87
  36.2 0.0 copy-start.2
  36.2 2.0 %copy-done.2 = bf16[16,512,256]{2,1,0:T(8,128)(2,1)} copy-done((bf16[16,512,256]{2,1,0:T(8,128)(2,1)}, bf16[16,512,256]{2,1,0:T(8,128)(2,1)S(1)}, u32[]{:S(2)}) %copy-start.2) | copy-done | bytes 4194328
  38.2 2.0 %copy-done.4 = bf16[16,512,256]{2,1,0:T(8,128)(2,1)} copy-done((bf16[16,512,256]{2,1,0:T(8,128)(2,1)}, bf16[16,512,256]{2,1,0:T(8,128)(2,1)S(1)}, u32[]{:S(2)}) %copy-start.4) | copy-done | bytes 4194328
  40.2 0.0 collective-permute-done
  40.2 0.0 collective-permute-done.3
  40.2 2.0 %collective-permute-done.2 = f32[128,256]{1,0:T(8,128)S(1)} collective-permute-done((f32[128,256]{1,0:T(8,128)}, f32[128,256]{1,0:T(8,128)S(1)}, u32[]{:S(2)}, u32[]{:S(2)}) %collective-permute-start.2) | collective-permute-done | bytes 131104 | tf_op jit(solution)/shard_map/ppermute | solution.py:181
  42.3 0.0 collective-permute-done.1
  42.3 1.2 %collective-permute-start.4 = (f32[4,128,256]{2,1,0:T(8,128)S(1)}, f32[4,128,256]{2,1,0:T(8,128)S(1)}, u32[]{:S(2)}, u32[]{:S(2)}) collective-permute-start(f32[4,128,256]{2,1,0:T(8,128)S(1)} %pad_maximum_fusion.refs_0_.refs_6_), channel_id=1, source_target_pairs={{0,2},{1,3},{2,0},{3,1},{4,6},{5,7},{6,4},{7,5},{8,10},{9,11},{10,... | collective-permute-start | bytes 1572872 | tf_op jit(solution)/shard_map/ppermute | solution.py:181
  43.5 1.0 collective-permute-start.9
  44.5 0.7 collective-permute-start.8
  45.2 2.0 %collective-permute-start.7 = (f32[2,64,256]{2,1,0:T(8,128)S(1)}, f32[2,64,256]{2,1,0:T(8,128)S(1)}, u32[]{:S(2)}, u32[]{:S(2)}) collective-permute-start(f32[2,64,256]{2,1,0:T(8,128)S(1)} %pad_maximum_fusion.4), channel_id=1, source_target_pairs={{0,4},{1,5},{2,6},{3,7},{4,8},{5,9},{6,10},{7,11},{8,12},{9,13},{1... | collective-permute-start | bytes 393224 | tf_op jit(solution)/shard_map/ppermute | solution.py:181
  47.2 0.0 collective-permute-start.5
  47.2 1.8 %collective-permute-done.9 = f32[2,64,256]{2,1,0:T(8,128)S(1)} collective-permute-done((f32[2,64,256]{2,1,0:T(8,128)S(1)}, f32[2,64,256]{2,1,0:T(8,128)S(1)}, u32[]{:S(2)}, u32[]{:S(2)}) %collective-permute-start.9) | collective-permute-done | bytes 131104 | tf_op jit(solution)/shard_map/ppermute | solution.py:181
  49.0 8.0 %collective-permute-done.8 = f32[2,64,256]{2,1,0:T(8,128)S(1)} collective-permute-done((f32[2,64,256]{2,1,0:T(8,128)S(1)}, f32[2,64,256]{2,1,0:T(8,128)S(1)}, u32[]{:S(2)}, u32[]{:S(2)}) %collective-permute-start.8) | collective-permute-done | bytes 131104 | tf_op jit(solution)/shard_map/ppermute | solution.py:181
  57.0 0.0 collective-permute-done.7
  57.1 0.1 collective-permute-start.10
  57.2 0.0 collective-permute-done.4.refs_1_.refs_7_
  57.2 0.5 collective-permute-start.6
  57.7 0.1 stack.145.order_ref
  57.7 0.0 collective-permute-done.5.refs_2_.refs_8_
  57.8 1.3 %collective-permute-done.10.refs_5_.refs_11_ = f32[4,2,64,256]{3,2,1,0:T(8,128)S(1)} collective-permute-done((f32[4,2,64,256]{3,2,1,0:T(8,128)S(1)}, f32[4,2,64,256]{3,2,1,0:T(8,128)S(1)}, u32[]{:S(2)}, u32[]{:S(2)}) %collective-permute-start.10) | collective-permute-done | bytes 524320 | tf_op jit(solution)/shard_map/ppermute | solution.py:181
  59.1 0.7 collective-permute-done.6.refs_3_.refs_9_
  59.8 2.2 %copy-done.3 = bf16[16,512,256]{2,1,0:T(8,128)(2,1)S(1)} copy-done((bf16[16,512,256]{2,1,0:T(8,128)(2,1)S(1)}, bf16[16,512,256]{2,1,0:T(8,128)(2,1)}, u32[]{:S(2)}) %copy-start.3) | copy-done | bytes 4194328
  62.0 2.2 %copy-done.5 = bf16[16,512,256]{2,1,0:T(8,128)(2,1)S(1)} copy-done((bf16[16,512,256]{2,1,0:T(8,128)(2,1)S(1)}, bf16[16,512,256]{2,1,0:T(8,128)(2,1)}, u32[]{:S(2)}) %copy-start.5) | copy-done | bytes 4194328
  64.2 3.5 %shard_map.67 = (f32[128,256]{1,0:T(8,128)S(1)}, f32[64,256]{1,0:T(8,128)S(1)}) custom-call(s32[16]{0:T(128)S(1)} %stack.145.order_ref, f32[4,128,256]{2,1,0:T(8,128)S(1)} %pad_maximum_fusion.refs_0_.refs_6_, f32[4,128,256]{2,1,0:T(8,128)S(1)} %collective-permute-done.4.refs_1_.refs_7_, f32[4,128,256]{2,1,0:T(8,128)S(1)} %collective-permute-done.5.refs_2_.refs_8_, ...), custom_call_target="tpu_custom_call" | custom-call | flops 2415919104 | bytes 1048576 | tf_op jit(solution)/shard_map/pallas_call | solution.py:141
  67.7 3.5 %collective-permute-start.12 = (f32[64,256]{1,0:T(8,128)S(1)}, f32[64,256]{1,0:T(8,128)S(1)}, u32[]{:S(2)}, u32[]{:S(2)}) collective-permute-start(f32[64,256]{1,0:T(8,128)S(1)} %get-tuple-element.32), channel_id=1, source_target_pairs={{0,18},{1,19},{2,16},{3,17},{4,22},{5,23},{6,20},{7,21},{8,26},{9,... | collective-permute-start | bytes 196616 | tf_op jit(solution)/shard_map/ppermute | solution.py:183
  71.2 1.3 %collective-permute-start.11 = (f32[64,256]{1,0:T(8,128)S(1)}, f32[64,256]{1,0:T(8,128)S(1)}, u32[]{:S(2)}, u32[]{:S(2)}) collective-permute-start(f32[64,256]{1,0:T(8,128)S(1)} %get-tuple-element.32), channel_id=1, source_target_pairs={{0,16},{1,17},{2,18},{3,19},{4,20},{5,21},{6,22},{7,23},{8,24},{9,... | collective-permute-start | bytes 196616 | tf_op jit(solution)/shard_map/ppermute | solution.py:183
  72.5 1.3 %collective-permute-start.16 = (f32[128,256]{1,0:T(8,128)S(1)}, f32[128,256]{1,0:T(8,128)S(1)}, u32[]{:S(2)}, u32[]{:S(2)}) collective-permute-start(f32[128,256]{1,0:T(8,128)S(1)} %get-tuple-element.33), channel_id=1, source_target_pairs={{0,28},{1,29},{2,30},{3,31},{4,16},{5,17},{6,18},{7,19},{8,20},{9,... | collective-permute-start | bytes 393224 | tf_op jit(solution)/shard_map/ppermute | solution.py:183
  73.8 2.1 %collective-permute-start.15 = (f32[128,256]{1,0:T(8,128)S(1)}, f32[128,256]{1,0:T(8,128)S(1)}, u32[]{:S(2)}, u32[]{:S(2)}) collective-permute-start(f32[128,256]{1,0:T(8,128)S(1)} %get-tuple-element.33), channel_id=1, source_target_pairs={{0,24},{1,25},{2,26},{3,27},{4,28},{5,29},{6,30},{7,31},{8,16},{9,... | collective-permute-start | bytes 393224 | tf_op jit(solution)/shard_map/ppermute | solution.py:183
  75.9 1.3 %collective-permute-start.14 = (f32[128,256]{1,0:T(8,128)S(1)}, f32[128,256]{1,0:T(8,128)S(1)}, u32[]{:S(2)}, u32[]{:S(2)}) collective-permute-start(f32[128,256]{1,0:T(8,128)S(1)} %get-tuple-element.33), channel_id=1, source_target_pairs={{0,20},{1,21},{2,22},{3,23},{4,24},{5,25},{6,26},{7,27},{8,28},{9,... | collective-permute-start | bytes 393224 | tf_op jit(solution)/shard_map/ppermute | solution.py:183
  77.2 0.0 collective-permute-done.12
  77.2 1.3 %collective-permute-start.13 = (f32[128,256]{1,0:T(8,128)S(1)}, f32[128,256]{1,0:T(8,128)S(1)}, u32[]{:S(2)}, u32[]{:S(2)}) collective-permute-start(f32[128,256]{1,0:T(8,128)S(1)} %get-tuple-element.33), channel_id=1, source_target_pairs={{0,16},{1,17},{2,18},{3,19},{4,20},{5,21},{6,22},{7,23},{8,24},{9,... | collective-permute-start | bytes 393224 | tf_op jit(solution)/shard_map/ppermute | solution.py:183
  78.5 0.0 copy-start.1
  78.5 3.4 %copy-done.1 = f32[2,256,4096]{2,1,0:T(8,128)S(1)} copy-done((f32[2,256,4096]{2,1,0:T(8,128)S(1)}, f32[2,256,4096]{2,1,0:T(8,128)}, u32[]{:S(2)}) %copy-start.1) | copy-done | bytes 8388632
  81.9 2.1 %shard_map.68 = (bf16[16,512,256]{2,1,0:T(8,128)(2,1)S(1)}, bf16[16,512,256]{2,1,0:T(8,128)(2,1)S(1)}) custom-call(f32[2,256,4096]{2,1,0:T(8,128)S(1)} %copy-done.1), custom_call_target="tpu_custom_call" | custom-call | flops 6291456 | bytes 16777216 | tf_op jit(solution)/shard_map/pallas_call | solution.py:87
  84.0 0.0 collective-permute-done.11
  84.1 0.0 collective-permute-done.16
  84.1 0.0 collective-permute-done.15
  84.1 0.0 collective-permute-done.14
  84.1 0.8 collective-permute-done.13
  84.9 0.8 collective-permute-start.17
  85.7 4.3 %collective-permute-start.22 = (f32[2,64,256]{2,1,0:T(8,128)S(1)}, f32[2,64,256]{2,1,0:T(8,128)S(1)}, u32[]{:S(2)}, u32[]{:S(2)}) collective-permute-start(f32[2,64,256]{2,1,0:T(8,128)S(1)} %pad_maximum_fusion.5), channel_id=1, source_target_pairs={{0,12},{1,13},{2,14},{3,15},{4,0},{5,1},{6,2},{7,3},{8,4},{9,5},{1... | collective-permute-start | bytes 393224 | tf_op jit(solution)/shard_map/ppermute | solution.py:181
  90.0 0.1 collective-permute-start.21
  90.1 0.5 collective-permute-start.20
  90.6 0.0 collective-permute-start.18
  90.6 3.3 %collective-permute-done.22 = f32[2,64,256]{2,1,0:T(8,128)S(1)} collective-permute-done((f32[2,64,256]{2,1,0:T(8,128)S(1)}, f32[2,64,256]{2,1,0:T(8,128)S(1)}, u32[]{:S(2)}, u32[]{:S(2)}) %collective-permute-start.22) | collective-permute-done | bytes 131104 | tf_op jit(solution)/shard_map/ppermute | solution.py:181
  93.9 7.6 %collective-permute-done.21 = f32[2,64,256]{2,1,0:T(8,128)S(1)} collective-permute-done((f32[2,64,256]{2,1,0:T(8,128)S(1)}, f32[2,64,256]{2,1,0:T(8,128)S(1)}, u32[]{:S(2)}, u32[]{:S(2)}) %collective-permute-start.21) | collective-permute-done | bytes 131104 | tf_op jit(solution)/shard_map/ppermute | solution.py:181
  101.5 0.0 collective-permute-done.20
  101.6 0.1 collective-permute-start.23
  101.6 0.0 collective-permute-done.17.refs_1_
  101.6 0.5 collective-permute-start.19
  102.1 0.0 collective-permute-done.18.refs_2_
  102.1 1.4 %collective-permute-done.23.refs_5_ = f32[4,2,64,256]{3,2,1,0:T(8,128)S(1)} collective-permute-done((f32[4,2,64,256]{3,2,1,0:T(8,128)S(1)}, f32[4,2,64,256]{3,2,1,0:T(8,128)S(1)}, u32[]{:S(2)}, u32[]{:S(2)}) %collective-permute-start.23) | collective-permute-done | bytes 524320 | tf_op jit(solution)/shard_map/ppermute | solution.py:181
  103.5 0.7 collective-permute-done.19.refs_3_
  104.3 4.4 %shard_map.69 = f32[192,256]{1,0:T(8,128)} custom-call(s32[16]{0:T(128)S(1)} %stack.145.order_ref, f32[4,128,256]{2,1,0:T(8,128)S(1)} %pad_maximum_fusion.2.refs_0_, f32[4,128,256]{2,1,0:T(8,128)S(1)} %collective-permute-done.17.refs_1_, f32[4,128,256]{2,1,0:T(8,128)S(1)} %collective-permute-done.18.refs_2_, ...), custom_call_target="tpu_custom_call" | custom-call | flops 2415919104 | bytes 1048576 | tf_op jit(solution)/shard_map/pallas_call | solution.py:141
  (14 shorter events, 0.2 us)
Async XLA Ops:
  26.4 13.8 %collective-permute-start = (f32[64,256]{1,0:T(8,128)}, f32[64,256]{1,0:T(8,128)S(1)}, u32[]{:S(2)}, u32[]{:S(2)}) collective-permute-start(f32[64,256]{1,0:T(8,128)} %get-tuple-element.23), channel_id=1, source_target_pairs={{0,2},{1,3},{2,0},{3,1},{4,6},{5,7},{6,4},{7,5},{8,10},{9,11},{10,... | collective-permute-start | bytes 196616 | tf_op jit(solution)/shard_map/ppermute | solution.py:181
  26.8 13.4 %collective-permute-start.3 = (f32[128,256]{1,0:T(8,128)}, f32[128,256]{1,0:T(8,128)S(1)}, u32[]{:S(2)}, u32[]{:S(2)}) collective-permute-start(f32[128,256]{1,0:T(8,128)} %get-tuple-element.24), channel_id=1, source_target_pairs={{0,12},{1,13},{2,14},{3,15},{4,0},{5,1},{6,2},{7,3},{8,4},{9,5},{1... | collective-permute-start | bytes 393224 | tf_op jit(solution)/shard_map/ppermute | solution.py:181
  29.7 12.6 %collective-permute-start.2 = (f32[128,256]{1,0:T(8,128)}, f32[128,256]{1,0:T(8,128)S(1)}, u32[]{:S(2)}, u32[]{:S(2)}) collective-permute-start(f32[128,256]{1,0:T(8,128)} %get-tuple-element.24), channel_id=1, source_target_pairs={{0,8},{1,9},{2,10},{3,11},{4,12},{5,13},{6,14},{7,15},{8,0},{9,1},... | collective-permute-start | bytes 393224 | tf_op jit(solution)/shard_map/ppermute | solution.py:181
  30.3 12.0 %collective-permute-start.1 = (f32[128,256]{1,0:T(8,128)}, f32[128,256]{1,0:T(8,128)S(1)}, u32[]{:S(2)}, u32[]{:S(2)}) collective-permute-start(f32[128,256]{1,0:T(8,128)} %get-tuple-element.24), channel_id=1, source_target_pairs={{0,4},{1,5},{2,6},{3,7},{4,8},{5,9},{6,10},{7,11},{8,12},{9,13},{1... | collective-permute-start | bytes 393224 | tf_op jit(solution)/shard_map/ppermute | solution.py:181
  30.7 3.4 %copy-start = (f32[2,256,4096]{2,1,0:T(8,128)S(1)}, f32[2,256,4096]{2,1,0:T(8,128)}, u32[]{:S(2)}) copy-start(f32[2,256,4096]{2,1,0:T(8,128)} %k_ref) | copy-start | bytes 25165828
  34.1 6.1 %copy-start.7 = (f32[64,256]{1,0:T(8,128)S(1)}, f32[64,256]{1,0:T(8,128)}, u32[]{:S(2)}) copy-start(f32[64,256]{1,0:T(8,128)} %get-tuple-element.23) | copy-start | bytes 196612
  34.1 8.2 %copy-start.6 = (f32[128,256]{1,0:T(8,128)S(1)}, f32[128,256]{1,0:T(8,128)}, u32[]{:S(2)}) copy-start(f32[128,256]{1,0:T(8,128)} %get-tuple-element.24) | copy-start | bytes 393220
  36.2 2.0 %copy-start.2 = (bf16[16,512,256]{2,1,0:T(8,128)(2,1)}, bf16[16,512,256]{2,1,0:T(8,128)(2,1)S(1)}, u32[]{:S(2)}) copy-start(bf16[16,512,256]{2,1,0:T(8,128)(2,1)S(1)} %get-tuple-element.30.refs_6_) | copy-start | bytes 12582916
  38.2 2.0 %copy-start.4 = (bf16[16,512,256]{2,1,0:T(8,128)(2,1)}, bf16[16,512,256]{2,1,0:T(8,128)(2,1)S(1)}, u32[]{:S(2)}) copy-start(bf16[16,512,256]{2,1,0:T(8,128)(2,1)S(1)} %get-tuple-element.31.refs_7_) | copy-start | bytes 12582916
  42.3 14.8 %collective-permute-start.4 = (f32[4,128,256]{2,1,0:T(8,128)S(1)}, f32[4,128,256]{2,1,0:T(8,128)S(1)}, u32[]{:S(2)}, u32[]{:S(2)}) collective-permute-start(f32[4,128,256]{2,1,0:T(8,128)S(1)} %pad_maximum_fusion.refs_0_.refs_6_), channel_id=1, source_target_pairs={{0,2},{1,3},{2,0},{3,1},{4,6},{5,7},{6,4},{7,5},{8,10},{9,11},{10,... | collective-permute-start | bytes 1572872 | tf_op jit(solution)/shard_map/ppermute | solution.py:181
  43.5 5.5 %collective-permute-start.9 = (f32[2,64,256]{2,1,0:T(8,128)S(1)}, f32[2,64,256]{2,1,0:T(8,128)S(1)}, u32[]{:S(2)}, u32[]{:S(2)}) collective-permute-start(f32[2,64,256]{2,1,0:T(8,128)S(1)} %pad_maximum_fusion.4), channel_id=1, source_target_pairs={{0,12},{1,13},{2,14},{3,15},{4,0},{5,1},{6,2},{7,3},{8,4},{9,5},{1... | collective-permute-start | bytes 393224 | tf_op jit(solution)/shard_map/ppermute | solution.py:181
  44.5 12.5 %collective-permute-start.8 = (f32[2,64,256]{2,1,0:T(8,128)S(1)}, f32[2,64,256]{2,1,0:T(8,128)S(1)}, u32[]{:S(2)}, u32[]{:S(2)}) collective-permute-start(f32[2,64,256]{2,1,0:T(8,128)S(1)} %pad_maximum_fusion.4), channel_id=1, source_target_pairs={{0,8},{1,9},{2,10},{3,11},{4,12},{5,13},{6,14},{7,15},{8,0},{9,1},... | collective-permute-start | bytes 393224 | tf_op jit(solution)/shard_map/ppermute | solution.py:181
  45.2 11.8 %collective-permute-start.7 = (f32[2,64,256]{2,1,0:T(8,128)S(1)}, f32[2,64,256]{2,1,0:T(8,128)S(1)}, u32[]{:S(2)}, u32[]{:S(2)}) collective-permute-start(f32[2,64,256]{2,1,0:T(8,128)S(1)} %pad_maximum_fusion.4), channel_id=1, source_target_pairs={{0,4},{1,5},{2,6},{3,7},{4,8},{5,9},{6,10},{7,11},{8,12},{9,13},{1... | collective-permute-start | bytes 393224 | tf_op jit(solution)/shard_map/ppermute | solution.py:181
  47.2 10.5 %collective-permute-start.5 = (f32[4,128,256]{2,1,0:T(8,128)S(1)}, f32[4,128,256]{2,1,0:T(8,128)S(1)}, u32[]{:S(2)}, u32[]{:S(2)}) collective-permute-start(f32[4,128,256]{2,1,0:T(8,128)S(1)} %pad_maximum_fusion.refs_0_.refs_6_), channel_id=1, source_target_pairs={{0,1},{1,0},{2,3},{3,2},{4,5},{5,4},{6,7},{7,6},{8,9},{9,8},{10,11... | collective-permute-start | bytes 1572872 | tf_op jit(solution)/shard_map/ppermute | solution.py:181
  57.1 2.0 %collective-permute-start.10 = (f32[4,2,64,256]{3,2,1,0:T(8,128)S(1)}, f32[4,2,64,256]{3,2,1,0:T(8,128)S(1)}, u32[]{:S(2)}, u32[]{:S(2)}) collective-permute-start(f32[4,2,64,256]{3,2,1,0:T(8,128)S(1)} %pad_maximum_fusion.1.refs_4_.refs_10_), channel_id=1, source_target_pairs={{0,1},{1,0},{2,3},{3,2},{4,5},{5,4},{6,7},{7,6},{8,9},{9,8},{10,11... | collective-permute-start | bytes 1572872 | tf_op jit(solution)/shard_map/ppermute | solution.py:181
  57.2 2.6 %collective-permute-start.6 = (f32[4,128,256]{2,1,0:T(8,128)S(1)}, f32[4,128,256]{2,1,0:T(8,128)S(1)}, u32[]{:S(2)}, u32[]{:S(2)}) collective-permute-start(f32[4,128,256]{2,1,0:T(8,128)S(1)} %collective-permute-done.4.refs_1_.refs_7_), channel_id=1, source_target_pairs={{0,1},{1,0},{2,3},{3,2},{4,5},{5,4},{6,7},{7,6},{8,9},{9,8},{10,11... | collective-permute-start | bytes 1572872 | tf_op jit(solution)/shard_map/ppermute | solution.py:181
  59.8 2.2 %copy-start.3 = (bf16[16,512,256]{2,1,0:T(8,128)(2,1)S(1)}, bf16[16,512,256]{2,1,0:T(8,128)(2,1)}, u32[]{:S(2)}) copy-start(bf16[16,512,256]{2,1,0:T(8,128)(2,1)} %copy-done.2) | copy-start | bytes 12582916
  62.0 2.2 %copy-start.5 = (bf16[16,512,256]{2,1,0:T(8,128)(2,1)S(1)}, bf16[16,512,256]{2,1,0:T(8,128)(2,1)}, u32[]{:S(2)}) copy-start(bf16[16,512,256]{2,1,0:T(8,128)(2,1)} %copy-done.4) | copy-start | bytes 12582916
  67.7 9.5 %collective-permute-start.12 = (f32[64,256]{1,0:T(8,128)S(1)}, f32[64,256]{1,0:T(8,128)S(1)}, u32[]{:S(2)}, u32[]{:S(2)}) collective-permute-start(f32[64,256]{1,0:T(8,128)S(1)} %get-tuple-element.32), channel_id=1, source_target_pairs={{0,18},{1,19},{2,16},{3,17},{4,22},{5,23},{6,20},{7,21},{8,26},{9,... | collective-permute-start | bytes 196616 | tf_op jit(solution)/shard_map/ppermute | solution.py:183
  71.2 12.8 %collective-permute-start.11 = (f32[64,256]{1,0:T(8,128)S(1)}, f32[64,256]{1,0:T(8,128)S(1)}, u32[]{:S(2)}, u32[]{:S(2)}) collective-permute-start(f32[64,256]{1,0:T(8,128)S(1)} %get-tuple-element.32), channel_id=1, source_target_pairs={{0,16},{1,17},{2,18},{3,19},{4,20},{5,21},{6,22},{7,23},{8,24},{9,... | collective-permute-start | bytes 196616 | tf_op jit(solution)/shard_map/ppermute | solution.py:183
  72.5 11.5 %collective-permute-start.16 = (f32[128,256]{1,0:T(8,128)S(1)}, f32[128,256]{1,0:T(8,128)S(1)}, u32[]{:S(2)}, u32[]{:S(2)}) collective-permute-start(f32[128,256]{1,0:T(8,128)S(1)} %get-tuple-element.33), channel_id=1, source_target_pairs={{0,28},{1,29},{2,30},{3,31},{4,16},{5,17},{6,18},{7,19},{8,20},{9,... | collective-permute-start | bytes 393224 | tf_op jit(solution)/shard_map/ppermute | solution.py:183
  73.8 10.2 %collective-permute-start.15 = (f32[128,256]{1,0:T(8,128)S(1)}, f32[128,256]{1,0:T(8,128)S(1)}, u32[]{:S(2)}, u32[]{:S(2)}) collective-permute-start(f32[128,256]{1,0:T(8,128)S(1)} %get-tuple-element.33), channel_id=1, source_target_pairs={{0,24},{1,25},{2,26},{3,27},{4,28},{5,29},{6,30},{7,31},{8,16},{9,... | collective-permute-start | bytes 393224 | tf_op jit(solution)/shard_map/ppermute | solution.py:183
  75.9 8.2 %collective-permute-start.14 = (f32[128,256]{1,0:T(8,128)S(1)}, f32[128,256]{1,0:T(8,128)S(1)}, u32[]{:S(2)}, u32[]{:S(2)}) collective-permute-start(f32[128,256]{1,0:T(8,128)S(1)} %get-tuple-element.33), channel_id=1, source_target_pairs={{0,20},{1,21},{2,22},{3,23},{4,24},{5,25},{6,26},{7,27},{8,28},{9,... | collective-permute-start | bytes 393224 | tf_op jit(solution)/shard_map/ppermute | solution.py:183
  77.2 7.7 %collective-permute-start.13 = (f32[128,256]{1,0:T(8,128)S(1)}, f32[128,256]{1,0:T(8,128)S(1)}, u32[]{:S(2)}, u32[]{:S(2)}) collective-permute-start(f32[128,256]{1,0:T(8,128)S(1)} %get-tuple-element.33), channel_id=1, source_target_pairs={{0,16},{1,17},{2,18},{3,19},{4,20},{5,21},{6,22},{7,23},{8,24},{9,... | collective-permute-start | bytes 393224 | tf_op jit(solution)/shard_map/ppermute | solution.py:183
  78.5 3.4 %copy-start.1 = (f32[2,256,4096]{2,1,0:T(8,128)S(1)}, f32[2,256,4096]{2,1,0:T(8,128)}, u32[]{:S(2)}) copy-start(f32[2,256,4096]{2,1,0:T(8,128)} %k_ref.1) | copy-start | bytes 25165828
  84.9 16.7 %collective-permute-start.17 = (f32[4,128,256]{2,1,0:T(8,128)S(1)}, f32[4,128,256]{2,1,0:T(8,128)S(1)}, u32[]{:S(2)}, u32[]{:S(2)}) collective-permute-start(f32[4,128,256]{2,1,0:T(8,128)S(1)} %pad_maximum_fusion.2.refs_0_), channel_id=1, source_target_pairs={{0,2},{1,3},{2,0},{3,1},{4,6},{5,7},{6,4},{7,5},{8,10},{9,11},{10,... | collective-permute-start | bytes 1572872 | tf_op jit(solution)/shard_map/ppermute | solution.py:181
  85.7 8.2 %collective-permute-start.22 = (f32[2,64,256]{2,1,0:T(8,128)S(1)}, f32[2,64,256]{2,1,0:T(8,128)S(1)}, u32[]{:S(2)}, u32[]{:S(2)}) collective-permute-start(f32[2,64,256]{2,1,0:T(8,128)S(1)} %pad_maximum_fusion.5), channel_id=1, source_target_pairs={{0,12},{1,13},{2,14},{3,15},{4,0},{5,1},{6,2},{7,3},{8,4},{9,5},{1... | collective-permute-start | bytes 393224 | tf_op jit(solution)/shard_map/ppermute | solution.py:181
  90.0 11.5 %collective-permute-start.21 = (f32[2,64,256]{2,1,0:T(8,128)S(1)}, f32[2,64,256]{2,1,0:T(8,128)S(1)}, u32[]{:S(2)}, u32[]{:S(2)}) collective-permute-start(f32[2,64,256]{2,1,0:T(8,128)S(1)} %pad_maximum_fusion.5), channel_id=1, source_target_pairs={{0,8},{1,9},{2,10},{3,11},{4,12},{5,13},{6,14},{7,15},{8,0},{9,1},... | collective-permute-start | bytes 393224 | tf_op jit(solution)/shard_map/ppermute | solution.py:181
  90.1 11.4 %collective-permute-start.20 = (f32[2,64,256]{2,1,0:T(8,128)S(1)}, f32[2,64,256]{2,1,0:T(8,128)S(1)}, u32[]{:S(2)}, u32[]{:S(2)}) collective-permute-start(f32[2,64,256]{2,1,0:T(8,128)S(1)} %pad_maximum_fusion.5), channel_id=1, source_target_pairs={{0,4},{1,5},{2,6},{3,7},{4,8},{5,9},{6,10},{7,11},{8,12},{9,13},{1... | collective-permute-start | bytes 393224 | tf_op jit(solution)/shard_map/ppermute | solution.py:181
  90.6 11.6 %collective-permute-start.18 = (f32[4,128,256]{2,1,0:T(8,128)S(1)}, f32[4,128,256]{2,1,0:T(8,128)S(1)}, u32[]{:S(2)}, u32[]{:S(2)}) collective-permute-start(f32[4,128,256]{2,1,0:T(8,128)S(1)} %pad_maximum_fusion.2.refs_0_), channel_id=1, source_target_pairs={{0,1},{1,0},{2,3},{3,2},{4,5},{5,4},{6,7},{7,6},{8,9},{9,8},{10,11... | collective-permute-start | bytes 1572872 | tf_op jit(solution)/shard_map/ppermute | solution.py:181
  101.6 2.0 %collective-permute-start.23 = (f32[4,2,64,256]{3,2,1,0:T(8,128)S(1)}, f32[4,2,64,256]{3,2,1,0:T(8,128)S(1)}, u32[]{:S(2)}, u32[]{:S(2)}) collective-permute-start(f32[4,2,64,256]{3,2,1,0:T(8,128)S(1)} %pad_maximum_fusion.3.refs_4_), channel_id=1, source_target_pairs={{0,1},{1,0},{2,3},{3,2},{4,5},{5,4},{6,7},{7,6},{8,9},{9,8},{10,11... | collective-permute-start | bytes 1572872 | tf_op jit(solution)/shard_map/ppermute | solution.py:181
  101.6 2.6 %collective-permute-start.19 = (f32[4,128,256]{2,1,0:T(8,128)S(1)}, f32[4,128,256]{2,1,0:T(8,128)S(1)}, u32[]{:S(2)}, u32[]{:S(2)}) collective-permute-start(f32[4,128,256]{2,1,0:T(8,128)S(1)} %collective-permute-done.17.refs_1_), channel_id=1, source_target_pairs={{0,1},{1,0},{2,3},{3,2},{4,5},{5,4},{6,7},{7,6},{8,9},{9,8},{10,11... | collective-permute-start | bytes 1572872 | tf_op jit(solution)/shard_map/ppermute | solution.py:181

commit v5 on v4

v5 whole, which is shorter than its diff:
```python
import functools

import jax
import jax.numpy as jnp
from jax import lax
from jax.experimental import pallas as pl
from jax.experimental.pallas import tpu as pltpu
from jax.sharding import PartitionSpec as P

MIB = 1 << 20
f32 = jnp.float32
bf16 = jnp.bfloat16
lanes_contract = (((1,), (1,)), ((), ()))


def halves_of(value):
    high = value.astype(bf16)
    return high, (value - high.astype(f32)).astype(bf16)


def thirds_of(value):
    high = value.astype(bf16)
    rest = value - high.astype(f32)
    middle = rest.astype(bf16)
    return high, middle, (rest - middle.astype(f32)).astype(bf16)


def kernel_params():
    return pltpu.CompilerParams(vmem_limit_bytes=56 * MIB)


def pack_kernel(own_rows, cap, tile_rows, counts_hbm, rows_hbm, updates_hbm, packed_ref, counts_ref, rows_ref, updates_ref, sems):
    moves = [
        pltpu.make_async_copy(counts_hbm, counts_ref, sems.at[0]),
        pltpu.make_async_copy(rows_hbm, rows_ref, sems.at[1]),
        pltpu.make_async_copy(updates_hbm, updates_ref, sems.at[2]),
    ]
    for move in moves:
        move.start()
    columns, entries = updates_ref.shape
    owners, height, width = packed_ref.shape
    slots = owners * cap
    entry = lax.broadcasted_iota(jnp.int32, (1, entries), 1)
    earlier = lax.broadcasted_iota(jnp.int32, (entries, entries), 0) < lax.broadcasted_iota(jnp.int32, (entries, entries), 1)
    for move in moves:
        move.wait()
    live = jnp.zeros((1, entries), jnp.bool_)
    for tile in range(entries // tile_rows):
        start = tile * tile_rows
        live = live | ((entry >= start) & (entry < start + counts_ref[tile]))
    rows = rows_ref[...]
    owner = rows // own_rows
    lane_owner = jnp.broadcast_to(owner.astype(f32), (entries, entries))
    rank = jnp.sum(jnp.where(earlier & (lane_owner.T == lane_owner), 1, 0), axis=0, keepdims=True)
    slot = owner * cap + rank
    choose = jnp.where(lax.broadcasted_iota(jnp.int32, (slots, entries), 0) == slot, 1.0, 0.0).astype(bf16)
    data = jnp.where(live, updates_ref[...], 0.0)
    local_row = (rows - owner * own_rows).astype(f32)
    folded = height > cap
    if not folded:
        tail = jnp.where(lax.broadcasted_iota(jnp.int32, (width - columns, entries), 0) == 0, local_row, 0.0)
        data = jnp.concatenate([data, tail], axis=0)
    packed = jnp.zeros((slots, data.shape[0]), f32)
    for piece in thirds_of(data):
        packed += lax.dot_general(choose, piece, lanes_contract, preferred_element_type=f32)
    packed = packed.reshape(owners, cap, data.shape[0])
    if not folded:
        packed_ref[...] = packed
        return
    half = cap // 2
    packed_ref[:, :cap, :] = packed[:, :, :width]
    packed_ref[:, cap:cap + half, :] = jnp.concatenate([packed[:, :half, width:], packed[:, half:, width:]], axis=2)
    first = lax.axis_index("tile") * cap
    by_owner = jnp.where(lax.broadcasted_iota(jnp.int32, (owners, entries), 0) == owner, local_row, 0.0).astype(bf16)
    by_lane = jnp.where(lax.broadcasted_iota(jnp.int32, (width, entries), 0) == first % width + rank, 1.0, 0.0).astype(bf16)
    numbers = lax.dot_general(by_owner, by_lane, lanes_contract, preferred_element_type=f32)
    line = lax.broadcasted_iota(jnp.int32, (owners, 8, width), 1)
    packed_ref[:, cap + half:, :] = jnp.where(line == first // width, numbers[:, None, :], 0.0)


def reduce_kernel(cap, received_ref, right_hbm, *refs):
    reduced_refs, right_ref, sem = refs[:-2], refs[-2], refs[-1]
    move = pltpu.make_async_copy(right_hbm, right_ref, sem)
    move.start()
    owners, height, width = received_ref.shape
    slots = owners * cap
    columns, own_rows = right_ref.shape
    if height > cap:
        half = cap // 2
        numbers = jnp.sum(received_ref[:, cap + half:, :], axis=0)
        numbers = jnp.concatenate([numbers[i:i + 1] for i in range(slots // width)], axis=1).astype(jnp.int32)
        rest = received_ref[:, cap:cap + half, :]
        rest = jnp.concatenate([rest[:, :, :width // 2], rest[:, :, width // 2:]], axis=1)
        sets = [received_ref[:, :cap, :].reshape(slots, width), rest.reshape(slots, width // 2)]
        place = jnp.where(lax.broadcasted_iota(jnp.int32, (own_rows, slots), 0) == numbers, 1.0, 0.0).astype(bf16)
        totals = []
        for value in sets:
            total = jnp.zeros((own_rows, value.shape[1]), f32)
            for piece in thirds_of(value):
                total += jnp.dot(place, piece, preferred_element_type=f32)
            totals.append(total.T)
        total = jnp.concatenate(totals, axis=0)
    else:
        received = received_ref[...].reshape(slots, width)
        local_row = received[:, columns:columns + 1].astype(jnp.int32)
        place = jnp.where(lax.broadcasted_iota(jnp.int32, (slots, own_rows), 1) == local_row, 1.0, 0.0).astype(bf16)
        total = jnp.zeros((columns, own_rows), f32)
        for piece in thirds_of(received[:, :columns].T):
            total += jnp.dot(piece, place, preferred_element_type=f32)
    move.wait()
    start = 0
    for reduced_ref in reduced_refs:
        rows = reduced_ref.shape[0]
        reduced_ref[...] = right_ref[start:start + rows, :] - total[start:start + rows]
        start += rows


def split_kernel(matrix_ref, high_ref, low_ref):
    parts, own_rows, full_rows = matrix_ref.shape
    blocks, rows, block = high_ref.shape
    height = 64
    for part in range(parts):
        for first in range(0, own_rows, height):
            for j in range(blocks):
                high, low = halves_of(matrix_ref[part, first:first + height, j * block:(j + 1) * block])
                start = part * own_rows + first
                high_ref[j, start:start + height, :] = high
                low_ref[j, start:start + height, :] = low


def split_blocks(matrix, block):
    parts, own_rows, full_rows = matrix.shape
    count = full_rows // block
    vmem = pl.BlockSpec(memory_space=pltpu.VMEM)
    shape = jax.ShapeDtypeStruct((count, parts * own_rows, block), bf16)
    return pl.pallas_call(
        split_kernel,
        in_specs=[vmem],
        out_specs=[vmem, vmem],
        out_shape=[shape, shape],
        compiler_params=pltpu.CompilerParams(vmem_limit_bytes=20 * MIB),
        cost_estimate=pl.CostEstimate(flops=3 * matrix.size, bytes_accessed=8 * matrix.size, transcendentals=0),
    )(matrix)


def tile_of(q, size):
    me = lax.axis_index("tile")
    layers = size // 4
    side, across, by = q // (2 * layers), q // layers % 2, q % layers
    layer = lax.rem(lax.div(me, 4) + (layers - by), layers)
    row = lax.rem(lax.div(me, 2) + across, 2)
    core = lax.rem(me + side, 2)
    return layer * 4 + row * 2 + core


def product_kernel(sources, layout, inputs, sets, begin, end, finish, onward, relative, *refs):
    high_ref, low_ref = refs[inputs * sets:inputs * sets + 2]
    rest = refs[inputs * sets + 2:]
    count, both_rows, block = high_ref.shape
    own_rows = both_rows // 2
    start_ref, rest = (rest[0], rest[1:]) if begin > 0 else (None, rest)
    out_refs, total_ref = (rest[:-1], rest[-1]) if finish else ((), rest[0])
    columns = total_ref.shape[0]
    per_step = 4 if (end - begin) % 4 == 0 else 1

    def block_of(q):
        pieces = []
        for group in layout:
            which, place = group[q]
            value = refs[which][place]
            if sets == 2:
                value = refs[inputs + which][place] - value
            pieces.append(value)
        return jnp.concatenate(pieces, axis=0)

    @pl.when(jnp.logical_not(onward) | (lax.axis_index("chain") < lax.axis_size("chain") - 1))
    def _():
        for first in range(begin, end, per_step):
            tiles = [tile_of(q, count) if relative else q for q in range(first, first + per_step)]
            x_high, x_low = halves_of(jnp.concatenate([block_of(q) for q in range(first, first + per_step)], axis=1))
            k_high = jnp.concatenate([high_ref[tile] for tile in tiles], axis=1)
            k_low = jnp.concatenate([low_ref[tile] for tile in tiles], axis=1)
            both = lax.dot_general(jnp.concatenate([x_high, x_low], axis=0), k_high, lanes_contract, preferred_element_type=f32)
            part = both[:columns] + both[columns:] + lax.dot_general(x_high, k_low, lanes_contract, preferred_element_type=f32)
            if first > begin:
                total_ref[...] += part
            elif start_ref is None:
                total_ref[...] = part
            else:
                total_ref[...] = start_ref[...] + part
        start = 0
        for out_ref in out_refs:
            for first in range(0, out_ref.shape[0], 2 * sources):
                real = pl.ds(start + first, sources)
                imag = pl.ds(start + first + sources, sources)
                out_ref[first:first + sources, :] = total_ref[real, :own_rows] - total_ref[imag, own_rows:]
                out_ref[first + sources:first + 2 * sources, :] = total_ref[imag, :own_rows] + total_ref[real, own_rows:]
            start += out_ref.shape[0]


def product_part(split, onward, layout, blocks, own, begin, end, started, sources, shares):
    count, both_rows, block = split[0].shape
    vmem = pl.BlockSpec(memory_space=pltpu.VMEM)
    finish = end == count
    whole = (sum(shares), both_rows)
    arrays = list(blocks) + list(own) + list(split) + ([] if started is None else [started])
    if finish:
        out_shape = [jax.ShapeDtypeStruct((rows, both_rows // 2), f32) for rows in shares]
    else:
        out_shape = jax.ShapeDtypeStruct(whole, f32)
    return pl.pallas_call(
        functools.partial(product_kernel, sources, layout, len(blocks), 2 if own else 1, begin, end, finish, onward, len(layout) > 1),
        in_specs=[vmem] * len(arrays),
        out_specs=[vmem] * len(shares) if finish else vmem,
        out_shape=out_shape,
        scratch_shapes=[pltpu.VMEM(whole, f32)] if finish else [],
        compiler_params=pltpu.CompilerParams(vmem_limit_bytes=20 * MIB),
        cost_estimate=pl.CostEstimate(flops=6 * sum(shares) * both_rows * block * (end - begin), bytes_accessed=MIB, transcendentals=0),
    )(*arrays)


def tied(value, to):
    return lax.optimization_barrier((value, to))[0]


def solve_paired(reduced, diag_inverse, coupling, sources):
    chain_size = lax.axis_size("chain")
    tile_size = lax.axis_size("tile")
    own_rows = reduced[0].shape[1]
    shares = [each.shape[0] for each in reduced]
    layers = tile_size // 4
    count = tile_size
    places = [(side, across, by) for side in range(2) for across in range(2) for by in range(layers)]

    def send(value, hop, target):
        if not hop:
            return lax.ppermute(value, "tile", [(t, target(t)) for t in range(tile_size)])
        pairs = [(c * tile_size + t, (c + 1) * tile_size + target(t)) for c in range(chain_size - 1) for t in range(tile_size)]
        return lax.ppermute(value, ("chain", "tile"), pairs)

    def first_stage(first, second, hop):
        pair = [second if across == 0 and not hop else send(second, hop, lambda t: t ^ (2 * across)) for across in range(2)]
        line = [first if by == 0 and not hop else send(first, hop, lambda t: (t + 4 * by) % tile_size) for by in range(layers)]
        return jnp.stack(pair), jnp.stack(line)

    def second_stage(pair, line):
        far = send(line, False, lambda t: t ^ 2)
        rest = [pair if by == 0 else send(pair, False, lambda t: (t + 4 * by) % tile_size) for by in range(layers)]
        return [line, far, jnp.stack(rest)]

    layout = [
        [(across, (by,)) for side, across, by in places],
        [(2, (by, across)) for side, across, by in places],
    ]

    def products(split, onward, held, own, shares):
        other = [send(each, False, lambda t: t ^ 1) for each in held]
        mine, theirs = own if own else ([], [])
        started = product_part(split, onward, layout, held, mine, 0, count // 2, None, sources, shares)
        return product_part(split, onward, layout, other, theirs, count // 2, count, started, sources, shares), other

    only = chain_size == 1
    pair, line = first_stage(*reduced, False)
    split = split_blocks(tied(diag_inverse if only else coupling, reduced[0]), own_rows)
    pair, line, split = lax.optimization_barrier((pair, line, split))
    held = second_stage(pair, line)
    if only:
        return products(split, False, held, None, [sum(shares)])[0][0]
    diag_split = split_blocks(tied(diag_inverse, line), own_rows)
    held[1], held[2], diag_split = lax.optimization_barrier((held[1], held[2], diag_split))
    carried, other = products(split, True, held, None, shares)
    own = (held, other)
    for step in range(chain_size - 1):
        held = second_stage(*lax.optimization_barrier(first_stage(*carried, True)))
        if step < chain_size - 2:
            carried = products(split, True, held, own, shares)[0]
    return products(diag_split, False, held, own, [sum(shares)])[0][0]


def solve_flat(reduced, diag_inverse, coupling, sources):
    chain_size = lax.axis_size("chain")
    reduced = reduced[0]
    columns = reduced.shape[0]
    full_rows = diag_inverse.shape[2]
    block = min(256, full_rows)
    count = full_rows // block
    layout = [[(0, (q,)) for q in range(count)]]
    onward = [(i, i + 1) for i in range(chain_size - 1)]
    diag_split = split_blocks(diag_inverse, block)
    coupling_split = split_blocks(coupling, block)

    def gathered(value):
        whole = lax.all_gather(value, "tile", axis=1, tiled=True)
        return [whole.reshape(columns, count, block).transpose(1, 0, 2)]

    current = reduced
    for _ in range(chain_size - 1):
        carried = product_part(coupling_split, True, layout, gathered(current), [], 0, count, None, sources, [columns])[0]
        current = reduced - lax.ppermute(carried, "chain", onward)
    return product_part(diag_split, False, layout, gathered(current), [], 0, count, None, sources, [columns])[0]


def body(right_side, diag_inverse, coupling, updates, update_rows, tile_counts):
    batches, halves, sources, own_rows = right_side.shape
    tile_size = lax.axis_size("tile")
    entries, columns = updates.shape
    tile_rows = entries // tile_counts.shape[0]
    cap = 2 * entries // tile_size
    slots = tile_size * cap
    vmem = pl.BlockSpec(memory_space=pltpu.VMEM)
    hbm = pl.BlockSpec(memory_space=pltpu.HBM)
    folded = cap % 16 == 0 and slots <= 1024 and columns == 192 and own_rows <= 256 and 128 % cap == 0
    width = 128 if folded else -(-(columns + 1) // 128) * 128
    height = cap + cap // 2 + 8 if folded else cap
    packed = pl.pallas_call(
        functools.partial(pack_kernel, own_rows, cap, tile_rows),
        in_specs=[hbm, hbm, hbm],
        out_specs=vmem,
        out_shape=jax.ShapeDtypeStruct((tile_size, height, width), f32),
        scratch_shapes=[
            pltpu.SMEM(tile_counts.shape, jnp.int32),
            pltpu.VMEM((1, entries), jnp.int32),
            pltpu.VMEM((columns, entries), f32),
            pltpu.SemaphoreType.DMA((3,)),
        ],
        compiler_params=kernel_params(),
    )(tile_counts, update_rows[None, :], updates.T)
    received = lax.all_to_all(packed, "tile", 0, 0, tiled=False)
    paired = own_rows % 128 == 0 and tile_size % 8 == 0 and batches > 1
    early = batches * 2 // 3 * halves * sources
    shares = [early, columns - early] if paired else [columns]
    reduced = pl.pallas_call(
        functools.partial(reduce_kernel, cap),
        in_specs=[vmem, hbm],
        out_specs=[vmem] * len(shares),
        out_shape=[jax.ShapeDtypeStruct((rows, own_rows), f32) for rows in shares],
        scratch_shapes=[pltpu.VMEM((columns, own_rows), f32), pltpu.SemaphoreType.DMA(())],
        compiler_params=kernel_params(),
    )(received, right_side.reshape(columns, own_rows))
    solve = solve_paired if paired else solve_flat
    return solve(reduced, diag_inverse, coupling, sources).reshape(right_side.shape)


def solution(mesh):
    in_specs = (
        P(None, None, None, ("chain", "tile")),
        P(None, ("chain", "tile"), None),
        P(None, ("chain", "tile"), None),
        P(("chain", "tile"), None),
        P(("chain", "tile")),
        P(("chain", "tile")),
    )
    out_specs = P(None, None, None, ("chain", "tile"))
    return jax.shard_map(body, mesh=mesh, in_specs=in_specs, out_specs=out_specs, check_vma=False)
```

time: 109 us -> 98 us (0.90)
  local copies, waits for them, and re-layouts: 15.2 us -> 3.39 us
  waiting for transfers between devices: 27.8 us -> 34 us
  starting transfers between devices: 26.7 us -> 23.7 us
  Pallas kernels: 16.6 us -> 14 us
  other arithmetic: 0.16 us -> 1.42 us
  blocking collectives: 22 us -> 20.8 us
    unnamed x16 -> x6, local copies, waits for them, and re-layouts: 15.1 us -> 3.39 us
    ppermute x6, waiting for transfers between devices: 0.8 us -> 7.8 us  [send(): return lax.ppermute(value, ('chain', 'tile'), pairs)]
    pallas_call x5 -> x7, Pallas kernels: 14.4 us -> 11.7 us  [the longest x4 7.19 us: product_part(): pl.pallas_call(functools.partial(product_kernel, sources, layout, len(blo...]
    ppermute x6, starting transfers between devices: 10.8 us -> 9.09 us  [send(): return lax.ppermute(value, ('chain', 'tile'), pairs)]
    ppermute x18, starting transfers between devices: 16 us -> 14.6 us  [send(): lax.ppermute(value, 'tile', [(t, target(t)) for t in range(tile_size)])]
    another operation x6, other arithmetic: 0.16 us -> 1.42 us  [the longest x4 1.36 us: first_stage(): return (jnp.stack(pair), jnp.stack(line))]
    all_to_all x1, blocking collectives: 22 us -> 20.8 us  [body(): received = lax.all_to_all(packed, 'tile', 0, 0, tiled=False)]
  transfers between devices with their start and end apart: 24 -> 24, of which waited for: 10 -> 10; matrix products, arithmetic and copies ran while one was open for 0% -> 1% of each run, Pallas kernels for 4% -> 5%
where the time goes in v5:
time: 98 us; the launch traced here: 97.5 us
  waiting for transfers between devices  34 us (35%)
  starting transfers between devices  23.7 us (24%)
  blocking collectives  20.8 us (21%)
  Pallas kernels  14 us (14%)
  local copies, waits for them, and re-layouts  3.39 us (3%)
  other arithmetic  1.42 us (1%)
    ppermute x18, waiting for transfers between devices, send(): lax.ppermute(value, 'tile', [(t, target(t)) for t in range(tile_size)])  26.2 us
    all_to_all x1, blocking collectives, body(): received = lax.all_to_all(packed, 'tile', 0, 0, tiled=False)  20.8 us
    ppermute x18, starting transfers between devices, send(): lax.ppermute(value, 'tile', [(t, target(t)) for t in range(tile_size)])  14.6 us
    ppermute x6, starting transfers between devices, send(): return lax.ppermute(value, ('chain', 'tile'), pairs)  9.09 us
    ppermute x6, waiting for transfers between devices, send(): return lax.ppermute(value, ('chain', 'tile'), pairs)  7.8 us
    pallas_call x4, Pallas kernels, product_part(): pl.pallas_call(functools.partial(product_kernel, sources, layout, len(blo...  7.19 us
    unnamed x6, local copies, waits for them, and re-layouts  3.39 us
    pallas_call x1, Pallas kernels, body(): pl.pallas_call(functools.partial(reduce_kernel, cap), in_specs=[vmem, hbm...  2.64 us
  transfers between devices with their start and end apart: 24, of which 10 were waited for; matrix products, arithmetic and copies ran while one was open for 1% of the time, Pallas kernels for 5%

profile of v5, /device:TPU:0, one launch (start us, length us, event | category | flops | bytes accessed | tf_op | source)
XLA Modules:
  0.0 97.5 jit_solution(13466676224000100585)
XLA Ops:
  0.0 2.3 %shard_map.64 = f32[16,56,128]{2,1,0:T(8,128)} custom-call(s32[2]{0:T(128)} %counts_hbm.1, s32[1,256]{1,0:T(1,128)} %bitcast.46, f32[192,256]{1,0:T(8,128)} %bitcast.26), custom_call_target="tpu_custom_call" | custom-call | tf_op jit(solution)/shard_map/pallas_call | solution.py:315
  2.3 20.8 %all_to_all.5.received_ref = f32[16,56,128]{2,1,0:T(8,128)} all-to-all(f32[16,56,128]{2,1,0:T(8,128)} %shard_map.64), channel_id=1, replica_groups=mesh['chain'=2,'tile'=16] {'tile'}, dimensions={0} | all-to-all | bytes 917504 | tf_op jit(solution)/shard_map/all_to_all | solution.py:328
  23.0 2.6 %shard_map.65 = (f32[128,256]{1,0:T(8,128)}, f32[64,256]{1,0:T(8,128)}) custom-call(f32[16,56,128]{2,1,0:T(8,128)} %all_to_all.5.received_ref, f32[192,256]{1,0:T(8,128)} %bitcast.27), custom_call_target="tpu_custom_call" | custom-call | tf_op jit(solution)/shard_map/pallas_call | solution.py:332
  25.7 0.4 collective-permute-start
  26.1 2.7 %collective-permute-start.3 = (f32[128,256]{1,0:T(8,128)}, f32[128,256]{1,0:T(8,128)S(1)}, u32[]{:S(2)}, u32[]{:S(2)}) collective-permute-start(f32[128,256]{1,0:T(8,128)} %get-tuple-element.26), channel_id=1, source_target_pairs={{0,12},{1,13},{2,14},{3,15},{4,0},{5,1},{6,2},{7,3},{8,4},{9,5},{1... | collective-permute-start | bytes 393224 | tf_op jit(solution)/shard_map/ppermute | solution.py:237
  28.8 0.5 collective-permute-start.2
  29.4 0.5 collective-permute-start.1
  29.9 0.0 copy-start
  29.9 3.4 %copy-done = f32[2,256,4096]{2,1,0:T(8,128)S(1)} copy-done((f32[2,256,4096]{2,1,0:T(8,128)S(1)}, f32[2,256,4096]{2,1,0:T(8,128)}, u32[]{:S(2)}) %copy-start) | copy-done | bytes 8388632
  33.3 0.0 copy-start.2
  33.3 0.0 copy-start.1
  33.3 0.9 shard_map.66
  34.3 0.0 collective-permute-done
  34.3 1.3 %pad_maximum_fusion.4 = f32[2,64,256]{2,1,0:T(8,128)S(1)} fusion(f32[1,64,256]{2,1,0:T(8,128)S(1)} %bitcast.45, f32[1,64,256]{2,1,0:T(8,128)} %bitcast.43), kind=kLoop, calls=%fused_computation.4 | loop fusion | flops 32768 | bytes 262144 | tf_op jit(solution)/shard_map/stack | solution.py:244
  35.5 0.0 collective-permute-done.3
  35.6 5.9 %collective-permute-done.2 = f32[128,256]{1,0:T(8,128)S(1)} collective-permute-done((f32[128,256]{1,0:T(8,128)}, f32[128,256]{1,0:T(8,128)S(1)}, u32[]{:S(2)}, u32[]{:S(2)}) %collective-permute-start.2) | collective-permute-done | bytes 131104 | tf_op jit(solution)/shard_map/ppermute | solution.py:237
  41.4 0.0 collective-permute-done.1
  41.4 0.0 copy-done.2
  41.5 1.2 %collective-permute-start.5 = (f32[4,128,256]{2,1,0:T(8,128)S(1)}, f32[4,128,256]{2,1,0:T(8,128)S(1)}, u32[]{:S(2)}, u32[]{:S(2)}) collective-permute-start(f32[4,128,256]{2,1,0:T(8,128)S(1)} %pad_maximum_fusion.refs_0_.refs_3_), channel_id=1, source_target_pairs={{0,2},{1,3},{2,0},{3,1},{4,6},{5,7},{6,4},{7,5},{8,10},{9,11},{10,... | collective-permute-start | bytes 1572872 | tf_op jit(solution)/shard_map/ppermute | solution.py:237
  42.7 0.0 collective-permute-start.8
  42.7 1.7 %collective-permute-start.7 = (f32[2,64,256]{2,1,0:T(8,128)S(1)}, f32[2,64,256]{2,1,0:T(8,128)S(1)}, u32[]{:S(2)}, u32[]{:S(2)}) collective-permute-start(f32[2,64,256]{2,1,0:T(8,128)S(1)} %pad_maximum_fusion.4), channel_id=1, source_target_pairs={{0,8},{1,9},{2,10},{3,11},{4,12},{5,13},{6,14},{7,15},{8,0},{9,1},... | collective-permute-start | bytes 393224 | tf_op jit(solution)/shard_map/ppermute | solution.py:237
  44.4 2.0 %collective-permute-start.6 = (f32[2,64,256]{2,1,0:T(8,128)S(1)}, f32[2,64,256]{2,1,0:T(8,128)S(1)}, u32[]{:S(2)}, u32[]{:S(2)}) collective-permute-start(f32[2,64,256]{2,1,0:T(8,128)S(1)} %pad_maximum_fusion.4), channel_id=1, source_target_pairs={{0,4},{1,5},{2,6},{3,7},{4,8},{5,9},{6,10},{7,11},{8,12},{9,13},{1... | collective-permute-start | bytes 393224 | tf_op jit(solution)/shard_map/ppermute | solution.py:237
  46.5 0.0 collective-permute-start.4
  46.5 0.0 copy-done.1
  46.5 0.9 shard_map.67
  47.4 0.8 collective-permute-done.8
  48.2 8.0 %collective-permute-done.7 = f32[2,64,256]{2,1,0:T(8,128)S(1)} collective-permute-done((f32[2,64,256]{2,1,0:T(8,128)S(1)}, f32[2,64,256]{2,1,0:T(8,128)S(1)}, u32[]{:S(2)}, u32[]{:S(2)}) %collective-permute-start.7) | collective-permute-done | bytes 131104 | tf_op jit(solution)/shard_map/ppermute | solution.py:237
  56.2 0.0 collective-permute-done.6
  56.2 0.0 collective-permute-done.5.refs_1_.refs_4_
  56.2 0.1 collective-permute-start.9
  56.3 0.5 collective-permute-start.10
  56.8 1.7 %shard_map.68.refs_5_ = f32[192,512]{1,0:T(8,128)S(1)} custom-call(f32[4,128,256]{2,1,0:T(8,128)S(1)} %pad_maximum_fusion.refs_0_.refs_3_, f32[4,128,256]{2,1,0:T(8,128)S(1)} %collective-permute-done.5.refs_1_.refs_4_, f32[4,2,64,256]{3,2,1,0:T(8,128)S(1)} %pad_maximum_fusion.1.refs_2_.refs_5_, bf16[16,512,256]{2,1,0:T(8,128)(2,1)S(1)} %get-tuple-element.37.refs_3_, ...), custom_call_target="tpu_custom_call" | custom-call | flops 1207959552 | bytes 1048576 | tf_op jit(solution)/shard_map/pallas_call | solution.py:211
  58.5 0.0 collective-permute-done.4.refs_0_.refs_3_
  58.5 0.0 collective-permute-done.9.refs_1_.refs_4_
  58.5 0.5 collective-permute-done.10.refs_2_.refs_5_
  59.0 1.6 %shard_map.69 = (f32[128,256]{1,0:T(8,128)S(1)}, f32[64,256]{1,0:T(8,128)S(1)}) custom-call(f32[4,128,256]{2,1,0:T(8,128)S(1)} %collective-permute-done.4.refs_0_.refs_3_, f32[4,128,256]{2,1,0:T(8,128)S(1)} %collective-permute-done.9.refs_1_.refs_4_, f32[4,2,64,256]{3,2,1,0:T(8,128)S(1)} %collective-permute-done.10.refs_2_.refs_5_, ...), custom_call_target="tpu_custom_call" | custom-call | flops 1207959552 | bytes 1048576 | tf_op jit(solution)/shard_map/pallas_call | solution.py:211
  60.6 1.6 %collective-permute-start.12 = (f32[64,256]{1,0:T(8,128)S(1)}, f32[64,256]{1,0:T(8,128)S(1)}, u32[]{:S(2)}, u32[]{:S(2)}) collective-permute-start(f32[64,256]{1,0:T(8,128)S(1)} %get-tuple-element.39), channel_id=1, source_target_pairs={{0,18},{1,19},{2,16},{3,17},{4,22},{5,23},{6,20},{7,21},{8,26},{9,... | collective-permute-start | bytes 196616 | tf_op jit(solution)/shard_map/ppermute | solution.py:239
  62.1 1.5 %collective-permute-start.11 = (f32[64,256]{1,0:T(8,128)S(1)}, f32[64,256]{1,0:T(8,128)S(1)}, u32[]{:S(2)}, u32[]{:S(2)}) collective-permute-start(f32[64,256]{1,0:T(8,128)S(1)} %get-tuple-element.39), channel_id=1, source_target_pairs={{0,16},{1,17},{2,18},{3,19},{4,20},{5,21},{6,22},{7,23},{8,24},{9,... | collective-permute-start | bytes 196616 | tf_op jit(solution)/shard_map/ppermute | solution.py:239
  63.7 1.3 %collective-permute-start.16 = (f32[128,256]{1,0:T(8,128)S(1)}, f32[128,256]{1,0:T(8,128)S(1)}, u32[]{:S(2)}, u32[]{:S(2)}) collective-permute-start(f32[128,256]{1,0:T(8,128)S(1)} %get-tuple-element.40), channel_id=1, source_target_pairs={{0,28},{1,29},{2,30},{3,31},{4,16},{5,17},{6,18},{7,19},{8,20},{9,... | collective-permute-start | bytes 393224 | tf_op jit(solution)/shard_map/ppermute | solution.py:239
  65.0 1.5 %collective-permute-start.15 = (f32[128,256]{1,0:T(8,128)S(1)}, f32[128,256]{1,0:T(8,128)S(1)}, u32[]{:S(2)}, u32[]{:S(2)}) collective-permute-start(f32[128,256]{1,0:T(8,128)S(1)} %get-tuple-element.40), channel_id=1, source_target_pairs={{0,24},{1,25},{2,26},{3,27},{4,28},{5,29},{6,30},{7,31},{8,16},{9,... | collective-permute-start | bytes 393224 | tf_op jit(solution)/shard_map/ppermute | solution.py:239
  66.5 1.3 %collective-permute-start.14 = (f32[128,256]{1,0:T(8,128)S(1)}, f32[128,256]{1,0:T(8,128)S(1)}, u32[]{:S(2)}, u32[]{:S(2)}) collective-permute-start(f32[128,256]{1,0:T(8,128)S(1)} %get-tuple-element.40), channel_id=1, source_target_pairs={{0,20},{1,21},{2,22},{3,23},{4,24},{5,25},{6,26},{7,27},{8,28},{9,... | collective-permute-start | bytes 393224 | tf_op jit(solution)/shard_map/ppermute | solution.py:239
  67.8 0.0 collective-permute-done.12
  67.8 1.9 %collective-permute-start.13 = (f32[128,256]{1,0:T(8,128)S(1)}, f32[128,256]{1,0:T(8,128)S(1)}, u32[]{:S(2)}, u32[]{:S(2)}) collective-permute-start(f32[128,256]{1,0:T(8,128)S(1)} %get-tuple-element.40), channel_id=1, source_target_pairs={{0,16},{1,17},{2,18},{3,19},{4,20},{5,21},{6,22},{7,23},{8,24},{9,... | collective-permute-start | bytes 393224 | tf_op jit(solution)/shard_map/ppermute | solution.py:239
  69.7 0.0 collective-permute-done.11
  69.7 0.0 collective-permute-done.16
  69.8 1.9 %collective-permute-done.15 = f32[128,256]{1,0:T(8,128)S(1)} collective-permute-done((f32[128,256]{1,0:T(8,128)S(1)}, f32[128,256]{1,0:T(8,128)S(1)}, u32[]{:S(2)}, u32[]{:S(2)}) %collective-permute-start.15) | collective-permute-done | bytes 131104 | tf_op jit(solution)/shard_map/ppermute | solution.py:239
  71.7 2.3 %collective-permute-done.14 = f32[128,256]{1,0:T(8,128)S(1)} collective-permute-done((f32[128,256]{1,0:T(8,128)S(1)}, f32[128,256]{1,0:T(8,128)S(1)}, u32[]{:S(2)}, u32[]{:S(2)}) %collective-permute-start.14) | collective-permute-done | bytes 131104 | tf_op jit(solution)/shard_map/ppermute | solution.py:239
  74.0 3.6 %collective-permute-done.13 = f32[128,256]{1,0:T(8,128)S(1)} collective-permute-done((f32[128,256]{1,0:T(8,128)S(1)}, f32[128,256]{1,0:T(8,128)S(1)}, u32[]{:S(2)}, u32[]{:S(2)}) %collective-permute-start.13) | collective-permute-done | bytes 131104 | tf_op jit(solution)/shard_map/ppermute | solution.py:239
  77.6 1.0 %collective-permute-start.18 = (f32[4,128,256]{2,1,0:T(8,128)S(1)}, f32[4,128,256]{2,1,0:T(8,128)S(1)}, u32[]{:S(2)}, u32[]{:S(2)}) collective-permute-start(f32[4,128,256]{2,1,0:T(8,128)S(1)} %pad_maximum_fusion.2.refs_0_), channel_id=1, source_target_pairs={{0,2},{1,3},{2,0},{3,1},{4,6},{5,7},{6,4},{7,5},{8,10},{9,11},{10,... | collective-permute-start | bytes 1572872 | tf_op jit(solution)/shard_map/ppermute | solution.py:237
  78.6 2.7 %collective-permute-start.22 = (f32[2,64,256]{2,1,0:T(8,128)S(1)}, f32[2,64,256]{2,1,0:T(8,128)S(1)}, u32[]{:S(2)}, u32[]{:S(2)}) collective-permute-start(f32[2,64,256]{2,1,0:T(8,128)S(1)} %pad_maximum_fusion.5), channel_id=1, source_target_pairs={{0,12},{1,13},{2,14},{3,15},{4,0},{5,1},{6,2},{7,3},{8,4},{9,5},{1... | collective-permute-start | bytes 393224 | tf_op jit(solution)/shard_map/ppermute | solution.py:237
  81.3 0.0 collective-permute-start.21
  81.3 0.6 collective-permute-start.20
  81.8 0.0 collective-permute-start.17
  81.8 3.3 %collective-permute-done.22 = f32[2,64,256]{2,1,0:T(8,128)S(1)} collective-permute-done((f32[2,64,256]{2,1,0:T(8,128)S(1)}, f32[2,64,256]{2,1,0:T(8,128)S(1)}, u32[]{:S(2)}, u32[]{:S(2)}) %collective-permute-start.22) | collective-permute-done | bytes 131104 | tf_op jit(solution)/shard_map/ppermute | solution.py:237
  85.2 7.3 %collective-permute-done.21 = f32[2,64,256]{2,1,0:T(8,128)S(1)} collective-permute-done((f32[2,64,256]{2,1,0:T(8,128)S(1)}, f32[2,64,256]{2,1,0:T(8,128)S(1)}, u32[]{:S(2)}, u32[]{:S(2)}) %collective-permute-start.21) | collective-permute-done | bytes 131104 | tf_op jit(solution)/shard_map/ppermute | solution.py:237
  92.5 0.0 collective-permute-done.20
  92.5 0.1 collective-permute-start.23
  92.6 0.0 collective-permute-done.18.refs_1_
  92.6 0.5 collective-permute-start.19
  93.1 1.7 %shard_map.70.refs_8_ = f32[192,512]{1,0:T(8,128)S(1)} custom-call(f32[4,128,256]{2,1,0:T(8,128)S(1)} %pad_maximum_fusion.2.refs_0_, f32[4,128,256]{2,1,0:T(8,128)S(1)} %collective-permute-done.18.refs_1_, f32[4,2,64,256]{3,2,1,0:T(8,128)S(1)} %pad_maximum_fusion.3.refs_2_, f32[4,128,256]{2,1,0:T(8,128)S(1)} %pad_maximum_fusion.refs_0_.refs_3_, ...), custom_call_target="tpu_custom_call" | custom-call | flops 1207959552 | bytes 1048576 | tf_op jit(solution)/shard_map/pallas_call | solution.py:211
  94.8 0.0 collective-permute-done.17.refs_0_
  94.8 0.0 collective-permute-done.23.refs_2_
  94.8 0.5 collective-permute-done.19.refs_1_
  95.2 2.3 %shard_map.71 = f32[192,256]{1,0:T(8,128)} custom-call(f32[4,128,256]{2,1,0:T(8,128)S(1)} %collective-permute-done.17.refs_0_, f32[4,128,256]{2,1,0:T(8,128)S(1)} %collective-permute-done.19.refs_1_, f32[4,2,64,256]{3,2,1,0:T(8,128)S(1)} %collective-permute-done.23.refs_2_, f32[4,128,256]{2,1,0:T(8,128)S(1)} %collective-permute-done.4.refs_0_.refs_3_, ...), custom_call_target="tpu_custom_call" | custom-call | flops 1207959552 | bytes 1048576 | tf_op jit(solution)/shard_map/pallas_call | solution.py:211
  (5 shorter events, 0.2 us)
Async XLA Ops:
  25.7 8.6 %collective-permute-start = (f32[64,256]{1,0:T(8,128)}, f32[64,256]{1,0:T(8,128)S(1)}, u32[]{:S(2)}, u32[]{:S(2)}) collective-permute-start(f32[64,256]{1,0:T(8,128)} %get-tuple-element.25), channel_id=1, source_target_pairs={{0,2},{1,3},{2,0},{3,1},{4,6},{5,7},{6,4},{7,5},{8,10},{9,11},{10,... | collective-permute-start | bytes 196616 | tf_op jit(solution)/shard_map/ppermute | solution.py:237
  26.1 9.4 %collective-permute-start.3 = (f32[128,256]{1,0:T(8,128)}, f32[128,256]{1,0:T(8,128)S(1)}, u32[]{:S(2)}, u32[]{:S(2)}) collective-permute-start(f32[128,256]{1,0:T(8,128)} %get-tuple-element.26), channel_id=1, source_target_pairs={{0,12},{1,13},{2,14},{3,15},{4,0},{5,1},{6,2},{7,3},{8,4},{9,5},{1... | collective-permute-start | bytes 393224 | tf_op jit(solution)/shard_map/ppermute | solution.py:237
  28.8 12.6 %collective-permute-start.2 = (f32[128,256]{1,0:T(8,128)}, f32[128,256]{1,0:T(8,128)S(1)}, u32[]{:S(2)}, u32[]{:S(2)}) collective-permute-start(f32[128,256]{1,0:T(8,128)} %get-tuple-element.26), channel_id=1, source_target_pairs={{0,8},{1,9},{2,10},{3,11},{4,12},{5,13},{6,14},{7,15},{8,0},{9,1},... | collective-permute-start | bytes 393224 | tf_op jit(solution)/shard_map/ppermute | solution.py:237
  29.4 12.0 %collective-permute-start.1 = (f32[128,256]{1,0:T(8,128)}, f32[128,256]{1,0:T(8,128)S(1)}, u32[]{:S(2)}, u32[]{:S(2)}) collective-permute-start(f32[128,256]{1,0:T(8,128)} %get-tuple-element.26), channel_id=1, source_target_pairs={{0,4},{1,5},{2,6},{3,7},{4,8},{5,9},{6,10},{7,11},{8,12},{9,13},{1... | collective-permute-start | bytes 393224 | tf_op jit(solution)/shard_map/ppermute | solution.py:237
  29.9 3.4 %copy-start = (f32[2,256,4096]{2,1,0:T(8,128)S(1)}, f32[2,256,4096]{2,1,0:T(8,128)}, u32[]{:S(2)}) copy-start(f32[2,256,4096]{2,1,0:T(8,128)} %matrix_ref) | copy-start | bytes 25165828
  33.3 8.1 %copy-start.2 = (f32[128,256]{1,0:T(8,128)S(1)}, f32[128,256]{1,0:T(8,128)}, u32[]{:S(2)}) copy-start(f32[128,256]{1,0:T(8,128)} %get-tuple-element.26) | copy-start | bytes 393220
  33.3 13.2 %copy-start.1 = (f32[2,256,4096]{2,1,0:T(8,128)S(1)}, f32[2,256,4096]{2,1,0:T(8,128)}, u32[]{:S(2)}) copy-start(f32[2,256,4096]{2,1,0:T(8,128)} %matrix_ref.1) | copy-start | bytes 25165828
  41.5 14.8 %collective-permute-start.5 = (f32[4,128,256]{2,1,0:T(8,128)S(1)}, f32[4,128,256]{2,1,0:T(8,128)S(1)}, u32[]{:S(2)}, u32[]{:S(2)}) collective-permute-start(f32[4,128,256]{2,1,0:T(8,128)S(1)} %pad_maximum_fusion.refs_0_.refs_3_), channel_id=1, source_target_pairs={{0,2},{1,3},{2,0},{3,1},{4,6},{5,7},{6,4},{7,5},{8,10},{9,11},{10,... | collective-permute-start | bytes 1572872 | tf_op jit(solution)/shard_map/ppermute | solution.py:237
  42.7 5.6 %collective-permute-start.8 = (f32[2,64,256]{2,1,0:T(8,128)S(1)}, f32[2,64,256]{2,1,0:T(8,128)S(1)}, u32[]{:S(2)}, u32[]{:S(2)}) collective-permute-start(f32[2,64,256]{2,1,0:T(8,128)S(1)} %pad_maximum_fusion.4), channel_id=1, source_target_pairs={{0,12},{1,13},{2,14},{3,15},{4,0},{5,1},{6,2},{7,3},{8,4},{9,5},{1... | collective-permute-start | bytes 393224 | tf_op jit(solution)/shard_map/ppermute | solution.py:237
  42.7 13.5 %collective-permute-start.7 = (f32[2,64,256]{2,1,0:T(8,128)S(1)}, f32[2,64,256]{2,1,0:T(8,128)S(1)}, u32[]{:S(2)}, u32[]{:S(2)}) collective-permute-start(f32[2,64,256]{2,1,0:T(8,128)S(1)} %pad_maximum_fusion.4), channel_id=1, source_target_pairs={{0,8},{1,9},{2,10},{3,11},{4,12},{5,13},{6,14},{7,15},{8,0},{9,1},... | collective-permute-start | bytes 393224 | tf_op jit(solution)/shard_map/ppermute | solution.py:237
  44.4 11.8 %collective-permute-start.6 = (f32[2,64,256]{2,1,0:T(8,128)S(1)}, f32[2,64,256]{2,1,0:T(8,128)S(1)}, u32[]{:S(2)}, u32[]{:S(2)}) collective-permute-start(f32[2,64,256]{2,1,0:T(8,128)S(1)} %pad_maximum_fusion.4), channel_id=1, source_target_pairs={{0,4},{1,5},{2,6},{3,7},{4,8},{5,9},{6,10},{7,11},{8,12},{9,13},{1... | collective-permute-start | bytes 393224 | tf_op jit(solution)/shard_map/ppermute | solution.py:237
  46.5 12.0 %collective-permute-start.4 = (f32[4,128,256]{2,1,0:T(8,128)S(1)}, f32[4,128,256]{2,1,0:T(8,128)S(1)}, u32[]{:S(2)}, u32[]{:S(2)}) collective-permute-start(f32[4,128,256]{2,1,0:T(8,128)S(1)} %pad_maximum_fusion.refs_0_.refs_3_), channel_id=1, source_target_pairs={{0,1},{1,0},{2,3},{3,2},{4,5},{5,4},{6,7},{7,6},{8,9},{9,8},{10,11... | collective-permute-start | bytes 1572872 | tf_op jit(solution)/shard_map/ppermute | solution.py:237
  56.2 2.3 %collective-permute-start.9 = (f32[4,128,256]{2,1,0:T(8,128)S(1)}, f32[4,128,256]{2,1,0:T(8,128)S(1)}, u32[]{:S(2)}, u32[]{:S(2)}) collective-permute-start(f32[4,128,256]{2,1,0:T(8,128)S(1)} %collective-permute-done.5.refs_1_.refs_4_), channel_id=1, source_target_pairs={{0,1},{1,0},{2,3},{3,2},{4,5},{5,4},{6,7},{7,6},{8,9},{9,8},{10,11... | collective-permute-start | bytes 1572872 | tf_op jit(solution)/shard_map/ppermute | solution.py:237
  56.3 2.6 %collective-permute-start.10 = (f32[4,2,64,256]{3,2,1,0:T(8,128)S(1)}, f32[4,2,64,256]{3,2,1,0:T(8,128)S(1)}, u32[]{:S(2)}, u32[]{:S(2)}) collective-permute-start(f32[4,2,64,256]{3,2,1,0:T(8,128)S(1)} %pad_maximum_fusion.1.refs_2_.refs_5_), channel_id=1, source_target_pairs={{0,1},{1,0},{2,3},{3,2},{4,5},{5,4},{6,7},{7,6},{8,9},{9,8},{10,11... | collective-permute-start | bytes 1572872 | tf_op jit(solution)/shard_map/ppermute | solution.py:237
  60.6 7.2 %collective-permute-start.12 = (f32[64,256]{1,0:T(8,128)S(1)}, f32[64,256]{1,0:T(8,128)S(1)}, u32[]{:S(2)}, u32[]{:S(2)}) collective-permute-start(f32[64,256]{1,0:T(8,128)S(1)} %get-tuple-element.39), channel_id=1, source_target_pairs={{0,18},{1,19},{2,16},{3,17},{4,22},{5,23},{6,20},{7,21},{8,26},{9,... | collective-permute-start | bytes 196616 | tf_op jit(solution)/shard_map/ppermute | solution.py:239
  62.1 7.6 %collective-permute-start.11 = (f32[64,256]{1,0:T(8,128)S(1)}, f32[64,256]{1,0:T(8,128)S(1)}, u32[]{:S(2)}, u32[]{:S(2)}) collective-permute-start(f32[64,256]{1,0:T(8,128)S(1)} %get-tuple-element.39), channel_id=1, source_target_pairs={{0,16},{1,17},{2,18},{3,19},{4,20},{5,21},{6,22},{7,23},{8,24},{9,... | collective-permute-start | bytes 196616 | tf_op jit(solution)/shard_map/ppermute | solution.py:239
  63.7 6.1 %collective-permute-start.16 = (f32[128,256]{1,0:T(8,128)S(1)}, f32[128,256]{1,0:T(8,128)S(1)}, u32[]{:S(2)}, u32[]{:S(2)}) collective-permute-start(f32[128,256]{1,0:T(8,128)S(1)} %get-tuple-element.40), channel_id=1, source_target_pairs={{0,28},{1,29},{2,30},{3,31},{4,16},{5,17},{6,18},{7,19},{8,20},{9,... | collective-permute-start | bytes 393224 | tf_op jit(solution)/shard_map/ppermute | solution.py:239
  65.0 6.7 %collective-permute-start.15 = (f32[128,256]{1,0:T(8,128)S(1)}, f32[128,256]{1,0:T(8,128)S(1)}, u32[]{:S(2)}, u32[]{:S(2)}) collective-permute-start(f32[128,256]{1,0:T(8,128)S(1)} %get-tuple-element.40), channel_id=1, source_target_pairs={{0,24},{1,25},{2,26},{3,27},{4,28},{5,29},{6,30},{7,31},{8,16},{9,... | collective-permute-start | bytes 393224 | tf_op jit(solution)/shard_map/ppermute | solution.py:239
  66.5 7.5 %collective-permute-start.14 = (f32[128,256]{1,0:T(8,128)S(1)}, f32[128,256]{1,0:T(8,128)S(1)}, u32[]{:S(2)}, u32[]{:S(2)}) collective-permute-start(f32[128,256]{1,0:T(8,128)S(1)} %get-tuple-element.40), channel_id=1, source_target_pairs={{0,20},{1,21},{2,22},{3,23},{4,24},{5,25},{6,26},{7,27},{8,28},{9,... | collective-permute-start | bytes 393224 | tf_op jit(solution)/shard_map/ppermute | solution.py:239
  67.8 9.8 %collective-permute-start.13 = (f32[128,256]{1,0:T(8,128)S(1)}, f32[128,256]{1,0:T(8,128)S(1)}, u32[]{:S(2)}, u32[]{:S(2)}) collective-permute-start(f32[128,256]{1,0:T(8,128)S(1)} %get-tuple-element.40), channel_id=1, source_target_pairs={{0,16},{1,17},{2,18},{3,19},{4,20},{5,21},{6,22},{7,23},{8,24},{9,... | collective-permute-start | bytes 393224 | tf_op jit(solution)/shard_map/ppermute | solution.py:239
  77.6 15.0 %collective-permute-start.18 = (f32[4,128,256]{2,1,0:T(8,128)S(1)}, f32[4,128,256]{2,1,0:T(8,128)S(1)}, u32[]{:S(2)}, u32[]{:S(2)}) collective-permute-start(f32[4,128,256]{2,1,0:T(8,128)S(1)} %pad_maximum_fusion.2.refs_0_), channel_id=1, source_target_pairs={{0,2},{1,3},{2,0},{3,1},{4,6},{5,7},{6,4},{7,5},{8,10},{9,11},{10,... | collective-permute-start | bytes 1572872 | tf_op jit(solution)/shard_map/ppermute | solution.py:237
  78.6 6.6 %collective-permute-start.22 = (f32[2,64,256]{2,1,0:T(8,128)S(1)}, f32[2,64,256]{2,1,0:T(8,128)S(1)}, u32[]{:S(2)}, u32[]{:S(2)}) collective-permute-start(f32[2,64,256]{2,1,0:T(8,128)S(1)} %pad_maximum_fusion.5), channel_id=1, source_target_pairs={{0,12},{1,13},{2,14},{3,15},{4,0},{5,1},{6,2},{7,3},{8,4},{9,5},{1... | collective-permute-start | bytes 393224 | tf_op jit(solution)/shard_map/ppermute | solution.py:237
  81.3 11.2 %collective-permute-start.21 = (f32[2,64,256]{2,1,0:T(8,128)S(1)}, f32[2,64,256]{2,1,0:T(8,128)S(1)}, u32[]{:S(2)}, u32[]{:S(2)}) collective-permute-start(f32[2,64,256]{2,1,0:T(8,128)S(1)} %pad_maximum_fusion.5), channel_id=1, source_target_pairs={{0,8},{1,9},{2,10},{3,11},{4,12},{5,13},{6,14},{7,15},{8,0},{9,1},... | collective-permute-start | bytes 393224 | tf_op jit(solution)/shard_map/ppermute | solution.py:237
  81.3 11.2 %collective-permute-start.20 = (f32[2,64,256]{2,1,0:T(8,128)S(1)}, f32[2,64,256]{2,1,0:T(8,128)S(1)}, u32[]{:S(2)}, u32[]{:S(2)}) collective-permute-start(f32[2,64,256]{2,1,0:T(8,128)S(1)} %pad_maximum_fusion.5), channel_id=1, source_target_pairs={{0,4},{1,5},{2,6},{3,7},{4,8},{5,9},{6,10},{7,11},{8,12},{9,13},{1... | collective-permute-start | bytes 393224 | tf_op jit(solution)/shard_map/ppermute | solution.py:237
  81.8 12.9 %collective-permute-start.17 = (f32[4,128,256]{2,1,0:T(8,128)S(1)}, f32[4,128,256]{2,1,0:T(8,128)S(1)}, u32[]{:S(2)}, u32[]{:S(2)}) collective-permute-start(f32[4,128,256]{2,1,0:T(8,128)S(1)} %pad_maximum_fusion.2.refs_0_), channel_id=1, source_target_pairs={{0,1},{1,0},{2,3},{3,2},{4,5},{5,4},{6,7},{7,6},{8,9},{9,8},{10,11... | collective-permute-start | bytes 1572872 | tf_op jit(solution)/shard_map/ppermute | solution.py:237
  92.5 2.3 %collective-permute-start.23 = (f32[4,2,64,256]{3,2,1,0:T(8,128)S(1)}, f32[4,2,64,256]{3,2,1,0:T(8,128)S(1)}, u32[]{:S(2)}, u32[]{:S(2)}) collective-permute-start(f32[4,2,64,256]{3,2,1,0:T(8,128)S(1)} %pad_maximum_fusion.3.refs_2_), channel_id=1, source_target_pairs={{0,1},{1,0},{2,3},{3,2},{4,5},{5,4},{6,7},{7,6},{8,9},{9,8},{10,11... | collective-permute-start | bytes 1572872 | tf_op jit(solution)/shard_map/ppermute | solution.py:237
  92.6 2.6 %collective-permute-start.19 = (f32[4,128,256]{2,1,0:T(8,128)S(1)}, f32[4,128,256]{2,1,0:T(8,128)S(1)}, u32[]{:S(2)}, u32[]{:S(2)}) collective-permute-start(f32[4,128,256]{2,1,0:T(8,128)S(1)} %collective-permute-done.18.refs_1_), channel_id=1, source_target_pairs={{0,1},{1,0},{2,3},{3,2},{4,5},{5,4},{6,7},{7,6},{8,9},{9,8},{10,11... | collective-permute-start | bytes 1572872 | tf_op jit(solution)/shard_map/ppermute | solution.py:237

commit v6 on v5

--- a/solution.py
+++ b/solution.py
@@ -25,11 +25,12 @@
     return high, middle, (rest - middle.astype(f32)).astype(bf16)
 
 
-def kernel_params():
-    return pltpu.CompilerParams(vmem_limit_bytes=56 * MIB)
-
-
-def pack_kernel(own_rows, cap, tile_rows, counts_hbm, rows_hbm, updates_hbm, packed_ref, counts_ref, rows_ref, updates_ref, sems):
+def kernel_params(size):
+    return pltpu.CompilerParams(vmem_limit_bytes=size * MIB)
+
+
+def pack_kernel(own_rows, cap, tile_rows, folded, counts_hbm, rows_hbm, updates_hbm, *refs):
+    packed_refs, (counts_ref, rows_ref, updates_ref, sems) = refs[:-4], refs[-4:]
     moves = [
         pltpu.make_async_copy(counts_hbm, counts_ref, sems.at[0]),
         pltpu.make_async_copy(rows_hbm, rows_ref, sems.at[1]),
@@ -38,7 +39,8 @@
     for move in moves:
         move.start()
     columns, entries = updates_ref.shape
-    owners, height, width = packed_ref.shape
+    owners = lax.axis_size("tile")
+    width = packed_refs[0].shape[-1]
     slots = owners * cap
     entry = lax.broadcasted_iota(jnp.int32, (1, entries), 1)
     earlier = lax.broadcasted_iota(jnp.int32, (entries, entries), 0) < lax.broadcasted_iota(jnp.int32, (entries, entries), 1)
@@ -50,13 +52,14 @@
         live = live | ((entry >= start) & (entry < start + counts_ref[tile]))
     rows = rows_ref[...]
     owner = rows // own_rows
+    local_row = (rows - owner * own_rows).astype(f32)
+    if folded:
+        owner = owner ^ lax.axis_index("tile")
     lane_owner = jnp.broadcast_to(owner.astype(f32), (entries, entries))
     rank = jnp.sum(jnp.where(earlier & (lane_owner.T == lane_owner), 1, 0), axis=0, keepdims=True)
     slot = owner * cap + rank
     choose = jnp.where(lax.broadcasted_iota(jnp.int32, (slots, entries), 0) == slot, 1.0, 0.0).astype(bf16)
     data = jnp.where(live, updates_ref[...], 0.0)
-    local_row = (rows - owner * own_rows).astype(f32)
-    folded = height > cap
     if not folded:
         tail = jnp.where(lax.broadcasted_iota(jnp.int32, (width - columns, entries), 0) == 0, local_row, 0.0)
         data = jnp.concatenate([data, tail], axis=0)
@@ -65,33 +68,36 @@
         packed += lax.dot_general(choose, piece, lanes_contract, preferred_element_type=f32)
     packed = packed.reshape(owners, cap, data.shape[0])
     if not folded:
-        packed_ref[...] = packed
+        packed_refs[0][...] = packed
         return
     half = cap // 2
-    packed_ref[:, :cap, :] = packed[:, :, :width]
-    packed_ref[:, cap:cap + half, :] = jnp.concatenate([packed[:, :half, width:], packed[:, half:, width:]], axis=2)
-    first = lax.axis_index("tile") * cap
     by_owner = jnp.where(lax.broadcasted_iota(jnp.int32, (owners, entries), 0) == owner, local_row, 0.0).astype(bf16)
-    by_lane = jnp.where(lax.broadcasted_iota(jnp.int32, (width, entries), 0) == first % width + rank, 1.0, 0.0).astype(bf16)
+    by_lane = jnp.where(lax.broadcasted_iota(jnp.int32, (width, entries), 0) == lax.rem(slot, width), 1.0, 0.0).astype(bf16)
     numbers = lax.dot_general(by_owner, by_lane, lanes_contract, preferred_element_type=f32)
-    line = lax.broadcasted_iota(jnp.int32, (owners, 8, width), 1)
-    packed_ref[:, cap + half:, :] = jnp.where(line == first // width, numbers[:, None, :], 0.0)
-
-
-def reduce_kernel(cap, received_ref, right_hbm, *refs):
-    reduced_refs, right_ref, sem = refs[:-2], refs[-2], refs[-1]
+    line = lax.broadcasted_iota(jnp.int32, (8, width), 0)
+    for i, packed_ref in enumerate(packed_refs):
+        packed_ref[:cap, :] = packed[i, :, :width]
+        packed_ref[cap:cap + half, :] = jnp.concatenate([packed[i, :half, width:], packed[i, half:, width:]], axis=1)
+        packed_ref[cap + half:, :] = jnp.where(line == i * cap // width, numbers[i:i + 1], 0.0)
+
+
+def reduce_kernel(cap, inputs, right_hbm, *refs):
+    received_refs, reduced_refs, right_ref, sem = refs[:inputs], refs[inputs:-2], refs[-2], refs[-1]
     move = pltpu.make_async_copy(right_hbm, right_ref, sem)
     move.start()
-    owners, height, width = received_ref.shape
-    slots = owners * cap
     columns, own_rows = right_ref.shape
-    if height > cap:
+    if inputs > 1:
+        slots = inputs * cap
         half = cap // 2
-        numbers = jnp.sum(received_ref[:, cap + half:, :], axis=0)
+        width = received_refs[0].shape[1]
+        numbers = received_refs[0][cap + half:, :]
+        for ref in received_refs[1:]:
+            numbers += ref[cap + half:, :]
         numbers = jnp.concatenate([numbers[i:i + 1] for i in range(slots // width)], axis=1).astype(jnp.int32)
-        rest = received_ref[:, cap:cap + half, :]
-        rest = jnp.concatenate([rest[:, :, :width // 2], rest[:, :, width // 2:]], axis=1)
-        sets = [received_ref[:, :cap, :].reshape(slots, width), rest.reshape(slots, width // 2)]
+        rest = []
+        for ref in received_refs:
+            rest += [ref[cap:cap + half, :width // 2], ref[cap:cap + half, width // 2:]]
+        sets = [jnp.concatenate([ref[:cap, :] for ref in received_refs], axis=0), jnp.concatenate(rest, axis=0)]
         place = jnp.where(lax.broadcasted_iota(jnp.int32, (own_rows, slots), 0) == numbers, 1.0, 0.0).astype(bf16)
         totals = []
         for value in sets:
@@ -101,7 +107,9 @@
             totals.append(total.T)
         total = jnp.concatenate(totals, axis=0)
     else:
-        received = received_ref[...].reshape(slots, width)
+        owners, height, width = received_refs[0].shape
+        slots = owners * height
+        received = received_refs[0][...].reshape(slots, width)
         local_row = received[:, columns:columns + 1].astype(jnp.int32)
         place = jnp.where(lax.broadcasted_iota(jnp.int32, (slots, own_rows), 1) == local_row, 1.0, 0.0).astype(bf16)
         total = jnp.zeros((columns, own_rows), f32)
@@ -138,7 +146,7 @@
         in_specs=[vmem],
         out_specs=[vmem, vmem],
         out_shape=[shape, shape],
-        compiler_params=pltpu.CompilerParams(vmem_limit_bytes=20 * MIB),
+        compiler_params=kernel_params(20),
         cost_estimate=pl.CostEstimate(flops=3 * matrix.size, bytes_accessed=8 * matrix.size, transcendentals=0),
     )(matrix)
 
@@ -214,7 +222,7 @@
         out_specs=[vmem] * len(shares) if finish else vmem,
         out_shape=out_shape,
         scratch_shapes=[pltpu.VMEM(whole, f32)] if finish else [],
-        compiler_params=pltpu.CompilerParams(vmem_limit_bytes=20 * MIB),
+        compiler_params=kernel_params(20),
         cost_estimate=pl.CostEstimate(flops=6 * sum(shares) * both_rows * block * (end - begin), bytes_accessed=MIB, transcendentals=0),
     )(*arrays)
 
@@ -310,33 +318,41 @@
     vmem = pl.BlockSpec(memory_space=pltpu.VMEM)
     hbm = pl.BlockSpec(memory_space=pltpu.HBM)
     folded = cap % 16 == 0 and slots <= 1024 and columns == 192 and own_rows <= 256 and 128 % cap == 0
-    width = 128 if folded else -(-(columns + 1) // 128) * 128
-    height = cap + cap // 2 + 8 if folded else cap
+    folded = folded and tile_size & (tile_size - 1) == 0
+    if folded:
+        packed_shape = [jax.ShapeDtypeStruct((cap + cap // 2 + 8, 128), f32)] * tile_size
+    else:
+        packed_shape = [jax.ShapeDtypeStruct((tile_size, cap, -(-(columns + 1) // 128) * 128), f32)]
     packed = pl.pallas_call(
-        functools.partial(pack_kernel, own_rows, cap, tile_rows),
+        functools.partial(pack_kernel, own_rows, cap, tile_rows, folded),
         in_specs=[hbm, hbm, hbm],
-        out_specs=vmem,
-        out_shape=jax.ShapeDtypeStruct((tile_size, height, width), f32),
+        out_specs=[vmem] * len(packed_shape),
+        out_shape=packed_shape,
         scratch_shapes=[
             pltpu.SMEM(tile_counts.shape, jnp.int32),
             pltpu.VMEM((1, entries), jnp.int32),
             pltpu.VMEM((columns, entries), f32),
             pltpu.SemaphoreType.DMA((3,)),
         ],
-        compiler_params=kernel_params(),
+        compiler_params=kernel_params(56),
     )(tile_counts, update_rows[None, :], updates.T)
-    received = lax.all_to_all(packed, "tile", 0, 0, tiled=False)
+    if folded:
+        received = [packed[0]]
+        for by in range(1, tile_size):
+            received.append(lax.ppermute(packed[by], "tile", [(t, t ^ by) for t in range(tile_size)]))
+    else:
+        received = [lax.all_to_all(packed[0], "tile", 0, 0, tiled=False)]
     paired = own_rows % 128 == 0 and tile_size % 8 == 0 and batches > 1
     early = batches * 2 // 3 * halves * sources
     shares = [early, columns - early] if paired else [columns]
     reduced = pl.pallas_call(
-        functools.partial(reduce_kernel, cap),
-        in_specs=[vmem, hbm],
+        functools.partial(reduce_kernel, cap, len(received)),
+        in_specs=[hbm] + [vmem] * len(received),
         out_specs=[vmem] * len(shares),
         out_shape=[jax.ShapeDtypeStruct((rows, own_rows), f32) for rows in shares],
         scratch_shapes=[pltpu.VMEM((columns, own_rows), f32), pltpu.SemaphoreType.DMA(())],
-        compiler_params=kernel_params(),
-    )(received, right_side.reshape(columns, own_rows))
+        compiler_params=kernel_params(20),
+    )(right_side.reshape(columns, own_rows), *received)
     solve = solve_paired if paired else solve_flat
     return solve(reduced, diag_inverse, coupling, sources).reshape(right_side.shape)
 

time: 98 us -> 104 us (1.061)
  starting transfers between devices: 23.7 us -> 45.5 us
  blocking collectives: 20.8 us -> 0 us
  waiting for transfers between devices: 34 us -> 40.4 us
  Pallas kernels: 14 us -> 12.2 us
  local copies, waits for them, and re-layouts: 3.39 us -> 5.06 us
  other arithmetic: 1.42 us -> 0.16 us
    ppermute x0 -> x15, starting transfers between devices: none -> 22.1 us  [body(): lax.ppermute(packed[by], 'tile', [(t, t ^ by) for t in range(tile_size)])]
    all_to_all x1 -> x0, blocking collectives: 20.8 us -> none  [body(): received = lax.all_to_all(packed, 'tile', 0, 0, tiled=False)]
    ppermute x0 -> x15, waiting for transfers between devices: none -> 6.11 us  [body(): lax.ppermute(packed[by], 'tile', [(t, t ^ by) for t in range(tile_size)])]
    pallas_call x2, Pallas kernels: 4.92 us -> 3.12 us  [the longest x1 2.19 us: body(): pl.pallas_call(functools.partial(pack_kernel, own_rows, cap, tile_rows, f...]
    unnamed x6 -> x8, local copies, waits for them, and re-layouts: 3.39 us -> 5.06 us
    another operation x4, other arithmetic: 1.36 us -> 0.09 us  [first_stage(): return (jnp.stack(pair), jnp.stack(line))]
  transfers between devices with their start and end apart: 24 -> 39, of which waited for: 10 -> 12; matrix products, arithmetic and copies ran while one was open for 1% -> 0% of each run, Pallas kernels for 5% -> 5%
where the time goes in v6:
time: 104 us
  starting transfers between devices  45.5 us (44%)
  waiting for transfers between devices  40.4 us (39%)
  Pallas kernels  12.2 us (12%)
  local copies, waits for them, and re-layouts  5.06 us (5%)
    ppermute x18, waiting for transfers between devices, send(): lax.ppermute(value, 'tile', [(t, target(t)) for t in range(tile_size)])  26.5 us
    ppermute x15, starting transfers between devices, body(): lax.ppermute(packed[by], 'tile', [(t, t ^ by) for t in range(tile_size)])  22.1 us
    ppermute x18, starting transfers between devices, send(): lax.ppermute(value, 'tile', [(t, target(t)) for t in range(tile_size)])  14.2 us
    ppermute x6, starting transfers between devices, send(): return lax.ppermute(value, ('chain', 'tile'), pairs)  9.1 us
    ppermute x6, waiting for transfers between devices, send(): return lax.ppermute(value, ('chain', 'tile'), pairs)  7.77 us
    pallas_call x4, Pallas kernels, product_part(): pl.pallas_call(functools.partial(product_kernel, sources, layout, len(blo...  7.19 us
    ppermute x15, waiting for transfers between devices, body(): lax.ppermute(packed[by], 'tile', [(t, t ^ by) for t in range(tile_size)])  6.11 us
    unnamed x8, local copies, waits for them, and re-layouts  5.06 us
  transfers between devices with their start and end apart: 39, of which 12 were waited for; matrix products, arithmetic and copies ran while one was open for 0% of the time, Pallas kernels for 5%

profile of v6, /device:TPU:0, one launch (start us, length us, event | category | flops | bytes accessed | tf_op | source)
XLA Modules:
  0.0 103.6 jit_solution(7677428353150850659)
XLA Ops:
  0.0 2.2 %shard_map.64 = (f32[56,128]{1,0:T(8,128)}, f32[56,128]{1,0:T(8,128)}, f32[56,128]{1,0:T(8,128)}, f32[56,128]{1,0:T(8,128)}, f32[56,128]{1,0:T(8,128)}, /*index=...) custom-call(s32[2]{0:T(128)} %counts_hbm.1, ...), custom_call_target="tpu_custom_call" | custom-call | tf_op jit(solution)/shard_map/pallas_call | solution.py:326
  2.2 0.5 collective-permute-start
  2.7 2.6 %collective-permute-start.1 = (f32[56,128]{1,0:T(8,128)}, f32[56,128]{1,0:T(8,128)S(1)}, u32[]{:S(2)}, u32[]{:S(2)}) collective-permute-start(f32[56,128]{1,0:T(8,128)} %get-tuple-element.43), channel_id=1, source_target_pairs={{0,2},{1,3},{2,0},{3,1},{4,6},{5,7},{6,4},{7,5},{8,10},{9,11},{10,... | collective-permute-start | bytes 86024 | tf_op jit(solution)/shard_map/ppermute | solution.py:342
  5.3 0.1 collective-permute-start.2
  5.4 1.8 %collective-permute-start.3 = (f32[56,128]{1,0:T(8,128)}, f32[56,128]{1,0:T(8,128)S(1)}, u32[]{:S(2)}, u32[]{:S(2)}) collective-permute-start(f32[56,128]{1,0:T(8,128)} %get-tuple-element.45), channel_id=1, source_target_pairs={{0,4},{1,5},{2,6},{3,7},{4,0},{5,1},{6,2},{7,3},{8,12},{9,13},{10,... | collective-permute-start | bytes 86024 | tf_op jit(solution)/shard_map/ppermute | solution.py:342
  7.2 2.6 %collective-permute-start.5 = (f32[56,128]{1,0:T(8,128)}, f32[56,128]{1,0:T(8,128)S(1)}, u32[]{:S(2)}, u32[]{:S(2)}) collective-permute-start(f32[56,128]{1,0:T(8,128)} %get-tuple-element.47), channel_id=1, source_target_pairs={{0,6},{1,7},{2,4},{3,5},{4,2},{5,3},{6,0},{7,1},{8,14},{9,15},{10,... | collective-permute-start | bytes 86024 | tf_op jit(solution)/shard_map/ppermute | solution.py:342
  9.8 0.1 collective-permute-start.6
  9.9 0.0 collective-permute-done.2.refs_3_
  9.9 2.6 %collective-permute-start.7 = (f32[56,128]{1,0:T(8,128)}, f32[56,128]{1,0:T(8,128)S(1)}, u32[]{:S(2)}, u32[]{:S(2)}) collective-permute-start(f32[56,128]{1,0:T(8,128)} %get-tuple-element.49), channel_id=1, source_target_pairs={{0,8},{1,9},{2,10},{3,11},{4,12},{5,13},{6,14},{7,15},{8,0},{9,1},... | collective-permute-start | bytes 86024 | tf_op jit(solution)/shard_map/ppermute | solution.py:342
  12.6 0.0 collective-permute-done.3.refs_4_
  12.6 0.4 collective-permute-start.8
  13.0 0.0 collective-permute-done.4.refs_5_
  13.0 3.1 %collective-permute-start.9 = (f32[56,128]{1,0:T(8,128)}, f32[56,128]{1,0:T(8,128)S(1)}, u32[]{:S(2)}, u32[]{:S(2)}) collective-permute-start(f32[56,128]{1,0:T(8,128)} %get-tuple-element.51), channel_id=1, source_target_pairs={{0,10},{1,11},{2,8},{3,9},{4,14},{5,15},{6,12},{7,13},{8,2},{9,3},... | collective-permute-start | bytes 86024 | tf_op jit(solution)/shard_map/ppermute | solution.py:342
  16.1 0.2 collective-permute-start.10
  16.3 0.0 collective-permute-done.6.refs_7_
  16.3 3.5 %collective-permute-start.11 = (f32[56,128]{1,0:T(8,128)}, f32[56,128]{1,0:T(8,128)S(1)}, u32[]{:S(2)}, u32[]{:S(2)}) collective-permute-start(f32[56,128]{1,0:T(8,128)} %get-tuple-element.53), channel_id=1, source_target_pairs={{0,12},{1,13},{2,14},{3,15},{4,8},{5,9},{6,10},{7,11},{8,4},{9,5},... | collective-permute-start | bytes 86024 | tf_op jit(solution)/shard_map/ppermute | solution.py:342
  19.8 0.0 collective-permute-done.7.refs_8_
  19.8 0.4 collective-permute-start.12
  20.2 4.1 %collective-permute-start.13 = (f32[56,128]{1,0:T(8,128)}, f32[56,128]{1,0:T(8,128)S(1)}, u32[]{:S(2)}, u32[]{:S(2)}) collective-permute-start(f32[56,128]{1,0:T(8,128)} %get-tuple-element.55), channel_id=1, source_target_pairs={{0,14},{1,15},{2,12},{3,13},{4,10},{5,11},{6,8},{7,9},{8,6},{9,7},... | collective-permute-start | bytes 86024 | tf_op jit(solution)/shard_map/ppermute | solution.py:342
  24.3 0.0 collective-permute-done.9.refs_10_
  24.3 0.1 collective-permute-start.14
  24.4 0.0 collective-permute-done.11.refs_12_
  24.4 0.8 collective-permute-done.12.refs_13_
  25.2 1.9 %collective-permute-done.13.refs_14_ = f32[56,128]{1,0:T(8,128)S(1)} collective-permute-done((f32[56,128]{1,0:T(8,128)}, f32[56,128]{1,0:T(8,128)S(1)}, u32[]{:S(2)}, u32[]{:S(2)}) %collective-permute-start.13) | collective-permute-done | bytes 28704 | tf_op jit(solution)/shard_map/ppermute | solution.py:342
  27.1 3.4 %collective-permute-done.14.refs_15_ = f32[56,128]{1,0:T(8,128)S(1)} collective-permute-done((f32[56,128]{1,0:T(8,128)}, f32[56,128]{1,0:T(8,128)S(1)}, u32[]{:S(2)}, u32[]{:S(2)}) %collective-permute-start.14) | collective-permute-done | bytes 28704 | tf_op jit(solution)/shard_map/ppermute | solution.py:342
  30.5 0.9 copy-done.2
  31.4 0.7 copy-done.3
  32.1 0.9 shard_map.65
  33.1 0.6 collective-permute-start.15
  33.7 1.0 collective-permute-start.18
  34.7 1.0 collective-permute-start.16
  35.7 3.4 %copy-done = f32[2,256,4096]{2,1,0:T(8,128)S(1)} copy-done((f32[2,256,4096]{2,1,0:T(8,128)S(1)}, f32[2,256,4096]{2,1,0:T(8,128)}, u32[]{:S(2)}) %copy-start) | copy-done | bytes 8388632
  39.1 0.9 shard_map.66
  40.1 6.1 %collective-permute-done.17 = f32[128,256]{1,0:T(8,128)S(1)} collective-permute-done((f32[128,256]{1,0:T(8,128)S(1)}, f32[128,256]{1,0:T(8,128)S(1)}, u32[]{:S(2)}, u32[]{:S(2)}) %collective-permute-start.17) | collective-permute-done | bytes 131104 | tf_op jit(solution)/shard_map/ppermute | solution.py:245
  46.2 1.1 %collective-permute-start.20 = (f32[4,128,256]{2,1,0:T(8,128)S(1)}, f32[4,128,256]{2,1,0:T(8,128)S(1)}, u32[]{:S(2)}, u32[]{:S(2)}) collective-permute-start(f32[4,128,256]{2,1,0:T(8,128)S(1)} %pad_maximum_fusion.refs_0_.refs_3_), channel_id=1, source_target_pairs={{0,2},{1,3},{2,0},{3,1},{4,6},{5,7},{6,4},{7,5},{8,10},{9,11},{10,... | collective-permute-start | bytes 1572872 | tf_op jit(solution)/shard_map/ppermute | solution.py:245
  47.3 1.3 %collective-permute-start.23 = (f32[2,64,256]{2,1,0:T(8,128)S(1)}, f32[2,64,256]{2,1,0:T(8,128)S(1)}, u32[]{:S(2)}, u32[]{:S(2)}) collective-permute-start(f32[2,64,256]{2,1,0:T(8,128)S(1)} %pad_maximum_fusion.4), channel_id=1, source_target_pairs={{0,12},{1,13},{2,14},{3,15},{4,0},{5,1},{6,2},{7,3},{8,4},{9,5},{1... | collective-permute-start | bytes 393224 | tf_op jit(solution)/shard_map/ppermute | solution.py:245
  48.6 1.8 %collective-permute-start.22 = (f32[2,64,256]{2,1,0:T(8,128)S(1)}, f32[2,64,256]{2,1,0:T(8,128)S(1)}, u32[]{:S(2)}, u32[]{:S(2)}) collective-permute-start(f32[2,64,256]{2,1,0:T(8,128)S(1)} %pad_maximum_fusion.4), channel_id=1, source_target_pairs={{0,8},{1,9},{2,10},{3,11},{4,12},{5,13},{6,14},{7,15},{8,0},{9,1},... | collective-permute-start | bytes 393224 | tf_op jit(solution)/shard_map/ppermute | solution.py:245
  50.4 2.0 %collective-permute-start.21 = (f32[2,64,256]{2,1,0:T(8,128)S(1)}, f32[2,64,256]{2,1,0:T(8,128)S(1)}, u32[]{:S(2)}, u32[]{:S(2)}) collective-permute-start(f32[2,64,256]{2,1,0:T(8,128)S(1)} %pad_maximum_fusion.4), channel_id=1, source_target_pairs={{0,4},{1,5},{2,6},{3,7},{4,8},{5,9},{6,10},{7,11},{8,12},{9,13},{1... | collective-permute-start | bytes 393224 | tf_op jit(solution)/shard_map/ppermute | solution.py:245
  52.4 0.9 shard_map.67
  53.4 8.8 %collective-permute-done.22 = f32[2,64,256]{2,1,0:T(8,128)S(1)} collective-permute-done((f32[2,64,256]{2,1,0:T(8,128)S(1)}, f32[2,64,256]{2,1,0:T(8,128)S(1)}, u32[]{:S(2)}, u32[]{:S(2)}) %collective-permute-start.22) | collective-permute-done | bytes 131104 | tf_op jit(solution)/shard_map/ppermute | solution.py:245
  62.3 0.1 collective-permute-start.24
  62.3 0.5 collective-permute-start.25
  62.8 1.7 %shard_map.68.refs_5_ = f32[192,512]{1,0:T(8,128)S(1)} custom-call(f32[4,128,256]{2,1,0:T(8,128)S(1)} %pad_maximum_fusion.refs_0_.refs_3_, f32[4,128,256]{2,1,0:T(8,128)S(1)} %collective-permute-done.20.refs_1_.refs_4_, f32[4,2,64,256]{3,2,1,0:T(8,128)S(1)} %pad_maximum_fusion.1.refs_2_.refs_5_, bf16[16,512,256]{2,1,0:T(8,128)(2,1)S(1)} %get-tuple-element.69.refs_3_, ...), custom_call_target="tpu_custom_call" | custom-call | flops 1207959552 | bytes 1048576 | tf_op jit(solution)/shard_map/pallas_call | solution.py:219
  64.5 0.5 collective-permute-done.25.refs_2_.refs_5_
  65.0 1.6 %shard_map.69 = (f32[128,256]{1,0:T(8,128)S(1)}, f32[64,256]{1,0:T(8,128)S(1)}) custom-call(f32[4,128,256]{2,1,0:T(8,128)S(1)} %collective-permute-done.19.refs_0_.refs_3_, f32[4,128,256]{2,1,0:T(8,128)S(1)} %collective-permute-done.24.refs_1_.refs_4_, f32[4,2,64,256]{3,2,1,0:T(8,128)S(1)} %collective-permute-done.25.refs_2_.refs_5_, ...), custom_call_target="tpu_custom_call" | custom-call | flops 1207959552 | bytes 1048576 | tf_op jit(solution)/shard_map/pallas_call | solution.py:219
  66.6 1.6 %collective-permute-start.27 = (f32[64,256]{1,0:T(8,128)S(1)}, f32[64,256]{1,0:T(8,128)S(1)}, u32[]{:S(2)}, u32[]{:S(2)}) collective-permute-start(f32[64,256]{1,0:T(8,128)S(1)} %get-tuple-element.71), channel_id=1, source_target_pairs={{0,18},{1,19},{2,16},{3,17},{4,22},{5,23},{6,20},{7,21},{8,26},{9,... | collective-permute-start | bytes 196616 | tf_op jit(solution)/shard_map/ppermute | solution.py:247
  68.2 1.5 %collective-permute-start.26 = (f32[64,256]{1,0:T(8,128)S(1)}, f32[64,256]{1,0:T(8,128)S(1)}, u32[]{:S(2)}, u32[]{:S(2)}) collective-permute-start(f32[64,256]{1,0:T(8,128)S(1)} %get-tuple-element.71), channel_id=1, source_target_pairs={{0,16},{1,17},{2,18},{3,19},{4,20},{5,21},{6,22},{7,23},{8,24},{9,... | collective-permute-start | bytes 196616 | tf_op jit(solution)/shard_map/ppermute | solution.py:247
  69.7 1.3 %collective-permute-start.31 = (f32[128,256]{1,0:T(8,128)S(1)}, f32[128,256]{1,0:T(8,128)S(1)}, u32[]{:S(2)}, u32[]{:S(2)}) collective-permute-start(f32[128,256]{1,0:T(8,128)S(1)} %get-tuple-element.72), channel_id=1, source_target_pairs={{0,28},{1,29},{2,30},{3,31},{4,16},{5,17},{6,18},{7,19},{8,20},{9,... | collective-permute-start | bytes 393224 | tf_op jit(solution)/shard_map/ppermute | solution.py:247
  71.0 1.5 %collective-permute-start.30 = (f32[128,256]{1,0:T(8,128)S(1)}, f32[128,256]{1,0:T(8,128)S(1)}, u32[]{:S(2)}, u32[]{:S(2)}) collective-permute-start(f32[128,256]{1,0:T(8,128)S(1)} %get-tuple-element.72), channel_id=1, source_target_pairs={{0,24},{1,25},{2,26},{3,27},{4,28},{5,29},{6,30},{7,31},{8,16},{9,... | collective-permute-start | bytes 393224 | tf_op jit(solution)/shard_map/ppermute | solution.py:247
  72.5 1.3 %collective-permute-start.29 = (f32[128,256]{1,0:T(8,128)S(1)}, f32[128,256]{1,0:T(8,128)S(1)}, u32[]{:S(2)}, u32[]{:S(2)}) collective-permute-start(f32[128,256]{1,0:T(8,128)S(1)} %get-tuple-element.72), channel_id=1, source_target_pairs={{0,20},{1,21},{2,22},{3,23},{4,24},{5,25},{6,26},{7,27},{8,28},{9,... | collective-permute-start | bytes 393224 | tf_op jit(solution)/shard_map/ppermute | solution.py:247
  73.8 2.0 %collective-permute-start.28 = (f32[128,256]{1,0:T(8,128)S(1)}, f32[128,256]{1,0:T(8,128)S(1)}, u32[]{:S(2)}, u32[]{:S(2)}) collective-permute-start(f32[128,256]{1,0:T(8,128)S(1)} %get-tuple-element.72), channel_id=1, source_target_pairs={{0,16},{1,17},{2,18},{3,19},{4,20},{5,21},{6,22},{7,23},{8,24},{9,... | collective-permute-start | bytes 393224 | tf_op jit(solution)/shard_map/ppermute | solution.py:247
  75.8 1.9 %collective-permute-done.30 = f32[128,256]{1,0:T(8,128)S(1)} collective-permute-done((f32[128,256]{1,0:T(8,128)S(1)}, f32[128,256]{1,0:T(8,128)S(1)}, u32[]{:S(2)}, u32[]{:S(2)}) %collective-permute-start.30) | collective-permute-done | bytes 131104 | tf_op jit(solution)/shard_map/ppermute | solution.py:247
  77.7 2.3 %collective-permute-done.29 = f32[128,256]{1,0:T(8,128)S(1)} collective-permute-done((f32[128,256]{1,0:T(8,128)S(1)}, f32[128,256]{1,0:T(8,128)S(1)}, u32[]{:S(2)}, u32[]{:S(2)}) %collective-permute-start.29) | collective-permute-done | bytes 131104 | tf_op jit(solution)/shard_map/ppermute | solution.py:247
  80.0 3.6 %collective-permute-done.28 = f32[128,256]{1,0:T(8,128)S(1)} collective-permute-done((f32[128,256]{1,0:T(8,128)S(1)}, f32[128,256]{1,0:T(8,128)S(1)}, u32[]{:S(2)}, u32[]{:S(2)}) %collective-permute-start.28) | collective-permute-done | bytes 131104 | tf_op jit(solution)/shard_map/ppermute | solution.py:247
  83.6 1.0 collective-permute-start.33
  84.6 2.7 %collective-permute-start.37 = (f32[2,64,256]{2,1,0:T(8,128)S(1)}, f32[2,64,256]{2,1,0:T(8,128)S(1)}, u32[]{:S(2)}, u32[]{:S(2)}) collective-permute-start(f32[2,64,256]{2,1,0:T(8,128)S(1)} %pad_maximum_fusion.5), channel_id=1, source_target_pairs={{0,12},{1,13},{2,14},{3,15},{4,0},{5,1},{6,2},{7,3},{8,4},{9,5},{1... | collective-permute-start | bytes 393224 | tf_op jit(solution)/shard_map/ppermute | solution.py:245
  87.3 0.6 collective-permute-start.35
  87.8 3.3 %collective-permute-done.37 = f32[2,64,256]{2,1,0:T(8,128)S(1)} collective-permute-done((f32[2,64,256]{2,1,0:T(8,128)S(1)}, f32[2,64,256]{2,1,0:T(8,128)S(1)}, u32[]{:S(2)}, u32[]{:S(2)}) %collective-permute-start.37) | collective-permute-done | bytes 131104 | tf_op jit(solution)/shard_map/ppermute | solution.py:245
  91.2 7.3 %collective-permute-done.36 = f32[2,64,256]{2,1,0:T(8,128)S(1)} collective-permute-done((f32[2,64,256]{2,1,0:T(8,128)S(1)}, f32[2,64,256]{2,1,0:T(8,128)S(1)}, u32[]{:S(2)}, u32[]{:S(2)}) %collective-permute-start.36) | collective-permute-done | bytes 131104 | tf_op jit(solution)/shard_map/ppermute | solution.py:245
  98.5 0.1 collective-permute-start.38
  98.6 0.5 collective-permute-start.34
  99.1 1.7 %shard_map.70.refs_8_ = f32[192,512]{1,0:T(8,128)S(1)} custom-call(f32[4,128,256]{2,1,0:T(8,128)S(1)} %pad_maximum_fusion.2.refs_0_, f32[4,128,256]{2,1,0:T(8,128)S(1)} %collective-permute-done.33.refs_1_, f32[4,2,64,256]{3,2,1,0:T(8,128)S(1)} %pad_maximum_fusion.3.refs_2_, f32[4,128,256]{2,1,0:T(8,128)S(1)} %pad_maximum_fusion.refs_0_.refs_3_, ...), custom_call_target="tpu_custom_call" | custom-call | flops 1207959552 | bytes 1048576 | tf_op jit(solution)/shard_map/pallas_call | solution.py:219
  100.8 0.5 collective-permute-done.34.refs_1_
  101.3 2.3 %shard_map.71 = f32[192,256]{1,0:T(8,128)} custom-call(f32[4,128,256]{2,1,0:T(8,128)S(1)} %collective-permute-done.32.refs_0_, f32[4,128,256]{2,1,0:T(8,128)S(1)} %collective-permute-done.34.refs_1_, f32[4,2,64,256]{3,2,1,0:T(8,128)S(1)} %collective-permute-done.38.refs_2_, f32[4,128,256]{2,1,0:T(8,128)S(1)} %collective-permute-done.19.refs_0_.refs_3_, ...), custom_call_target="tpu_custom_call" | custom-call | flops 1207959552 | bytes 1048576 | tf_op jit(solution)/shard_map/pallas_call | solution.py:219
  (36 shorter events, 0.2 us)
Async XLA Ops:
  2.2 5.0 %collective-permute-start = (f32[56,128]{1,0:T(8,128)}, f32[56,128]{1,0:T(8,128)S(1)}, u32[]{:S(2)}, u32[]{:S(2)}) collective-permute-start(f32[56,128]{1,0:T(8,128)} %get-tuple-element.42), channel_id=1, source_target_pairs={{0,1},{1,0},{2,3},{3,2},{4,5},{5,4},{6,7},{7,6},{8,9},{9,8},{10,11... | collective-permute-start | bytes 86024 | tf_op jit(solution)/shard_map/ppermute | solution.py:342
  2.7 7.1 %collective-permute-start.1 = (f32[56,128]{1,0:T(8,128)}, f32[56,128]{1,0:T(8,128)S(1)}, u32[]{:S(2)}, u32[]{:S(2)}) collective-permute-start(f32[56,128]{1,0:T(8,128)} %get-tuple-element.43), channel_id=1, source_target_pairs={{0,2},{1,3},{2,0},{3,1},{4,6},{5,7},{6,4},{7,5},{8,10},{9,11},{10,... | collective-permute-start | bytes 86024 | tf_op jit(solution)/shard_map/ppermute | solution.py:342
  5.3 4.6 %collective-permute-start.2 = (f32[56,128]{1,0:T(8,128)}, f32[56,128]{1,0:T(8,128)S(1)}, u32[]{:S(2)}, u32[]{:S(2)}) collective-permute-start(f32[56,128]{1,0:T(8,128)} %get-tuple-element.44), channel_id=1, source_target_pairs={{0,3},{1,2},{2,1},{3,0},{4,7},{5,6},{6,5},{7,4},{8,11},{9,10},{10,... | collective-permute-start | bytes 86024 | tf_op jit(solution)/shard_map/ppermute | solution.py:342
  5.4 7.2 %collective-permute-start.3 = (f32[56,128]{1,0:T(8,128)}, f32[56,128]{1,0:T(8,128)S(1)}, u32[]{:S(2)}, u32[]{:S(2)}) collective-permute-start(f32[56,128]{1,0:T(8,128)} %get-tuple-element.45), channel_id=1, source_target_pairs={{0,4},{1,5},{2,6},{3,7},{4,0},{5,1},{6,2},{7,3},{8,12},{9,13},{10,... | collective-permute-start | bytes 86024 | tf_op jit(solution)/shard_map/ppermute | solution.py:342
  7.2 5.9 %collective-permute-start.4 = (f32[56,128]{1,0:T(8,128)}, f32[56,128]{1,0:T(8,128)S(1)}, u32[]{:S(2)}, u32[]{:S(2)}) collective-permute-start(f32[56,128]{1,0:T(8,128)} %get-tuple-element.46), channel_id=1, source_target_pairs={{0,5},{1,4},{2,7},{3,6},{4,1},{5,0},{6,3},{7,2},{8,13},{9,12},{10,... | collective-permute-start | bytes 86024 | tf_op jit(solution)/shard_map/ppermute | solution.py:342
  7.2 9.0 %collective-permute-start.5 = (f32[56,128]{1,0:T(8,128)}, f32[56,128]{1,0:T(8,128)S(1)}, u32[]{:S(2)}, u32[]{:S(2)}) collective-permute-start(f32[56,128]{1,0:T(8,128)} %get-tuple-element.47), channel_id=1, source_target_pairs={{0,6},{1,7},{2,4},{3,5},{4,2},{5,3},{6,0},{7,1},{8,14},{9,15},{10,... | collective-permute-start | bytes 86024 | tf_op jit(solution)/shard_map/ppermute | solution.py:342
  9.8 6.5 %collective-permute-start.6 = (f32[56,128]{1,0:T(8,128)}, f32[56,128]{1,0:T(8,128)S(1)}, u32[]{:S(2)}, u32[]{:S(2)}) collective-permute-start(f32[56,128]{1,0:T(8,128)} %get-tuple-element.48), channel_id=1, source_target_pairs={{0,7},{1,6},{2,5},{3,4},{4,3},{5,2},{6,1},{7,0},{8,15},{9,14},{10,... | collective-permute-start | bytes 86024 | tf_op jit(solution)/shard_map/ppermute | solution.py:342
  9.9 9.9 %collective-permute-start.7 = (f32[56,128]{1,0:T(8,128)}, f32[56,128]{1,0:T(8,128)S(1)}, u32[]{:S(2)}, u32[]{:S(2)}) collective-permute-start(f32[56,128]{1,0:T(8,128)} %get-tuple-element.49), channel_id=1, source_target_pairs={{0,8},{1,9},{2,10},{3,11},{4,12},{5,13},{6,14},{7,15},{8,0},{9,1},... | collective-permute-start | bytes 86024 | tf_op jit(solution)/shard_map/ppermute | solution.py:342
  12.6 7.6 %collective-permute-start.8 = (f32[56,128]{1,0:T(8,128)}, f32[56,128]{1,0:T(8,128)S(1)}, u32[]{:S(2)}, u32[]{:S(2)}) collective-permute-start(f32[56,128]{1,0:T(8,128)} %get-tuple-element.50), channel_id=1, source_target_pairs={{0,9},{1,8},{2,11},{3,10},{4,13},{5,12},{6,15},{7,14},{8,1},{9,0},... | collective-permute-start | bytes 86024 | tf_op jit(solution)/shard_map/ppermute | solution.py:342
  13.0 11.2 %collective-permute-start.9 = (f32[56,128]{1,0:T(8,128)}, f32[56,128]{1,0:T(8,128)S(1)}, u32[]{:S(2)}, u32[]{:S(2)}) collective-permute-start(f32[56,128]{1,0:T(8,128)} %get-tuple-element.51), channel_id=1, source_target_pairs={{0,10},{1,11},{2,8},{3,9},{4,14},{5,15},{6,12},{7,13},{8,2},{9,3},... | collective-permute-start | bytes 86024 | tf_op jit(solution)/shard_map/ppermute | solution.py:342
  16.1 8.2 %collective-permute-start.10 = (f32[56,128]{1,0:T(8,128)}, f32[56,128]{1,0:T(8,128)S(1)}, u32[]{:S(2)}, u32[]{:S(2)}) collective-permute-start(f32[56,128]{1,0:T(8,128)} %get-tuple-element.52), channel_id=1, source_target_pairs={{0,11},{1,10},{2,9},{3,8},{4,15},{5,14},{6,13},{7,12},{8,3},{9,2},... | collective-permute-start | bytes 86024 | tf_op jit(solution)/shard_map/ppermute | solution.py:342
  16.3 8.1 %collective-permute-start.11 = (f32[56,128]{1,0:T(8,128)}, f32[56,128]{1,0:T(8,128)S(1)}, u32[]{:S(2)}, u32[]{:S(2)}) collective-permute-start(f32[56,128]{1,0:T(8,128)} %get-tuple-element.53), channel_id=1, source_target_pairs={{0,12},{1,13},{2,14},{3,15},{4,8},{5,9},{6,10},{7,11},{8,4},{9,5},... | collective-permute-start | bytes 86024 | tf_op jit(solution)/shard_map/ppermute | solution.py:342
  19.8 5.4 %collective-permute-start.12 = (f32[56,128]{1,0:T(8,128)}, f32[56,128]{1,0:T(8,128)S(1)}, u32[]{:S(2)}, u32[]{:S(2)}) collective-permute-start(f32[56,128]{1,0:T(8,128)} %get-tuple-element.54), channel_id=1, source_target_pairs={{0,13},{1,12},{2,15},{3,14},{4,9},{5,8},{6,11},{7,10},{8,5},{9,4},... | collective-permute-start | bytes 86024 | tf_op jit(solution)/shard_map/ppermute | solution.py:342
  20.2 6.9 %collective-permute-start.13 = (f32[56,128]{1,0:T(8,128)}, f32[56,128]{1,0:T(8,128)S(1)}, u32[]{:S(2)}, u32[]{:S(2)}) collective-permute-start(f32[56,128]{1,0:T(8,128)} %get-tuple-element.55), channel_id=1, source_target_pairs={{0,14},{1,15},{2,12},{3,13},{4,10},{5,11},{6,8},{7,9},{8,6},{9,7},... | collective-permute-start | bytes 86024 | tf_op jit(solution)/shard_map/ppermute | solution.py:342
  24.3 6.2 %collective-permute-start.14 = (f32[56,128]{1,0:T(8,128)}, f32[56,128]{1,0:T(8,128)S(1)}, u32[]{:S(2)}, u32[]{:S(2)}) collective-permute-start(f32[56,128]{1,0:T(8,128)} %get-tuple-element.56), channel_id=1, source_target_pairs={{0,15},{1,14},{2,13},{3,12},{4,11},{5,10},{6,9},{7,8},{8,7},{9,6},... | collective-permute-start | bytes 86024 | tf_op jit(solution)/shard_map/ppermute | solution.py:342
  30.5 0.9 copy-start.2
  31.4 0.7 copy-start.3
  33.1 6.9 %collective-permute-start.15 = (f32[64,256]{1,0:T(8,128)S(1)}, f32[64,256]{1,0:T(8,128)S(1)}, u32[]{:S(2)}, u32[]{:S(2)}) collective-permute-start(f32[64,256]{1,0:T(8,128)S(1)} %get-tuple-element.57), channel_id=1, source_target_pairs={{0,2},{1,3},{2,0},{3,1},{4,6},{5,7},{6,4},{7,5},{8,10},{9,11},{10,... | collective-permute-start | bytes 196616 | tf_op jit(solution)/shard_map/ppermute | solution.py:245
  33.7 6.4 %collective-permute-start.18 = (f32[128,256]{1,0:T(8,128)S(1)}, f32[128,256]{1,0:T(8,128)S(1)}, u32[]{:S(2)}, u32[]{:S(2)}) collective-permute-start(f32[128,256]{1,0:T(8,128)S(1)} %get-tuple-element.58), channel_id=1, source_target_pairs={{0,12},{1,13},{2,14},{3,15},{4,0},{5,1},{6,2},{7,3},{8,4},{9,5},{1... | collective-permute-start | bytes 393224 | tf_op jit(solution)/shard_map/ppermute | solution.py:245
  34.7 11.5 %collective-permute-start.17 = (f32[128,256]{1,0:T(8,128)S(1)}, f32[128,256]{1,0:T(8,128)S(1)}, u32[]{:S(2)}, u32[]{:S(2)}) collective-permute-start(f32[128,256]{1,0:T(8,128)S(1)} %get-tuple-element.58), channel_id=1, source_target_pairs={{0,8},{1,9},{2,10},{3,11},{4,12},{5,13},{6,14},{7,15},{8,0},{9,1},... | collective-permute-start | bytes 393224 | tf_op jit(solution)/shard_map/ppermute | solution.py:245
  34.7 11.5 %collective-permute-start.16 = (f32[128,256]{1,0:T(8,128)S(1)}, f32[128,256]{1,0:T(8,128)S(1)}, u32[]{:S(2)}, u32[]{:S(2)}) collective-permute-start(f32[128,256]{1,0:T(8,128)S(1)} %get-tuple-element.58), channel_id=1, source_target_pairs={{0,4},{1,5},{2,6},{3,7},{4,8},{5,9},{6,10},{7,11},{8,12},{9,13},{1... | collective-permute-start | bytes 393224 | tf_op jit(solution)/shard_map/ppermute | solution.py:245
  35.7 3.4 %copy-start = (f32[2,256,4096]{2,1,0:T(8,128)S(1)}, f32[2,256,4096]{2,1,0:T(8,128)}, u32[]{:S(2)}) copy-start(f32[2,256,4096]{2,1,0:T(8,128)} %matrix_ref) | copy-start | bytes 25165828
  39.1 13.3 %copy-start.1 = (f32[2,256,4096]{2,1,0:T(8,128)S(1)}, f32[2,256,4096]{2,1,0:T(8,128)}, u32[]{:S(2)}) copy-start(f32[2,256,4096]{2,1,0:T(8,128)} %matrix_ref.1) | copy-start | bytes 25165828
  46.2 16.1 %collective-permute-start.20 = (f32[4,128,256]{2,1,0:T(8,128)S(1)}, f32[4,128,256]{2,1,0:T(8,128)S(1)}, u32[]{:S(2)}, u32[]{:S(2)}) collective-permute-start(f32[4,128,256]{2,1,0:T(8,128)S(1)} %pad_maximum_fusion.refs_0_.refs_3_), channel_id=1, source_target_pairs={{0,2},{1,3},{2,0},{3,1},{4,6},{5,7},{6,4},{7,5},{8,10},{9,11},{10,... | collective-permute-start | bytes 1572872 | tf_op jit(solution)/shard_map/ppermute | solution.py:245
  47.3 6.1 %collective-permute-start.23 = (f32[2,64,256]{2,1,0:T(8,128)S(1)}, f32[2,64,256]{2,1,0:T(8,128)S(1)}, u32[]{:S(2)}, u32[]{:S(2)}) collective-permute-start(f32[2,64,256]{2,1,0:T(8,128)S(1)} %pad_maximum_fusion.4), channel_id=1, source_target_pairs={{0,12},{1,13},{2,14},{3,15},{4,0},{5,1},{6,2},{7,3},{8,4},{9,5},{1... | collective-permute-start | bytes 393224 | tf_op jit(solution)/shard_map/ppermute | solution.py:245
  48.6 13.6 %collective-permute-start.22 = (f32[2,64,256]{2,1,0:T(8,128)S(1)}, f32[2,64,256]{2,1,0:T(8,128)S(1)}, u32[]{:S(2)}, u32[]{:S(2)}) collective-permute-start(f32[2,64,256]{2,1,0:T(8,128)S(1)} %pad_maximum_fusion.4), channel_id=1, source_target_pairs={{0,8},{1,9},{2,10},{3,11},{4,12},{5,13},{6,14},{7,15},{8,0},{9,1},... | collective-permute-start | bytes 393224 | tf_op jit(solution)/shard_map/ppermute | solution.py:245
  50.4 11.8 %collective-permute-start.21 = (f32[2,64,256]{2,1,0:T(8,128)S(1)}, f32[2,64,256]{2,1,0:T(8,128)S(1)}, u32[]{:S(2)}, u32[]{:S(2)}) collective-permute-start(f32[2,64,256]{2,1,0:T(8,128)S(1)} %pad_maximum_fusion.4), channel_id=1, source_target_pairs={{0,4},{1,5},{2,6},{3,7},{4,8},{5,9},{6,10},{7,11},{8,12},{9,13},{1... | collective-permute-start | bytes 393224 | tf_op jit(solution)/shard_map/ppermute | solution.py:245
  52.4 12.1 %collective-permute-start.19 = (f32[4,128,256]{2,1,0:T(8,128)S(1)}, f32[4,128,256]{2,1,0:T(8,128)S(1)}, u32[]{:S(2)}, u32[]{:S(2)}) collective-permute-start(f32[4,128,256]{2,1,0:T(8,128)S(1)} %pad_maximum_fusion.refs_0_.refs_3_), channel_id=1, source_target_pairs={{0,1},{1,0},{2,3},{3,2},{4,5},{5,4},{6,7},{7,6},{8,9},{9,8},{10,11... | collective-permute-start | bytes 1572872 | tf_op jit(solution)/shard_map/ppermute | solution.py:245
  62.3 2.3 %collective-permute-start.24 = (f32[4,128,256]{2,1,0:T(8,128)S(1)}, f32[4,128,256]{2,1,0:T(8,128)S(1)}, u32[]{:S(2)}, u32[]{:S(2)}) collective-permute-start(f32[4,128,256]{2,1,0:T(8,128)S(1)} %collective-permute-done.20.refs_1_.refs_4_), channel_id=1, source_target_pairs={{0,1},{1,0},{2,3},{3,2},{4,5},{5,4},{6,7},{7,6},{8,9},{9,8},{10,11... | collective-permute-start | bytes 1572872 | tf_op jit(solution)/shard_map/ppermute | solution.py:245
  62.3 2.6 %collective-permute-start.25 = (f32[4,2,64,256]{3,2,1,0:T(8,128)S(1)}, f32[4,2,64,256]{3,2,1,0:T(8,128)S(1)}, u32[]{:S(2)}, u32[]{:S(2)}) collective-permute-start(f32[4,2,64,256]{3,2,1,0:T(8,128)S(1)} %pad_maximum_fusion.1.refs_2_.refs_5_), channel_id=1, source_target_pairs={{0,1},{1,0},{2,3},{3,2},{4,5},{5,4},{6,7},{7,6},{8,9},{9,8},{10,11... | collective-permute-start | bytes 1572872 | tf_op jit(solution)/shard_map/ppermute | solution.py:245
  66.6 7.2 %collective-permute-start.27 = (f32[64,256]{1,0:T(8,128)S(1)}, f32[64,256]{1,0:T(8,128)S(1)}, u32[]{:S(2)}, u32[]{:S(2)}) collective-permute-start(f32[64,256]{1,0:T(8,128)S(1)} %get-tuple-element.71), channel_id=1, source_target_pairs={{0,18},{1,19},{2,16},{3,17},{4,22},{5,23},{6,20},{7,21},{8,26},{9,... | collective-permute-start | bytes 196616 | tf_op jit(solution)/shard_map/ppermute | solution.py:247
  68.2 7.6 %collective-permute-start.26 = (f32[64,256]{1,0:T(8,128)S(1)}, f32[64,256]{1,0:T(8,128)S(1)}, u32[]{:S(2)}, u32[]{:S(2)}) collective-permute-start(f32[64,256]{1,0:T(8,128)S(1)} %get-tuple-element.71), channel_id=1, source_target_pairs={{0,16},{1,17},{2,18},{3,19},{4,20},{5,21},{6,22},{7,23},{8,24},{9,... | collective-permute-start | bytes 196616 | tf_op jit(solution)/shard_map/ppermute | solution.py:247
  69.7 6.1 %collective-permute-start.31 = (f32[128,256]{1,0:T(8,128)S(1)}, f32[128,256]{1,0:T(8,128)S(1)}, u32[]{:S(2)}, u32[]{:S(2)}) collective-permute-start(f32[128,256]{1,0:T(8,128)S(1)} %get-tuple-element.72), channel_id=1, source_target_pairs={{0,28},{1,29},{2,30},{3,31},{4,16},{5,17},{6,18},{7,19},{8,20},{9,... | collective-permute-start | bytes 393224 | tf_op jit(solution)/shard_map/ppermute | solution.py:247
  71.0 6.7 %collective-permute-start.30 = (f32[128,256]{1,0:T(8,128)S(1)}, f32[128,256]{1,0:T(8,128)S(1)}, u32[]{:S(2)}, u32[]{:S(2)}) collective-permute-start(f32[128,256]{1,0:T(8,128)S(1)} %get-tuple-element.72), channel_id=1, source_target_pairs={{0,24},{1,25},{2,26},{3,27},{4,28},{5,29},{6,30},{7,31},{8,16},{9,... | collective-permute-start | bytes 393224 | tf_op jit(solution)/shard_map/ppermute | solution.py:247
  72.5 7.5 %collective-permute-start.29 = (f32[128,256]{1,0:T(8,128)S(1)}, f32[128,256]{1,0:T(8,128)S(1)}, u32[]{:S(2)}, u32[]{:S(2)}) collective-permute-start(f32[128,256]{1,0:T(8,128)S(1)} %get-tuple-element.72), channel_id=1, source_target_pairs={{0,20},{1,21},{2,22},{3,23},{4,24},{5,25},{6,26},{7,27},{8,28},{9,... | collective-permute-start | bytes 393224 | tf_op jit(solution)/shard_map/ppermute | solution.py:247
  73.8 9.8 %collective-permute-start.28 = (f32[128,256]{1,0:T(8,128)S(1)}, f32[128,256]{1,0:T(8,128)S(1)}, u32[]{:S(2)}, u32[]{:S(2)}) collective-permute-start(f32[128,256]{1,0:T(8,128)S(1)} %get-tuple-element.72), channel_id=1, source_target_pairs={{0,16},{1,17},{2,18},{3,19},{4,20},{5,21},{6,22},{7,23},{8,24},{9,... | collective-permute-start | bytes 393224 | tf_op jit(solution)/shard_map/ppermute | solution.py:247
  83.6 15.0 %collective-permute-start.33 = (f32[4,128,256]{2,1,0:T(8,128)S(1)}, f32[4,128,256]{2,1,0:T(8,128)S(1)}, u32[]{:S(2)}, u32[]{:S(2)}) collective-permute-start(f32[4,128,256]{2,1,0:T(8,128)S(1)} %pad_maximum_fusion.2.refs_0_), channel_id=1, source_target_pairs={{0,2},{1,3},{2,0},{3,1},{4,6},{5,7},{6,4},{7,5},{8,10},{9,11},{10,... | collective-permute-start | bytes 1572872 | tf_op jit(solution)/shard_map/ppermute | solution.py:245
  84.6 6.6 %collective-permute-start.37 = (f32[2,64,256]{2,1,0:T(8,128)S(1)}, f32[2,64,256]{2,1,0:T(8,128)S(1)}, u32[]{:S(2)}, u32[]{:S(2)}) collective-permute-start(f32[2,64,256]{2,1,0:T(8,128)S(1)} %pad_maximum_fusion.5), channel_id=1, source_target_pairs={{0,12},{1,13},{2,14},{3,15},{4,0},{5,1},{6,2},{7,3},{8,4},{9,5},{1... | collective-permute-start | bytes 393224 | tf_op jit(solution)/shard_map/ppermute | solution.py:245
  87.3 11.2 %collective-permute-start.36 = (f32[2,64,256]{2,1,0:T(8,128)S(1)}, f32[2,64,256]{2,1,0:T(8,128)S(1)}, u32[]{:S(2)}, u32[]{:S(2)}) collective-permute-start(f32[2,64,256]{2,1,0:T(8,128)S(1)} %pad_maximum_fusion.5), channel_id=1, source_target_pairs={{0,8},{1,9},{2,10},{3,11},{4,12},{5,13},{6,14},{7,15},{8,0},{9,1},... | collective-permute-start | bytes 393224 | tf_op jit(solution)/shard_map/ppermute | solution.py:245
  87.3 11.2 %collective-permute-start.35 = (f32[2,64,256]{2,1,0:T(8,128)S(1)}, f32[2,64,256]{2,1,0:T(8,128)S(1)}, u32[]{:S(2)}, u32[]{:S(2)}) collective-permute-start(f32[2,64,256]{2,1,0:T(8,128)S(1)} %pad_maximum_fusion.5), channel_id=1, source_target_pairs={{0,4},{1,5},{2,6},{3,7},{4,8},{5,9},{6,10},{7,11},{8,12},{9,13},{1... | collective-permute-start | bytes 393224 | tf_op jit(solution)/shard_map/ppermute | solution.py:245
  87.8 12.9 %collective-permute-start.32 = (f32[4,128,256]{2,1,0:T(8,128)S(1)}, f32[4,128,256]{2,1,0:T(8,128)S(1)}, u32[]{:S(2)}, u32[]{:S(2)}) collective-permute-start(f32[4,128,256]{2,1,0:T(8,128)S(1)} %pad_maximum_fusion.2.refs_0_), channel_id=1, source_target_pairs={{0,1},{1,0},{2,3},{3,2},{4,5},{5,4},{6,7},{7,6},{8,9},{9,8},{10,11... | collective-permute-start | bytes 1572872 | tf_op jit(solution)/shard_map/ppermute | solution.py:245
  98.5 2.3 %collective-permute-start.38 = (f32[4,2,64,256]{3,2,1,0:T(8,128)S(1)}, f32[4,2,64,256]{3,2,1,0:T(8,128)S(1)}, u32[]{:S(2)}, u32[]{:S(2)}) collective-permute-start(f32[4,2,64,256]{3,2,1,0:T(8,128)S(1)} %pad_maximum_fusion.3.refs_2_), channel_id=1, source_target_pairs={{0,1},{1,0},{2,3},{3,2},{4,5},{5,4},{6,7},{7,6},{8,9},{9,8},{10,11... | collective-permute-start | bytes 1572872 | tf_op jit(solution)/shard_map/ppermute | solution.py:245
  98.6 2.6 %collective-permute-start.34 = (f32[4,128,256]{2,1,0:T(8,128)S(1)}, f32[4,128,256]{2,1,0:T(8,128)S(1)}, u32[]{:S(2)}, u32[]{:S(2)}) collective-permute-start(f32[4,128,256]{2,1,0:T(8,128)S(1)} %collective-permute-done.33.refs_1_), channel_id=1, source_target_pairs={{0,1},{1,0},{2,3},{3,2},{4,5},{5,4},{6,7},{7,6},{8,9},{9,8},{10,11... | collective-permute-start | bytes 1572872 | tf_op jit(solution)/shard_map/ppermute | solution.py:245

commit v7 on v5

--- a/solution.py
+++ b/solution.py
@@ -25,8 +25,8 @@
     return high, middle, (rest - middle.astype(f32)).astype(bf16)
 
 
-def kernel_params():
-    return pltpu.CompilerParams(vmem_limit_bytes=56 * MIB)
+def kernel_params(size):
+    return pltpu.CompilerParams(vmem_limit_bytes=int(size * MIB))
 
 
 def pack_kernel(own_rows, cap, tile_rows, counts_hbm, rows_hbm, updates_hbm, packed_ref, counts_ref, rows_ref, updates_ref, sems):
@@ -138,7 +138,7 @@
         in_specs=[vmem],
         out_specs=[vmem, vmem],
         out_shape=[shape, shape],
-        compiler_params=pltpu.CompilerParams(vmem_limit_bytes=20 * MIB),
+        compiler_params=kernel_params(20),
         cost_estimate=pl.CostEstimate(flops=3 * matrix.size, bytes_accessed=8 * matrix.size, transcendentals=0),
     )(matrix)
 
@@ -214,7 +214,7 @@
         out_specs=[vmem] * len(shares) if finish else vmem,
         out_shape=out_shape,
         scratch_shapes=[pltpu.VMEM(whole, f32)] if finish else [],
-        compiler_params=pltpu.CompilerParams(vmem_limit_bytes=20 * MIB),
+        compiler_params=kernel_params(20),
         cost_estimate=pl.CostEstimate(flops=6 * sum(shares) * both_rows * block * (end - begin), bytes_accessed=MIB, transcendentals=0),
     )(*arrays)
 
@@ -239,7 +239,8 @@
         return lax.ppermute(value, ("chain", "tile"), pairs)
 
     def first_stage(first, second, hop):
-        pair = [second if across == 0 and not hop else send(second, hop, lambda t: t ^ (2 * across)) for across in range(2)]
+        second = send(second, True, lambda t: t) if hop else second
+        pair = [second, send(second, False, lambda t: t ^ 2)]
         line = [first if by == 0 and not hop else send(first, hop, lambda t: (t + 4 * by) % tile_size) for by in range(layers)]
         return jnp.stack(pair), jnp.stack(line)
 
@@ -323,7 +324,7 @@
             pltpu.VMEM((columns, entries), f32),
             pltpu.SemaphoreType.DMA((3,)),
         ],
-        compiler_params=kernel_params(),
+        compiler_params=kernel_params(56),
     )(tile_counts, update_rows[None, :], updates.T)
     received = lax.all_to_all(packed, "tile", 0, 0, tiled=False)
     paired = own_rows % 128 == 0 and tile_size % 8 == 0 and batches > 1
@@ -335,7 +336,7 @@
         out_specs=[vmem] * len(shares),
         out_shape=[jax.ShapeDtypeStruct((rows, own_rows), f32) for rows in shares],
         scratch_shapes=[pltpu.VMEM((columns, own_rows), f32), pltpu.SemaphoreType.DMA(())],
-        compiler_params=kernel_params(),
+        compiler_params=kernel_params(20),
     )(received, right_side.reshape(columns, own_rows))
     solve = solve_paired if paired else solve_flat
     return solve(reduced, diag_inverse, coupling, sources).reshape(right_side.shape)

time: 98 us -> 99.4 us (1.014)
  starting transfers between devices: 23.7 us -> 26.2 us
  Pallas kernels: 14 us -> 12.3 us
  other arithmetic: 1.42 us -> 0.16 us
  waiting for transfers between devices: 34 us -> 35.2 us
    ppermute x6 -> x5, starting transfers between devices: 9.09 us -> 10.9 us  [send(): return lax.ppermute(value, ('chain', 'tile'), pairs)]
    pallas_call x1, Pallas kernels: 2.64 us -> 0.9 us  [body(): pl.pallas_call(functools.partial(reduce_kernel, cap), in_specs=[vmem, hbm...]
    another operation x4, other arithmetic: 1.36 us -> 0.09 us  [first_stage(): return (jnp.stack(pair), jnp.stack(line))]
    ppermute x6 -> x5, waiting for transfers between devices: 7.8 us -> 8.79 us  [send(): return lax.ppermute(value, ('chain', 'tile'), pairs)]
    ppermute x18 -> x19, starting transfers between devices: 14.6 us -> 15.2 us  [send(): lax.ppermute(value, 'tile', [(t, target(t)) for t in range(tile_size)])]
    ppermute x18 -> x19, waiting for transfers between devices: 26.2 us -> 26.4 us  [send(): lax.ppermute(value, 'tile', [(t, target(t)) for t in range(tile_size)])]
  transfers between devices with their start and end apart: 24 -> 24, of which waited for: 10 -> 11; matrix products, arithmetic and copies ran while one was open for 1% -> 0% of each run, Pallas kernels for 5% -> 5%
where the time goes in v7:
time: 99.4 us; the launch traced here: 99 us
  waiting for transfers between devices  35.2 us (35%)
  starting transfers between devices  26.2 us (26%)
  blocking collectives  20.6 us (21%)
  Pallas kernels  12.3 us (12%)
  local copies, waits for them, and re-layouts  4.31 us (4%)
    ppermute x19, waiting for transfers between devices, send(): lax.ppermute(value, 'tile', [(t, target(t)) for t in range(tile_size)])  26.4 us
    all_to_all x1, blocking collectives, body(): received = lax.all_to_all(packed, 'tile', 0, 0, tiled=False)  20.6 us
    ppermute x19, starting transfers between devices, send(): lax.ppermute(value, 'tile', [(t, target(t)) for t in range(tile_size)])  15.2 us
    ppermute x5, starting transfers between devices, send(): return lax.ppermute(value, ('chain', 'tile'), pairs)  10.9 us
    ppermute x5, waiting for transfers between devices, send(): return lax.ppermute(value, ('chain', 'tile'), pairs)  8.79 us
    pallas_call x4, Pallas kernels, product_part(): pl.pallas_call(functools.partial(product_kernel, sources, layout, len(blo...  7.2 us
    unnamed x6, local copies, waits for them, and re-layouts  4.31 us
    pallas_call x1, Pallas kernels, body(): pl.pallas_call(functools.partial(pack_kernel, own_rows, cap, tile_rows),...  2.27 us
  transfers between devices with their start and end apart: 24, of which 11 were waited for; matrix products, arithmetic and copies ran while one was open for 0% of the time, Pallas kernels for 5%

profile of v7, /device:TPU:0, one launch (start us, length us, event | category | flops | bytes accessed | tf_op | source)
XLA Modules:
  0.0 99.0 jit_solution(5299250228258123370)
XLA Ops:
  0.0 2.3 %shard_map.64 = f32[16,56,128]{2,1,0:T(8,128)} custom-call(s32[2]{0:T(128)} %counts_hbm.1, s32[1,256]{1,0:T(1,128)} %bitcast.46, f32[192,256]{1,0:T(8,128)} %bitcast.29), custom_call_target="tpu_custom_call" | custom-call | tf_op jit(solution)/shard_map/pallas_call | solution.py:316
  2.3 20.6 %all_to_all.5.received_ref = f32[16,56,128]{2,1,0:T(8,128)S(1)} all-to-all(f32[16,56,128]{2,1,0:T(8,128)} %shard_map.64), channel_id=1, replica_groups=mesh['chain'=2,'tile'=16] {'tile'}, dimensions={0} | all-to-all | bytes 917504 | tf_op jit(solution)/shard_map/all_to_all | solution.py:329
  22.9 0.0 copy-start.2
  22.9 0.9 copy-done.2
  23.9 0.9 shard_map.65
  24.8 0.4 collective-permute-start
  25.2 2.7 %collective-permute-start.3 = (f32[128,256]{1,0:T(8,128)S(1)}, f32[128,256]{1,0:T(8,128)S(1)}, u32[]{:S(2)}, u32[]{:S(2)}) collective-permute-start(f32[128,256]{1,0:T(8,128)S(1)} %get-tuple-element.26), channel_id=1, source_target_pairs={{0,12},{1,13},{2,14},{3,15},{4,0},{5,1},{6,2},{7,3},{8,4},{9,5},{1... | collective-permute-start | bytes 393224 | tf_op jit(solution)/shard_map/ppermute | solution.py:237
  27.9 0.5 collective-permute-start.2
  28.5 0.5 collective-permute-start.1
  29.0 0.0 copy-start
  29.0 3.4 %copy-done = f32[2,256,4096]{2,1,0:T(8,128)S(1)} copy-done((f32[2,256,4096]{2,1,0:T(8,128)S(1)}, f32[2,256,4096]{2,1,0:T(8,128)}, u32[]{:S(2)}) %copy-start) | copy-done | bytes 8388632
  32.4 0.0 copy-start.1
  32.4 0.9 shard_map.66
  33.3 0.0 collective-permute-done
  33.4 0.0 collective-permute-done.3
  33.4 6.9 %collective-permute-done.2 = f32[128,256]{1,0:T(8,128)S(1)} collective-permute-done((f32[128,256]{1,0:T(8,128)S(1)}, f32[128,256]{1,0:T(8,128)S(1)}, u32[]{:S(2)}, u32[]{:S(2)}) %collective-permute-start.2) | collective-permute-done | bytes 131104 | tf_op jit(solution)/shard_map/ppermute | solution.py:237
  40.3 0.0 collective-permute-done.1
  40.3 1.2 %collective-permute-start.5 = (f32[4,128,256]{2,1,0:T(8,128)S(1)}, f32[4,128,256]{2,1,0:T(8,128)S(1)}, u32[]{:S(2)}, u32[]{:S(2)}) collective-permute-start(f32[4,128,256]{2,1,0:T(8,128)S(1)} %pad_maximum_fusion.refs_0_.refs_3_), channel_id=1, source_target_pairs={{0,2},{1,3},{2,0},{3,1},{4,6},{5,7},{6,4},{7,5},{8,10},{9,11},{10,... | collective-permute-start | bytes 1572872 | tf_op jit(solution)/shard_map/ppermute | solution.py:237
  41.5 0.0 collective-permute-start.8
  41.5 1.7 %collective-permute-start.7 = (f32[2,64,256]{2,1,0:T(8,128)S(1)}, f32[2,64,256]{2,1,0:T(8,128)S(1)}, u32[]{:S(2)}, u32[]{:S(2)}) collective-permute-start(f32[2,64,256]{2,1,0:T(8,128)S(1)} %pad_maximum_fusion.4), channel_id=1, source_target_pairs={{0,8},{1,9},{2,10},{3,11},{4,12},{5,13},{6,14},{7,15},{8,0},{9,1},... | collective-permute-start | bytes 393224 | tf_op jit(solution)/shard_map/ppermute | solution.py:237
  43.3 2.0 %collective-permute-start.6 = (f32[2,64,256]{2,1,0:T(8,128)S(1)}, f32[2,64,256]{2,1,0:T(8,128)S(1)}, u32[]{:S(2)}, u32[]{:S(2)}) collective-permute-start(f32[2,64,256]{2,1,0:T(8,128)S(1)} %pad_maximum_fusion.4), channel_id=1, source_target_pairs={{0,4},{1,5},{2,6},{3,7},{4,8},{5,9},{6,10},{7,11},{8,12},{9,13},{1... | collective-permute-start | bytes 393224 | tf_op jit(solution)/shard_map/ppermute | solution.py:237
  45.3 0.0 collective-permute-start.4
  45.3 0.0 copy-done.1
  45.3 0.9 shard_map.67
  46.3 0.8 collective-permute-done.8
  47.1 7.9 %collective-permute-done.7 = f32[2,64,256]{2,1,0:T(8,128)S(1)} collective-permute-done((f32[2,64,256]{2,1,0:T(8,128)S(1)}, f32[2,64,256]{2,1,0:T(8,128)S(1)}, u32[]{:S(2)}, u32[]{:S(2)}) %collective-permute-start.7) | collective-permute-done | bytes 131104 | tf_op jit(solution)/shard_map/ppermute | solution.py:237
  55.0 0.0 collective-permute-done.6
  55.1 0.0 collective-permute-done.5.refs_1_.refs_4_
  55.1 0.1 collective-permute-start.9
  55.2 0.5 collective-permute-start.10
  55.7 1.7 %shard_map.68.refs_5_ = f32[192,512]{1,0:T(8,128)S(1)} custom-call(f32[4,128,256]{2,1,0:T(8,128)S(1)} %pad_maximum_fusion.refs_0_.refs_3_, f32[4,128,256]{2,1,0:T(8,128)S(1)} %collective-permute-done.5.refs_1_.refs_4_, f32[4,2,64,256]{3,2,1,0:T(8,128)S(1)} %pad_maximum_fusion.1.refs_2_.refs_5_, bf16[16,512,256]{2,1,0:T(8,128)(2,1)S(1)} %get-tuple-element.37.refs_3_, ...), custom_call_target="tpu_custom_call" | custom-call | flops 1207959552 | bytes 1048576 | tf_op jit(solution)/shard_map/pallas_call | solution.py:211
  57.3 0.0 collective-permute-done.4.refs_0_.refs_3_
  57.4 0.0 collective-permute-done.9.refs_1_.refs_4_
  57.4 0.5 collective-permute-done.10.refs_2_.refs_5_
  57.8 1.6 %shard_map.69 = (f32[128,256]{1,0:T(8,128)S(1)}, f32[64,256]{1,0:T(8,128)S(1)}) custom-call(f32[4,128,256]{2,1,0:T(8,128)S(1)} %collective-permute-done.4.refs_0_.refs_3_, f32[4,128,256]{2,1,0:T(8,128)S(1)} %collective-permute-done.9.refs_1_.refs_4_, f32[4,2,64,256]{3,2,1,0:T(8,128)S(1)} %collective-permute-done.10.refs_2_.refs_5_, ...), custom_call_target="tpu_custom_call" | custom-call | flops 1207959552 | bytes 1048576 | tf_op jit(solution)/shard_map/pallas_call | solution.py:211
  59.4 1.8 %collective-permute-start.11 = (f32[64,256]{1,0:T(8,128)S(1)}, f32[64,256]{1,0:T(8,128)S(1)}, u32[]{:S(2)}, u32[]{:S(2)}) collective-permute-start(f32[64,256]{1,0:T(8,128)S(1)} %get-tuple-element.39), channel_id=1, source_target_pairs={{0,16},{1,17},{2,18},{3,19},{4,20},{5,21},{6,22},{7,23},{8,24},{9,... | collective-permute-start | bytes 196616 | tf_op jit(solution)/shard_map/ppermute | solution.py:239
  61.2 1.9 %collective-permute-done.11 = f32[64,256]{1,0:T(8,128)S(1)} collective-permute-done((f32[64,256]{1,0:T(8,128)S(1)}, f32[64,256]{1,0:T(8,128)S(1)}, u32[]{:S(2)}, u32[]{:S(2)}) %collective-permute-start.11) | collective-permute-done | bytes 65568 | tf_op jit(solution)/shard_map/ppermute | solution.py:239
  63.1 0.3 collective-permute-start.12
  63.5 3.3 %collective-permute-start.16 = (f32[128,256]{1,0:T(8,128)S(1)}, f32[128,256]{1,0:T(8,128)S(1)}, u32[]{:S(2)}, u32[]{:S(2)}) collective-permute-start(f32[128,256]{1,0:T(8,128)S(1)} %get-tuple-element.40), channel_id=1, source_target_pairs={{0,28},{1,29},{2,30},{3,31},{4,16},{5,17},{6,18},{7,19},{8,20},{9,... | collective-permute-start | bytes 393224 | tf_op jit(solution)/shard_map/ppermute | solution.py:239
  66.8 3.2 %collective-permute-start.15 = (f32[128,256]{1,0:T(8,128)S(1)}, f32[128,256]{1,0:T(8,128)S(1)}, u32[]{:S(2)}, u32[]{:S(2)}) collective-permute-start(f32[128,256]{1,0:T(8,128)S(1)} %get-tuple-element.40), channel_id=1, source_target_pairs={{0,24},{1,25},{2,26},{3,27},{4,28},{5,29},{6,30},{7,31},{8,16},{9,... | collective-permute-start | bytes 393224 | tf_op jit(solution)/shard_map/ppermute | solution.py:239
  70.0 1.3 %collective-permute-start.14 = (f32[128,256]{1,0:T(8,128)S(1)}, f32[128,256]{1,0:T(8,128)S(1)}, u32[]{:S(2)}, u32[]{:S(2)}) collective-permute-start(f32[128,256]{1,0:T(8,128)S(1)} %get-tuple-element.40), channel_id=1, source_target_pairs={{0,20},{1,21},{2,22},{3,23},{4,24},{5,25},{6,26},{7,27},{8,28},{9,... | collective-permute-start | bytes 393224 | tf_op jit(solution)/shard_map/ppermute | solution.py:239
  71.3 1.3 %collective-permute-start.13 = (f32[128,256]{1,0:T(8,128)S(1)}, f32[128,256]{1,0:T(8,128)S(1)}, u32[]{:S(2)}, u32[]{:S(2)}) collective-permute-start(f32[128,256]{1,0:T(8,128)S(1)} %get-tuple-element.40), channel_id=1, source_target_pairs={{0,16},{1,17},{2,18},{3,19},{4,20},{5,21},{6,22},{7,23},{8,24},{9,... | collective-permute-start | bytes 393224 | tf_op jit(solution)/shard_map/ppermute | solution.py:239
  72.6 0.0 collective-permute-done.12
  72.7 0.0 collective-permute-done.16
  72.7 0.9 collective-permute-done.15
  73.5 1.7 %collective-permute-done.14 = f32[128,256]{1,0:T(8,128)S(1)} collective-permute-done((f32[128,256]{1,0:T(8,128)S(1)}, f32[128,256]{1,0:T(8,128)S(1)}, u32[]{:S(2)}, u32[]{:S(2)}) %collective-permute-start.14) | collective-permute-done | bytes 131104 | tf_op jit(solution)/shard_map/ppermute | solution.py:239
  75.2 4.3 %collective-permute-done.13 = f32[128,256]{1,0:T(8,128)S(1)} collective-permute-done((f32[128,256]{1,0:T(8,128)S(1)}, f32[128,256]{1,0:T(8,128)S(1)}, u32[]{:S(2)}, u32[]{:S(2)}) %collective-permute-start.13) | collective-permute-done | bytes 131104 | tf_op jit(solution)/shard_map/ppermute | solution.py:239
  79.6 1.7 %collective-permute-start.18 = (f32[4,128,256]{2,1,0:T(8,128)S(1)}, f32[4,128,256]{2,1,0:T(8,128)S(1)}, u32[]{:S(2)}, u32[]{:S(2)}) collective-permute-start(f32[4,128,256]{2,1,0:T(8,128)S(1)} %pad_maximum_fusion.2.refs_0_), channel_id=1, source_target_pairs={{0,2},{1,3},{2,0},{3,1},{4,6},{5,7},{6,4},{7,5},{8,10},{9,11},{10,... | collective-permute-start | bytes 1572872 | tf_op jit(solution)/shard_map/ppermute | solution.py:237
  81.3 1.3 %collective-permute-start.22 = (f32[2,64,256]{2,1,0:T(8,128)S(1)}, f32[2,64,256]{2,1,0:T(8,128)S(1)}, u32[]{:S(2)}, u32[]{:S(2)}) collective-permute-start(f32[2,64,256]{2,1,0:T(8,128)S(1)} %pad_maximum_fusion.5), channel_id=1, source_target_pairs={{0,12},{1,13},{2,14},{3,15},{4,0},{5,1},{6,2},{7,3},{8,4},{9,5},{1... | collective-permute-start | bytes 393224 | tf_op jit(solution)/shard_map/ppermute | solution.py:237
  82.6 0.0 collective-permute-start.21
  82.6 1.6 %collective-permute-start.20 = (f32[2,64,256]{2,1,0:T(8,128)S(1)}, f32[2,64,256]{2,1,0:T(8,128)S(1)}, u32[]{:S(2)}, u32[]{:S(2)}) collective-permute-start(f32[2,64,256]{2,1,0:T(8,128)S(1)} %pad_maximum_fusion.5), channel_id=1, source_target_pairs={{0,4},{1,5},{2,6},{3,7},{4,8},{5,9},{6,10},{7,11},{8,12},{9,13},{1... | collective-permute-start | bytes 393224 | tf_op jit(solution)/shard_map/ppermute | solution.py:237
  84.1 0.0 collective-permute-start.17
  84.1 3.0 %collective-permute-done.22 = f32[2,64,256]{2,1,0:T(8,128)S(1)} collective-permute-done((f32[2,64,256]{2,1,0:T(8,128)S(1)}, f32[2,64,256]{2,1,0:T(8,128)S(1)}, u32[]{:S(2)}, u32[]{:S(2)}) %collective-permute-start.22) | collective-permute-done | bytes 131104 | tf_op jit(solution)/shard_map/ppermute | solution.py:237
  87.1 6.8 %collective-permute-done.21 = f32[2,64,256]{2,1,0:T(8,128)S(1)} collective-permute-done((f32[2,64,256]{2,1,0:T(8,128)S(1)}, f32[2,64,256]{2,1,0:T(8,128)S(1)}, u32[]{:S(2)}, u32[]{:S(2)}) %collective-permute-start.21) | collective-permute-done | bytes 131104 | tf_op jit(solution)/shard_map/ppermute | solution.py:237
  93.9 0.0 collective-permute-done.20
  94.0 0.1 collective-permute-start.23
  94.1 0.0 collective-permute-done.18.refs_1_
  94.1 0.5 collective-permute-start.19
  94.6 1.7 %shard_map.70.refs_8_ = f32[192,512]{1,0:T(8,128)S(1)} custom-call(f32[4,128,256]{2,1,0:T(8,128)S(1)} %pad_maximum_fusion.2.refs_0_, f32[4,128,256]{2,1,0:T(8,128)S(1)} %collective-permute-done.18.refs_1_, f32[4,2,64,256]{3,2,1,0:T(8,128)S(1)} %pad_maximum_fusion.3.refs_2_, f32[4,128,256]{2,1,0:T(8,128)S(1)} %pad_maximum_fusion.refs_0_.refs_3_, ...), custom_call_target="tpu_custom_call" | custom-call | flops 1207959552 | bytes 1048576 | tf_op jit(solution)/shard_map/pallas_call | solution.py:211
  96.2 0.0 collective-permute-done.17.refs_0_
  96.2 0.0 collective-permute-done.23.refs_2_
  96.2 0.5 collective-permute-done.19.refs_1_
  96.7 2.3 %shard_map.71 = f32[192,256]{1,0:T(8,128)} custom-call(f32[4,128,256]{2,1,0:T(8,128)S(1)} %collective-permute-done.17.refs_0_, f32[4,128,256]{2,1,0:T(8,128)S(1)} %collective-permute-done.19.refs_1_, f32[4,2,64,256]{3,2,1,0:T(8,128)S(1)} %collective-permute-done.23.refs_2_, f32[4,128,256]{2,1,0:T(8,128)S(1)} %collective-permute-done.4.refs_0_.refs_3_, ...), custom_call_target="tpu_custom_call" | custom-call | flops 1207959552 | bytes 1048576 | tf_op jit(solution)/shard_map/pallas_call | solution.py:211
  (6 shorter events, 0.2 us)
Async XLA Ops:
  22.9 0.9 copy-start.2
  24.8 8.6 %collective-permute-start = (f32[64,256]{1,0:T(8,128)S(1)}, f32[64,256]{1,0:T(8,128)S(1)}, u32[]{:S(2)}, u32[]{:S(2)}) collective-permute-start(f32[64,256]{1,0:T(8,128)S(1)} %get-tuple-element.25), channel_id=1, source_target_pairs={{0,2},{1,3},{2,0},{3,1},{4,6},{5,7},{6,4},{7,5},{8,10},{9,11},{10,... | collective-permute-start | bytes 196616 | tf_op jit(solution)/shard_map/ppermute | solution.py:237
  25.2 8.2 %collective-permute-start.3 = (f32[128,256]{1,0:T(8,128)S(1)}, f32[128,256]{1,0:T(8,128)S(1)}, u32[]{:S(2)}, u32[]{:S(2)}) collective-permute-start(f32[128,256]{1,0:T(8,128)S(1)} %get-tuple-element.26), channel_id=1, source_target_pairs={{0,12},{1,13},{2,14},{3,15},{4,0},{5,1},{6,2},{7,3},{8,4},{9,5},{1... | collective-permute-start | bytes 393224 | tf_op jit(solution)/shard_map/ppermute | solution.py:237
  27.9 12.4 %collective-permute-start.2 = (f32[128,256]{1,0:T(8,128)S(1)}, f32[128,256]{1,0:T(8,128)S(1)}, u32[]{:S(2)}, u32[]{:S(2)}) collective-permute-start(f32[128,256]{1,0:T(8,128)S(1)} %get-tuple-element.26), channel_id=1, source_target_pairs={{0,8},{1,9},{2,10},{3,11},{4,12},{5,13},{6,14},{7,15},{8,0},{9,1},... | collective-permute-start | bytes 393224 | tf_op jit(solution)/shard_map/ppermute | solution.py:237
  28.5 11.8 %collective-permute-start.1 = (f32[128,256]{1,0:T(8,128)S(1)}, f32[128,256]{1,0:T(8,128)S(1)}, u32[]{:S(2)}, u32[]{:S(2)}) collective-permute-start(f32[128,256]{1,0:T(8,128)S(1)} %get-tuple-element.26), channel_id=1, source_target_pairs={{0,4},{1,5},{2,6},{3,7},{4,8},{5,9},{6,10},{7,11},{8,12},{9,13},{1... | collective-permute-start | bytes 393224 | tf_op jit(solution)/shard_map/ppermute | solution.py:237
  29.0 3.4 %copy-start = (f32[2,256,4096]{2,1,0:T(8,128)S(1)}, f32[2,256,4096]{2,1,0:T(8,128)}, u32[]{:S(2)}) copy-start(f32[2,256,4096]{2,1,0:T(8,128)} %matrix_ref) | copy-start | bytes 25165828
  32.4 12.9 %copy-start.1 = (f32[2,256,4096]{2,1,0:T(8,128)S(1)}, f32[2,256,4096]{2,1,0:T(8,128)}, u32[]{:S(2)}) copy-start(f32[2,256,4096]{2,1,0:T(8,128)} %matrix_ref.1) | copy-start | bytes 25165828
  40.3 14.8 %collective-permute-start.5 = (f32[4,128,256]{2,1,0:T(8,128)S(1)}, f32[4,128,256]{2,1,0:T(8,128)S(1)}, u32[]{:S(2)}, u32[]{:S(2)}) collective-permute-start(f32[4,128,256]{2,1,0:T(8,128)S(1)} %pad_maximum_fusion.refs_0_.refs_3_), channel_id=1, source_target_pairs={{0,2},{1,3},{2,0},{3,1},{4,6},{5,7},{6,4},{7,5},{8,10},{9,11},{10,... | collective-permute-start | bytes 1572872 | tf_op jit(solution)/shard_map/ppermute | solution.py:237
  41.5 5.6 %collective-permute-start.8 = (f32[2,64,256]{2,1,0:T(8,128)S(1)}, f32[2,64,256]{2,1,0:T(8,128)S(1)}, u32[]{:S(2)}, u32[]{:S(2)}) collective-permute-start(f32[2,64,256]{2,1,0:T(8,128)S(1)} %pad_maximum_fusion.4), channel_id=1, source_target_pairs={{0,12},{1,13},{2,14},{3,15},{4,0},{5,1},{6,2},{7,3},{8,4},{9,5},{1... | collective-permute-start | bytes 393224 | tf_op jit(solution)/shard_map/ppermute | solution.py:237
  41.5 13.5 %collective-permute-start.7 = (f32[2,64,256]{2,1,0:T(8,128)S(1)}, f32[2,64,256]{2,1,0:T(8,128)S(1)}, u32[]{:S(2)}, u32[]{:S(2)}) collective-permute-start(f32[2,64,256]{2,1,0:T(8,128)S(1)} %pad_maximum_fusion.4), channel_id=1, source_target_pairs={{0,8},{1,9},{2,10},{3,11},{4,12},{5,13},{6,14},{7,15},{8,0},{9,1},... | collective-permute-start | bytes 393224 | tf_op jit(solution)/shard_map/ppermute | solution.py:237
  43.3 11.8 %collective-permute-start.6 = (f32[2,64,256]{2,1,0:T(8,128)S(1)}, f32[2,64,256]{2,1,0:T(8,128)S(1)}, u32[]{:S(2)}, u32[]{:S(2)}) collective-permute-start(f32[2,64,256]{2,1,0:T(8,128)S(1)} %pad_maximum_fusion.4), channel_id=1, source_target_pairs={{0,4},{1,5},{2,6},{3,7},{4,8},{5,9},{6,10},{7,11},{8,12},{9,13},{1... | collective-permute-start | bytes 393224 | tf_op jit(solution)/shard_map/ppermute | solution.py:237
  45.3 12.0 %collective-permute-start.4 = (f32[4,128,256]{2,1,0:T(8,128)S(1)}, f32[4,128,256]{2,1,0:T(8,128)S(1)}, u32[]{:S(2)}, u32[]{:S(2)}) collective-permute-start(f32[4,128,256]{2,1,0:T(8,128)S(1)} %pad_maximum_fusion.refs_0_.refs_3_), channel_id=1, source_target_pairs={{0,1},{1,0},{2,3},{3,2},{4,5},{5,4},{6,7},{7,6},{8,9},{9,8},{10,11... | collective-permute-start | bytes 1572872 | tf_op jit(solution)/shard_map/ppermute | solution.py:237
  55.1 2.3 %collective-permute-start.9 = (f32[4,128,256]{2,1,0:T(8,128)S(1)}, f32[4,128,256]{2,1,0:T(8,128)S(1)}, u32[]{:S(2)}, u32[]{:S(2)}) collective-permute-start(f32[4,128,256]{2,1,0:T(8,128)S(1)} %collective-permute-done.5.refs_1_.refs_4_), channel_id=1, source_target_pairs={{0,1},{1,0},{2,3},{3,2},{4,5},{5,4},{6,7},{7,6},{8,9},{9,8},{10,11... | collective-permute-start | bytes 1572872 | tf_op jit(solution)/shard_map/ppermute | solution.py:237
  55.2 2.6 %collective-permute-start.10 = (f32[4,2,64,256]{3,2,1,0:T(8,128)S(1)}, f32[4,2,64,256]{3,2,1,0:T(8,128)S(1)}, u32[]{:S(2)}, u32[]{:S(2)}) collective-permute-start(f32[4,2,64,256]{3,2,1,0:T(8,128)S(1)} %pad_maximum_fusion.1.refs_2_.refs_5_), channel_id=1, source_target_pairs={{0,1},{1,0},{2,3},{3,2},{4,5},{5,4},{6,7},{7,6},{8,9},{9,8},{10,11... | collective-permute-start | bytes 1572872 | tf_op jit(solution)/shard_map/ppermute | solution.py:237
  59.4 3.7 %collective-permute-start.11 = (f32[64,256]{1,0:T(8,128)S(1)}, f32[64,256]{1,0:T(8,128)S(1)}, u32[]{:S(2)}, u32[]{:S(2)}) collective-permute-start(f32[64,256]{1,0:T(8,128)S(1)} %get-tuple-element.39), channel_id=1, source_target_pairs={{0,16},{1,17},{2,18},{3,19},{4,20},{5,21},{6,22},{7,23},{8,24},{9,... | collective-permute-start | bytes 196616 | tf_op jit(solution)/shard_map/ppermute | solution.py:239
  63.1 9.5 %collective-permute-start.12 = (f32[64,256]{1,0:T(8,128)S(1)}, f32[64,256]{1,0:T(8,128)S(1)}, u32[]{:S(2)}, u32[]{:S(2)}) collective-permute-start(f32[64,256]{1,0:T(8,128)S(1)} %collective-permute-done.11), channel_id=1, source_target_pairs={{0,2},{1,3},{2,0},{3,1},{4,6},{5,7},{6,4},{7,5},{8,10},{9,11},{10,... | collective-permute-start | bytes 196616 | tf_op jit(solution)/shard_map/ppermute | solution.py:237
  63.5 9.2 %collective-permute-start.16 = (f32[128,256]{1,0:T(8,128)S(1)}, f32[128,256]{1,0:T(8,128)S(1)}, u32[]{:S(2)}, u32[]{:S(2)}) collective-permute-start(f32[128,256]{1,0:T(8,128)S(1)} %get-tuple-element.40), channel_id=1, source_target_pairs={{0,28},{1,29},{2,30},{3,31},{4,16},{5,17},{6,18},{7,19},{8,20},{9,... | collective-permute-start | bytes 393224 | tf_op jit(solution)/shard_map/ppermute | solution.py:239
  66.8 6.7 %collective-permute-start.15 = (f32[128,256]{1,0:T(8,128)S(1)}, f32[128,256]{1,0:T(8,128)S(1)}, u32[]{:S(2)}, u32[]{:S(2)}) collective-permute-start(f32[128,256]{1,0:T(8,128)S(1)} %get-tuple-element.40), channel_id=1, source_target_pairs={{0,24},{1,25},{2,26},{3,27},{4,28},{5,29},{6,30},{7,31},{8,16},{9,... | collective-permute-start | bytes 393224 | tf_op jit(solution)/shard_map/ppermute | solution.py:239
  70.0 5.2 %collective-permute-start.14 = (f32[128,256]{1,0:T(8,128)S(1)}, f32[128,256]{1,0:T(8,128)S(1)}, u32[]{:S(2)}, u32[]{:S(2)}) collective-permute-start(f32[128,256]{1,0:T(8,128)S(1)} %get-tuple-element.40), channel_id=1, source_target_pairs={{0,20},{1,21},{2,22},{3,23},{4,24},{5,25},{6,26},{7,27},{8,28},{9,... | collective-permute-start | bytes 393224 | tf_op jit(solution)/shard_map/ppermute | solution.py:239
  71.3 8.2 %collective-permute-start.13 = (f32[128,256]{1,0:T(8,128)S(1)}, f32[128,256]{1,0:T(8,128)S(1)}, u32[]{:S(2)}, u32[]{:S(2)}) collective-permute-start(f32[128,256]{1,0:T(8,128)S(1)} %get-tuple-element.40), channel_id=1, source_target_pairs={{0,16},{1,17},{2,18},{3,19},{4,20},{5,21},{6,22},{7,23},{8,24},{9,... | collective-permute-start | bytes 393224 | tf_op jit(solution)/shard_map/ppermute | solution.py:239
  79.6 14.5 %collective-permute-start.18 = (f32[4,128,256]{2,1,0:T(8,128)S(1)}, f32[4,128,256]{2,1,0:T(8,128)S(1)}, u32[]{:S(2)}, u32[]{:S(2)}) collective-permute-start(f32[4,128,256]{2,1,0:T(8,128)S(1)} %pad_maximum_fusion.2.refs_0_), channel_id=1, source_target_pairs={{0,2},{1,3},{2,0},{3,1},{4,6},{5,7},{6,4},{7,5},{8,10},{9,11},{10,... | collective-permute-start | bytes 1572872 | tf_op jit(solution)/shard_map/ppermute | solution.py:237
  81.3 5.8 %collective-permute-start.22 = (f32[2,64,256]{2,1,0:T(8,128)S(1)}, f32[2,64,256]{2,1,0:T(8,128)S(1)}, u32[]{:S(2)}, u32[]{:S(2)}) collective-permute-start(f32[2,64,256]{2,1,0:T(8,128)S(1)} %pad_maximum_fusion.5), channel_id=1, source_target_pairs={{0,12},{1,13},{2,14},{3,15},{4,0},{5,1},{6,2},{7,3},{8,4},{9,5},{1... | collective-permute-start | bytes 393224 | tf_op jit(solution)/shard_map/ppermute | solution.py:237
  82.6 11.4 %collective-permute-start.21 = (f32[2,64,256]{2,1,0:T(8,128)S(1)}, f32[2,64,256]{2,1,0:T(8,128)S(1)}, u32[]{:S(2)}, u32[]{:S(2)}) collective-permute-start(f32[2,64,256]{2,1,0:T(8,128)S(1)} %pad_maximum_fusion.5), channel_id=1, source_target_pairs={{0,8},{1,9},{2,10},{3,11},{4,12},{5,13},{6,14},{7,15},{8,0},{9,1},... | collective-permute-start | bytes 393224 | tf_op jit(solution)/shard_map/ppermute | solution.py:237
  82.6 11.4 %collective-permute-start.20 = (f32[2,64,256]{2,1,0:T(8,128)S(1)}, f32[2,64,256]{2,1,0:T(8,128)S(1)}, u32[]{:S(2)}, u32[]{:S(2)}) collective-permute-start(f32[2,64,256]{2,1,0:T(8,128)S(1)} %pad_maximum_fusion.5), channel_id=1, source_target_pairs={{0,4},{1,5},{2,6},{3,7},{4,8},{5,9},{6,10},{7,11},{8,12},{9,13},{1... | collective-permute-start | bytes 393224 | tf_op jit(solution)/shard_map/ppermute | solution.py:237
  84.1 12.1 %collective-permute-start.17 = (f32[4,128,256]{2,1,0:T(8,128)S(1)}, f32[4,128,256]{2,1,0:T(8,128)S(1)}, u32[]{:S(2)}, u32[]{:S(2)}) collective-permute-start(f32[4,128,256]{2,1,0:T(8,128)S(1)} %pad_maximum_fusion.2.refs_0_), channel_id=1, source_target_pairs={{0,1},{1,0},{2,3},{3,2},{4,5},{5,4},{6,7},{7,6},{8,9},{9,8},{10,11... | collective-permute-start | bytes 1572872 | tf_op jit(solution)/shard_map/ppermute | solution.py:237
  94.0 2.3 %collective-permute-start.23 = (f32[4,2,64,256]{3,2,1,0:T(8,128)S(1)}, f32[4,2,64,256]{3,2,1,0:T(8,128)S(1)}, u32[]{:S(2)}, u32[]{:S(2)}) collective-permute-start(f32[4,2,64,256]{3,2,1,0:T(8,128)S(1)} %pad_maximum_fusion.3.refs_2_), channel_id=1, source_target_pairs={{0,1},{1,0},{2,3},{3,2},{4,5},{5,4},{6,7},{7,6},{8,9},{9,8},{10,11... | collective-permute-start | bytes 1572872 | tf_op jit(solution)/shard_map/ppermute | solution.py:237
  94.1 2.6 %collective-permute-start.19 = (f32[4,128,256]{2,1,0:T(8,128)S(1)}, f32[4,128,256]{2,1,0:T(8,128)S(1)}, u32[]{:S(2)}, u32[]{:S(2)}) collective-permute-start(f32[4,128,256]{2,1,0:T(8,128)S(1)} %collective-permute-done.18.refs_1_), channel_id=1, source_target_pairs={{0,1},{1,0},{2,3},{3,2},{4,5},{5,4},{6,7},{7,6},{8,9},{9,8},{10,11... | collective-permute-start | bytes 1572872 | tf_op jit(solution)/shard_map/ppermute | solution.py:237

commit v8 on v7

--- a/solution.py
+++ b/solution.py
@@ -115,26 +115,29 @@
         start += rows
 
 
-def split_kernel(matrix_ref, high_ref, low_ref):
+def split_kernel(block, relative, matrix_ref, high_ref, low_ref):
     parts, own_rows, full_rows = matrix_ref.shape
-    blocks, rows, block = high_ref.shape
+    groups, rows, width = high_ref.shape
+    layers = width // block
     height = 64
     for part in range(parts):
         for first in range(0, own_rows, height):
-            for j in range(blocks):
-                high, low = halves_of(matrix_ref[part, first:first + height, j * block:(j + 1) * block])
-                start = part * own_rows + first
-                high_ref[j, start:start + height, :] = high
-                low_ref[j, start:start + height, :] = low
-
-
-def split_blocks(matrix, block):
+            start = part * own_rows + first
+            for group in range(groups):
+                for layer in range(layers):
+                    column = (layer * groups + group if relative else group * layers + layer) * block
+                    high, low = halves_of(matrix_ref[part, first:first + height, column:column + block])
+                    high_ref[group, start:start + height, layer * block:(layer + 1) * block] = high
+                    low_ref[group, start:start + height, layer * block:(layer + 1) * block] = low
+
+
+def split_blocks(matrix, block, relative):
     parts, own_rows, full_rows = matrix.shape
-    count = full_rows // block
+    groups = 4 if full_rows % (4 * block) == 0 else 1
     vmem = pl.BlockSpec(memory_space=pltpu.VMEM)
-    shape = jax.ShapeDtypeStruct((count, parts * own_rows, block), bf16)
+    shape = jax.ShapeDtypeStruct((groups, parts * own_rows, full_rows // groups), bf16)
     return pl.pallas_call(
-        split_kernel,
+        functools.partial(split_kernel, block, relative),
         in_specs=[vmem],
         out_specs=[vmem, vmem],
         out_shape=[shape, shape],
@@ -143,30 +146,22 @@
     )(matrix)
 
 
-def tile_of(q, size):
-    me = lax.axis_index("tile")
-    layers = size // 4
-    side, across, by = q // (2 * layers), q // layers % 2, q % layers
-    layer = lax.rem(lax.div(me, 4) + (layers - by), layers)
-    row = lax.rem(lax.div(me, 2) + across, 2)
-    core = lax.rem(me + side, 2)
-    return layer * 4 + row * 2 + core
-
-
-def product_kernel(sources, layout, inputs, sets, begin, end, finish, onward, relative, *refs):
+def product_kernel(sources, layout, inputs, sets, block, begin, end, onward, relative, *refs):
     high_ref, low_ref = refs[inputs * sets:inputs * sets + 2]
     rest = refs[inputs * sets + 2:]
-    count, both_rows, block = high_ref.shape
+    groups, both_rows, width = high_ref.shape
+    layers = width // block
     own_rows = both_rows // 2
     start_ref, rest = (rest[0], rest[1:]) if begin > 0 else (None, rest)
-    out_refs, total_ref = (rest[:-1], rest[-1]) if finish else ((), rest[0])
+    out_refs, total_ref = (rest[:-1], rest[-1]) if end == groups else ((), rest[0])
     columns = total_ref.shape[0]
-    per_step = 4 if (end - begin) % 4 == 0 else 1
-
-    def block_of(q):
+    me = lax.axis_index("tile")
+
+    def block_of(step, layer):
+        held = lax.rem(lax.div(me, 4) + (layers - layer), layers) if relative else layer
         pieces = []
         for group in layout:
-            which, place = group[q]
+            which, place = group(step, held)
             value = refs[which][place]
             if sets == 2:
                 value = refs[inputs + which][place] - value
@@ -175,14 +170,16 @@
 
     @pl.when(jnp.logical_not(onward) | (lax.axis_index("chain") < lax.axis_size("chain") - 1))
     def _():
-        for first in range(begin, end, per_step):
-            tiles = [tile_of(q, count) if relative else q for q in range(first, first + per_step)]
-            x_high, x_low = halves_of(jnp.concatenate([block_of(q) for q in range(first, first + per_step)], axis=1))
-            k_high = jnp.concatenate([high_ref[tile] for tile in tiles], axis=1)
-            k_low = jnp.concatenate([low_ref[tile] for tile in tiles], axis=1)
-            both = lax.dot_general(jnp.concatenate([x_high, x_low], axis=0), k_high, lanes_contract, preferred_element_type=f32)
-            part = both[:columns] + both[columns:] + lax.dot_general(x_high, k_low, lanes_contract, preferred_element_type=f32)
-            if first > begin:
+        for step in range(begin, end):
+            group = step
+            if relative:
+                group = lax.rem(lax.div(me, 2) + step % 2, 2) * 2 + lax.rem(me + step // 2, 2)
+            x_high, x_low = halves_of(jnp.concatenate([block_of(step, layer) for layer in range(layers)], axis=1))
+            lhs = jnp.concatenate([x_high, x_low], axis=0)
+            both = lax.dot_general(lhs, high_ref[group], lanes_contract, preferred_element_type=f32)
+            part = both[:columns] + both[columns:]
+            part += lax.dot_general(x_high, low_ref[group], lanes_contract, preferred_element_type=f32)
+            if step > begin:
                 total_ref[...] += part
             elif start_ref is None:
                 total_ref[...] = part
@@ -198,10 +195,11 @@
             start += out_ref.shape[0]
 
 
-def product_part(split, onward, layout, blocks, own, begin, end, started, sources, shares):
-    count, both_rows, block = split[0].shape
+def product_part(split, onward, layout, blocks, own, begin, end, started, sources, shares, relative):
+    groups, both_rows, width = split[0].shape
+    block = blocks[0].shape[-1]
     vmem = pl.BlockSpec(memory_space=pltpu.VMEM)
-    finish = end == count
+    finish = end == groups
     whole = (sum(shares), both_rows)
     arrays = list(blocks) + list(own) + list(split) + ([] if started is None else [started])
     if finish:
@@ -209,13 +207,13 @@
     else:
         out_shape = jax.ShapeDtypeStruct(whole, f32)
     return pl.pallas_call(
-        functools.partial(product_kernel, sources, layout, len(blocks), 2 if own else 1, begin, end, finish, onward, len(layout) > 1),
+        functools.partial(product_kernel, sources, layout, len(blocks), 2 if own else 1, block, begin, end, onward, relative),
         in_specs=[vmem] * len(arrays),
         out_specs=[vmem] * len(shares) if finish else vmem,
         out_shape=out_shape,
         scratch_shapes=[pltpu.VMEM(whole, f32)] if finish else [],
         compiler_params=kernel_params(20),
-        cost_estimate=pl.CostEstimate(flops=6 * sum(shares) * both_rows * block * (end - begin), bytes_accessed=MIB, transcendentals=0),
+        cost_estimate=pl.CostEstimate(flops=6 * sum(shares) * both_rows * width * (end - begin), bytes_accessed=MIB, transcendentals=0),
     )(*arrays)
 
 
@@ -229,8 +227,6 @@
     own_rows = reduced[0].shape[1]
     shares = [each.shape[0] for each in reduced]
     layers = tile_size // 4
-    count = tile_size
-    places = [(side, across, by) for side in range(2) for across in range(2) for by in range(layers)]
 
     def send(value, hop, target):
         if not hop:
@@ -239,8 +235,7 @@
         return lax.ppermute(value, ("chain", "tile"), pairs)
 
     def first_stage(first, second, hop):
-        second = send(second, True, lambda t: t) if hop else second
-        pair = [second, send(second, False, lambda t: t ^ 2)]
+        pair = [second if across == 0 and not hop else send(second, hop, lambda t: t ^ (2 * across)) for across in range(2)]
         line = [first if by == 0 and not hop else send(first, hop, lambda t: (t + 4 * by) % tile_size) for by in range(layers)]
         return jnp.stack(pair), jnp.stack(line)
 
@@ -249,25 +244,22 @@
         rest = [pair if by == 0 else send(pair, False, lambda t: (t + 4 * by) % tile_size) for by in range(layers)]
         return [line, far, jnp.stack(rest)]
 
-    layout = [
-        [(across, (by,)) for side, across, by in places],
-        [(2, (by, across)) for side, across, by in places],
-    ]
+    layout = [lambda step, held: (step % 2, (held,)), lambda step, held: (2, (held, step % 2))]
 
     def products(split, onward, held, own, shares):
         other = [send(each, False, lambda t: t ^ 1) for each in held]
         mine, theirs = own if own else ([], [])
-        started = product_part(split, onward, layout, held, mine, 0, count // 2, None, sources, shares)
-        return product_part(split, onward, layout, other, theirs, count // 2, count, started, sources, shares), other
+        started = product_part(split, onward, layout, held, mine, 0, 2, None, sources, shares, True)
+        return product_part(split, onward, layout, other, theirs, 2, 4, started, sources, shares, True), other
 
     only = chain_size == 1
     pair, line = first_stage(*reduced, False)
-    split = split_blocks(tied(diag_inverse if only else coupling, reduced[0]), own_rows)
+    split = split_blocks(tied(diag_inverse if only else coupling, reduced[0]), own_rows, True)
     pair, line, split = lax.optimization_barrier((pair, line, split))
     held = second_stage(pair, line)
     if only:
         return products(split, False, held, None, [sum(shares)])[0][0]
-    diag_split = split_blocks(tied(diag_inverse, line), own_rows)
+    diag_split = split_blocks(tied(diag_inverse, line), own_rows, True)
     held[1], held[2], diag_split = lax.optimization_barrier((held[1], held[2], diag_split))
     carried, other = products(split, True, held, None, shares)
     own = (held, other)
@@ -285,10 +277,12 @@
     full_rows = diag_inverse.shape[2]
     block = min(256, full_rows)
     count = full_rows // block
-    layout = [[(0, (q,)) for q in range(count)]]
+    layout = [lambda step, held: (0, (step * layers + held,))]
     onward = [(i, i + 1) for i in range(chain_size - 1)]
-    diag_split = split_blocks(diag_inverse, block)
-    coupling_split = split_blocks(coupling, block)
+    diag_split = split_blocks(diag_inverse, block, False)
+    coupling_split = split_blocks(coupling, block, False)
+    groups = diag_split[0].shape[0]
+    layers = count // groups
 
     def gathered(value):
         whole = lax.all_gather(value, "tile", axis=1, tiled=True)
@@ -296,9 +290,9 @@
 
     current = reduced
     for _ in range(chain_size - 1):
-        carried = product_part(coupling_split, True, layout, gathered(current), [], 0, count, None, sources, [columns])[0]
+        carried = product_part(coupling_split, True, layout, gathered(current), [], 0, groups, None, sources, [columns], False)[0]
         current = reduced - lax.ppermute(carried, "chain", onward)
-    return product_part(diag_split, False, layout, gathered(current), [], 0, count, None, sources, [columns])[0]
+    return product_part(diag_split, False, layout, gathered(current), [], 0, groups, None, sources, [columns], False)[0]
 
 
 def body(right_side, diag_inverse, coupling, updates, update_rows, tile_counts):

time: 99.4 us -> 96.8 us (0.974)
  starting transfers between devices: 26.2 us -> 23.7 us
    ppermute x5 -> x6, starting transfers between devices: 10.9 us -> 9.09 us  [send(): return lax.ppermute(value, ('chain', 'tile'), pairs)]
    ppermute x5 -> x6, waiting for transfers between devices: 8.79 us -> 7.8 us  [send(): return lax.ppermute(value, ('chain', 'tile'), pairs)]
    ppermute x19 -> x18, waiting for transfers between devices: 26.4 us -> 27.2 us  [send(): lax.ppermute(value, 'tile', [(t, target(t)) for t in range(tile_size)])]
    ppermute x19 -> x18, starting transfers between devices: 15.2 us -> 14.6 us  [send(): lax.ppermute(value, 'tile', [(t, target(t)) for t in range(tile_size)])]
  transfers between devices with their start and end apart: 24 -> 24, of which waited for: 11 -> 10; matrix products, arithmetic and copies ran while one was open for 0% -> 0% of each run, Pallas kernels for 5% -> 5%
where the time goes in v8:
time: 96.8 us; the launch traced here: 96.4 us
  waiting for transfers between devices  35 us (36%)
  starting transfers between devices  23.7 us (24%)
  blocking collectives  20.6 us (21%)
  Pallas kernels  12.3 us (13%)
  local copies, waits for them, and re-layouts  4.31 us (4%)
    ppermute x18, waiting for transfers between devices, send(): lax.ppermute(value, 'tile', [(t, target(t)) for t in range(tile_size)])  27.2 us
    all_to_all x1, blocking collectives, body(): received = lax.all_to_all(packed, 'tile', 0, 0, tiled=False)  20.6 us
    ppermute x18, starting transfers between devices, send(): lax.ppermute(value, 'tile', [(t, target(t)) for t in range(tile_size)])  14.6 us
    ppermute x6, starting transfers between devices, send(): return lax.ppermute(value, ('chain', 'tile'), pairs)  9.09 us
    ppermute x6, waiting for transfers between devices, send(): return lax.ppermute(value, ('chain', 'tile'), pairs)  7.8 us
    pallas_call x4, Pallas kernels, product_part(): pl.pallas_call(functools.partial(product_kernel, sources, layout, len(blo...  7.2 us
    unnamed x6, local copies, waits for them, and re-layouts  4.31 us
    pallas_call x1, Pallas kernels, body(): pl.pallas_call(functools.partial(pack_kernel, own_rows, cap, tile_rows),...  2.27 us
  transfers between devices with their start and end apart: 24, of which 10 were waited for; matrix products, arithmetic and copies ran while one was open for 0% of the time, Pallas kernels for 5%

profile of v8, /device:TPU:0, one launch (start us, length us, event | category | flops | bytes accessed | tf_op | source)
XLA Modules:
  0.0 96.4 jit_solution(13243302357946505453)
XLA Ops:
  0.0 2.3 %shard_map.64 = f32[16,56,128]{2,1,0:T(8,128)} custom-call(s32[2]{0:T(128)} %counts_hbm.1, s32[1,256]{1,0:T(1,128)} %bitcast.46, f32[192,256]{1,0:T(8,128)} %bitcast.29), custom_call_target="tpu_custom_call" | custom-call | tf_op jit(solution)/shard_map/pallas_call | solution.py:310
  2.3 20.6 %all_to_all.5.received_ref = f32[16,56,128]{2,1,0:T(8,128)S(1)} all-to-all(f32[16,56,128]{2,1,0:T(8,128)} %shard_map.64), channel_id=1, replica_groups=mesh['chain'=2,'tile'=16] {'tile'}, dimensions={0} | all-to-all | bytes 917504 | tf_op jit(solution)/shard_map/all_to_all | solution.py:323
  22.9 0.0 copy-start.2
  22.9 0.9 copy-done.2
  23.9 0.9 shard_map.65
  24.8 0.4 collective-permute-start
  25.2 2.7 %collective-permute-start.3 = (f32[128,256]{1,0:T(8,128)S(1)}, f32[128,256]{1,0:T(8,128)S(1)}, u32[]{:S(2)}, u32[]{:S(2)}) collective-permute-start(f32[128,256]{1,0:T(8,128)S(1)} %get-tuple-element.26), channel_id=1, source_target_pairs={{0,12},{1,13},{2,14},{3,15},{4,0},{5,1},{6,2},{7,3},{8,4},{9,5},{1... | collective-permute-start | bytes 393224 | tf_op jit(solution)/shard_map/ppermute | solution.py:233
  27.9 0.5 collective-permute-start.2
  28.5 0.5 collective-permute-start.1
  29.0 0.0 copy-start
  29.0 3.4 %copy-done = f32[2,256,4096]{2,1,0:T(8,128)S(1)} copy-done((f32[2,256,4096]{2,1,0:T(8,128)S(1)}, f32[2,256,4096]{2,1,0:T(8,128)}, u32[]{:S(2)}) %copy-start) | copy-done | bytes 8388632
  32.4 0.0 copy-start.1
  32.4 1.0 %shard_map.66 = (bf16[4,512,1024]{2,1,0:T(8,128)(2,1)S(1)}, bf16[4,512,1024]{2,1,0:T(8,128)(2,1)S(1)}) custom-call(f32[2,256,4096]{2,1,0:T(8,128)S(1)} %copy-done), custom_call_target="tpu_custom_call" | custom-call | flops 6291456 | bytes 16777216 | tf_op jit(solution)/shard_map/pallas_call | solution.py:139
  33.4 0.0 collective-permute-done
  33.4 0.0 collective-permute-done.3
  33.4 6.9 %collective-permute-done.2 = f32[128,256]{1,0:T(8,128)S(1)} collective-permute-done((f32[128,256]{1,0:T(8,128)S(1)}, f32[128,256]{1,0:T(8,128)S(1)}, u32[]{:S(2)}, u32[]{:S(2)}) %collective-permute-start.2) | collective-permute-done | bytes 131104 | tf_op jit(solution)/shard_map/ppermute | solution.py:233
  40.3 0.0 collective-permute-done.1
  40.3 1.2 %collective-permute-start.5 = (f32[4,128,256]{2,1,0:T(8,128)S(1)}, f32[4,128,256]{2,1,0:T(8,128)S(1)}, u32[]{:S(2)}, u32[]{:S(2)}) collective-permute-start(f32[4,128,256]{2,1,0:T(8,128)S(1)} %pad_maximum_fusion.refs_0_.refs_3_), channel_id=1, source_target_pairs={{0,2},{1,3},{2,0},{3,1},{4,6},{5,7},{6,4},{7,5},{8,10},{9,11},{10,... | collective-permute-start | bytes 1572872 | tf_op jit(solution)/shard_map/ppermute | solution.py:233
  41.5 0.0 collective-permute-start.8
  41.5 1.7 %collective-permute-start.7 = (f32[2,64,256]{2,1,0:T(8,128)S(1)}, f32[2,64,256]{2,1,0:T(8,128)S(1)}, u32[]{:S(2)}, u32[]{:S(2)}) collective-permute-start(f32[2,64,256]{2,1,0:T(8,128)S(1)} %pad_maximum_fusion.4), channel_id=1, source_target_pairs={{0,8},{1,9},{2,10},{3,11},{4,12},{5,13},{6,14},{7,15},{8,0},{9,1},... | collective-permute-start | bytes 393224 | tf_op jit(solution)/shard_map/ppermute | solution.py:233
  43.3 2.0 %collective-permute-start.6 = (f32[2,64,256]{2,1,0:T(8,128)S(1)}, f32[2,64,256]{2,1,0:T(8,128)S(1)}, u32[]{:S(2)}, u32[]{:S(2)}) collective-permute-start(f32[2,64,256]{2,1,0:T(8,128)S(1)} %pad_maximum_fusion.4), channel_id=1, source_target_pairs={{0,4},{1,5},{2,6},{3,7},{4,8},{5,9},{6,10},{7,11},{8,12},{9,13},{1... | collective-permute-start | bytes 393224 | tf_op jit(solution)/shard_map/ppermute | solution.py:233
  45.3 0.0 collective-permute-start.4
  45.3 0.0 copy-done.1
  45.3 1.0 %shard_map.67 = (bf16[4,512,1024]{2,1,0:T(8,128)(2,1)S(1)}, bf16[4,512,1024]{2,1,0:T(8,128)(2,1)S(1)}) custom-call(f32[2,256,4096]{2,1,0:T(8,128)S(1)} %copy-done.1), custom_call_target="tpu_custom_call" | custom-call | flops 6291456 | bytes 16777216 | tf_op jit(solution)/shard_map/pallas_call | solution.py:139
  46.3 0.8 collective-permute-done.8
  47.1 7.9 %collective-permute-done.7 = f32[2,64,256]{2,1,0:T(8,128)S(1)} collective-permute-done((f32[2,64,256]{2,1,0:T(8,128)S(1)}, f32[2,64,256]{2,1,0:T(8,128)S(1)}, u32[]{:S(2)}, u32[]{:S(2)}) %collective-permute-start.7) | collective-permute-done | bytes 131104 | tf_op jit(solution)/shard_map/ppermute | solution.py:233
  55.0 0.0 collective-permute-done.6
  55.1 0.0 collective-permute-done.5.refs_1_.refs_4_
  55.1 0.1 collective-permute-start.9
  55.2 0.5 collective-permute-start.10
  55.7 1.7 %shard_map.68.refs_5_ = f32[192,512]{1,0:T(8,128)S(1)} custom-call(f32[4,128,256]{2,1,0:T(8,128)S(1)} %pad_maximum_fusion.refs_0_.refs_3_, f32[4,128,256]{2,1,0:T(8,128)S(1)} %collective-permute-done.5.refs_1_.refs_4_, f32[4,2,64,256]{3,2,1,0:T(8,128)S(1)} %pad_maximum_fusion.1.refs_2_.refs_5_, bf16[4,512,1024]{2,1,0:T(8,128)(2,1)S(1)} %get-tuple-element.37.refs_3_, ...), custom_call_target="tpu_custom_call" | custom-call | flops 1207959552 | bytes 1048576 | tf_op jit(solution)/shard_map/pallas_call | solution.py:209
  57.3 0.0 collective-permute-done.4.refs_0_.refs_3_
  57.4 0.0 collective-permute-done.9.refs_1_.refs_4_
  57.4 0.5 collective-permute-done.10.refs_2_.refs_5_
  57.8 1.6 %shard_map.69 = (f32[128,256]{1,0:T(8,128)S(1)}, f32[64,256]{1,0:T(8,128)S(1)}) custom-call(f32[4,128,256]{2,1,0:T(8,128)S(1)} %collective-permute-done.4.refs_0_.refs_3_, f32[4,128,256]{2,1,0:T(8,128)S(1)} %collective-permute-done.9.refs_1_.refs_4_, f32[4,2,64,256]{3,2,1,0:T(8,128)S(1)} %collective-permute-done.10.refs_2_.refs_5_, ...), custom_call_target="tpu_custom_call" | custom-call | flops 1207959552 | bytes 1048576 | tf_op jit(solution)/shard_map/pallas_call | solution.py:209
  59.4 1.6 %collective-permute-start.12 = (f32[64,256]{1,0:T(8,128)S(1)}, f32[64,256]{1,0:T(8,128)S(1)}, u32[]{:S(2)}, u32[]{:S(2)}) collective-permute-start(f32[64,256]{1,0:T(8,128)S(1)} %get-tuple-element.39), channel_id=1, source_target_pairs={{0,18},{1,19},{2,16},{3,17},{4,22},{5,23},{6,20},{7,21},{8,26},{9,... | collective-permute-start | bytes 196616 | tf_op jit(solution)/shard_map/ppermute | solution.py:235
  61.0 1.5 %collective-permute-start.11 = (f32[64,256]{1,0:T(8,128)S(1)}, f32[64,256]{1,0:T(8,128)S(1)}, u32[]{:S(2)}, u32[]{:S(2)}) collective-permute-start(f32[64,256]{1,0:T(8,128)S(1)} %get-tuple-element.39), channel_id=1, source_target_pairs={{0,16},{1,17},{2,18},{3,19},{4,20},{5,21},{6,22},{7,23},{8,24},{9,... | collective-permute-start | bytes 196616 | tf_op jit(solution)/shard_map/ppermute | solution.py:235
  62.5 1.3 %collective-permute-start.16 = (f32[128,256]{1,0:T(8,128)S(1)}, f32[128,256]{1,0:T(8,128)S(1)}, u32[]{:S(2)}, u32[]{:S(2)}) collective-permute-start(f32[128,256]{1,0:T(8,128)S(1)} %get-tuple-element.40), channel_id=1, source_target_pairs={{0,28},{1,29},{2,30},{3,31},{4,16},{5,17},{6,18},{7,19},{8,20},{9,... | collective-permute-start | bytes 393224 | tf_op jit(solution)/shard_map/ppermute | solution.py:235
  63.8 1.5 %collective-permute-start.15 = (f32[128,256]{1,0:T(8,128)S(1)}, f32[128,256]{1,0:T(8,128)S(1)}, u32[]{:S(2)}, u32[]{:S(2)}) collective-permute-start(f32[128,256]{1,0:T(8,128)S(1)} %get-tuple-element.40), channel_id=1, source_target_pairs={{0,24},{1,25},{2,26},{3,27},{4,28},{5,29},{6,30},{7,31},{8,16},{9,... | collective-permute-start | bytes 393224 | tf_op jit(solution)/shard_map/ppermute | solution.py:235
  65.3 1.3 %collective-permute-start.14 = (f32[128,256]{1,0:T(8,128)S(1)}, f32[128,256]{1,0:T(8,128)S(1)}, u32[]{:S(2)}, u32[]{:S(2)}) collective-permute-start(f32[128,256]{1,0:T(8,128)S(1)} %get-tuple-element.40), channel_id=1, source_target_pairs={{0,20},{1,21},{2,22},{3,23},{4,24},{5,25},{6,26},{7,27},{8,28},{9,... | collective-permute-start | bytes 393224 | tf_op jit(solution)/shard_map/ppermute | solution.py:235
  66.6 0.0 collective-permute-done.12
  66.7 1.9 %collective-permute-start.13 = (f32[128,256]{1,0:T(8,128)S(1)}, f32[128,256]{1,0:T(8,128)S(1)}, u32[]{:S(2)}, u32[]{:S(2)}) collective-permute-start(f32[128,256]{1,0:T(8,128)S(1)} %get-tuple-element.40), channel_id=1, source_target_pairs={{0,16},{1,17},{2,18},{3,19},{4,20},{5,21},{6,22},{7,23},{8,24},{9,... | collective-permute-start | bytes 393224 | tf_op jit(solution)/shard_map/ppermute | solution.py:235
  68.6 0.0 collective-permute-done.11
  68.6 0.0 collective-permute-done.16
  68.6 1.9 %collective-permute-done.15 = f32[128,256]{1,0:T(8,128)S(1)} collective-permute-done((f32[128,256]{1,0:T(8,128)S(1)}, f32[128,256]{1,0:T(8,128)S(1)}, u32[]{:S(2)}, u32[]{:S(2)}) %collective-permute-start.15) | collective-permute-done | bytes 131104 | tf_op jit(solution)/shard_map/ppermute | solution.py:235
  70.5 2.3 %collective-permute-done.14 = f32[128,256]{1,0:T(8,128)S(1)} collective-permute-done((f32[128,256]{1,0:T(8,128)S(1)}, f32[128,256]{1,0:T(8,128)S(1)}, u32[]{:S(2)}, u32[]{:S(2)}) %collective-permute-start.14) | collective-permute-done | bytes 131104 | tf_op jit(solution)/shard_map/ppermute | solution.py:235
  72.8 3.6 %collective-permute-done.13 = f32[128,256]{1,0:T(8,128)S(1)} collective-permute-done((f32[128,256]{1,0:T(8,128)S(1)}, f32[128,256]{1,0:T(8,128)S(1)}, u32[]{:S(2)}, u32[]{:S(2)}) %collective-permute-start.13) | collective-permute-done | bytes 131104 | tf_op jit(solution)/shard_map/ppermute | solution.py:235
  76.5 1.0 %collective-permute-start.18 = (f32[4,128,256]{2,1,0:T(8,128)S(1)}, f32[4,128,256]{2,1,0:T(8,128)S(1)}, u32[]{:S(2)}, u32[]{:S(2)}) collective-permute-start(f32[4,128,256]{2,1,0:T(8,128)S(1)} %pad_maximum_fusion.2.refs_0_), channel_id=1, source_target_pairs={{0,2},{1,3},{2,0},{3,1},{4,6},{5,7},{6,4},{7,5},{8,10},{9,11},{10,... | collective-permute-start | bytes 1572872 | tf_op jit(solution)/shard_map/ppermute | solution.py:233
  77.4 2.7 %collective-permute-start.22 = (f32[2,64,256]{2,1,0:T(8,128)S(1)}, f32[2,64,256]{2,1,0:T(8,128)S(1)}, u32[]{:S(2)}, u32[]{:S(2)}) collective-permute-start(f32[2,64,256]{2,1,0:T(8,128)S(1)} %pad_maximum_fusion.5), channel_id=1, source_target_pairs={{0,12},{1,13},{2,14},{3,15},{4,0},{5,1},{6,2},{7,3},{8,4},{9,5},{1... | collective-permute-start | bytes 393224 | tf_op jit(solution)/shard_map/ppermute | solution.py:233
  80.1 0.0 collective-permute-start.21
  80.1 0.6 collective-permute-start.20
  80.7 0.0 collective-permute-start.17
  80.7 3.3 %collective-permute-done.22 = f32[2,64,256]{2,1,0:T(8,128)S(1)} collective-permute-done((f32[2,64,256]{2,1,0:T(8,128)S(1)}, f32[2,64,256]{2,1,0:T(8,128)S(1)}, u32[]{:S(2)}, u32[]{:S(2)}) %collective-permute-start.22) | collective-permute-done | bytes 131104 | tf_op jit(solution)/shard_map/ppermute | solution.py:233
  84.0 7.3 %collective-permute-done.21 = f32[2,64,256]{2,1,0:T(8,128)S(1)} collective-permute-done((f32[2,64,256]{2,1,0:T(8,128)S(1)}, f32[2,64,256]{2,1,0:T(8,128)S(1)}, u32[]{:S(2)}, u32[]{:S(2)}) %collective-permute-start.21) | collective-permute-done | bytes 131104 | tf_op jit(solution)/shard_map/ppermute | solution.py:233
  91.3 0.0 collective-permute-done.20
  91.4 0.1 collective-permute-start.23
  91.5 0.0 collective-permute-done.18.refs_1_
  91.5 0.5 collective-permute-start.19
  92.0 1.7 %shard_map.70.refs_8_ = f32[192,512]{1,0:T(8,128)S(1)} custom-call(f32[4,128,256]{2,1,0:T(8,128)S(1)} %pad_maximum_fusion.2.refs_0_, f32[4,128,256]{2,1,0:T(8,128)S(1)} %collective-permute-done.18.refs_1_, f32[4,2,64,256]{3,2,1,0:T(8,128)S(1)} %pad_maximum_fusion.3.refs_2_, f32[4,128,256]{2,1,0:T(8,128)S(1)} %pad_maximum_fusion.refs_0_.refs_3_, ...), custom_call_target="tpu_custom_call" | custom-call | flops 1207959552 | bytes 1048576 | tf_op jit(solution)/shard_map/pallas_call | solution.py:209
  93.6 0.0 collective-permute-done.17.refs_0_
  93.6 0.0 collective-permute-done.23.refs_2_
  93.6 0.5 collective-permute-done.19.refs_1_
  94.1 2.3 %shard_map.71 = f32[192,256]{1,0:T(8,128)} custom-call(f32[4,128,256]{2,1,0:T(8,128)S(1)} %collective-permute-done.17.refs_0_, f32[4,128,256]{2,1,0:T(8,128)S(1)} %collective-permute-done.19.refs_1_, f32[4,2,64,256]{3,2,1,0:T(8,128)S(1)} %collective-permute-done.23.refs_2_, f32[4,128,256]{2,1,0:T(8,128)S(1)} %collective-permute-done.4.refs_0_.refs_3_, ...), custom_call_target="tpu_custom_call" | custom-call | flops 1207959552 | bytes 1048576 | tf_op jit(solution)/shard_map/pallas_call | solution.py:209
  (6 shorter events, 0.2 us)
Async XLA Ops:
  22.9 0.9 copy-start.2
  24.8 8.6 %collective-permute-start = (f32[64,256]{1,0:T(8,128)S(1)}, f32[64,256]{1,0:T(8,128)S(1)}, u32[]{:S(2)}, u32[]{:S(2)}) collective-permute-start(f32[64,256]{1,0:T(8,128)S(1)} %get-tuple-element.25), channel_id=1, source_target_pairs={{0,2},{1,3},{2,0},{3,1},{4,6},{5,7},{6,4},{7,5},{8,10},{9,11},{10,... | collective-permute-start | bytes 196616 | tf_op jit(solution)/shard_map/ppermute | solution.py:233
  25.2 8.2 %collective-permute-start.3 = (f32[128,256]{1,0:T(8,128)S(1)}, f32[128,256]{1,0:T(8,128)S(1)}, u32[]{:S(2)}, u32[]{:S(2)}) collective-permute-start(f32[128,256]{1,0:T(8,128)S(1)} %get-tuple-element.26), channel_id=1, source_target_pairs={{0,12},{1,13},{2,14},{3,15},{4,0},{5,1},{6,2},{7,3},{8,4},{9,5},{1... | collective-permute-start | bytes 393224 | tf_op jit(solution)/shard_map/ppermute | solution.py:233
  27.9 12.4 %collective-permute-start.2 = (f32[128,256]{1,0:T(8,128)S(1)}, f32[128,256]{1,0:T(8,128)S(1)}, u32[]{:S(2)}, u32[]{:S(2)}) collective-permute-start(f32[128,256]{1,0:T(8,128)S(1)} %get-tuple-element.26), channel_id=1, source_target_pairs={{0,8},{1,9},{2,10},{3,11},{4,12},{5,13},{6,14},{7,15},{8,0},{9,1},... | collective-permute-start | bytes 393224 | tf_op jit(solution)/shard_map/ppermute | solution.py:233
  28.5 11.8 %collective-permute-start.1 = (f32[128,256]{1,0:T(8,128)S(1)}, f32[128,256]{1,0:T(8,128)S(1)}, u32[]{:S(2)}, u32[]{:S(2)}) collective-permute-start(f32[128,256]{1,0:T(8,128)S(1)} %get-tuple-element.26), channel_id=1, source_target_pairs={{0,4},{1,5},{2,6},{3,7},{4,8},{5,9},{6,10},{7,11},{8,12},{9,13},{1... | collective-permute-start | bytes 393224 | tf_op jit(solution)/shard_map/ppermute | solution.py:233
  29.0 3.4 %copy-start = (f32[2,256,4096]{2,1,0:T(8,128)S(1)}, f32[2,256,4096]{2,1,0:T(8,128)}, u32[]{:S(2)}) copy-start(f32[2,256,4096]{2,1,0:T(8,128)} %matrix_ref) | copy-start | bytes 25165828
  32.4 12.9 %copy-start.1 = (f32[2,256,4096]{2,1,0:T(8,128)S(1)}, f32[2,256,4096]{2,1,0:T(8,128)}, u32[]{:S(2)}) copy-start(f32[2,256,4096]{2,1,0:T(8,128)} %matrix_ref.1) | copy-start | bytes 25165828
  40.3 14.8 %collective-permute-start.5 = (f32[4,128,256]{2,1,0:T(8,128)S(1)}, f32[4,128,256]{2,1,0:T(8,128)S(1)}, u32[]{:S(2)}, u32[]{:S(2)}) collective-permute-start(f32[4,128,256]{2,1,0:T(8,128)S(1)} %pad_maximum_fusion.refs_0_.refs_3_), channel_id=1, source_target_pairs={{0,2},{1,3},{2,0},{3,1},{4,6},{5,7},{6,4},{7,5},{8,10},{9,11},{10,... | collective-permute-start | bytes 1572872 | tf_op jit(solution)/shard_map/ppermute | solution.py:233
  41.5 5.6 %collective-permute-start.8 = (f32[2,64,256]{2,1,0:T(8,128)S(1)}, f32[2,64,256]{2,1,0:T(8,128)S(1)}, u32[]{:S(2)}, u32[]{:S(2)}) collective-permute-start(f32[2,64,256]{2,1,0:T(8,128)S(1)} %pad_maximum_fusion.4), channel_id=1, source_target_pairs={{0,12},{1,13},{2,14},{3,15},{4,0},{5,1},{6,2},{7,3},{8,4},{9,5},{1... | collective-permute-start | bytes 393224 | tf_op jit(solution)/shard_map/ppermute | solution.py:233
  41.5 13.5 %collective-permute-start.7 = (f32[2,64,256]{2,1,0:T(8,128)S(1)}, f32[2,64,256]{2,1,0:T(8,128)S(1)}, u32[]{:S(2)}, u32[]{:S(2)}) collective-permute-start(f32[2,64,256]{2,1,0:T(8,128)S(1)} %pad_maximum_fusion.4), channel_id=1, source_target_pairs={{0,8},{1,9},{2,10},{3,11},{4,12},{5,13},{6,14},{7,15},{8,0},{9,1},... | collective-permute-start | bytes 393224 | tf_op jit(solution)/shard_map/ppermute | solution.py:233
  43.3 11.8 %collective-permute-start.6 = (f32[2,64,256]{2,1,0:T(8,128)S(1)}, f32[2,64,256]{2,1,0:T(8,128)S(1)}, u32[]{:S(2)}, u32[]{:S(2)}) collective-permute-start(f32[2,64,256]{2,1,0:T(8,128)S(1)} %pad_maximum_fusion.4), channel_id=1, source_target_pairs={{0,4},{1,5},{2,6},{3,7},{4,8},{5,9},{6,10},{7,11},{8,12},{9,13},{1... | collective-permute-start | bytes 393224 | tf_op jit(solution)/shard_map/ppermute | solution.py:233
  45.3 12.0 %collective-permute-start.4 = (f32[4,128,256]{2,1,0:T(8,128)S(1)}, f32[4,128,256]{2,1,0:T(8,128)S(1)}, u32[]{:S(2)}, u32[]{:S(2)}) collective-permute-start(f32[4,128,256]{2,1,0:T(8,128)S(1)} %pad_maximum_fusion.refs_0_.refs_3_), channel_id=1, source_target_pairs={{0,1},{1,0},{2,3},{3,2},{4,5},{5,4},{6,7},{7,6},{8,9},{9,8},{10,11... | collective-permute-start | bytes 1572872 | tf_op jit(solution)/shard_map/ppermute | solution.py:233
  55.1 2.3 %collective-permute-start.9 = (f32[4,128,256]{2,1,0:T(8,128)S(1)}, f32[4,128,256]{2,1,0:T(8,128)S(1)}, u32[]{:S(2)}, u32[]{:S(2)}) collective-permute-start(f32[4,128,256]{2,1,0:T(8,128)S(1)} %collective-permute-done.5.refs_1_.refs_4_), channel_id=1, source_target_pairs={{0,1},{1,0},{2,3},{3,2},{4,5},{5,4},{6,7},{7,6},{8,9},{9,8},{10,11... | collective-permute-start | bytes 1572872 | tf_op jit(solution)/shard_map/ppermute | solution.py:233
  55.2 2.6 %collective-permute-start.10 = (f32[4,2,64,256]{3,2,1,0:T(8,128)S(1)}, f32[4,2,64,256]{3,2,1,0:T(8,128)S(1)}, u32[]{:S(2)}, u32[]{:S(2)}) collective-permute-start(f32[4,2,64,256]{3,2,1,0:T(8,128)S(1)} %pad_maximum_fusion.1.refs_2_.refs_5_), channel_id=1, source_target_pairs={{0,1},{1,0},{2,3},{3,2},{4,5},{5,4},{6,7},{7,6},{8,9},{9,8},{10,11... | collective-permute-start | bytes 1572872 | tf_op jit(solution)/shard_map/ppermute | solution.py:233
  59.4 7.2 %collective-permute-start.12 = (f32[64,256]{1,0:T(8,128)S(1)}, f32[64,256]{1,0:T(8,128)S(1)}, u32[]{:S(2)}, u32[]{:S(2)}) collective-permute-start(f32[64,256]{1,0:T(8,128)S(1)} %get-tuple-element.39), channel_id=1, source_target_pairs={{0,18},{1,19},{2,16},{3,17},{4,22},{5,23},{6,20},{7,21},{8,26},{9,... | collective-permute-start | bytes 196616 | tf_op jit(solution)/shard_map/ppermute | solution.py:235
  61.0 7.6 %collective-permute-start.11 = (f32[64,256]{1,0:T(8,128)S(1)}, f32[64,256]{1,0:T(8,128)S(1)}, u32[]{:S(2)}, u32[]{:S(2)}) collective-permute-start(f32[64,256]{1,0:T(8,128)S(1)} %get-tuple-element.39), channel_id=1, source_target_pairs={{0,16},{1,17},{2,18},{3,19},{4,20},{5,21},{6,22},{7,23},{8,24},{9,... | collective-permute-start | bytes 196616 | tf_op jit(solution)/shard_map/ppermute | solution.py:235
  62.5 6.1 %collective-permute-start.16 = (f32[128,256]{1,0:T(8,128)S(1)}, f32[128,256]{1,0:T(8,128)S(1)}, u32[]{:S(2)}, u32[]{:S(2)}) collective-permute-start(f32[128,256]{1,0:T(8,128)S(1)} %get-tuple-element.40), channel_id=1, source_target_pairs={{0,28},{1,29},{2,30},{3,31},{4,16},{5,17},{6,18},{7,19},{8,20},{9,... | collective-permute-start | bytes 393224 | tf_op jit(solution)/shard_map/ppermute | solution.py:235
  63.8 6.7 %collective-permute-start.15 = (f32[128,256]{1,0:T(8,128)S(1)}, f32[128,256]{1,0:T(8,128)S(1)}, u32[]{:S(2)}, u32[]{:S(2)}) collective-permute-start(f32[128,256]{1,0:T(8,128)S(1)} %get-tuple-element.40), channel_id=1, source_target_pairs={{0,24},{1,25},{2,26},{3,27},{4,28},{5,29},{6,30},{7,31},{8,16},{9,... | collective-permute-start | bytes 393224 | tf_op jit(solution)/shard_map/ppermute | solution.py:235
  65.3 7.5 %collective-permute-start.14 = (f32[128,256]{1,0:T(8,128)S(1)}, f32[128,256]{1,0:T(8,128)S(1)}, u32[]{:S(2)}, u32[]{:S(2)}) collective-permute-start(f32[128,256]{1,0:T(8,128)S(1)} %get-tuple-element.40), channel_id=1, source_target_pairs={{0,20},{1,21},{2,22},{3,23},{4,24},{5,25},{6,26},{7,27},{8,28},{9,... | collective-permute-start | bytes 393224 | tf_op jit(solution)/shard_map/ppermute | solution.py:235
  66.7 9.8 %collective-permute-start.13 = (f32[128,256]{1,0:T(8,128)S(1)}, f32[128,256]{1,0:T(8,128)S(1)}, u32[]{:S(2)}, u32[]{:S(2)}) collective-permute-start(f32[128,256]{1,0:T(8,128)S(1)} %get-tuple-element.40), channel_id=1, source_target_pairs={{0,16},{1,17},{2,18},{3,19},{4,20},{5,21},{6,22},{7,23},{8,24},{9,... | collective-permute-start | bytes 393224 | tf_op jit(solution)/shard_map/ppermute | solution.py:235
  76.5 15.0 %collective-permute-start.18 = (f32[4,128,256]{2,1,0:T(8,128)S(1)}, f32[4,128,256]{2,1,0:T(8,128)S(1)}, u32[]{:S(2)}, u32[]{:S(2)}) collective-permute-start(f32[4,128,256]{2,1,0:T(8,128)S(1)} %pad_maximum_fusion.2.refs_0_), channel_id=1, source_target_pairs={{0,2},{1,3},{2,0},{3,1},{4,6},{5,7},{6,4},{7,5},{8,10},{9,11},{10,... | collective-permute-start | bytes 1572872 | tf_op jit(solution)/shard_map/ppermute | solution.py:233
  77.4 6.6 %collective-permute-start.22 = (f32[2,64,256]{2,1,0:T(8,128)S(1)}, f32[2,64,256]{2,1,0:T(8,128)S(1)}, u32[]{:S(2)}, u32[]{:S(2)}) collective-permute-start(f32[2,64,256]{2,1,0:T(8,128)S(1)} %pad_maximum_fusion.5), channel_id=1, source_target_pairs={{0,12},{1,13},{2,14},{3,15},{4,0},{5,1},{6,2},{7,3},{8,4},{9,5},{1... | collective-permute-start | bytes 393224 | tf_op jit(solution)/shard_map/ppermute | solution.py:233
  80.1 11.2 %collective-permute-start.21 = (f32[2,64,256]{2,1,0:T(8,128)S(1)}, f32[2,64,256]{2,1,0:T(8,128)S(1)}, u32[]{:S(2)}, u32[]{:S(2)}) collective-permute-start(f32[2,64,256]{2,1,0:T(8,128)S(1)} %pad_maximum_fusion.5), channel_id=1, source_target_pairs={{0,8},{1,9},{2,10},{3,11},{4,12},{5,13},{6,14},{7,15},{8,0},{9,1},... | collective-permute-start | bytes 393224 | tf_op jit(solution)/shard_map/ppermute | solution.py:233
  80.1 11.2 %collective-permute-start.20 = (f32[2,64,256]{2,1,0:T(8,128)S(1)}, f32[2,64,256]{2,1,0:T(8,128)S(1)}, u32[]{:S(2)}, u32[]{:S(2)}) collective-permute-start(f32[2,64,256]{2,1,0:T(8,128)S(1)} %pad_maximum_fusion.5), channel_id=1, source_target_pairs={{0,4},{1,5},{2,6},{3,7},{4,8},{5,9},{6,10},{7,11},{8,12},{9,13},{1... | collective-permute-start | bytes 393224 | tf_op jit(solution)/shard_map/ppermute | solution.py:233
  80.7 12.9 %collective-permute-start.17 = (f32[4,128,256]{2,1,0:T(8,128)S(1)}, f32[4,128,256]{2,1,0:T(8,128)S(1)}, u32[]{:S(2)}, u32[]{:S(2)}) collective-permute-start(f32[4,128,256]{2,1,0:T(8,128)S(1)} %pad_maximum_fusion.2.refs_0_), channel_id=1, source_target_pairs={{0,1},{1,0},{2,3},{3,2},{4,5},{5,4},{6,7},{7,6},{8,9},{9,8},{10,11... | collective-permute-start | bytes 1572872 | tf_op jit(solution)/shard_map/ppermute | solution.py:233
  91.4 2.3 %collective-permute-start.23 = (f32[4,2,64,256]{3,2,1,0:T(8,128)S(1)}, f32[4,2,64,256]{3,2,1,0:T(8,128)S(1)}, u32[]{:S(2)}, u32[]{:S(2)}) collective-permute-start(f32[4,2,64,256]{3,2,1,0:T(8,128)S(1)} %pad_maximum_fusion.3.refs_2_), channel_id=1, source_target_pairs={{0,1},{1,0},{2,3},{3,2},{4,5},{5,4},{6,7},{7,6},{8,9},{9,8},{10,11... | collective-permute-start | bytes 1572872 | tf_op jit(solution)/shard_map/ppermute | solution.py:233
  91.5 2.6 %collective-permute-start.19 = (f32[4,128,256]{2,1,0:T(8,128)S(1)}, f32[4,128,256]{2,1,0:T(8,128)S(1)}, u32[]{:S(2)}, u32[]{:S(2)}) collective-permute-start(f32[4,128,256]{2,1,0:T(8,128)S(1)} %collective-permute-done.18.refs_1_), channel_id=1, source_target_pairs={{0,1},{1,0},{2,3},{3,2},{4,5},{5,4},{6,7},{7,6},{8,9},{9,8},{10,11... | collective-permute-start | bytes 1572872 | tf_op jit(solution)/shard_map/ppermute | solution.py:233

commit v9 on v8

--- a/solution.py
+++ b/solution.py
@@ -16,13 +16,6 @@
 def halves_of(value):
     high = value.astype(bf16)
     return high, (value - high.astype(f32)).astype(bf16)
-
-
-def thirds_of(value):
-    high = value.astype(bf16)
-    rest = value - high.astype(f32)
-    middle = rest.astype(bf16)
-    return high, middle, (rest - middle.astype(f32)).astype(bf16)
 
 
 def kernel_params(size):
@@ -61,7 +54,7 @@
         tail = jnp.where(lax.broadcasted_iota(jnp.int32, (width - columns, entries), 0) == 0, local_row, 0.0)
         data = jnp.concatenate([data, tail], axis=0)
     packed = jnp.zeros((slots, data.shape[0]), f32)
-    for piece in thirds_of(data):
+    for piece in halves_of(data):
         packed += lax.dot_general(choose, piece, lanes_contract, preferred_element_type=f32)
     packed = packed.reshape(owners, cap, data.shape[0])
     if not folded:
@@ -96,7 +89,7 @@
         totals = []
         for value in sets:
             total = jnp.zeros((own_rows, value.shape[1]), f32)
-            for piece in thirds_of(value):
+            for piece in halves_of(value):
                 total += jnp.dot(place, piece, preferred_element_type=f32)
             totals.append(total.T)
         total = jnp.concatenate(totals, axis=0)
@@ -105,7 +98,7 @@
         local_row = received[:, columns:columns + 1].astype(jnp.int32)
         place = jnp.where(lax.broadcasted_iota(jnp.int32, (slots, own_rows), 1) == local_row, 1.0, 0.0).astype(bf16)
         total = jnp.zeros((columns, own_rows), f32)
-        for piece in thirds_of(received[:, :columns].T):
+        for piece in halves_of(received[:, :columns].T):
             total += jnp.dot(piece, place, preferred_element_type=f32)
     move.wait()
     start = 0
@@ -164,11 +157,19 @@
             which, place = group(step, held)
             value = refs[which][place]
             if sets == 2:
-                value = refs[inputs + which][place] - value
+                own = refs[inputs + which][place]
+                value = jnp.where(lax.axis_index("chain") == 0, own, own - value)
             pieces.append(value)
         return jnp.concatenate(pieces, axis=0)
 
-    @pl.when(jnp.logical_not(onward) | (lax.axis_index("chain") < lax.axis_size("chain") - 1))
+    active = jnp.logical_not(onward) | (lax.axis_index("chain") < lax.axis_size("chain") - 1)
+
+    @pl.when(jnp.logical_not(active))
+    def _():
+        for out_ref in out_refs:
+            out_ref[...] = jnp.zeros_like(out_ref)
+
+    @pl.when(active)
     def _():
         for step in range(begin, end):
             group = step
@@ -231,12 +232,14 @@
     def send(value, hop, target):
         if not hop:
             return lax.ppermute(value, "tile", [(t, target(t)) for t in range(tile_size)])
-        pairs = [(c * tile_size + t, (c + 1) * tile_size + target(t)) for c in range(chain_size - 1) for t in range(tile_size)]
+        pairs = [(c * tile_size + t, (c + 1) % chain_size * tile_size + target(t)) for c in range(chain_size) for t in range(tile_size)]
         return lax.ppermute(value, ("chain", "tile"), pairs)
 
     def first_stage(first, second, hop):
-        pair = [second if across == 0 and not hop else send(second, hop, lambda t: t ^ (2 * across)) for across in range(2)]
         line = [first if by == 0 and not hop else send(first, hop, lambda t: (t + 4 * by) % tile_size) for by in range(layers)]
+        if hop:
+            second, line[-1] = lax.optimization_barrier((send(second, True, lambda t: t), line[-1]))
+        pair = [second, send(second, False, lambda t: t ^ 2)]
         return jnp.stack(pair), jnp.stack(line)
 
     def second_stage(pair, line):

time: 96.8 us -> 98.7 us (1.020)
  waiting for transfers between devices: 35 us -> 41.1 us
  starting transfers between devices: 23.7 us -> 19.9 us
    ppermute x6 -> x5, starting transfers between devices: 9.09 us -> 5.25 us  [send(): return lax.ppermute(value, ('chain', 'tile'), pairs)]
    ppermute x6 -> x5, waiting for transfers between devices: 7.8 us -> 11.1 us  [send(): return lax.ppermute(value, ('chain', 'tile'), pairs)]
    ppermute x18 -> x19, waiting for transfers between devices: 27.2 us -> 30 us  [send(): lax.ppermute(value, 'tile', [(t, target(t)) for t in range(tile_size)])]
    ppermute x18 -> x19, starting transfers between devices: 14.6 us -> 14.7 us  [send(): lax.ppermute(value, 'tile', [(t, target(t)) for t in range(tile_size)])]
  transfers between devices with their start and end apart: 24 -> 24, of which waited for: 10 -> 9; matrix products, arithmetic and copies ran while one was open for 0% -> 0% of each run, Pallas kernels for 5% -> 5%
where the time goes in v9:
time: 98.7 us; the launch traced here: 98.4 us
  waiting for transfers between devices  41.1 us (42%)
  blocking collectives  20.6 us (21%)
  starting transfers between devices  19.9 us (20%)
  Pallas kernels  12.1 us (12%)
  local copies, waits for them, and re-layouts  4.31 us (4%)
    ppermute x19, waiting for transfers between devices, send(): lax.ppermute(value, 'tile', [(t, target(t)) for t in range(tile_size)])  30 us
    all_to_all x1, blocking collectives, body(): received = lax.all_to_all(packed, 'tile', 0, 0, tiled=False)  20.6 us
    ppermute x19, starting transfers between devices, send(): lax.ppermute(value, 'tile', [(t, target(t)) for t in range(tile_size)])  14.7 us
    ppermute x5, waiting for transfers between devices, send(): return lax.ppermute(value, ('chain', 'tile'), pairs)  11.1 us
    pallas_call x4, Pallas kernels, product_part(): pl.pallas_call(functools.partial(product_kernel, sources, layout, len(blo...  7.19 us
    ppermute x5, starting transfers between devices, send(): return lax.ppermute(value, ('chain', 'tile'), pairs)  5.25 us
    unnamed x6, local copies, waits for them, and re-layouts  4.31 us
    pallas_call x1, Pallas kernels, body(): pl.pallas_call(functools.partial(pack_kernel, own_rows, cap, tile_rows),...  2.19 us
  transfers between devices with their start and end apart: 24, of which 9 were waited for; matrix products, arithmetic and copies ran while one was open for 0% of the time, Pallas kernels for 5%

profile of v9, /device:TPU:0, one launch (start us, length us, event | category | flops | bytes accessed | tf_op | source)
XLA Modules:
  0.0 98.4 jit_solution(14882024518602089232)
XLA Ops:
  0.0 2.2 %shard_map.64 = f32[16,56,128]{2,1,0:T(8,128)} custom-call(s32[2]{0:T(128)} %counts_hbm.1, s32[1,256]{1,0:T(1,128)} %bitcast.46, f32[192,256]{1,0:T(8,128)} %bitcast.29), custom_call_target="tpu_custom_call" | custom-call | tf_op jit(solution)/shard_map/pallas_call | solution.py:313
  2.2 20.6 %all_to_all.5.received_ref = f32[16,56,128]{2,1,0:T(8,128)S(1)} all-to-all(f32[16,56,128]{2,1,0:T(8,128)} %shard_map.64), channel_id=1, replica_groups=mesh['chain'=2,'tile'=16] {'tile'}, dimensions={0} | all-to-all | bytes 917504 | tf_op jit(solution)/shard_map/all_to_all | solution.py:326
  22.9 0.0 copy-start.2
  22.9 0.9 copy-done.2
  23.8 0.8 shard_map.65
  24.5 0.4 collective-permute-start
  25.0 2.7 %collective-permute-start.3 = (f32[128,256]{1,0:T(8,128)S(1)}, f32[128,256]{1,0:T(8,128)S(1)}, u32[]{:S(2)}, u32[]{:S(2)}) collective-permute-start(f32[128,256]{1,0:T(8,128)S(1)} %get-tuple-element.28), channel_id=1, source_target_pairs={{0,12},{1,13},{2,14},{3,15},{4,0},{5,1},{6,2},{7,3},{8,4},{9,5},{1... | collective-permute-start | bytes 393224 | tf_op jit(solution)/shard_map/ppermute | solution.py:234
  27.7 0.5 collective-permute-start.2
  28.2 0.5 collective-permute-start.1
  28.8 0.0 copy-start
  28.8 3.4 %copy-done = f32[2,256,4096]{2,1,0:T(8,128)S(1)} copy-done((f32[2,256,4096]{2,1,0:T(8,128)S(1)}, f32[2,256,4096]{2,1,0:T(8,128)}, u32[]{:S(2)}) %copy-start) | copy-done | bytes 8388632
  32.2 0.0 copy-start.1
  32.2 1.0 shard_map.66
  33.1 0.0 collective-permute-done
  33.2 0.0 collective-permute-done.3
  33.2 6.9 %collective-permute-done.2 = f32[128,256]{1,0:T(8,128)S(1)} collective-permute-done((f32[128,256]{1,0:T(8,128)S(1)}, f32[128,256]{1,0:T(8,128)S(1)}, u32[]{:S(2)}, u32[]{:S(2)}) %collective-permute-start.2) | collective-permute-done | bytes 131104 | tf_op jit(solution)/shard_map/ppermute | solution.py:234
  40.1 0.0 collective-permute-done.1
  40.1 1.2 %collective-permute-start.5 = (f32[4,128,256]{2,1,0:T(8,128)S(1)}, f32[4,128,256]{2,1,0:T(8,128)S(1)}, u32[]{:S(2)}, u32[]{:S(2)}) collective-permute-start(f32[4,128,256]{2,1,0:T(8,128)S(1)} %pad_maximum_fusion.refs_0_.refs_3_), channel_id=1, source_target_pairs={{0,2},{1,3},{2,0},{3,1},{4,6},{5,7},{6,4},{7,5},{8,10},{9,11},{10,... | collective-permute-start | bytes 1572872 | tf_op jit(solution)/shard_map/ppermute | solution.py:234
  41.3 0.0 collective-permute-start.8
  41.3 1.8 %collective-permute-start.7 = (f32[2,64,256]{2,1,0:T(8,128)S(1)}, f32[2,64,256]{2,1,0:T(8,128)S(1)}, u32[]{:S(2)}, u32[]{:S(2)}) collective-permute-start(f32[2,64,256]{2,1,0:T(8,128)S(1)} %pad_maximum_fusion.4), channel_id=1, source_target_pairs={{0,8},{1,9},{2,10},{3,11},{4,12},{5,13},{6,14},{7,15},{8,0},{9,1},... | collective-permute-start | bytes 393224 | tf_op jit(solution)/shard_map/ppermute | solution.py:234
  43.1 2.0 %collective-permute-start.6 = (f32[2,64,256]{2,1,0:T(8,128)S(1)}, f32[2,64,256]{2,1,0:T(8,128)S(1)}, u32[]{:S(2)}, u32[]{:S(2)}) collective-permute-start(f32[2,64,256]{2,1,0:T(8,128)S(1)} %pad_maximum_fusion.4), channel_id=1, source_target_pairs={{0,4},{1,5},{2,6},{3,7},{4,8},{5,9},{6,10},{7,11},{8,12},{9,13},{1... | collective-permute-start | bytes 393224 | tf_op jit(solution)/shard_map/ppermute | solution.py:234
  45.1 0.0 collective-permute-start.4
  45.1 0.0 copy-done.1
  45.1 1.0 shard_map.67
  46.1 0.8 collective-permute-done.8
  46.9 8.0 %collective-permute-done.7 = f32[2,64,256]{2,1,0:T(8,128)S(1)} collective-permute-done((f32[2,64,256]{2,1,0:T(8,128)S(1)}, f32[2,64,256]{2,1,0:T(8,128)S(1)}, u32[]{:S(2)}, u32[]{:S(2)}) %collective-permute-start.7) | collective-permute-done | bytes 131104 | tf_op jit(solution)/shard_map/ppermute | solution.py:234
  54.8 0.0 collective-permute-done.6
  54.9 0.0 collective-permute-done.5.refs_1_.refs_4_
  54.9 0.1 collective-permute-start.9
  55.0 0.5 collective-permute-start.10
  55.5 1.7 %shard_map.68.refs_5_ = f32[192,512]{1,0:T(8,128)S(1)} custom-call(f32[4,128,256]{2,1,0:T(8,128)S(1)} %pad_maximum_fusion.refs_0_.refs_3_, f32[4,128,256]{2,1,0:T(8,128)S(1)} %collective-permute-done.5.refs_1_.refs_4_, f32[4,2,64,256]{3,2,1,0:T(8,128)S(1)} %pad_maximum_fusion.1.refs_2_.refs_5_, bf16[4,512,1024]{2,1,0:T(8,128)(2,1)S(1)} %get-tuple-element.39.refs_3_, ...), custom_call_target="tpu_custom_call" | custom-call | flops 1207959552 | bytes 1048576 | tf_op jit(solution)/shard_map/pallas_call | solution.py:210
  57.1 0.0 collective-permute-done.4.refs_0_.refs_3_
  57.1 0.0 collective-permute-done.9.refs_1_.refs_4_
  57.1 0.5 collective-permute-done.10.refs_2_.refs_5_
  57.6 1.6 %shard_map.69 = (f32[128,256]{1,0:T(8,128)S(1)}, f32[64,256]{1,0:T(8,128)S(1)}) custom-call(f32[4,128,256]{2,1,0:T(8,128)S(1)} %collective-permute-done.4.refs_0_.refs_3_, f32[4,128,256]{2,1,0:T(8,128)S(1)} %collective-permute-done.9.refs_1_.refs_4_, f32[4,2,64,256]{3,2,1,0:T(8,128)S(1)} %collective-permute-done.10.refs_2_.refs_5_, ...), custom_call_target="tpu_custom_call" | custom-call | flops 1207959552 | bytes 1048576 | tf_op jit(solution)/shard_map/pallas_call | solution.py:210
  59.2 0.1 collective-permute-start.12
  59.3 1.2 %collective-permute-start.16 = (f32[128,256]{1,0:T(8,128)S(1)}, f32[128,256]{1,0:T(8,128)S(1)}, u32[]{:S(2)}, u32[]{:S(2)}) collective-permute-start(f32[128,256]{1,0:T(8,128)S(1)} %get-tuple-element.42), channel_id=1, source_target_pairs={{0,24},{1,25},{2,26},{3,27},{4,28},{5,29},{6,30},{7,31},{8,16},{9,... | collective-permute-start | bytes 393224 | tf_op jit(solution)/shard_map/ppermute | solution.py:236
  60.5 1.8 %collective-permute-start.15 = (f32[128,256]{1,0:T(8,128)S(1)}, f32[128,256]{1,0:T(8,128)S(1)}, u32[]{:S(2)}, u32[]{:S(2)}) collective-permute-start(f32[128,256]{1,0:T(8,128)S(1)} %get-tuple-element.42), channel_id=1, source_target_pairs={{0,20},{1,21},{2,22},{3,23},{4,24},{5,25},{6,26},{7,27},{8,28},{9,... | collective-permute-start | bytes 393224 | tf_op jit(solution)/shard_map/ppermute | solution.py:236
  62.3 2.1 %collective-permute-start.14 = (f32[128,256]{1,0:T(8,128)S(1)}, f32[128,256]{1,0:T(8,128)S(1)}, u32[]{:S(2)}, u32[]{:S(2)}) collective-permute-start(f32[128,256]{1,0:T(8,128)S(1)} %get-tuple-element.42), channel_id=1, source_target_pairs={{0,16},{1,17},{2,18},{3,19},{4,20},{5,21},{6,22},{7,23},{8,24},{9,... | collective-permute-start | bytes 393224 | tf_op jit(solution)/shard_map/ppermute | solution.py:236
  64.4 0.0 collective-permute-start.11
  64.5 11.1 %collective-permute-done.11 = f32[64,256]{1,0:T(8,128)S(1)} collective-permute-done((f32[64,256]{1,0:T(8,128)S(1)}, f32[64,256]{1,0:T(8,128)S(1)}, u32[]{:S(2)}, u32[]{:S(2)}) %collective-permute-start.11) | collective-permute-done | bytes 65568 | tf_op jit(solution)/shard_map/ppermute | solution.py:236
  75.5 0.0 collective-permute-done.12
  75.5 0.4 collective-permute-start.13
  75.9 0.0 collective-permute-done.16
  75.9 0.0 collective-permute-done.15
  75.9 0.0 collective-permute-done.14
  75.9 3.9 %collective-permute-done.13 = f32[64,256]{1,0:T(8,128)S(1)} collective-permute-done((f32[64,256]{1,0:T(8,128)S(1)}, f32[64,256]{1,0:T(8,128)S(1)}, u32[]{:S(2)}, u32[]{:S(2)}) %collective-permute-start.13) | collective-permute-done | bytes 65568 | tf_op jit(solution)/shard_map/ppermute | solution.py:234
  79.8 0.4 collective-permute-start.18
  80.2 2.0 %collective-permute-start.22 = (f32[2,64,256]{2,1,0:T(8,128)S(1)}, f32[2,64,256]{2,1,0:T(8,128)S(1)}, u32[]{:S(2)}, u32[]{:S(2)}) collective-permute-start(f32[2,64,256]{2,1,0:T(8,128)S(1)} %pad_maximum_fusion.5), channel_id=1, source_target_pairs={{0,12},{1,13},{2,14},{3,15},{4,0},{5,1},{6,2},{7,3},{8,4},{9,5},{1... | collective-permute-start | bytes 393224 | tf_op jit(solution)/shard_map/ppermute | solution.py:234
  82.3 0.0 collective-permute-start.21
  82.3 1.5 %collective-permute-start.20 = (f32[2,64,256]{2,1,0:T(8,128)S(1)}, f32[2,64,256]{2,1,0:T(8,128)S(1)}, u32[]{:S(2)}, u32[]{:S(2)}) collective-permute-start(f32[2,64,256]{2,1,0:T(8,128)S(1)} %pad_maximum_fusion.5), channel_id=1, source_target_pairs={{0,4},{1,5},{2,6},{3,7},{4,8},{5,9},{6,10},{7,11},{8,12},{9,13},{1... | collective-permute-start | bytes 393224 | tf_op jit(solution)/shard_map/ppermute | solution.py:234
  83.8 0.0 collective-permute-start.17
  83.8 2.4 %collective-permute-done.22 = f32[2,64,256]{2,1,0:T(8,128)S(1)} collective-permute-done((f32[2,64,256]{2,1,0:T(8,128)S(1)}, f32[2,64,256]{2,1,0:T(8,128)S(1)}, u32[]{:S(2)}, u32[]{:S(2)}) %collective-permute-start.22) | collective-permute-done | bytes 131104 | tf_op jit(solution)/shard_map/ppermute | solution.py:234
  86.2 7.2 %collective-permute-done.21 = f32[2,64,256]{2,1,0:T(8,128)S(1)} collective-permute-done((f32[2,64,256]{2,1,0:T(8,128)S(1)}, f32[2,64,256]{2,1,0:T(8,128)S(1)}, u32[]{:S(2)}, u32[]{:S(2)}) %collective-permute-start.21) | collective-permute-done | bytes 131104 | tf_op jit(solution)/shard_map/ppermute | solution.py:234
  93.4 0.0 collective-permute-done.20
  93.4 0.1 collective-permute-start.23
  93.5 0.0 collective-permute-done.18.refs_1_
  93.5 0.5 collective-permute-start.19
  94.0 1.6 %shard_map.70.refs_8_ = f32[192,512]{1,0:T(8,128)S(1)} custom-call(f32[4,128,256]{2,1,0:T(8,128)S(1)} %pad_maximum_fusion.2.refs_0_, f32[4,128,256]{2,1,0:T(8,128)S(1)} %collective-permute-done.18.refs_1_, f32[4,2,64,256]{3,2,1,0:T(8,128)S(1)} %pad_maximum_fusion.3.refs_2_, f32[4,128,256]{2,1,0:T(8,128)S(1)} %pad_maximum_fusion.refs_0_.refs_3_, ...), custom_call_target="tpu_custom_call" | custom-call | flops 1207959552 | bytes 1048576 | tf_op jit(solution)/shard_map/pallas_call | solution.py:210
  95.7 0.0 collective-permute-done.17.refs_0_
  95.7 0.0 collective-permute-done.23.refs_2_
  95.7 0.5 collective-permute-done.19.refs_1_
  96.2 2.3 %shard_map.71 = f32[192,256]{1,0:T(8,128)} custom-call(f32[4,128,256]{2,1,0:T(8,128)S(1)} %collective-permute-done.17.refs_0_, f32[4,128,256]{2,1,0:T(8,128)S(1)} %collective-permute-done.19.refs_1_, f32[4,2,64,256]{3,2,1,0:T(8,128)S(1)} %collective-permute-done.23.refs_2_, f32[4,128,256]{2,1,0:T(8,128)S(1)} %collective-permute-done.4.refs_0_.refs_3_, ...), custom_call_target="tpu_custom_call" | custom-call | flops 1207959552 | bytes 1048576 | tf_op jit(solution)/shard_map/pallas_call | solution.py:210
  (6 shorter events, 0.2 us)
Async XLA Ops:
  22.9 0.9 copy-start.2
  24.5 8.6 %collective-permute-start = (f32[64,256]{1,0:T(8,128)S(1)}, f32[64,256]{1,0:T(8,128)S(1)}, u32[]{:S(2)}, u32[]{:S(2)}) collective-permute-start(f32[64,256]{1,0:T(8,128)S(1)} %get-tuple-element.27), channel_id=1, source_target_pairs={{0,2},{1,3},{2,0},{3,1},{4,6},{5,7},{6,4},{7,5},{8,10},{9,11},{10,... | collective-permute-start | bytes 196616 | tf_op jit(solution)/shard_map/ppermute | solution.py:234
  25.0 8.2 %collective-permute-start.3 = (f32[128,256]{1,0:T(8,128)S(1)}, f32[128,256]{1,0:T(8,128)S(1)}, u32[]{:S(2)}, u32[]{:S(2)}) collective-permute-start(f32[128,256]{1,0:T(8,128)S(1)} %get-tuple-element.28), channel_id=1, source_target_pairs={{0,12},{1,13},{2,14},{3,15},{4,0},{5,1},{6,2},{7,3},{8,4},{9,5},{1... | collective-permute-start | bytes 393224 | tf_op jit(solution)/shard_map/ppermute | solution.py:234
  27.7 12.4 %collective-permute-start.2 = (f32[128,256]{1,0:T(8,128)S(1)}, f32[128,256]{1,0:T(8,128)S(1)}, u32[]{:S(2)}, u32[]{:S(2)}) collective-permute-start(f32[128,256]{1,0:T(8,128)S(1)} %get-tuple-element.28), channel_id=1, source_target_pairs={{0,8},{1,9},{2,10},{3,11},{4,12},{5,13},{6,14},{7,15},{8,0},{9,1},... | collective-permute-start | bytes 393224 | tf_op jit(solution)/shard_map/ppermute | solution.py:234
  28.2 11.8 %collective-permute-start.1 = (f32[128,256]{1,0:T(8,128)S(1)}, f32[128,256]{1,0:T(8,128)S(1)}, u32[]{:S(2)}, u32[]{:S(2)}) collective-permute-start(f32[128,256]{1,0:T(8,128)S(1)} %get-tuple-element.28), channel_id=1, source_target_pairs={{0,4},{1,5},{2,6},{3,7},{4,8},{5,9},{6,10},{7,11},{8,12},{9,13},{1... | collective-permute-start | bytes 393224 | tf_op jit(solution)/shard_map/ppermute | solution.py:234
  28.8 3.4 %copy-start = (f32[2,256,4096]{2,1,0:T(8,128)S(1)}, f32[2,256,4096]{2,1,0:T(8,128)}, u32[]{:S(2)}) copy-start(f32[2,256,4096]{2,1,0:T(8,128)} %matrix_ref) | copy-start | bytes 25165828
  32.2 12.9 %copy-start.1 = (f32[2,256,4096]{2,1,0:T(8,128)S(1)}, f32[2,256,4096]{2,1,0:T(8,128)}, u32[]{:S(2)}) copy-start(f32[2,256,4096]{2,1,0:T(8,128)} %matrix_ref.1) | copy-start | bytes 25165828
  40.1 14.8 %collective-permute-start.5 = (f32[4,128,256]{2,1,0:T(8,128)S(1)}, f32[4,128,256]{2,1,0:T(8,128)S(1)}, u32[]{:S(2)}, u32[]{:S(2)}) collective-permute-start(f32[4,128,256]{2,1,0:T(8,128)S(1)} %pad_maximum_fusion.refs_0_.refs_3_), channel_id=1, source_target_pairs={{0,2},{1,3},{2,0},{3,1},{4,6},{5,7},{6,4},{7,5},{8,10},{9,11},{10,... | collective-permute-start | bytes 1572872 | tf_op jit(solution)/shard_map/ppermute | solution.py:234
  41.3 5.5 %collective-permute-start.8 = (f32[2,64,256]{2,1,0:T(8,128)S(1)}, f32[2,64,256]{2,1,0:T(8,128)S(1)}, u32[]{:S(2)}, u32[]{:S(2)}) collective-permute-start(f32[2,64,256]{2,1,0:T(8,128)S(1)} %pad_maximum_fusion.4), channel_id=1, source_target_pairs={{0,12},{1,13},{2,14},{3,15},{4,0},{5,1},{6,2},{7,3},{8,4},{9,5},{1... | collective-permute-start | bytes 393224 | tf_op jit(solution)/shard_map/ppermute | solution.py:234
  41.3 13.5 %collective-permute-start.7 = (f32[2,64,256]{2,1,0:T(8,128)S(1)}, f32[2,64,256]{2,1,0:T(8,128)S(1)}, u32[]{:S(2)}, u32[]{:S(2)}) collective-permute-start(f32[2,64,256]{2,1,0:T(8,128)S(1)} %pad_maximum_fusion.4), channel_id=1, source_target_pairs={{0,8},{1,9},{2,10},{3,11},{4,12},{5,13},{6,14},{7,15},{8,0},{9,1},... | collective-permute-start | bytes 393224 | tf_op jit(solution)/shard_map/ppermute | solution.py:234
  43.1 11.8 %collective-permute-start.6 = (f32[2,64,256]{2,1,0:T(8,128)S(1)}, f32[2,64,256]{2,1,0:T(8,128)S(1)}, u32[]{:S(2)}, u32[]{:S(2)}) collective-permute-start(f32[2,64,256]{2,1,0:T(8,128)S(1)} %pad_maximum_fusion.4), channel_id=1, source_target_pairs={{0,4},{1,5},{2,6},{3,7},{4,8},{5,9},{6,10},{7,11},{8,12},{9,13},{1... | collective-permute-start | bytes 393224 | tf_op jit(solution)/shard_map/ppermute | solution.py:234
  45.1 12.0 %collective-permute-start.4 = (f32[4,128,256]{2,1,0:T(8,128)S(1)}, f32[4,128,256]{2,1,0:T(8,128)S(1)}, u32[]{:S(2)}, u32[]{:S(2)}) collective-permute-start(f32[4,128,256]{2,1,0:T(8,128)S(1)} %pad_maximum_fusion.refs_0_.refs_3_), channel_id=1, source_target_pairs={{0,1},{1,0},{2,3},{3,2},{4,5},{5,4},{6,7},{7,6},{8,9},{9,8},{10,11... | collective-permute-start | bytes 1572872 | tf_op jit(solution)/shard_map/ppermute | solution.py:234
  54.9 2.3 %collective-permute-start.9 = (f32[4,128,256]{2,1,0:T(8,128)S(1)}, f32[4,128,256]{2,1,0:T(8,128)S(1)}, u32[]{:S(2)}, u32[]{:S(2)}) collective-permute-start(f32[4,128,256]{2,1,0:T(8,128)S(1)} %collective-permute-done.5.refs_1_.refs_4_), channel_id=1, source_target_pairs={{0,1},{1,0},{2,3},{3,2},{4,5},{5,4},{6,7},{7,6},{8,9},{9,8},{10,11... | collective-permute-start | bytes 1572872 | tf_op jit(solution)/shard_map/ppermute | solution.py:234
  55.0 2.6 %collective-permute-start.10 = (f32[4,2,64,256]{3,2,1,0:T(8,128)S(1)}, f32[4,2,64,256]{3,2,1,0:T(8,128)S(1)}, u32[]{:S(2)}, u32[]{:S(2)}) collective-permute-start(f32[4,2,64,256]{3,2,1,0:T(8,128)S(1)} %pad_maximum_fusion.1.refs_2_.refs_5_), channel_id=1, source_target_pairs={{0,1},{1,0},{2,3},{3,2},{4,5},{5,4},{6,7},{7,6},{8,9},{9,8},{10,11... | collective-permute-start | bytes 1572872 | tf_op jit(solution)/shard_map/ppermute | solution.py:234
  59.2 16.3 %collective-permute-start.12 = (f32[128,256]{1,0:T(8,128)S(1)}, f32[128,256]{1,0:T(8,128)S(1)}, u32[]{:S(2)}, u32[]{:S(2)}) collective-permute-start(f32[128,256]{1,0:T(8,128)S(1)} %get-tuple-element.42), channel_id=1, source_target_pairs={{0,28},{1,29},{2,30},{3,31},{4,16},{5,17},{6,18},{7,19},{8,20},{9,... | collective-permute-start | bytes 393224 | tf_op jit(solution)/shard_map/ppermute | solution.py:236
  59.3 16.6 %collective-permute-start.16 = (f32[128,256]{1,0:T(8,128)S(1)}, f32[128,256]{1,0:T(8,128)S(1)}, u32[]{:S(2)}, u32[]{:S(2)}) collective-permute-start(f32[128,256]{1,0:T(8,128)S(1)} %get-tuple-element.42), channel_id=1, source_target_pairs={{0,24},{1,25},{2,26},{3,27},{4,28},{5,29},{6,30},{7,31},{8,16},{9,... | collective-permute-start | bytes 393224 | tf_op jit(solution)/shard_map/ppermute | solution.py:236
  60.5 15.4 %collective-permute-start.15 = (f32[128,256]{1,0:T(8,128)S(1)}, f32[128,256]{1,0:T(8,128)S(1)}, u32[]{:S(2)}, u32[]{:S(2)}) collective-permute-start(f32[128,256]{1,0:T(8,128)S(1)} %get-tuple-element.42), channel_id=1, source_target_pairs={{0,20},{1,21},{2,22},{3,23},{4,24},{5,25},{6,26},{7,27},{8,28},{9,... | collective-permute-start | bytes 393224 | tf_op jit(solution)/shard_map/ppermute | solution.py:236
  62.3 13.6 %collective-permute-start.14 = (f32[128,256]{1,0:T(8,128)S(1)}, f32[128,256]{1,0:T(8,128)S(1)}, u32[]{:S(2)}, u32[]{:S(2)}) collective-permute-start(f32[128,256]{1,0:T(8,128)S(1)} %get-tuple-element.42), channel_id=1, source_target_pairs={{0,16},{1,17},{2,18},{3,19},{4,20},{5,21},{6,22},{7,23},{8,24},{9,... | collective-permute-start | bytes 393224 | tf_op jit(solution)/shard_map/ppermute | solution.py:236
  64.4 11.1 %collective-permute-start.11 = (f32[64,256]{1,0:T(8,128)S(1)}, f32[64,256]{1,0:T(8,128)S(1)}, u32[]{:S(2)}, u32[]{:S(2)}) collective-permute-start(f32[64,256]{1,0:T(8,128)S(1)} %get-tuple-element.41), channel_id=1, source_target_pairs={{0,16},{1,17},{2,18},{3,19},{4,20},{5,21},{6,22},{7,23},{8,24},{9,... | collective-permute-start | bytes 196616 | tf_op jit(solution)/shard_map/ppermute | solution.py:236
  75.5 4.3 %collective-permute-start.13 = (f32[64,256]{1,0:T(8,128)S(1)}, f32[64,256]{1,0:T(8,128)S(1)}, u32[]{:S(2)}, u32[]{:S(2)}) collective-permute-start(f32[64,256]{1,0:T(8,128)S(1)} %collective-permute-done.11), channel_id=1, source_target_pairs={{0,2},{1,3},{2,0},{3,1},{4,6},{5,7},{6,4},{7,5},{8,10},{9,11},{10,... | collective-permute-start | bytes 196616 | tf_op jit(solution)/shard_map/ppermute | solution.py:234
  79.8 13.7 %collective-permute-start.18 = (f32[4,128,256]{2,1,0:T(8,128)S(1)}, f32[4,128,256]{2,1,0:T(8,128)S(1)}, u32[]{:S(2)}, u32[]{:S(2)}) collective-permute-start(f32[4,128,256]{2,1,0:T(8,128)S(1)} %pad_maximum_fusion.2.refs_0_), channel_id=1, source_target_pairs={{0,2},{1,3},{2,0},{3,1},{4,6},{5,7},{6,4},{7,5},{8,10},{9,11},{10,... | collective-permute-start | bytes 1572872 | tf_op jit(solution)/shard_map/ppermute | solution.py:234
  80.2 6.0 %collective-permute-start.22 = (f32[2,64,256]{2,1,0:T(8,128)S(1)}, f32[2,64,256]{2,1,0:T(8,128)S(1)}, u32[]{:S(2)}, u32[]{:S(2)}) collective-permute-start(f32[2,64,256]{2,1,0:T(8,128)S(1)} %pad_maximum_fusion.5), channel_id=1, source_target_pairs={{0,12},{1,13},{2,14},{3,15},{4,0},{5,1},{6,2},{7,3},{8,4},{9,5},{1... | collective-permute-start | bytes 393224 | tf_op jit(solution)/shard_map/ppermute | solution.py:234
  82.3 11.1 %collective-permute-start.21 = (f32[2,64,256]{2,1,0:T(8,128)S(1)}, f32[2,64,256]{2,1,0:T(8,128)S(1)}, u32[]{:S(2)}, u32[]{:S(2)}) collective-permute-start(f32[2,64,256]{2,1,0:T(8,128)S(1)} %pad_maximum_fusion.5), channel_id=1, source_target_pairs={{0,8},{1,9},{2,10},{3,11},{4,12},{5,13},{6,14},{7,15},{8,0},{9,1},... | collective-permute-start | bytes 393224 | tf_op jit(solution)/shard_map/ppermute | solution.py:234
  82.3 11.1 %collective-permute-start.20 = (f32[2,64,256]{2,1,0:T(8,128)S(1)}, f32[2,64,256]{2,1,0:T(8,128)S(1)}, u32[]{:S(2)}, u32[]{:S(2)}) collective-permute-start(f32[2,64,256]{2,1,0:T(8,128)S(1)} %pad_maximum_fusion.5), channel_id=1, source_target_pairs={{0,4},{1,5},{2,6},{3,7},{4,8},{5,9},{6,10},{7,11},{8,12},{9,13},{1... | collective-permute-start | bytes 393224 | tf_op jit(solution)/shard_map/ppermute | solution.py:234
  83.8 11.9 %collective-permute-start.17 = (f32[4,128,256]{2,1,0:T(8,128)S(1)}, f32[4,128,256]{2,1,0:T(8,128)S(1)}, u32[]{:S(2)}, u32[]{:S(2)}) collective-permute-start(f32[4,128,256]{2,1,0:T(8,128)S(1)} %pad_maximum_fusion.2.refs_0_), channel_id=1, source_target_pairs={{0,1},{1,0},{2,3},{3,2},{4,5},{5,4},{6,7},{7,6},{8,9},{9,8},{10,11... | collective-permute-start | bytes 1572872 | tf_op jit(solution)/shard_map/ppermute | solution.py:234
  93.4 2.2 %collective-permute-start.23 = (f32[4,2,64,256]{3,2,1,0:T(8,128)S(1)}, f32[4,2,64,256]{3,2,1,0:T(8,128)S(1)}, u32[]{:S(2)}, u32[]{:S(2)}) collective-permute-start(f32[4,2,64,256]{3,2,1,0:T(8,128)S(1)} %pad_maximum_fusion.3.refs_2_), channel_id=1, source_target_pairs={{0,1},{1,0},{2,3},{3,2},{4,5},{5,4},{6,7},{7,6},{8,9},{9,8},{10,11... | collective-permute-start | bytes 1572872 | tf_op jit(solution)/shard_map/ppermute | solution.py:234
  93.5 2.6 %collective-permute-start.19 = (f32[4,128,256]{2,1,0:T(8,128)S(1)}, f32[4,128,256]{2,1,0:T(8,128)S(1)}, u32[]{:S(2)}, u32[]{:S(2)}) collective-permute-start(f32[4,128,256]{2,1,0:T(8,128)S(1)} %collective-permute-done.18.refs_1_), channel_id=1, source_target_pairs={{0,1},{1,0},{2,3},{3,2},{4,5},{5,4},{6,7},{7,6},{8,9},{9,8},{10,11... | collective-permute-start | bytes 1572872 | tf_op jit(solution)/shard_map/ppermute | solution.py:234

commit v10 on v8

--- a/solution.py
+++ b/solution.py
@@ -8,6 +8,7 @@
 from jax.sharding import PartitionSpec as P
 
 MIB = 1 << 20
+CHAINS = 2
 f32 = jnp.float32
 bf16 = jnp.bfloat16
 lanes_contract = (((1,), (1,)), ((), ()))
@@ -16,13 +17,6 @@
 def halves_of(value):
     high = value.astype(bf16)
     return high, (value - high.astype(f32)).astype(bf16)
-
-
-def thirds_of(value):
-    high = value.astype(bf16)
-    rest = value - high.astype(f32)
-    middle = rest.astype(bf16)
-    return high, middle, (rest - middle.astype(f32)).astype(bf16)
 
 
 def kernel_params(size):
@@ -61,7 +55,7 @@
         tail = jnp.where(lax.broadcasted_iota(jnp.int32, (width - columns, entries), 0) == 0, local_row, 0.0)
         data = jnp.concatenate([data, tail], axis=0)
     packed = jnp.zeros((slots, data.shape[0]), f32)
-    for piece in thirds_of(data):
+    for piece in halves_of(data):
         packed += lax.dot_general(choose, piece, lanes_contract, preferred_element_type=f32)
     packed = packed.reshape(owners, cap, data.shape[0])
     if not folded:
@@ -78,7 +72,7 @@
     packed_ref[:, cap + half:, :] = jnp.where(line == first // width, numbers[:, None, :], 0.0)
 
 
-def reduce_kernel(cap, received_ref, right_hbm, *refs):
+def reduce_kernel(cap, sources, received_ref, right_hbm, *refs):
     reduced_refs, right_ref, sem = refs[:-2], refs[-2], refs[-1]
     move = pltpu.make_async_copy(right_hbm, right_ref, sem)
     move.start()
@@ -96,7 +90,7 @@
         totals = []
         for value in sets:
             total = jnp.zeros((own_rows, value.shape[1]), f32)
-            for piece in thirds_of(value):
+            for piece in halves_of(value):
                 total += jnp.dot(place, piece, preferred_element_type=f32)
             totals.append(total.T)
         total = jnp.concatenate(totals, axis=0)
@@ -105,14 +99,15 @@
         local_row = received[:, columns:columns + 1].astype(jnp.int32)
         place = jnp.where(lax.broadcasted_iota(jnp.int32, (slots, own_rows), 1) == local_row, 1.0, 0.0).astype(bf16)
         total = jnp.zeros((columns, own_rows), f32)
-        for piece in thirds_of(received[:, :columns].T):
+        for piece in halves_of(received[:, :columns].T):
             total += jnp.dot(piece, place, preferred_element_type=f32)
     move.wait()
-    start = 0
-    for reduced_ref in reduced_refs:
-        rows = reduced_ref.shape[0]
-        reduced_ref[...] = right_ref[start:start + rows, :] - total[start:start + rows]
-        start += rows
+    reduced = right_ref[...] - total
+    share = sources // len(reduced_refs)
+    for group in range(columns // sources):
+        for chain, reduced_ref in enumerate(reduced_refs):
+            start = group * sources + chain * share
+            reduced_ref[group * share:(group + 1) * share, :] = reduced[start:start + share]
 
 
 def split_kernel(block, relative, matrix_ref, high_ref, low_ref):
@@ -146,27 +141,23 @@
     )(matrix)
 
 
-def product_kernel(sources, layout, inputs, sets, block, begin, end, onward, relative, *refs):
+def product_kernel(share, layout, inputs, sets, block, begin, end, onward, relative, merged, *refs):
     high_ref, low_ref = refs[inputs * sets:inputs * sets + 2]
     rest = refs[inputs * sets + 2:]
     groups, both_rows, width = high_ref.shape
     layers = width // block
     own_rows = both_rows // 2
     start_ref, rest = (rest[0], rest[1:]) if begin > 0 else (None, rest)
-    out_refs, total_ref = (rest[:-1], rest[-1]) if end == groups else ((), rest[0])
+    earlier_refs, rest = rest[:merged], rest[merged:]
+    out_ref, total_ref = rest if end == groups else (None, rest[0])
     columns = total_ref.shape[0]
     me = lax.axis_index("tile")
 
     def block_of(step, layer):
         held = lax.rem(lax.div(me, 4) + (layers - layer), layers) if relative else layer
-        pieces = []
-        for group in layout:
-            which, place = group(step, held)
-            value = refs[which][place]
-            if sets == 2:
-                value = refs[inputs + which][place] - value
-            pieces.append(value)
-        return jnp.concatenate(pieces, axis=0)
+        which, place = layout(step, held)
+        value = refs[which][place]
+        return refs[inputs + which][place] - value if sets == 2 else value
 
     @pl.when(jnp.logical_not(onward) | (lax.axis_index("chain") < lax.axis_size("chain") - 1))
     def _():
@@ -185,35 +176,39 @@
                 total_ref[...] = part
             else:
                 total_ref[...] = start_ref[...] + part
-        start = 0
-        for out_ref in out_refs:
-            for first in range(0, out_ref.shape[0], 2 * sources):
-                real = pl.ds(start + first, sources)
-                imag = pl.ds(start + first + sources, sources)
-                out_ref[first:first + sources, :] = total_ref[real, :own_rows] - total_ref[imag, own_rows:]
-                out_ref[first + sources:first + 2 * sources, :] = total_ref[imag, :own_rows] + total_ref[real, own_rows:]
-            start += out_ref.shape[0]
-
-
-def product_part(split, onward, layout, blocks, own, begin, end, started, sources, shares, relative):
+        if out_ref is None:
+            return
+        for first in range(0, columns, 2 * share):
+            real = pl.ds(first, share)
+            imag = pl.ds(first + share, share)
+            results = [
+                total_ref[real, :own_rows] - total_ref[imag, own_rows:],
+                total_ref[imag, :own_rows] + total_ref[real, own_rows:],
+            ]
+            for half, result in enumerate(results):
+                row = first + half * share
+                place = row * (merged + 1)
+                for chain, earlier_ref in enumerate(earlier_refs):
+                    out_ref[place + chain * share:place + (chain + 1) * share, :] = earlier_ref[row:row + share, :]
+                out_ref[place + merged * share:place + (merged + 1) * share, :] = result
+
+
+def product_part(split, onward, layout, blocks, own, begin, end, started, share, relative, earlier=()):
     groups, both_rows, width = split[0].shape
-    block = blocks[0].shape[-1]
+    columns, block = blocks[0].shape[-2:]
     vmem = pl.BlockSpec(memory_space=pltpu.VMEM)
     finish = end == groups
-    whole = (sum(shares), both_rows)
-    arrays = list(blocks) + list(own) + list(split) + ([] if started is None else [started])
-    if finish:
-        out_shape = [jax.ShapeDtypeStruct((rows, both_rows // 2), f32) for rows in shares]
-    else:
-        out_shape = jax.ShapeDtypeStruct(whole, f32)
+    arrays = list(blocks) + list(own) + list(split) + ([] if started is None else [started]) + list(earlier)
+    out_rows = columns * (len(earlier) + 1)
+    sets = 2 if own else 1
     return pl.pallas_call(
-        functools.partial(product_kernel, sources, layout, len(blocks), 2 if own else 1, block, begin, end, onward, relative),
+        functools.partial(product_kernel, share, layout, len(blocks), sets, block, begin, end, onward, relative, len(earlier)),
         in_specs=[vmem] * len(arrays),
-        out_specs=[vmem] * len(shares) if finish else vmem,
-        out_shape=out_shape,
-        scratch_shapes=[pltpu.VMEM(whole, f32)] if finish else [],
+        out_specs=vmem,
+        out_shape=jax.ShapeDtypeStruct((out_rows, both_rows // 2) if finish else (columns, both_rows), f32),
+        scratch_shapes=[pltpu.VMEM((columns, both_rows), f32)] if finish else [],
         compiler_params=kernel_params(20),
-        cost_estimate=pl.CostEstimate(flops=6 * sum(shares) * both_rows * width * (end - begin), bytes_accessed=MIB, transcendentals=0),
+        cost_estimate=pl.CostEstimate(flops=6 * columns * both_rows * width * (end - begin), bytes_accessed=MIB, transcendentals=0),
     )(*arrays)
 
 
@@ -221,11 +216,10 @@
     return lax.optimization_barrier((value, to))[0]
 
 
-def solve_paired(reduced, diag_inverse, coupling, sources):
+def solve_paired(reduced, diag_inverse, coupling, share):
     chain_size = lax.axis_size("chain")
     tile_size = lax.axis_size("tile")
     own_rows = reduced[0].shape[1]
-    shares = [each.shape[0] for each in reduced]
     layers = tile_size // 4
 
     def send(value, hop, target):
@@ -234,40 +228,49 @@
         pairs = [(c * tile_size + t, (c + 1) * tile_size + target(t)) for c in range(chain_size - 1) for t in range(tile_size)]
         return lax.ppermute(value, ("chain", "tile"), pairs)
 
-    def first_stage(first, second, hop):
-        pair = [second if across == 0 and not hop else send(second, hop, lambda t: t ^ (2 * across)) for across in range(2)]
-        line = [first if by == 0 and not hop else send(first, hop, lambda t: (t + 4 * by) % tile_size) for by in range(layers)]
-        return jnp.stack(pair), jnp.stack(line)
-
-    def second_stage(pair, line):
+    def along(value, hop):
+        return [value if by == 0 and not hop else send(value, hop, lambda t: (t + 4 * by) % tile_size) for by in range(layers)]
+
+    def finished(line, after):
         far = send(line, False, lambda t: t ^ 2)
-        rest = [pair if by == 0 else send(pair, False, lambda t: (t + 4 * by) % tile_size) for by in range(layers)]
-        return [line, far, jnp.stack(rest)]
-
-    layout = [lambda step, held: (step % 2, (held,)), lambda step, held: (2, (held, step % 2))]
-
-    def products(split, onward, held, own, shares):
-        other = [send(each, False, lambda t: t ^ 1) for each in held]
+        held = [line, far if after is None else tied(far, after)]
+        return held, [send(each, False, lambda t: t ^ 1) for each in held]
+
+    def layout(step, held):
+        return step % 2, (held,)
+
+    def products(split, onward, held, other, own, earlier=()):
         mine, theirs = own if own else ([], [])
-        started = product_part(split, onward, layout, held, mine, 0, 2, None, sources, shares, True)
-        return product_part(split, onward, layout, other, theirs, 2, 4, started, sources, shares, True), other
+        started = product_part(split, onward, layout, held, mine, 0, 2, None, share, True)
+        return product_part(split, onward, layout, other, theirs, 2, 4, started, share, True, earlier)
 
     only = chain_size == 1
-    pair, line = first_stage(*reduced, False)
+    first = along(reduced[0], False)
     split = split_blocks(tied(diag_inverse if only else coupling, reduced[0]), own_rows, True)
-    pair, line, split = lax.optimization_barrier((pair, line, split))
-    held = second_stage(pair, line)
-    if only:
-        return products(split, False, held, None, [sum(shares)])[0][0]
-    diag_split = split_blocks(tied(diag_inverse, line), own_rows, True)
-    held[1], held[2], diag_split = lax.optimization_barrier((held[1], held[2], diag_split))
-    carried, other = products(split, True, held, None, shares)
-    own = (held, other)
-    for step in range(chain_size - 1):
-        held = second_stage(*lax.optimization_barrier(first_stage(*carried, True)))
-        if step < chain_size - 2:
-            carried = products(split, True, held, own, shares)[0]
-    return products(diag_split, False, held, own, [sum(shares)])[0][0]
+    lines = [tied(jnp.stack(first), split)]
+    lines += [jnp.stack(along(tied(value, split), False)) for value in reduced[1:]]
+    after = None
+    if not only:
+        after = diag_split = split_blocks(tied(diag_inverse, lines[0]), own_rows, True)
+    own, carried, pieces = [], [], []
+    for chain in range(CHAINS):
+        own.append(finished(lines[chain], after))
+        carried.append(products(split, not only, *own[chain], None, tuple(carried) if only else ()))
+        pieces.append(along(carried[chain], not only))
+        after = carried[chain]
+    for step in range(1, chain_size):
+        last = step == chain_size - 1
+        lines = [jnp.stack(each) for each in pieces]
+        lines[0] = tied(lines[0], carried[-1])
+        carried, pieces, after = [], [], None
+        for chain in range(CHAINS):
+            arrived = finished(lines[chain], after)
+            matrix = diag_split if last else split
+            carried.append(products(matrix, not last, *arrived, own[chain], tuple(carried) if last else ()))
+            after = carried[chain]
+            if not last:
+                pieces.append(along(carried[chain], True))
+    return carried[-1]
 
 
 def solve_flat(reduced, diag_inverse, coupling, sources):
@@ -277,7 +280,10 @@
     full_rows = diag_inverse.shape[2]
     block = min(256, full_rows)
     count = full_rows // block
-    layout = [lambda step, held: (0, (step * layers + held,))]
+
+    def layout(step, held):
+        return 0, (step * layers + held,)
+
     onward = [(i, i + 1) for i in range(chain_size - 1)]
     diag_split = split_blocks(diag_inverse, block, False)
     coupling_split = split_blocks(coupling, block, False)
@@ -290,9 +296,9 @@
 
     current = reduced
     for _ in range(chain_size - 1):
-        carried = product_part(coupling_split, True, layout, gathered(current), [], 0, groups, None, sources, [columns], False)[0]
+        carried = product_part(coupling_split, True, layout, gathered(current), [], 0, groups, None, sources, False)
         current = reduced - lax.ppermute(carried, "chain", onward)
-    return product_part(diag_split, False, layout, gathered(current), [], 0, groups, None, sources, [columns], False)[0]
+    return product_part(diag_split, False, layout, gathered(current), [], 0, groups, None, sources, False)
 
 
 def body(right_side, diag_inverse, coupling, updates, update_rows, tile_counts):
@@ -321,19 +327,19 @@
         compiler_params=kernel_params(56),
     )(tile_counts, update_rows[None, :], updates.T)
     received = lax.all_to_all(packed, "tile", 0, 0, tiled=False)
-    paired = own_rows % 128 == 0 and tile_size % 8 == 0 and batches > 1
-    early = batches * 2 // 3 * halves * sources
-    shares = [early, columns - early] if paired else [columns]
+    paired = own_rows % 128 == 0 and tile_size % 8 == 0 and sources % (8 * CHAINS) == 0
+    shares = [columns // CHAINS] * CHAINS if paired else [columns]
     reduced = pl.pallas_call(
-        functools.partial(reduce_kernel, cap),
+        functools.partial(reduce_kernel, cap, sources),
         in_specs=[vmem, hbm],
         out_specs=[vmem] * len(shares),
         out_shape=[jax.ShapeDtypeStruct((rows, own_rows), f32) for rows in shares],
         scratch_shapes=[pltpu.VMEM((columns, own_rows), f32), pltpu.SemaphoreType.DMA(())],
         compiler_params=kernel_params(20),
     )(received, right_side.reshape(columns, own_rows))
-    solve = solve_paired if paired else solve_flat
-    return solve(reduced, diag_inverse, coupling, sources).reshape(right_side.shape)
+    if paired:
+        return solve_paired(reduced, diag_inverse, coupling, sources // CHAINS).reshape(right_side.shape)
+    return solve_flat(reduced, diag_inverse, coupling, sources).reshape(right_side.shape)
 
 
 def solution(mesh):

time: 96.8 us -> 105 us (1.085)
  the two profiles are of different devices: /device:TPU:0 before, /device:TPU:3 now
where the time goes in v10:
time: 105 us
  waiting for transfers between devices  37.9 us (36%)
  starting transfers between devices  31.2 us (30%)
  blocking collectives  19.5 us (19%)
  Pallas kernels  11.4 us (11%)
  local copies, waits for them, and re-layouts  4.31 us (4%)
    ppermute x18, waiting for transfers between devices, send(): lax.ppermute(value, 'tile', [(t, target(t)) for t in range(tile_size)])  22.9 us
    ppermute x18, starting transfers between devices, send(): lax.ppermute(value, 'tile', [(t, target(t)) for t in range(tile_size)])  20.8 us
    all_to_all x1, blocking collectives, body(): received = lax.all_to_all(packed, 'tile', 0, 0, tiled=False)  19.5 us
    ppermute x8, waiting for transfers between devices, send(): return lax.ppermute(value, ('chain', 'tile'), pairs)  15 us
    ppermute x8, starting transfers between devices, send(): return lax.ppermute(value, ('chain', 'tile'), pairs)  10.5 us
    pallas_call x8, Pallas kernels, product_part(): pl.pallas_call(functools.partial(product_kernel, share, layout, len(block...  6.49 us
    unnamed x6, local copies, waits for them, and re-layouts  4.31 us
    pallas_call x1, Pallas kernels, body(): pl.pallas_call(functools.partial(pack_kernel, own_rows, cap, tile_rows),...  2.21 us
  transfers between devices with their start and end apart: 26, of which 11 were waited for; matrix products, arithmetic and copies ran while one was open for 0% of the time, Pallas kernels for 6%

profile of v10, /device:TPU:3, one launch (start us, length us, event | category | flops | bytes accessed | tf_op | source)
XLA Modules:
  0.0 104.7 jit_solution(2663496342281407173)
XLA Ops:
  0.0 2.2 %shard_map.64 = f32[16,56,128]{2,1,0:T(8,128)} custom-call(s32[2]{0:T(128)} %counts_hbm.1, s32[1,256]{1,0:T(1,128)} %bitcast.38, f32[192,256]{1,0:T(8,128)} %bitcast.23), custom_call_target="tpu_custom_call" | custom-call | tf_op jit(solution)/shard_map/pallas_call | solution.py:316
  2.2 19.5 %all_to_all.5.received_ref = f32[16,56,128]{2,1,0:T(8,128)S(1)} all-to-all(f32[16,56,128]{2,1,0:T(8,128)} %shard_map.64), channel_id=1, replica_groups=mesh['chain'=2,'tile'=16] {'tile'}, dimensions={0} | all-to-all | bytes 917504 | tf_op jit(solution)/shard_map/all_to_all | solution.py:329
  21.7 0.9 copy-done.2
  22.6 0.8 shard_map.65
  23.4 1.6 %collective-permute-start.7 = (f32[96,256]{1,0:T(8,128)S(1)}, f32[96,256]{1,0:T(8,128)S(1)}, u32[]{:S(2)}, u32[]{:S(2)}) collective-permute-start(f32[96,256]{1,0:T(8,128)S(1)} %get-tuple-element.20), channel_id=1, source_target_pairs={{0,12},{1,13},{2,14},{3,15},{4,0},{5,1},{6,2},{7,3},{8,4},{9,5},{1... | collective-permute-start | bytes 294920 | tf_op jit(solution)/shard_map/ppermute | solution.py:227
  24.9 0.9 collective-permute-start.6
  25.8 0.2 collective-permute-start.5
  26.1 3.4 %copy-done = f32[2,256,4096]{2,1,0:T(8,128)S(1)} copy-done((f32[2,256,4096]{2,1,0:T(8,128)S(1)}, f32[2,256,4096]{2,1,0:T(8,128)}, u32[]{:S(2)}) %copy-start) | copy-done | bytes 8388632
  29.5 1.0 shard_map.66
  30.4 0.0 collective-permute-done.7
  30.4 4.8 %collective-permute-done.6 = f32[96,256]{1,0:T(8,128)S(1)} collective-permute-done((f32[96,256]{1,0:T(8,128)S(1)}, f32[96,256]{1,0:T(8,128)S(1)}, u32[]{:S(2)}, u32[]{:S(2)}) %collective-permute-start.6) | collective-permute-done | bytes 98336 | tf_op jit(solution)/shard_map/ppermute | solution.py:227
  35.2 0.0 collective-permute-done.5
  35.2 0.7 collective-permute-start.9
  35.9 0.0 collective-permute-start.2
  36.0 1.0 collective-permute-start.1
  37.0 1.4 %collective-permute-start = (f32[96,256]{1,0:T(8,128)S(1)}, f32[96,256]{1,0:T(8,128)S(1)}, u32[]{:S(2)}, u32[]{:S(2)}) collective-permute-start(f32[96,256]{1,0:T(8,128)S(1)} %get-tuple-element.24), channel_id=1, source_target_pairs={{0,4},{1,5},{2,6},{3,7},{4,8},{5,9},{6,10},{7,11},{8,12},{9,13},{1... | collective-permute-start | bytes 294920 | tf_op jit(solution)/shard_map/ppermute | solution.py:227
  38.4 2.1 %collective-permute-start.8 = (f32[4,96,256]{2,1,0:T(8,128)S(1)}, f32[4,96,256]{2,1,0:T(8,128)S(1)}, u32[]{:S(2)}, u32[]{:S(2)}) collective-permute-start(f32[4,96,256]{2,1,0:T(8,128)S(1)} %pad_maximum_fusion.1.refs_0_.refs_2_), channel_id=1, source_target_pairs={{0,1},{1,0},{2,3},{3,2},{4,5},{5,4},{6,7},{7,6},{8,9},{9,8},{10,11... | collective-permute-start | bytes 1179656 | tf_op jit(solution)/shard_map/ppermute | solution.py:227
  40.4 0.0 copy-done.1
  40.4 1.0 shard_map.67
  41.4 3.9 %collective-permute-done.9.refs_1_.refs_3_ = f32[4,96,256]{2,1,0:T(8,128)S(1)} collective-permute-done((f32[4,96,256]{2,1,0:T(8,128)S(1)}, f32[4,96,256]{2,1,0:T(8,128)S(1)}, u32[]{:S(2)}, u32[]{:S(2)}) %collective-permute-start.9) | collective-permute-done | bytes 393248 | tf_op jit(solution)/shard_map/ppermute | solution.py:227
  45.3 1.5 %collective-permute-start.10 = (f32[4,96,256]{2,1,0:T(8,128)S(1)}, f32[4,96,256]{2,1,0:T(8,128)S(1)}, u32[]{:S(2)}, u32[]{:S(2)}) collective-permute-start(f32[4,96,256]{2,1,0:T(8,128)S(1)} %collective-permute-done.9.refs_1_.refs_3_), channel_id=1, source_target_pairs={{0,1},{1,0},{2,3},{3,2},{4,5},{5,4},{6,7},{7,6},{8,9},{9,8},{10,11... | collective-permute-start | bytes 1179656 | tf_op jit(solution)/shard_map/ppermute | solution.py:227
  46.8 0.0 collective-permute-done.2
  46.8 0.0 collective-permute-done.1
  46.9 0.0 collective-permute-done
  46.9 0.7 collective-permute-start.4
  47.6 1.2 %collective-permute-start.3 = (f32[4,96,256]{2,1,0:T(8,128)S(1)}, f32[4,96,256]{2,1,0:T(8,128)S(1)}, u32[]{:S(2)}, u32[]{:S(2)}) collective-permute-start(f32[4,96,256]{2,1,0:T(8,128)S(1)} %pad_maximum_fusion.refs_0_.refs_2_), channel_id=1, source_target_pairs={{0,1},{1,0},{2,3},{3,2},{4,5},{5,4},{6,7},{7,6},{8,9},{9,8},{10,11... | collective-permute-start | bytes 1179656 | tf_op jit(solution)/shard_map/ppermute | solution.py:227
  48.8 0.0 collective-permute-done.8.refs_0_.refs_2_
  48.8 0.0 collective-permute-done.10.refs_1_.refs_3_
  48.8 8.4 %collective-permute-done.4.refs_1_.refs_3_ = f32[4,96,256]{2,1,0:T(8,128)S(1)} collective-permute-done((f32[4,96,256]{2,1,0:T(8,128)S(1)}, f32[4,96,256]{2,1,0:T(8,128)S(1)}, u32[]{:S(2)}, u32[]{:S(2)}) %collective-permute-start.4) | collective-permute-done | bytes 393248 | tf_op jit(solution)/shard_map/ppermute | solution.py:227
  57.2 1.3 %collective-permute-start.11 = (f32[4,96,256]{2,1,0:T(8,128)S(1)}, f32[4,96,256]{2,1,0:T(8,128)S(1)}, u32[]{:S(2)}, u32[]{:S(2)}) collective-permute-start(f32[4,96,256]{2,1,0:T(8,128)S(1)} %collective-permute-done.4.refs_1_.refs_3_), channel_id=1, source_target_pairs={{0,1},{1,0},{2,3},{3,2},{4,5},{5,4},{6,7},{7,6},{8,9},{9,8},{10,11... | collective-permute-start | bytes 1179656 | tf_op jit(solution)/shard_map/ppermute | solution.py:227
  58.5 1.3 %collective-permute-start.21 = (f32[96,256]{1,0:T(8,128)S(1)}, f32[96,256]{1,0:T(8,128)S(1)}, u32[]{:S(2)}, u32[]{:S(2)}) collective-permute-start(f32[96,256]{1,0:T(8,128)S(1)} %shard_map.69), channel_id=1, source_target_pairs={{0,28},{1,29},{2,30},{3,31},{4,16},{5,17},{6,18},{7,19},{8,20},{9,... | collective-permute-start | bytes 294920 | tf_op jit(solution)/shard_map/ppermute | solution.py:229
  59.8 1.3 %collective-permute-start.20 = (f32[96,256]{1,0:T(8,128)S(1)}, f32[96,256]{1,0:T(8,128)S(1)}, u32[]{:S(2)}, u32[]{:S(2)}) collective-permute-start(f32[96,256]{1,0:T(8,128)S(1)} %shard_map.69), channel_id=1, source_target_pairs={{0,24},{1,25},{2,26},{3,27},{4,28},{5,29},{6,30},{7,31},{8,16},{9,... | collective-permute-start | bytes 294920 | tf_op jit(solution)/shard_map/ppermute | solution.py:229
  61.1 1.3 %collective-permute-start.19 = (f32[96,256]{1,0:T(8,128)S(1)}, f32[96,256]{1,0:T(8,128)S(1)}, u32[]{:S(2)}, u32[]{:S(2)}) collective-permute-start(f32[96,256]{1,0:T(8,128)S(1)} %shard_map.69), channel_id=1, source_target_pairs={{0,20},{1,21},{2,22},{3,23},{4,24},{5,25},{6,26},{7,27},{8,28},{9,... | collective-permute-start | bytes 294920 | tf_op jit(solution)/shard_map/ppermute | solution.py:229
  62.4 3.3 %collective-permute-done.21 = f32[96,256]{1,0:T(8,128)S(1)} collective-permute-done((f32[96,256]{1,0:T(8,128)S(1)}, f32[96,256]{1,0:T(8,128)S(1)}, u32[]{:S(2)}, u32[]{:S(2)}) %collective-permute-start.21) | collective-permute-done | bytes 98336 | tf_op jit(solution)/shard_map/ppermute | solution.py:229
  65.7 1.3 %collective-permute-start.18 = (f32[96,256]{1,0:T(8,128)S(1)}, f32[96,256]{1,0:T(8,128)S(1)}, u32[]{:S(2)}, u32[]{:S(2)}) collective-permute-start(f32[96,256]{1,0:T(8,128)S(1)} %shard_map.69), channel_id=1, source_target_pairs={{0,16},{1,17},{2,18},{3,19},{4,20},{5,21},{6,22},{7,23},{8,24},{9,... | collective-permute-start | bytes 294920 | tf_op jit(solution)/shard_map/ppermute | solution.py:229
  67.0 5.1 %collective-permute-done.20 = f32[96,256]{1,0:T(8,128)S(1)} collective-permute-done((f32[96,256]{1,0:T(8,128)S(1)}, f32[96,256]{1,0:T(8,128)S(1)}, u32[]{:S(2)}, u32[]{:S(2)}) %collective-permute-start.20) | collective-permute-done | bytes 98336 | tf_op jit(solution)/shard_map/ppermute | solution.py:229
  72.1 0.0 collective-permute-done.19
  72.1 2.4 %collective-permute-done.18 = f32[96,256]{1,0:T(8,128)S(1)} collective-permute-done((f32[96,256]{1,0:T(8,128)S(1)}, f32[96,256]{1,0:T(8,128)S(1)}, u32[]{:S(2)}, u32[]{:S(2)}) %collective-permute-start.18) | collective-permute-done | bytes 98336 | tf_op jit(solution)/shard_map/ppermute | solution.py:229
  74.5 0.0 collective-permute-done.3.refs_0_.refs_2_
  74.5 0.0 collective-permute-done.11.refs_1_.refs_3_
  74.6 0.7 collective-permute-start.23
  75.3 1.3 %collective-permute-start.15 = (f32[96,256]{1,0:T(8,128)S(1)}, f32[96,256]{1,0:T(8,128)S(1)}, u32[]{:S(2)}, u32[]{:S(2)}) collective-permute-start(f32[96,256]{1,0:T(8,128)S(1)} %shard_map.71), channel_id=1, source_target_pairs={{0,28},{1,29},{2,30},{3,31},{4,16},{5,17},{6,18},{7,19},{8,20},{9,... | collective-permute-start | bytes 294920 | tf_op jit(solution)/shard_map/ppermute | solution.py:229
  76.6 1.3 %collective-permute-start.14 = (f32[96,256]{1,0:T(8,128)S(1)}, f32[96,256]{1,0:T(8,128)S(1)}, u32[]{:S(2)}, u32[]{:S(2)}) collective-permute-start(f32[96,256]{1,0:T(8,128)S(1)} %shard_map.71), channel_id=1, source_target_pairs={{0,24},{1,25},{2,26},{3,27},{4,28},{5,29},{6,30},{7,31},{8,16},{9,... | collective-permute-start | bytes 294920 | tf_op jit(solution)/shard_map/ppermute | solution.py:229
  77.9 1.3 %collective-permute-start.13 = (f32[96,256]{1,0:T(8,128)S(1)}, f32[96,256]{1,0:T(8,128)S(1)}, u32[]{:S(2)}, u32[]{:S(2)}) collective-permute-start(f32[96,256]{1,0:T(8,128)S(1)} %shard_map.71), channel_id=1, source_target_pairs={{0,20},{1,21},{2,22},{3,23},{4,24},{5,25},{6,26},{7,27},{8,28},{9,... | collective-permute-start | bytes 294920 | tf_op jit(solution)/shard_map/ppermute | solution.py:229
  79.2 1.5 %collective-permute-start.12 = (f32[96,256]{1,0:T(8,128)S(1)}, f32[96,256]{1,0:T(8,128)S(1)}, u32[]{:S(2)}, u32[]{:S(2)}) collective-permute-start(f32[96,256]{1,0:T(8,128)S(1)} %shard_map.71), channel_id=1, source_target_pairs={{0,16},{1,17},{2,18},{3,19},{4,20},{5,21},{6,22},{7,23},{8,24},{9,... | collective-permute-start | bytes 294920 | tf_op jit(solution)/shard_map/ppermute | solution.py:229
  80.7 0.9 collective-permute-done.15
  81.5 1.9 %collective-permute-start.22 = (f32[4,96,256]{2,1,0:T(8,128)S(1)}, f32[4,96,256]{2,1,0:T(8,128)S(1)}, u32[]{:S(2)}, u32[]{:S(2)}) collective-permute-start(f32[4,96,256]{2,1,0:T(8,128)S(1)} %pad_maximum_fusion.3.refs_0_), channel_id=1, source_target_pairs={{0,1},{1,0},{2,3},{3,2},{4,5},{5,4},{6,7},{7,6},{8,9},{9,8},{10,11... | collective-permute-start | bytes 1179656 | tf_op jit(solution)/shard_map/ppermute | solution.py:227
  83.5 1.4 %collective-permute-done.23.refs_1_ = f32[4,96,256]{2,1,0:T(8,128)S(1)} collective-permute-done((f32[4,96,256]{2,1,0:T(8,128)S(1)}, f32[4,96,256]{2,1,0:T(8,128)S(1)}, u32[]{:S(2)}, u32[]{:S(2)}) %collective-permute-start.23) | collective-permute-done | bytes 393248 | tf_op jit(solution)/shard_map/ppermute | solution.py:227
  84.8 1.3 %collective-permute-start.24 = (f32[4,96,256]{2,1,0:T(8,128)S(1)}, f32[4,96,256]{2,1,0:T(8,128)S(1)}, u32[]{:S(2)}, u32[]{:S(2)}) collective-permute-start(f32[4,96,256]{2,1,0:T(8,128)S(1)} %collective-permute-done.23.refs_1_), channel_id=1, source_target_pairs={{0,1},{1,0},{2,3},{3,2},{4,5},{5,4},{6,7},{7,6},{8,9},{9,8},{10,11... | collective-permute-start | bytes 1179656 | tf_op jit(solution)/shard_map/ppermute | solution.py:227
  86.2 2.4 %collective-permute-done.14 = f32[96,256]{1,0:T(8,128)S(1)} collective-permute-done((f32[96,256]{1,0:T(8,128)S(1)}, f32[96,256]{1,0:T(8,128)S(1)}, u32[]{:S(2)}, u32[]{:S(2)}) %collective-permute-start.14) | collective-permute-done | bytes 98336 | tf_op jit(solution)/shard_map/ppermute | solution.py:229
  88.6 0.0 collective-permute-done.13
  88.6 0.9 collective-permute-done.12
  89.5 0.8 collective-permute-start.17
  90.3 1.4 %collective-permute-start.16 = (f32[4,96,256]{2,1,0:T(8,128)S(1)}, f32[4,96,256]{2,1,0:T(8,128)S(1)}, u32[]{:S(2)}, u32[]{:S(2)}) collective-permute-start(f32[4,96,256]{2,1,0:T(8,128)S(1)} %pad_maximum_fusion.2.refs_0_), channel_id=1, source_target_pairs={{0,1},{1,0},{2,3},{3,2},{4,5},{5,4},{6,7},{7,6},{8,9},{9,8},{10,11... | collective-permute-start | bytes 1179656 | tf_op jit(solution)/shard_map/ppermute | solution.py:227
  91.7 1.4 %shard_map.72.refs_6_ = f32[96,512]{1,0:T(8,128)S(1)} custom-call(f32[4,96,256]{2,1,0:T(8,128)S(1)} %pad_maximum_fusion.3.refs_0_, f32[4,96,256]{2,1,0:T(8,128)S(1)} %collective-permute-done.23.refs_1_, f32[4,96,256]{2,1,0:T(8,128)S(1)} %pad_maximum_fusion.1.refs_0_.refs_2_, f32[4,96,256]{2,1,0:T(8,128)S(1)} %collective-permute-done.9.refs_1_.refs_3_, ...), custom_call_target="tpu_custom_call" | custom-call | flops 603979776 | bytes 1048576 | tf_op jit(solution)/shard_map/pallas_call | solution.py:204
  93.2 0.0 collective-permute-done.22.refs_0_
  93.2 0.0 collective-permute-done.24.refs_1_
  93.2 1.4 %shard_map.73.refs_7_ = f32[96,256]{1,0:T(8,128)S(1)} custom-call(f32[4,96,256]{2,1,0:T(8,128)S(1)} %collective-permute-done.22.refs_0_, f32[4,96,256]{2,1,0:T(8,128)S(1)} %collective-permute-done.24.refs_1_, f32[4,96,256]{2,1,0:T(8,128)S(1)} %collective-permute-done.8.refs_0_.refs_2_, f32[4,96,256]{2,1,0:T(8,128)S(1)} %collective-permute-done.10.refs_1_.refs_3_, ...), custom_call_target="tpu_custom_call" | custom-call | flops 603979776 | bytes 1048576 | tf_op jit(solution)/shard_map/pallas_call | solution.py:204
  94.7 4.5 %collective-permute-done.17.refs_1_ = f32[4,96,256]{2,1,0:T(8,128)S(1)} collective-permute-done((f32[4,96,256]{2,1,0:T(8,128)S(1)}, f32[4,96,256]{2,1,0:T(8,128)S(1)}, u32[]{:S(2)}, u32[]{:S(2)}) %collective-permute-start.17) | collective-permute-done | bytes 393248 | tf_op jit(solution)/shard_map/ppermute | solution.py:227
  99.1 2.0 %collective-permute-start.25 = (f32[4,96,256]{2,1,0:T(8,128)S(1)}, f32[4,96,256]{2,1,0:T(8,128)S(1)}, u32[]{:S(2)}, u32[]{:S(2)}) collective-permute-start(f32[4,96,256]{2,1,0:T(8,128)S(1)} %collective-permute-done.17.refs_1_), channel_id=1, source_target_pairs={{0,1},{1,0},{2,3},{3,2},{4,5},{5,4},{6,7},{7,6},{8,9},{9,8},{10,11... | collective-permute-start | bytes 1179656 | tf_op jit(solution)/shard_map/ppermute | solution.py:227
  101.1 1.4 %shard_map.74.refs_6_ = f32[96,512]{1,0:T(8,128)S(1)} custom-call(f32[4,96,256]{2,1,0:T(8,128)S(1)} %pad_maximum_fusion.2.refs_0_, f32[4,96,256]{2,1,0:T(8,128)S(1)} %collective-permute-done.17.refs_1_, f32[4,96,256]{2,1,0:T(8,128)S(1)} %pad_maximum_fusion.refs_0_.refs_2_, f32[4,96,256]{2,1,0:T(8,128)S(1)} %collective-permute-done.4.refs_1_.refs_3_, ...), custom_call_target="tpu_custom_call" | custom-call | flops 603979776 | bytes 1048576 | tf_op jit(solution)/shard_map/pallas_call | solution.py:204
  102.6 0.0 collective-permute-done.16.refs_0_
  102.6 0.0 collective-permute-done.25.refs_1_
  102.6 2.1 %shard_map.75 = f32[192,256]{1,0:T(8,128)} custom-call(f32[4,96,256]{2,1,0:T(8,128)S(1)} %collective-permute-done.16.refs_0_, f32[4,96,256]{2,1,0:T(8,128)S(1)} %collective-permute-done.25.refs_1_, f32[4,96,256]{2,1,0:T(8,128)S(1)} %collective-permute-done.3.refs_0_.refs_2_, f32[4,96,256]{2,1,0:T(8,128)S(1)} %collective-permute-done.11.refs_1_.refs_3_, ...), custom_call_target="tpu_custom_call" | custom-call | flops 603979776 | bytes 1048576 | tf_op jit(solution)/shard_map/pallas_call | solution.py:204
  (11 shorter events, 0.1 us)
Async XLA Ops:
  21.7 0.9 copy-start.2
  23.4 7.0 %collective-permute-start.7 = (f32[96,256]{1,0:T(8,128)S(1)}, f32[96,256]{1,0:T(8,128)S(1)}, u32[]{:S(2)}, u32[]{:S(2)}) collective-permute-start(f32[96,256]{1,0:T(8,128)S(1)} %get-tuple-element.20), channel_id=1, source_target_pairs={{0,12},{1,13},{2,14},{3,15},{4,0},{5,1},{6,2},{7,3},{8,4},{9,5},{1... | collective-permute-start | bytes 294920 | tf_op jit(solution)/shard_map/ppermute | solution.py:227
  24.9 10.3 %collective-permute-start.6 = (f32[96,256]{1,0:T(8,128)S(1)}, f32[96,256]{1,0:T(8,128)S(1)}, u32[]{:S(2)}, u32[]{:S(2)}) collective-permute-start(f32[96,256]{1,0:T(8,128)S(1)} %get-tuple-element.20), channel_id=1, source_target_pairs={{0,8},{1,9},{2,10},{3,11},{4,12},{5,13},{6,14},{7,15},{8,0},{9,1},... | collective-permute-start | bytes 294920 | tf_op jit(solution)/shard_map/ppermute | solution.py:227
  25.8 9.4 %collective-permute-start.5 = (f32[96,256]{1,0:T(8,128)S(1)}, f32[96,256]{1,0:T(8,128)S(1)}, u32[]{:S(2)}, u32[]{:S(2)}) collective-permute-start(f32[96,256]{1,0:T(8,128)S(1)} %get-tuple-element.20), channel_id=1, source_target_pairs={{0,4},{1,5},{2,6},{3,7},{4,8},{5,9},{6,10},{7,11},{8,12},{9,13},{1... | collective-permute-start | bytes 294920 | tf_op jit(solution)/shard_map/ppermute | solution.py:227
  26.1 3.4 %copy-start = (f32[2,256,4096]{2,1,0:T(8,128)S(1)}, f32[2,256,4096]{2,1,0:T(8,128)}, u32[]{:S(2)}) copy-start(f32[2,256,4096]{2,1,0:T(8,128)} %matrix_ref) | copy-start | bytes 25165828
  29.4 11.0 %copy-start.1 = (f32[2,256,4096]{2,1,0:T(8,128)S(1)}, f32[2,256,4096]{2,1,0:T(8,128)}, u32[]{:S(2)}) copy-start(f32[2,256,4096]{2,1,0:T(8,128)} %matrix_ref.1) | copy-start | bytes 25165828
  35.2 10.1 %collective-permute-start.9 = (f32[4,96,256]{2,1,0:T(8,128)S(1)}, f32[4,96,256]{2,1,0:T(8,128)S(1)}, u32[]{:S(2)}, u32[]{:S(2)}) collective-permute-start(f32[4,96,256]{2,1,0:T(8,128)S(1)} %pad_maximum_fusion.1.refs_0_.refs_2_), channel_id=1, source_target_pairs={{0,2},{1,3},{2,0},{3,1},{4,6},{5,7},{6,4},{7,5},{8,10},{9,11},{10,... | collective-permute-start | bytes 1179656 | tf_op jit(solution)/shard_map/ppermute | solution.py:227
  35.9 10.9 %collective-permute-start.2 = (f32[96,256]{1,0:T(8,128)S(1)}, f32[96,256]{1,0:T(8,128)S(1)}, u32[]{:S(2)}, u32[]{:S(2)}) collective-permute-start(f32[96,256]{1,0:T(8,128)S(1)} %get-tuple-element.24), channel_id=1, source_target_pairs={{0,12},{1,13},{2,14},{3,15},{4,0},{5,1},{6,2},{7,3},{8,4},{9,5},{1... | collective-permute-start | bytes 294920 | tf_op jit(solution)/shard_map/ppermute | solution.py:227
  36.0 10.9 %collective-permute-start.1 = (f32[96,256]{1,0:T(8,128)S(1)}, f32[96,256]{1,0:T(8,128)S(1)}, u32[]{:S(2)}, u32[]{:S(2)}) collective-permute-start(f32[96,256]{1,0:T(8,128)S(1)} %get-tuple-element.24), channel_id=1, source_target_pairs={{0,8},{1,9},{2,10},{3,11},{4,12},{5,13},{6,14},{7,15},{8,0},{9,1},... | collective-permute-start | bytes 294920 | tf_op jit(solution)/shard_map/ppermute | solution.py:227
  37.0 9.9 %collective-permute-start = (f32[96,256]{1,0:T(8,128)S(1)}, f32[96,256]{1,0:T(8,128)S(1)}, u32[]{:S(2)}, u32[]{:S(2)}) collective-permute-start(f32[96,256]{1,0:T(8,128)S(1)} %get-tuple-element.24), channel_id=1, source_target_pairs={{0,4},{1,5},{2,6},{3,7},{4,8},{5,9},{6,10},{7,11},{8,12},{9,13},{1... | collective-permute-start | bytes 294920 | tf_op jit(solution)/shard_map/ppermute | solution.py:227
  38.4 10.4 %collective-permute-start.8 = (f32[4,96,256]{2,1,0:T(8,128)S(1)}, f32[4,96,256]{2,1,0:T(8,128)S(1)}, u32[]{:S(2)}, u32[]{:S(2)}) collective-permute-start(f32[4,96,256]{2,1,0:T(8,128)S(1)} %pad_maximum_fusion.1.refs_0_.refs_2_), channel_id=1, source_target_pairs={{0,1},{1,0},{2,3},{3,2},{4,5},{5,4},{6,7},{7,6},{8,9},{9,8},{10,11... | collective-permute-start | bytes 1179656 | tf_op jit(solution)/shard_map/ppermute | solution.py:227
  45.3 3.5 %collective-permute-start.10 = (f32[4,96,256]{2,1,0:T(8,128)S(1)}, f32[4,96,256]{2,1,0:T(8,128)S(1)}, u32[]{:S(2)}, u32[]{:S(2)}) collective-permute-start(f32[4,96,256]{2,1,0:T(8,128)S(1)} %collective-permute-done.9.refs_1_.refs_3_), channel_id=1, source_target_pairs={{0,1},{1,0},{2,3},{3,2},{4,5},{5,4},{6,7},{7,6},{8,9},{9,8},{10,11... | collective-permute-start | bytes 1179656 | tf_op jit(solution)/shard_map/ppermute | solution.py:227
  46.9 10.3 %collective-permute-start.4 = (f32[4,96,256]{2,1,0:T(8,128)S(1)}, f32[4,96,256]{2,1,0:T(8,128)S(1)}, u32[]{:S(2)}, u32[]{:S(2)}) collective-permute-start(f32[4,96,256]{2,1,0:T(8,128)S(1)} %pad_maximum_fusion.refs_0_.refs_2_), channel_id=1, source_target_pairs={{0,2},{1,3},{2,0},{3,1},{4,6},{5,7},{6,4},{7,5},{8,10},{9,11},{10,... | collective-permute-start | bytes 1179656 | tf_op jit(solution)/shard_map/ppermute | solution.py:227
  47.6 26.9 %collective-permute-start.3 = (f32[4,96,256]{2,1,0:T(8,128)S(1)}, f32[4,96,256]{2,1,0:T(8,128)S(1)}, u32[]{:S(2)}, u32[]{:S(2)}) collective-permute-start(f32[4,96,256]{2,1,0:T(8,128)S(1)} %pad_maximum_fusion.refs_0_.refs_2_), channel_id=1, source_target_pairs={{0,1},{1,0},{2,3},{3,2},{4,5},{5,4},{6,7},{7,6},{8,9},{9,8},{10,11... | collective-permute-start | bytes 1179656 | tf_op jit(solution)/shard_map/ppermute | solution.py:227
  57.2 17.4 %collective-permute-start.11 = (f32[4,96,256]{2,1,0:T(8,128)S(1)}, f32[4,96,256]{2,1,0:T(8,128)S(1)}, u32[]{:S(2)}, u32[]{:S(2)}) collective-permute-start(f32[4,96,256]{2,1,0:T(8,128)S(1)} %collective-permute-done.4.refs_1_.refs_3_), channel_id=1, source_target_pairs={{0,1},{1,0},{2,3},{3,2},{4,5},{5,4},{6,7},{7,6},{8,9},{9,8},{10,11... | collective-permute-start | bytes 1179656 | tf_op jit(solution)/shard_map/ppermute | solution.py:227
  58.5 7.2 %collective-permute-start.21 = (f32[96,256]{1,0:T(8,128)S(1)}, f32[96,256]{1,0:T(8,128)S(1)}, u32[]{:S(2)}, u32[]{:S(2)}) collective-permute-start(f32[96,256]{1,0:T(8,128)S(1)} %shard_map.69), channel_id=1, source_target_pairs={{0,28},{1,29},{2,30},{3,31},{4,16},{5,17},{6,18},{7,19},{8,20},{9,... | collective-permute-start | bytes 294920 | tf_op jit(solution)/shard_map/ppermute | solution.py:229
  59.8 12.3 %collective-permute-start.20 = (f32[96,256]{1,0:T(8,128)S(1)}, f32[96,256]{1,0:T(8,128)S(1)}, u32[]{:S(2)}, u32[]{:S(2)}) collective-permute-start(f32[96,256]{1,0:T(8,128)S(1)} %shard_map.69), channel_id=1, source_target_pairs={{0,24},{1,25},{2,26},{3,27},{4,28},{5,29},{6,30},{7,31},{8,16},{9,... | collective-permute-start | bytes 294920 | tf_op jit(solution)/shard_map/ppermute | solution.py:229
  61.1 11.0 %collective-permute-start.19 = (f32[96,256]{1,0:T(8,128)S(1)}, f32[96,256]{1,0:T(8,128)S(1)}, u32[]{:S(2)}, u32[]{:S(2)}) collective-permute-start(f32[96,256]{1,0:T(8,128)S(1)} %shard_map.69), channel_id=1, source_target_pairs={{0,20},{1,21},{2,22},{3,23},{4,24},{5,25},{6,26},{7,27},{8,28},{9,... | collective-permute-start | bytes 294920 | tf_op jit(solution)/shard_map/ppermute | solution.py:229
  65.7 8.8 %collective-permute-start.18 = (f32[96,256]{1,0:T(8,128)S(1)}, f32[96,256]{1,0:T(8,128)S(1)}, u32[]{:S(2)}, u32[]{:S(2)}) collective-permute-start(f32[96,256]{1,0:T(8,128)S(1)} %shard_map.69), channel_id=1, source_target_pairs={{0,16},{1,17},{2,18},{3,19},{4,20},{5,21},{6,22},{7,23},{8,24},{9,... | collective-permute-start | bytes 294920 | tf_op jit(solution)/shard_map/ppermute | solution.py:229
  74.6 10.3 %collective-permute-start.23 = (f32[4,96,256]{2,1,0:T(8,128)S(1)}, f32[4,96,256]{2,1,0:T(8,128)S(1)}, u32[]{:S(2)}, u32[]{:S(2)}) collective-permute-start(f32[4,96,256]{2,1,0:T(8,128)S(1)} %pad_maximum_fusion.3.refs_0_), channel_id=1, source_target_pairs={{0,2},{1,3},{2,0},{3,1},{4,6},{5,7},{6,4},{7,5},{8,10},{9,11},{10,... | collective-permute-start | bytes 1179656 | tf_op jit(solution)/shard_map/ppermute | solution.py:227
  75.3 6.2 %collective-permute-start.15 = (f32[96,256]{1,0:T(8,128)S(1)}, f32[96,256]{1,0:T(8,128)S(1)}, u32[]{:S(2)}, u32[]{:S(2)}) collective-permute-start(f32[96,256]{1,0:T(8,128)S(1)} %shard_map.71), channel_id=1, source_target_pairs={{0,28},{1,29},{2,30},{3,31},{4,16},{5,17},{6,18},{7,19},{8,20},{9,... | collective-permute-start | bytes 294920 | tf_op jit(solution)/shard_map/ppermute | solution.py:229
  76.6 12.0 %collective-permute-start.14 = (f32[96,256]{1,0:T(8,128)S(1)}, f32[96,256]{1,0:T(8,128)S(1)}, u32[]{:S(2)}, u32[]{:S(2)}) collective-permute-start(f32[96,256]{1,0:T(8,128)S(1)} %shard_map.71), channel_id=1, source_target_pairs={{0,24},{1,25},{2,26},{3,27},{4,28},{5,29},{6,30},{7,31},{8,16},{9,... | collective-permute-start | bytes 294920 | tf_op jit(solution)/shard_map/ppermute | solution.py:229
  77.9 10.7 %collective-permute-start.13 = (f32[96,256]{1,0:T(8,128)S(1)}, f32[96,256]{1,0:T(8,128)S(1)}, u32[]{:S(2)}, u32[]{:S(2)}) collective-permute-start(f32[96,256]{1,0:T(8,128)S(1)} %shard_map.71), channel_id=1, source_target_pairs={{0,20},{1,21},{2,22},{3,23},{4,24},{5,25},{6,26},{7,27},{8,28},{9,... | collective-permute-start | bytes 294920 | tf_op jit(solution)/shard_map/ppermute | solution.py:229
  79.2 10.3 %collective-permute-start.12 = (f32[96,256]{1,0:T(8,128)S(1)}, f32[96,256]{1,0:T(8,128)S(1)}, u32[]{:S(2)}, u32[]{:S(2)}) collective-permute-start(f32[96,256]{1,0:T(8,128)S(1)} %shard_map.71), channel_id=1, source_target_pairs={{0,16},{1,17},{2,18},{3,19},{4,20},{5,21},{6,22},{7,23},{8,24},{9,... | collective-permute-start | bytes 294920 | tf_op jit(solution)/shard_map/ppermute | solution.py:229
  81.5 11.7 %collective-permute-start.22 = (f32[4,96,256]{2,1,0:T(8,128)S(1)}, f32[4,96,256]{2,1,0:T(8,128)S(1)}, u32[]{:S(2)}, u32[]{:S(2)}) collective-permute-start(f32[4,96,256]{2,1,0:T(8,128)S(1)} %pad_maximum_fusion.3.refs_0_), channel_id=1, source_target_pairs={{0,1},{1,0},{2,3},{3,2},{4,5},{5,4},{6,7},{7,6},{8,9},{9,8},{10,11... | collective-permute-start | bytes 1179656 | tf_op jit(solution)/shard_map/ppermute | solution.py:227
  84.8 8.4 %collective-permute-start.24 = (f32[4,96,256]{2,1,0:T(8,128)S(1)}, f32[4,96,256]{2,1,0:T(8,128)S(1)}, u32[]{:S(2)}, u32[]{:S(2)}) collective-permute-start(f32[4,96,256]{2,1,0:T(8,128)S(1)} %collective-permute-done.23.refs_1_), channel_id=1, source_target_pairs={{0,1},{1,0},{2,3},{3,2},{4,5},{5,4},{6,7},{7,6},{8,9},{9,8},{10,11... | collective-permute-start | bytes 1179656 | tf_op jit(solution)/shard_map/ppermute | solution.py:227
  89.5 9.6 %collective-permute-start.17 = (f32[4,96,256]{2,1,0:T(8,128)S(1)}, f32[4,96,256]{2,1,0:T(8,128)S(1)}, u32[]{:S(2)}, u32[]{:S(2)}) collective-permute-start(f32[4,96,256]{2,1,0:T(8,128)S(1)} %pad_maximum_fusion.2.refs_0_), channel_id=1, source_target_pairs={{0,2},{1,3},{2,0},{3,1},{4,6},{5,7},{6,4},{7,5},{8,10},{9,11},{10,... | collective-permute-start | bytes 1179656 | tf_op jit(solution)/shard_map/ppermute | solution.py:227
  90.3 12.3 %collective-permute-start.16 = (f32[4,96,256]{2,1,0:T(8,128)S(1)}, f32[4,96,256]{2,1,0:T(8,128)S(1)}, u32[]{:S(2)}, u32[]{:S(2)}) collective-permute-start(f32[4,96,256]{2,1,0:T(8,128)S(1)} %pad_maximum_fusion.2.refs_0_), channel_id=1, source_target_pairs={{0,1},{1,0},{2,3},{3,2},{4,5},{5,4},{6,7},{7,6},{8,9},{9,8},{10,11... | collective-permute-start | bytes 1179656 | tf_op jit(solution)/shard_map/ppermute | solution.py:227
  99.1 3.5 %collective-permute-start.25 = (f32[4,96,256]{2,1,0:T(8,128)S(1)}, f32[4,96,256]{2,1,0:T(8,128)S(1)}, u32[]{:S(2)}, u32[]{:S(2)}) collective-permute-start(f32[4,96,256]{2,1,0:T(8,128)S(1)} %collective-permute-done.17.refs_1_), channel_id=1, source_target_pairs={{0,1},{1,0},{2,3},{3,2},{4,5},{5,4},{6,7},{7,6},{8,9},{9,8},{10,11... | collective-permute-start | bytes 1179656 | tf_op jit(solution)/shard_map/ppermute | solution.py:227

commit v11 on v9

--- a/solution.py
+++ b/solution.py
@@ -236,10 +236,8 @@
         return lax.ppermute(value, ("chain", "tile"), pairs)
 
     def first_stage(first, second, hop):
+        pair = [second if across == 0 and not hop else send(second, hop, lambda t: t ^ (2 * across)) for across in range(2)]
         line = [first if by == 0 and not hop else send(first, hop, lambda t: (t + 4 * by) % tile_size) for by in range(layers)]
-        if hop:
-            second, line[-1] = lax.optimization_barrier((send(second, True, lambda t: t), line[-1]))
-        pair = [second, send(second, False, lambda t: t ^ 2)]
         return jnp.stack(pair), jnp.stack(line)
 
     def second_stage(pair, line):

time: 98.7 us -> 95.4 us (0.967)
  waiting for transfers between devices: 41.1 us -> 35 us
  starting transfers between devices: 19.9 us -> 22.7 us
    ppermute x19 -> x18, waiting for transfers between devices: 30 us -> 26.2 us  [send(): lax.ppermute(value, 'tile', [(t, target(t)) for t in range(tile_size)])]
    ppermute x5 -> x6, starting transfers between devices: 5.25 us -> 7.81 us  [send(): return lax.ppermute(value, ('chain', 'tile'), pairs)]
    ppermute x5 -> x6, waiting for transfers between devices: 11.1 us -> 8.78 us  [send(): return lax.ppermute(value, ('chain', 'tile'), pairs)]
    ppermute x19 -> x18, starting transfers between devices: 14.7 us -> 14.9 us  [send(): lax.ppermute(value, 'tile', [(t, target(t)) for t in range(tile_size)])]
  transfers between devices with their start and end apart: 24 -> 24, of which waited for: 9 -> 10; matrix products, arithmetic and copies ran while one was open for 0% -> 0% of each run, Pallas kernels for 5% -> 6%
where the time goes in v11:
time: 95.4 us; the launch traced here: 95.1 us
  waiting for transfers between devices  35 us (37%)
  starting transfers between devices  22.7 us (24%)
  blocking collectives  20.6 us (22%)
  Pallas kernels  12.1 us (13%)
  local copies, waits for them, and re-layouts  4.31 us (5%)
    ppermute x18, waiting for transfers between devices, send(): lax.ppermute(value, 'tile', [(t, target(t)) for t in range(tile_size)])  26.2 us
    all_to_all x1, blocking collectives, body(): received = lax.all_to_all(packed, 'tile', 0, 0, tiled=False)  20.6 us
    ppermute x18, starting transfers between devices, send(): lax.ppermute(value, 'tile', [(t, target(t)) for t in range(tile_size)])  14.9 us
    ppermute x6, waiting for transfers between devices, send(): return lax.ppermute(value, ('chain', 'tile'), pairs)  8.78 us
    ppermute x6, starting transfers between devices, send(): return lax.ppermute(value, ('chain', 'tile'), pairs)  7.81 us
    pallas_call x4, Pallas kernels, product_part(): pl.pallas_call(functools.partial(product_kernel, sources, layout, len(blo...  7.19 us
    unnamed x6, local copies, waits for them, and re-layouts  4.31 us
    pallas_call x1, Pallas kernels, body(): pl.pallas_call(functools.partial(pack_kernel, own_rows, cap, tile_rows),...  2.19 us
  transfers between devices with their start and end apart: 24, of which 10 were waited for; matrix products, arithmetic and copies ran while one was open for 0% of the time, Pallas kernels for 6%

profile of v11, /device:TPU:0, one launch (start us, length us, event | category | flops | bytes accessed | tf_op | source)
XLA Modules:
  0.0 95.1 jit_solution(2921663687801785832)
XLA Ops:
  0.0 2.2 %shard_map.64 = f32[16,56,128]{2,1,0:T(8,128)} custom-call(s32[2]{0:T(128)} %counts_hbm.1, s32[1,256]{1,0:T(1,128)} %bitcast.46, f32[192,256]{1,0:T(8,128)} %bitcast.29), custom_call_target="tpu_custom_call" | custom-call | tf_op jit(solution)/shard_map/pallas_call | solution.py:311
  2.2 20.6 %all_to_all.5.received_ref = f32[16,56,128]{2,1,0:T(8,128)S(1)} all-to-all(f32[16,56,128]{2,1,0:T(8,128)} %shard_map.64), channel_id=1, replica_groups=mesh['chain'=2,'tile'=16] {'tile'}, dimensions={0} | all-to-all | bytes 917504 | tf_op jit(solution)/shard_map/all_to_all | solution.py:324
  22.9 0.0 copy-start.2
  22.9 0.9 copy-done.2
  23.8 0.8 shard_map.65
  24.5 0.4 collective-permute-start
  25.0 2.7 %collective-permute-start.3 = (f32[128,256]{1,0:T(8,128)S(1)}, f32[128,256]{1,0:T(8,128)S(1)}, u32[]{:S(2)}, u32[]{:S(2)}) collective-permute-start(f32[128,256]{1,0:T(8,128)S(1)} %get-tuple-element.26), channel_id=1, source_target_pairs={{0,12},{1,13},{2,14},{3,15},{4,0},{5,1},{6,2},{7,3},{8,4},{9,5},{1... | collective-permute-start | bytes 393224 | tf_op jit(solution)/shard_map/ppermute | solution.py:234
  27.7 0.5 collective-permute-start.2
  28.2 0.5 collective-permute-start.1
  28.8 0.0 copy-start
  28.8 3.4 %copy-done = f32[2,256,4096]{2,1,0:T(8,128)S(1)} copy-done((f32[2,256,4096]{2,1,0:T(8,128)S(1)}, f32[2,256,4096]{2,1,0:T(8,128)}, u32[]{:S(2)}) %copy-start) | copy-done | bytes 8388632
  32.2 0.0 copy-start.1
  32.2 1.0 %shard_map.66 = (bf16[4,512,1024]{2,1,0:T(8,128)(2,1)S(1)}, bf16[4,512,1024]{2,1,0:T(8,128)(2,1)S(1)}) custom-call(f32[2,256,4096]{2,1,0:T(8,128)S(1)} %copy-done), custom_call_target="tpu_custom_call" | custom-call | flops 6291456 | bytes 16777216 | tf_op jit(solution)/shard_map/pallas_call | solution.py:132
  33.1 0.0 collective-permute-done
  33.2 0.0 collective-permute-done.3
  33.2 6.9 %collective-permute-done.2 = f32[128,256]{1,0:T(8,128)S(1)} collective-permute-done((f32[128,256]{1,0:T(8,128)S(1)}, f32[128,256]{1,0:T(8,128)S(1)}, u32[]{:S(2)}, u32[]{:S(2)}) %collective-permute-start.2) | collective-permute-done | bytes 131104 | tf_op jit(solution)/shard_map/ppermute | solution.py:234
  40.1 0.0 collective-permute-done.1
  40.1 1.2 %collective-permute-start.5 = (f32[4,128,256]{2,1,0:T(8,128)S(1)}, f32[4,128,256]{2,1,0:T(8,128)S(1)}, u32[]{:S(2)}, u32[]{:S(2)}) collective-permute-start(f32[4,128,256]{2,1,0:T(8,128)S(1)} %pad_maximum_fusion.refs_0_.refs_3_), channel_id=1, source_target_pairs={{0,2},{1,3},{2,0},{3,1},{4,6},{5,7},{6,4},{7,5},{8,10},{9,11},{10,... | collective-permute-start | bytes 1572872 | tf_op jit(solution)/shard_map/ppermute | solution.py:234
  41.3 0.0 collective-permute-start.8
  41.3 1.8 %collective-permute-start.7 = (f32[2,64,256]{2,1,0:T(8,128)S(1)}, f32[2,64,256]{2,1,0:T(8,128)S(1)}, u32[]{:S(2)}, u32[]{:S(2)}) collective-permute-start(f32[2,64,256]{2,1,0:T(8,128)S(1)} %pad_maximum_fusion.4), channel_id=1, source_target_pairs={{0,8},{1,9},{2,10},{3,11},{4,12},{5,13},{6,14},{7,15},{8,0},{9,1},... | collective-permute-start | bytes 393224 | tf_op jit(solution)/shard_map/ppermute | solution.py:234
  43.1 2.0 %collective-permute-start.6 = (f32[2,64,256]{2,1,0:T(8,128)S(1)}, f32[2,64,256]{2,1,0:T(8,128)S(1)}, u32[]{:S(2)}, u32[]{:S(2)}) collective-permute-start(f32[2,64,256]{2,1,0:T(8,128)S(1)} %pad_maximum_fusion.4), channel_id=1, source_target_pairs={{0,4},{1,5},{2,6},{3,7},{4,8},{5,9},{6,10},{7,11},{8,12},{9,13},{1... | collective-permute-start | bytes 393224 | tf_op jit(solution)/shard_map/ppermute | solution.py:234
  45.1 0.0 collective-permute-start.4
  45.1 0.0 copy-done.1
  45.1 1.0 %shard_map.67 = (bf16[4,512,1024]{2,1,0:T(8,128)(2,1)S(1)}, bf16[4,512,1024]{2,1,0:T(8,128)(2,1)S(1)}) custom-call(f32[2,256,4096]{2,1,0:T(8,128)S(1)} %copy-done.1), custom_call_target="tpu_custom_call" | custom-call | flops 6291456 | bytes 16777216 | tf_op jit(solution)/shard_map/pallas_call | solution.py:132
  46.1 0.8 collective-permute-done.8
  46.9 8.0 %collective-permute-done.7 = f32[2,64,256]{2,1,0:T(8,128)S(1)} collective-permute-done((f32[2,64,256]{2,1,0:T(8,128)S(1)}, f32[2,64,256]{2,1,0:T(8,128)S(1)}, u32[]{:S(2)}, u32[]{:S(2)}) %collective-permute-start.7) | collective-permute-done | bytes 131104 | tf_op jit(solution)/shard_map/ppermute | solution.py:234
  54.8 0.0 collective-permute-done.6
  54.9 0.0 collective-permute-done.5.refs_1_.refs_4_
  54.9 0.1 collective-permute-start.9
  55.0 0.5 collective-permute-start.10
  55.5 1.7 %shard_map.68.refs_5_ = f32[192,512]{1,0:T(8,128)S(1)} custom-call(f32[4,128,256]{2,1,0:T(8,128)S(1)} %pad_maximum_fusion.refs_0_.refs_3_, f32[4,128,256]{2,1,0:T(8,128)S(1)} %collective-permute-done.5.refs_1_.refs_4_, f32[4,2,64,256]{3,2,1,0:T(8,128)S(1)} %pad_maximum_fusion.1.refs_2_.refs_5_, bf16[4,512,1024]{2,1,0:T(8,128)(2,1)S(1)} %get-tuple-element.37.refs_3_, ...), custom_call_target="tpu_custom_call" | custom-call | flops 1207959552 | bytes 1048576 | tf_op jit(solution)/shard_map/pallas_call | solution.py:210
  57.1 0.0 collective-permute-done.4.refs_0_.refs_3_
  57.1 0.0 collective-permute-done.9.refs_1_.refs_4_
  57.1 0.5 collective-permute-done.10.refs_2_.refs_5_
  57.6 1.6 %shard_map.69 = (f32[128,256]{1,0:T(8,128)S(1)}, f32[64,256]{1,0:T(8,128)S(1)}) custom-call(f32[4,128,256]{2,1,0:T(8,128)S(1)} %collective-permute-done.4.refs_0_.refs_3_, f32[4,128,256]{2,1,0:T(8,128)S(1)} %collective-permute-done.9.refs_1_.refs_4_, f32[4,2,64,256]{3,2,1,0:T(8,128)S(1)} %collective-permute-done.10.refs_2_.refs_5_, ...), custom_call_target="tpu_custom_call" | custom-call | flops 1207959552 | bytes 1048576 | tf_op jit(solution)/shard_map/pallas_call | solution.py:210
  59.2 0.1 collective-permute-start.12
  59.3 1.8 %collective-permute-start.11 = (f32[64,256]{1,0:T(8,128)S(1)}, f32[64,256]{1,0:T(8,128)S(1)}, u32[]{:S(2)}, u32[]{:S(2)}) collective-permute-start(f32[64,256]{1,0:T(8,128)S(1)} %get-tuple-element.39), channel_id=1, source_target_pairs={{0,16},{1,17},{2,18},{3,19},{4,20},{5,21},{6,22},{7,23},{8,24},{9,... | collective-permute-start | bytes 196616 | tf_op jit(solution)/shard_map/ppermute | solution.py:236
  61.1 0.0 collective-permute-start.16
  61.1 2.0 %collective-permute-start.15 = (f32[128,256]{1,0:T(8,128)S(1)}, f32[128,256]{1,0:T(8,128)S(1)}, u32[]{:S(2)}, u32[]{:S(2)}) collective-permute-start(f32[128,256]{1,0:T(8,128)S(1)} %get-tuple-element.40), channel_id=1, source_target_pairs={{0,24},{1,25},{2,26},{3,27},{4,28},{5,29},{6,30},{7,31},{8,16},{9,... | collective-permute-start | bytes 393224 | tf_op jit(solution)/shard_map/ppermute | solution.py:236
  63.1 1.9 %collective-permute-start.14 = (f32[128,256]{1,0:T(8,128)S(1)}, f32[128,256]{1,0:T(8,128)S(1)}, u32[]{:S(2)}, u32[]{:S(2)}) collective-permute-start(f32[128,256]{1,0:T(8,128)S(1)} %get-tuple-element.40), channel_id=1, source_target_pairs={{0,20},{1,21},{2,22},{3,23},{4,24},{5,25},{6,26},{7,27},{8,28},{9,... | collective-permute-start | bytes 393224 | tf_op jit(solution)/shard_map/ppermute | solution.py:236
  65.0 0.0 collective-permute-done.12
  65.0 2.0 %collective-permute-start.13 = (f32[128,256]{1,0:T(8,128)S(1)}, f32[128,256]{1,0:T(8,128)S(1)}, u32[]{:S(2)}, u32[]{:S(2)}) collective-permute-start(f32[128,256]{1,0:T(8,128)S(1)} %get-tuple-element.40), channel_id=1, source_target_pairs={{0,16},{1,17},{2,18},{3,19},{4,20},{5,21},{6,22},{7,23},{8,24},{9,... | collective-permute-start | bytes 393224 | tf_op jit(solution)/shard_map/ppermute | solution.py:236
  67.0 2.8 %collective-permute-done.11 = f32[64,256]{1,0:T(8,128)S(1)} collective-permute-done((f32[64,256]{1,0:T(8,128)S(1)}, f32[64,256]{1,0:T(8,128)S(1)}, u32[]{:S(2)}, u32[]{:S(2)}) %collective-permute-start.11) | collective-permute-done | bytes 65568 | tf_op jit(solution)/shard_map/ppermute | solution.py:236
  69.9 0.0 collective-permute-done.16
  69.9 4.7 %collective-permute-done.15 = f32[128,256]{1,0:T(8,128)S(1)} collective-permute-done((f32[128,256]{1,0:T(8,128)S(1)}, f32[128,256]{1,0:T(8,128)S(1)}, u32[]{:S(2)}, u32[]{:S(2)}) %collective-permute-start.15) | collective-permute-done | bytes 131104 | tf_op jit(solution)/shard_map/ppermute | solution.py:236
  74.6 0.0 collective-permute-done.14
  74.6 1.3 %collective-permute-done.13 = f32[128,256]{1,0:T(8,128)S(1)} collective-permute-done((f32[128,256]{1,0:T(8,128)S(1)}, f32[128,256]{1,0:T(8,128)S(1)}, u32[]{:S(2)}, u32[]{:S(2)}) %collective-permute-start.13) | collective-permute-done | bytes 131104 | tf_op jit(solution)/shard_map/ppermute | solution.py:236
  75.9 1.7 %collective-permute-start.18 = (f32[4,128,256]{2,1,0:T(8,128)S(1)}, f32[4,128,256]{2,1,0:T(8,128)S(1)}, u32[]{:S(2)}, u32[]{:S(2)}) collective-permute-start(f32[4,128,256]{2,1,0:T(8,128)S(1)} %pad_maximum_fusion.2.refs_0_), channel_id=1, source_target_pairs={{0,2},{1,3},{2,0},{3,1},{4,6},{5,7},{6,4},{7,5},{8,10},{9,11},{10,... | collective-permute-start | bytes 1572872 | tf_op jit(solution)/shard_map/ppermute | solution.py:234
  77.6 1.1 %collective-permute-start.22 = (f32[2,64,256]{2,1,0:T(8,128)S(1)}, f32[2,64,256]{2,1,0:T(8,128)S(1)}, u32[]{:S(2)}, u32[]{:S(2)}) collective-permute-start(f32[2,64,256]{2,1,0:T(8,128)S(1)} %pad_maximum_fusion.5), channel_id=1, source_target_pairs={{0,12},{1,13},{2,14},{3,15},{4,0},{5,1},{6,2},{7,3},{8,4},{9,5},{1... | collective-permute-start | bytes 393224 | tf_op jit(solution)/shard_map/ppermute | solution.py:234
  78.8 0.0 collective-permute-start.21
  78.8 1.7 %collective-permute-start.20 = (f32[2,64,256]{2,1,0:T(8,128)S(1)}, f32[2,64,256]{2,1,0:T(8,128)S(1)}, u32[]{:S(2)}, u32[]{:S(2)}) collective-permute-start(f32[2,64,256]{2,1,0:T(8,128)S(1)} %pad_maximum_fusion.5), channel_id=1, source_target_pairs={{0,4},{1,5},{2,6},{3,7},{4,8},{5,9},{6,10},{7,11},{8,12},{9,13},{1... | collective-permute-start | bytes 393224 | tf_op jit(solution)/shard_map/ppermute | solution.py:234
  80.4 0.0 collective-permute-start.17
  80.4 3.3 %collective-permute-done.22 = f32[2,64,256]{2,1,0:T(8,128)S(1)} collective-permute-done((f32[2,64,256]{2,1,0:T(8,128)S(1)}, f32[2,64,256]{2,1,0:T(8,128)S(1)}, u32[]{:S(2)}, u32[]{:S(2)}) %collective-permute-start.22) | collective-permute-done | bytes 131104 | tf_op jit(solution)/shard_map/ppermute | solution.py:234
  83.7 6.3 %collective-permute-done.21 = f32[2,64,256]{2,1,0:T(8,128)S(1)} collective-permute-done((f32[2,64,256]{2,1,0:T(8,128)S(1)}, f32[2,64,256]{2,1,0:T(8,128)S(1)}, u32[]{:S(2)}, u32[]{:S(2)}) %collective-permute-start.21) | collective-permute-done | bytes 131104 | tf_op jit(solution)/shard_map/ppermute | solution.py:234
  90.0 0.0 collective-permute-done.20
  90.1 0.1 collective-permute-start.23
  90.2 0.0 collective-permute-done.18.refs_1_
  90.2 0.5 collective-permute-start.19
  90.7 1.7 %shard_map.70.refs_8_ = f32[192,512]{1,0:T(8,128)S(1)} custom-call(f32[4,128,256]{2,1,0:T(8,128)S(1)} %pad_maximum_fusion.2.refs_0_, f32[4,128,256]{2,1,0:T(8,128)S(1)} %collective-permute-done.18.refs_1_, f32[4,2,64,256]{3,2,1,0:T(8,128)S(1)} %pad_maximum_fusion.3.refs_2_, f32[4,128,256]{2,1,0:T(8,128)S(1)} %pad_maximum_fusion.refs_0_.refs_3_, ...), custom_call_target="tpu_custom_call" | custom-call | flops 1207959552 | bytes 1048576 | tf_op jit(solution)/shard_map/pallas_call | solution.py:210
  92.3 0.0 collective-permute-done.17.refs_0_
  92.3 0.0 collective-permute-done.23.refs_2_
  92.3 0.5 collective-permute-done.19.refs_1_
  92.8 2.3 %shard_map.71 = f32[192,256]{1,0:T(8,128)} custom-call(f32[4,128,256]{2,1,0:T(8,128)S(1)} %collective-permute-done.17.refs_0_, f32[4,128,256]{2,1,0:T(8,128)S(1)} %collective-permute-done.19.refs_1_, f32[4,2,64,256]{3,2,1,0:T(8,128)S(1)} %collective-permute-done.23.refs_2_, f32[4,128,256]{2,1,0:T(8,128)S(1)} %collective-permute-done.4.refs_0_.refs_3_, ...), custom_call_target="tpu_custom_call" | custom-call | flops 1207959552 | bytes 1048576 | tf_op jit(solution)/shard_map/pallas_call | solution.py:210
  (6 shorter events, 0.2 us)
Async XLA Ops:
  22.9 0.9 copy-start.2
  24.5 8.6 %collective-permute-start = (f32[64,256]{1,0:T(8,128)S(1)}, f32[64,256]{1,0:T(8,128)S(1)}, u32[]{:S(2)}, u32[]{:S(2)}) collective-permute-start(f32[64,256]{1,0:T(8,128)S(1)} %get-tuple-element.25), channel_id=1, source_target_pairs={{0,2},{1,3},{2,0},{3,1},{4,6},{5,7},{6,4},{7,5},{8,10},{9,11},{10,... | collective-permute-start | bytes 196616 | tf_op jit(solution)/shard_map/ppermute | solution.py:234
  25.0 8.2 %collective-permute-start.3 = (f32[128,256]{1,0:T(8,128)S(1)}, f32[128,256]{1,0:T(8,128)S(1)}, u32[]{:S(2)}, u32[]{:S(2)}) collective-permute-start(f32[128,256]{1,0:T(8,128)S(1)} %get-tuple-element.26), channel_id=1, source_target_pairs={{0,12},{1,13},{2,14},{3,15},{4,0},{5,1},{6,2},{7,3},{8,4},{9,5},{1... | collective-permute-start | bytes 393224 | tf_op jit(solution)/shard_map/ppermute | solution.py:234
  27.7 12.4 %collective-permute-start.2 = (f32[128,256]{1,0:T(8,128)S(1)}, f32[128,256]{1,0:T(8,128)S(1)}, u32[]{:S(2)}, u32[]{:S(2)}) collective-permute-start(f32[128,256]{1,0:T(8,128)S(1)} %get-tuple-element.26), channel_id=1, source_target_pairs={{0,8},{1,9},{2,10},{3,11},{4,12},{5,13},{6,14},{7,15},{8,0},{9,1},... | collective-permute-start | bytes 393224 | tf_op jit(solution)/shard_map/ppermute | solution.py:234
  28.2 11.8 %collective-permute-start.1 = (f32[128,256]{1,0:T(8,128)S(1)}, f32[128,256]{1,0:T(8,128)S(1)}, u32[]{:S(2)}, u32[]{:S(2)}) collective-permute-start(f32[128,256]{1,0:T(8,128)S(1)} %get-tuple-element.26), channel_id=1, source_target_pairs={{0,4},{1,5},{2,6},{3,7},{4,8},{5,9},{6,10},{7,11},{8,12},{9,13},{1... | collective-permute-start | bytes 393224 | tf_op jit(solution)/shard_map/ppermute | solution.py:234
  28.8 3.4 %copy-start = (f32[2,256,4096]{2,1,0:T(8,128)S(1)}, f32[2,256,4096]{2,1,0:T(8,128)}, u32[]{:S(2)}) copy-start(f32[2,256,4096]{2,1,0:T(8,128)} %matrix_ref) | copy-start | bytes 25165828
  32.2 12.9 %copy-start.1 = (f32[2,256,4096]{2,1,0:T(8,128)S(1)}, f32[2,256,4096]{2,1,0:T(8,128)}, u32[]{:S(2)}) copy-start(f32[2,256,4096]{2,1,0:T(8,128)} %matrix_ref.1) | copy-start | bytes 25165828
  40.1 14.8 %collective-permute-start.5 = (f32[4,128,256]{2,1,0:T(8,128)S(1)}, f32[4,128,256]{2,1,0:T(8,128)S(1)}, u32[]{:S(2)}, u32[]{:S(2)}) collective-permute-start(f32[4,128,256]{2,1,0:T(8,128)S(1)} %pad_maximum_fusion.refs_0_.refs_3_), channel_id=1, source_target_pairs={{0,2},{1,3},{2,0},{3,1},{4,6},{5,7},{6,4},{7,5},{8,10},{9,11},{10,... | collective-permute-start | bytes 1572872 | tf_op jit(solution)/shard_map/ppermute | solution.py:234
  41.3 5.5 %collective-permute-start.8 = (f32[2,64,256]{2,1,0:T(8,128)S(1)}, f32[2,64,256]{2,1,0:T(8,128)S(1)}, u32[]{:S(2)}, u32[]{:S(2)}) collective-permute-start(f32[2,64,256]{2,1,0:T(8,128)S(1)} %pad_maximum_fusion.4), channel_id=1, source_target_pairs={{0,12},{1,13},{2,14},{3,15},{4,0},{5,1},{6,2},{7,3},{8,4},{9,5},{1... | collective-permute-start | bytes 393224 | tf_op jit(solution)/shard_map/ppermute | solution.py:234
  41.3 13.5 %collective-permute-start.7 = (f32[2,64,256]{2,1,0:T(8,128)S(1)}, f32[2,64,256]{2,1,0:T(8,128)S(1)}, u32[]{:S(2)}, u32[]{:S(2)}) collective-permute-start(f32[2,64,256]{2,1,0:T(8,128)S(1)} %pad_maximum_fusion.4), channel_id=1, source_target_pairs={{0,8},{1,9},{2,10},{3,11},{4,12},{5,13},{6,14},{7,15},{8,0},{9,1},... | collective-permute-start | bytes 393224 | tf_op jit(solution)/shard_map/ppermute | solution.py:234
  43.1 11.8 %collective-permute-start.6 = (f32[2,64,256]{2,1,0:T(8,128)S(1)}, f32[2,64,256]{2,1,0:T(8,128)S(1)}, u32[]{:S(2)}, u32[]{:S(2)}) collective-permute-start(f32[2,64,256]{2,1,0:T(8,128)S(1)} %pad_maximum_fusion.4), channel_id=1, source_target_pairs={{0,4},{1,5},{2,6},{3,7},{4,8},{5,9},{6,10},{7,11},{8,12},{9,13},{1... | collective-permute-start | bytes 393224 | tf_op jit(solution)/shard_map/ppermute | solution.py:234
  45.1 12.0 %collective-permute-start.4 = (f32[4,128,256]{2,1,0:T(8,128)S(1)}, f32[4,128,256]{2,1,0:T(8,128)S(1)}, u32[]{:S(2)}, u32[]{:S(2)}) collective-permute-start(f32[4,128,256]{2,1,0:T(8,128)S(1)} %pad_maximum_fusion.refs_0_.refs_3_), channel_id=1, source_target_pairs={{0,1},{1,0},{2,3},{3,2},{4,5},{5,4},{6,7},{7,6},{8,9},{9,8},{10,11... | collective-permute-start | bytes 1572872 | tf_op jit(solution)/shard_map/ppermute | solution.py:234
  54.9 2.3 %collective-permute-start.9 = (f32[4,128,256]{2,1,0:T(8,128)S(1)}, f32[4,128,256]{2,1,0:T(8,128)S(1)}, u32[]{:S(2)}, u32[]{:S(2)}) collective-permute-start(f32[4,128,256]{2,1,0:T(8,128)S(1)} %collective-permute-done.5.refs_1_.refs_4_), channel_id=1, source_target_pairs={{0,1},{1,0},{2,3},{3,2},{4,5},{5,4},{6,7},{7,6},{8,9},{9,8},{10,11... | collective-permute-start | bytes 1572872 | tf_op jit(solution)/shard_map/ppermute | solution.py:234
  55.0 2.6 %collective-permute-start.10 = (f32[4,2,64,256]{3,2,1,0:T(8,128)S(1)}, f32[4,2,64,256]{3,2,1,0:T(8,128)S(1)}, u32[]{:S(2)}, u32[]{:S(2)}) collective-permute-start(f32[4,2,64,256]{3,2,1,0:T(8,128)S(1)} %pad_maximum_fusion.1.refs_2_.refs_5_), channel_id=1, source_target_pairs={{0,1},{1,0},{2,3},{3,2},{4,5},{5,4},{6,7},{7,6},{8,9},{9,8},{10,11... | collective-permute-start | bytes 1572872 | tf_op jit(solution)/shard_map/ppermute | solution.py:234
  59.2 5.8 %collective-permute-start.12 = (f32[64,256]{1,0:T(8,128)S(1)}, f32[64,256]{1,0:T(8,128)S(1)}, u32[]{:S(2)}, u32[]{:S(2)}) collective-permute-start(f32[64,256]{1,0:T(8,128)S(1)} %get-tuple-element.39), channel_id=1, source_target_pairs={{0,18},{1,19},{2,16},{3,17},{4,22},{5,23},{6,20},{7,21},{8,26},{9,... | collective-permute-start | bytes 196616 | tf_op jit(solution)/shard_map/ppermute | solution.py:236
  59.3 10.6 %collective-permute-start.11 = (f32[64,256]{1,0:T(8,128)S(1)}, f32[64,256]{1,0:T(8,128)S(1)}, u32[]{:S(2)}, u32[]{:S(2)}) collective-permute-start(f32[64,256]{1,0:T(8,128)S(1)} %get-tuple-element.39), channel_id=1, source_target_pairs={{0,16},{1,17},{2,18},{3,19},{4,20},{5,21},{6,22},{7,23},{8,24},{9,... | collective-permute-start | bytes 196616 | tf_op jit(solution)/shard_map/ppermute | solution.py:236
  61.1 8.8 %collective-permute-start.16 = (f32[128,256]{1,0:T(8,128)S(1)}, f32[128,256]{1,0:T(8,128)S(1)}, u32[]{:S(2)}, u32[]{:S(2)}) collective-permute-start(f32[128,256]{1,0:T(8,128)S(1)} %get-tuple-element.40), channel_id=1, source_target_pairs={{0,28},{1,29},{2,30},{3,31},{4,16},{5,17},{6,18},{7,19},{8,20},{9,... | collective-permute-start | bytes 393224 | tf_op jit(solution)/shard_map/ppermute | solution.py:236
  61.1 13.5 %collective-permute-start.15 = (f32[128,256]{1,0:T(8,128)S(1)}, f32[128,256]{1,0:T(8,128)S(1)}, u32[]{:S(2)}, u32[]{:S(2)}) collective-permute-start(f32[128,256]{1,0:T(8,128)S(1)} %get-tuple-element.40), channel_id=1, source_target_pairs={{0,24},{1,25},{2,26},{3,27},{4,28},{5,29},{6,30},{7,31},{8,16},{9,... | collective-permute-start | bytes 393224 | tf_op jit(solution)/shard_map/ppermute | solution.py:236
  63.1 11.5 %collective-permute-start.14 = (f32[128,256]{1,0:T(8,128)S(1)}, f32[128,256]{1,0:T(8,128)S(1)}, u32[]{:S(2)}, u32[]{:S(2)}) collective-permute-start(f32[128,256]{1,0:T(8,128)S(1)} %get-tuple-element.40), channel_id=1, source_target_pairs={{0,20},{1,21},{2,22},{3,23},{4,24},{5,25},{6,26},{7,27},{8,28},{9,... | collective-permute-start | bytes 393224 | tf_op jit(solution)/shard_map/ppermute | solution.py:236
  65.0 10.8 %collective-permute-start.13 = (f32[128,256]{1,0:T(8,128)S(1)}, f32[128,256]{1,0:T(8,128)S(1)}, u32[]{:S(2)}, u32[]{:S(2)}) collective-permute-start(f32[128,256]{1,0:T(8,128)S(1)} %get-tuple-element.40), channel_id=1, source_target_pairs={{0,16},{1,17},{2,18},{3,19},{4,20},{5,21},{6,22},{7,23},{8,24},{9,... | collective-permute-start | bytes 393224 | tf_op jit(solution)/shard_map/ppermute | solution.py:236
  75.9 14.3 %collective-permute-start.18 = (f32[4,128,256]{2,1,0:T(8,128)S(1)}, f32[4,128,256]{2,1,0:T(8,128)S(1)}, u32[]{:S(2)}, u32[]{:S(2)}) collective-permute-start(f32[4,128,256]{2,1,0:T(8,128)S(1)} %pad_maximum_fusion.2.refs_0_), channel_id=1, source_target_pairs={{0,2},{1,3},{2,0},{3,1},{4,6},{5,7},{6,4},{7,5},{8,10},{9,11},{10,... | collective-permute-start | bytes 1572872 | tf_op jit(solution)/shard_map/ppermute | solution.py:234
  77.6 6.1 %collective-permute-start.22 = (f32[2,64,256]{2,1,0:T(8,128)S(1)}, f32[2,64,256]{2,1,0:T(8,128)S(1)}, u32[]{:S(2)}, u32[]{:S(2)}) collective-permute-start(f32[2,64,256]{2,1,0:T(8,128)S(1)} %pad_maximum_fusion.5), channel_id=1, source_target_pairs={{0,12},{1,13},{2,14},{3,15},{4,0},{5,1},{6,2},{7,3},{8,4},{9,5},{1... | collective-permute-start | bytes 393224 | tf_op jit(solution)/shard_map/ppermute | solution.py:234
  78.8 11.3 %collective-permute-start.21 = (f32[2,64,256]{2,1,0:T(8,128)S(1)}, f32[2,64,256]{2,1,0:T(8,128)S(1)}, u32[]{:S(2)}, u32[]{:S(2)}) collective-permute-start(f32[2,64,256]{2,1,0:T(8,128)S(1)} %pad_maximum_fusion.5), channel_id=1, source_target_pairs={{0,8},{1,9},{2,10},{3,11},{4,12},{5,13},{6,14},{7,15},{8,0},{9,1},... | collective-permute-start | bytes 393224 | tf_op jit(solution)/shard_map/ppermute | solution.py:234
  78.8 11.3 %collective-permute-start.20 = (f32[2,64,256]{2,1,0:T(8,128)S(1)}, f32[2,64,256]{2,1,0:T(8,128)S(1)}, u32[]{:S(2)}, u32[]{:S(2)}) collective-permute-start(f32[2,64,256]{2,1,0:T(8,128)S(1)} %pad_maximum_fusion.5), channel_id=1, source_target_pairs={{0,4},{1,5},{2,6},{3,7},{4,8},{5,9},{6,10},{7,11},{8,12},{9,13},{1... | collective-permute-start | bytes 393224 | tf_op jit(solution)/shard_map/ppermute | solution.py:234
  80.4 11.9 %collective-permute-start.17 = (f32[4,128,256]{2,1,0:T(8,128)S(1)}, f32[4,128,256]{2,1,0:T(8,128)S(1)}, u32[]{:S(2)}, u32[]{:S(2)}) collective-permute-start(f32[4,128,256]{2,1,0:T(8,128)S(1)} %pad_maximum_fusion.2.refs_0_), channel_id=1, source_target_pairs={{0,1},{1,0},{2,3},{3,2},{4,5},{5,4},{6,7},{7,6},{8,9},{9,8},{10,11... | collective-permute-start | bytes 1572872 | tf_op jit(solution)/shard_map/ppermute | solution.py:234
  90.1 2.3 %collective-permute-start.23 = (f32[4,2,64,256]{3,2,1,0:T(8,128)S(1)}, f32[4,2,64,256]{3,2,1,0:T(8,128)S(1)}, u32[]{:S(2)}, u32[]{:S(2)}) collective-permute-start(f32[4,2,64,256]{3,2,1,0:T(8,128)S(1)} %pad_maximum_fusion.3.refs_2_), channel_id=1, source_target_pairs={{0,1},{1,0},{2,3},{3,2},{4,5},{5,4},{6,7},{7,6},{8,9},{9,8},{10,11... | collective-permute-start | bytes 1572872 | tf_op jit(solution)/shard_map/ppermute | solution.py:234
  90.2 2.6 %collective-permute-start.19 = (f32[4,128,256]{2,1,0:T(8,128)S(1)}, f32[4,128,256]{2,1,0:T(8,128)S(1)}, u32[]{:S(2)}, u32[]{:S(2)}) collective-permute-start(f32[4,128,256]{2,1,0:T(8,128)S(1)} %collective-permute-done.18.refs_1_), channel_id=1, source_target_pairs={{0,1},{1,0},{2,3},{3,2},{4,5},{5,4},{6,7},{7,6},{8,9},{9,8},{10,11... | collective-permute-start | bytes 1572872 | tf_op jit(solution)/shard_map/ppermute | solution.py:234

commit v12 on v11

--- a/solution.py
+++ b/solution.py
@@ -139,6 +139,16 @@
     )(matrix)
 
 
+def put(out_refs, first, value):
+    start = 0
+    for out_ref in out_refs:
+        low = max(first, start)
+        high = min(first + value.shape[0], start + out_ref.shape[0])
+        if low < high:
+            out_ref[low - start:high - start, :] = value[low - first:high - first]
+        start += out_ref.shape[0]
+
+
 def product_kernel(sources, layout, inputs, sets, block, begin, end, onward, relative, *refs):
     high_ref, low_ref = refs[inputs * sets:inputs * sets + 2]
     rest = refs[inputs * sets + 2:]
@@ -186,14 +196,12 @@
                 total_ref[...] = part
             else:
                 total_ref[...] = start_ref[...] + part
-        start = 0
-        for out_ref in out_refs:
-            for first in range(0, out_ref.shape[0], 2 * sources):
-                real = pl.ds(start + first, sources)
-                imag = pl.ds(start + first + sources, sources)
-                out_ref[first:first + sources, :] = total_ref[real, :own_rows] - total_ref[imag, own_rows:]
-                out_ref[first + sources:first + 2 * sources, :] = total_ref[imag, :own_rows] + total_ref[real, own_rows:]
-            start += out_ref.shape[0]
+        for first in range(0, columns, 2 * sources if out_refs else columns):
+            real = pl.ds(first, sources)
+            imag = pl.ds(first + sources, sources)
+            if out_refs:
+                put(out_refs, first, total_ref[real, :own_rows] - total_ref[imag, own_rows:])
+                put(out_refs, first + sources, total_ref[imag, :own_rows] + total_ref[real, own_rows:])
 
 
 def product_part(split, onward, layout, blocks, own, begin, end, started, sources, shares, relative):
@@ -322,8 +330,8 @@
         compiler_params=kernel_params(56),
     )(tile_counts, update_rows[None, :], updates.T)
     received = lax.all_to_all(packed, "tile", 0, 0, tiled=False)
-    paired = own_rows % 128 == 0 and tile_size % 8 == 0 and batches > 1
-    early = batches * 2 // 3 * halves * sources
+    paired = own_rows % 128 == 0 and tile_size % 8 == 0 and columns % 8 == 0 and columns >= 24
+    early = columns * 17 // 24 // 8 * 8
     shares = [early, columns - early] if paired else [columns]
     reduced = pl.pallas_call(
         functools.partial(reduce_kernel, cap),

time: 95.4 us -> 95.3 us (level)
  waiting for transfers between devices: 35 us -> 32.9 us
  starting transfers between devices: 22.7 us -> 24 us
    ppermute x6, starting transfers between devices: 7.81 us -> 9.6 us  [send(): return lax.ppermute(value, ('chain', 'tile'), pairs)]
    ppermute x18, waiting for transfers between devices: 26.2 us -> 24.4 us  [send(): lax.ppermute(value, 'tile', [(t, target(t)) for t in range(tile_size)])]
  transfers between devices with their start and end apart: 24 -> 24, of which waited for: 10 -> 11; matrix products, arithmetic and copies ran while one was open for 0% -> 0% of each run, Pallas kernels for 6% -> 6%
where the time goes in v12:
time: 95.3 us; the launch traced here: 94.3 us
  waiting for transfers between devices  32.9 us (35%)
  starting transfers between devices  24 us (25%)
  blocking collectives  20.6 us (22%)
  Pallas kernels  12.1 us (13%)
  local copies, waits for them, and re-layouts  4.31 us (5%)
    ppermute x18, waiting for transfers between devices, send(): lax.ppermute(value, 'tile', [(t, target(t)) for t in range(tile_size)])  24.4 us
    all_to_all x1, blocking collectives, body(): received = lax.all_to_all(packed, 'tile', 0, 0, tiled=False)  20.6 us
    ppermute x18, starting transfers between devices, send(): lax.ppermute(value, 'tile', [(t, target(t)) for t in range(tile_size)])  14.4 us
    ppermute x6, starting transfers between devices, send(): return lax.ppermute(value, ('chain', 'tile'), pairs)  9.6 us
    ppermute x6, waiting for transfers between devices, send(): return lax.ppermute(value, ('chain', 'tile'), pairs)  8.5 us
    pallas_call x4, Pallas kernels, product_part(): pl.pallas_call(functools.partial(product_kernel, sources, layout, len(blo...  7.25 us
    unnamed x6, local copies, waits for them, and re-layouts  4.31 us
    pallas_call x1, Pallas kernels, body(): pl.pallas_call(functools.partial(pack_kernel, own_rows, cap, tile_rows),...  2.19 us
  transfers between devices with their start and end apart: 24, of which 11 were waited for; matrix products, arithmetic and copies ran while one was open for 0% of the time, Pallas kernels for 6%

profile of v12, /device:TPU:0, one launch (start us, length us, event | category | flops | bytes accessed | tf_op | source)
XLA Modules:
  0.0 94.3 jit_solution(11332817121565311704)
XLA Ops:
  0.0 2.2 %shard_map.64 = f32[16,56,128]{2,1,0:T(8,128)} custom-call(s32[2]{0:T(128)} %counts_hbm.1, s32[1,256]{1,0:T(1,128)} %bitcast.46, f32[192,256]{1,0:T(8,128)} %bitcast.29), custom_call_target="tpu_custom_call" | custom-call | tf_op jit(solution)/shard_map/pallas_call | solution.py:319
  2.2 20.6 %all_to_all.5.received_ref = f32[16,56,128]{2,1,0:T(8,128)S(1)} all-to-all(f32[16,56,128]{2,1,0:T(8,128)} %shard_map.64), channel_id=1, replica_groups=mesh['chain'=2,'tile'=16] {'tile'}, dimensions={0} | all-to-all | bytes 917504 | tf_op jit(solution)/shard_map/all_to_all | solution.py:332
  22.9 0.0 copy-start.2
  22.9 0.9 copy-done.2
  23.8 0.8 shard_map.65
  24.5 0.4 collective-permute-start
  25.0 2.7 %collective-permute-start.3 = (f32[136,256]{1,0:T(8,128)S(1)}, f32[136,256]{1,0:T(8,128)S(1)}, u32[]{:S(2)}, u32[]{:S(2)}) collective-permute-start(f32[136,256]{1,0:T(8,128)S(1)} %get-tuple-element.26), channel_id=1, source_target_pairs={{0,12},{1,13},{2,14},{3,15},{4,0},{5,1},{6,2},{7,3},{8,4},{9,5},{1... | collective-permute-start | bytes 417800 | tf_op jit(solution)/shard_map/ppermute | solution.py:242
  27.7 0.5 collective-permute-start.2
  28.2 0.5 collective-permute-start.1
  28.8 0.0 copy-start
  28.8 3.4 %copy-done = f32[2,256,4096]{2,1,0:T(8,128)S(1)} copy-done((f32[2,256,4096]{2,1,0:T(8,128)S(1)}, f32[2,256,4096]{2,1,0:T(8,128)}, u32[]{:S(2)}) %copy-start) | copy-done | bytes 8388632
  32.2 0.0 copy-start.1
  32.2 1.0 %shard_map.66 = (bf16[4,512,1024]{2,1,0:T(8,128)(2,1)S(1)}, bf16[4,512,1024]{2,1,0:T(8,128)(2,1)S(1)}) custom-call(f32[2,256,4096]{2,1,0:T(8,128)S(1)} %copy-done), custom_call_target="tpu_custom_call" | custom-call | flops 6291456 | bytes 16777216 | tf_op jit(solution)/shard_map/pallas_call | solution.py:132
  33.1 0.0 collective-permute-done
  33.2 0.0 collective-permute-done.3
  33.2 7.6 %collective-permute-done.2 = f32[136,256]{1,0:T(8,128)S(1)} collective-permute-done((f32[136,256]{1,0:T(8,128)S(1)}, f32[136,256]{1,0:T(8,128)S(1)}, u32[]{:S(2)}, u32[]{:S(2)}) %collective-permute-start.2) | collective-permute-done | bytes 139296 | tf_op jit(solution)/shard_map/ppermute | solution.py:242
  40.8 0.0 collective-permute-done.1
  40.8 1.2 %collective-permute-start.5 = (f32[4,136,256]{2,1,0:T(8,128)S(1)}, f32[4,136,256]{2,1,0:T(8,128)S(1)}, u32[]{:S(2)}, u32[]{:S(2)}) collective-permute-start(f32[4,136,256]{2,1,0:T(8,128)S(1)} %pad_maximum_fusion.refs_0_.refs_3_), channel_id=1, source_target_pairs={{0,2},{1,3},{2,0},{3,1},{4,6},{5,7},{6,4},{7,5},{8,10},{9,11},{10,... | collective-permute-start | bytes 1671176 | tf_op jit(solution)/shard_map/ppermute | solution.py:242
  42.0 0.0 collective-permute-start.8
  42.0 1.8 %collective-permute-start.7 = (f32[2,56,256]{2,1,0:T(8,128)S(1)}, f32[2,56,256]{2,1,0:T(8,128)S(1)}, u32[]{:S(2)}, u32[]{:S(2)}) collective-permute-start(f32[2,56,256]{2,1,0:T(8,128)S(1)} %pad_maximum_fusion.4), channel_id=1, source_target_pairs={{0,8},{1,9},{2,10},{3,11},{4,12},{5,13},{6,14},{7,15},{8,0},{9,1},... | collective-permute-start | bytes 344072 | tf_op jit(solution)/shard_map/ppermute | solution.py:242
  43.8 2.0 %collective-permute-start.6 = (f32[2,56,256]{2,1,0:T(8,128)S(1)}, f32[2,56,256]{2,1,0:T(8,128)S(1)}, u32[]{:S(2)}, u32[]{:S(2)}) collective-permute-start(f32[2,56,256]{2,1,0:T(8,128)S(1)} %pad_maximum_fusion.4), channel_id=1, source_target_pairs={{0,4},{1,5},{2,6},{3,7},{4,8},{5,9},{6,10},{7,11},{8,12},{9,13},{1... | collective-permute-start | bytes 344072 | tf_op jit(solution)/shard_map/ppermute | solution.py:242
  45.8 0.0 collective-permute-start.4
  45.8 0.0 copy-done.1
  45.8 1.0 %shard_map.67 = (bf16[4,512,1024]{2,1,0:T(8,128)(2,1)S(1)}, bf16[4,512,1024]{2,1,0:T(8,128)(2,1)S(1)}) custom-call(f32[2,256,4096]{2,1,0:T(8,128)S(1)} %copy-done.1), custom_call_target="tpu_custom_call" | custom-call | flops 6291456 | bytes 16777216 | tf_op jit(solution)/shard_map/pallas_call | solution.py:132
  46.8 0.7 collective-permute-done.8
  47.5 6.7 %collective-permute-done.7 = f32[2,56,256]{2,1,0:T(8,128)S(1)} collective-permute-done((f32[2,56,256]{2,1,0:T(8,128)S(1)}, f32[2,56,256]{2,1,0:T(8,128)S(1)}, u32[]{:S(2)}, u32[]{:S(2)}) %collective-permute-start.7) | collective-permute-done | bytes 114720 | tf_op jit(solution)/shard_map/ppermute | solution.py:242
  54.1 0.0 collective-permute-done.6
  54.2 0.4 collective-permute-done.5.refs_1_.refs_4_
  54.6 0.0 collective-permute-start.9
  54.6 0.5 collective-permute-start.10
  55.1 1.7 %shard_map.68.refs_5_ = f32[192,512]{1,0:T(8,128)S(1)} custom-call(f32[4,136,256]{2,1,0:T(8,128)S(1)} %pad_maximum_fusion.refs_0_.refs_3_, f32[4,136,256]{2,1,0:T(8,128)S(1)} %collective-permute-done.5.refs_1_.refs_4_, f32[4,2,56,256]{3,2,1,0:T(8,128)S(1)} %pad_maximum_fusion.2.refs_2_.refs_5_, bf16[4,512,1024]{2,1,0:T(8,128)(2,1)S(1)} %get-tuple-element.37.refs_3_, ...), custom_call_target="tpu_custom_call" | custom-call | flops 1207959552 | bytes 1048576 | tf_op jit(solution)/shard_map/pallas_call | solution.py:218
  56.8 0.0 collective-permute-done.4.refs_0_.refs_3_
  56.8 0.4 collective-permute-done.10.refs_2_.refs_5_
  57.2 0.0 collective-permute-done.9.refs_1_.refs_4_
  57.2 1.6 %shard_map.69 = (f32[136,256]{1,0:T(8,128)S(1)}, f32[56,256]{1,0:T(8,128)S(1)}) custom-call(f32[4,136,256]{2,1,0:T(8,128)S(1)} %collective-permute-done.4.refs_0_.refs_3_, f32[4,136,256]{2,1,0:T(8,128)S(1)} %collective-permute-done.9.refs_1_.refs_4_, f32[4,2,56,256]{3,2,1,0:T(8,128)S(1)} %collective-permute-done.10.refs_2_.refs_5_, ...), custom_call_target="tpu_custom_call" | custom-call | flops 1207959552 | bytes 1048576 | tf_op jit(solution)/shard_map/pallas_call | solution.py:218
  58.8 0.9 collective-permute-start.12
  59.7 2.1 %collective-permute-start.11 = (f32[56,256]{1,0:T(8,128)S(1)}, f32[56,256]{1,0:T(8,128)S(1)}, u32[]{:S(2)}, u32[]{:S(2)}) collective-permute-start(f32[56,256]{1,0:T(8,128)S(1)} %get-tuple-element.39), channel_id=1, source_target_pairs={{0,16},{1,17},{2,18},{3,19},{4,20},{5,21},{6,22},{7,23},{8,24},{9,... | collective-permute-start | bytes 172040 | tf_op jit(solution)/shard_map/ppermute | solution.py:244
  61.8 0.0 collective-permute-start.16
  61.8 2.6 %collective-permute-start.15 = (f32[136,256]{1,0:T(8,128)S(1)}, f32[136,256]{1,0:T(8,128)S(1)}, u32[]{:S(2)}, u32[]{:S(2)}) collective-permute-start(f32[136,256]{1,0:T(8,128)S(1)} %get-tuple-element.40), channel_id=1, source_target_pairs={{0,24},{1,25},{2,26},{3,27},{4,28},{5,29},{6,30},{7,31},{8,16},{9,... | collective-permute-start | bytes 417800 | tf_op jit(solution)/shard_map/ppermute | solution.py:244
  64.5 1.9 %collective-permute-start.14 = (f32[136,256]{1,0:T(8,128)S(1)}, f32[136,256]{1,0:T(8,128)S(1)}, u32[]{:S(2)}, u32[]{:S(2)}) collective-permute-start(f32[136,256]{1,0:T(8,128)S(1)} %get-tuple-element.40), channel_id=1, source_target_pairs={{0,20},{1,21},{2,22},{3,23},{4,24},{5,25},{6,26},{7,27},{8,28},{9,... | collective-permute-start | bytes 417800 | tf_op jit(solution)/shard_map/ppermute | solution.py:244
  66.4 0.0 collective-permute-done.12
  66.4 2.0 %collective-permute-start.13 = (f32[136,256]{1,0:T(8,128)S(1)}, f32[136,256]{1,0:T(8,128)S(1)}, u32[]{:S(2)}, u32[]{:S(2)}) collective-permute-start(f32[136,256]{1,0:T(8,128)S(1)} %get-tuple-element.40), channel_id=1, source_target_pairs={{0,16},{1,17},{2,18},{3,19},{4,20},{5,21},{6,22},{7,23},{8,24},{9,... | collective-permute-start | bytes 417800 | tf_op jit(solution)/shard_map/ppermute | solution.py:244
  68.4 0.0 collective-permute-done.11
  68.4 0.8 collective-permute-done.16
  69.2 7.4 %collective-permute-done.15 = f32[136,256]{1,0:T(8,128)S(1)} collective-permute-done((f32[136,256]{1,0:T(8,128)S(1)}, f32[136,256]{1,0:T(8,128)S(1)}, u32[]{:S(2)}, u32[]{:S(2)}) %collective-permute-start.15) | collective-permute-done | bytes 139296 | tf_op jit(solution)/shard_map/ppermute | solution.py:244
  76.6 0.0 collective-permute-done.14
  76.6 0.3 collective-permute-done.13
  77.0 0.6 collective-permute-start.18
  77.6 2.1 %collective-permute-start.22 = (f32[2,56,256]{2,1,0:T(8,128)S(1)}, f32[2,56,256]{2,1,0:T(8,128)S(1)}, u32[]{:S(2)}, u32[]{:S(2)}) collective-permute-start(f32[2,56,256]{2,1,0:T(8,128)S(1)} %pad_maximum_fusion.5), channel_id=1, source_target_pairs={{0,12},{1,13},{2,14},{3,15},{4,0},{5,1},{6,2},{7,3},{8,4},{9,5},{1... | collective-permute-start | bytes 344072 | tf_op jit(solution)/shard_map/ppermute | solution.py:242
  79.6 0.3 collective-permute-start.21
  79.9 1.6 %collective-permute-start.20 = (f32[2,56,256]{2,1,0:T(8,128)S(1)}, f32[2,56,256]{2,1,0:T(8,128)S(1)}, u32[]{:S(2)}, u32[]{:S(2)}) collective-permute-start(f32[2,56,256]{2,1,0:T(8,128)S(1)} %pad_maximum_fusion.5), channel_id=1, source_target_pairs={{0,4},{1,5},{2,6},{3,7},{4,8},{5,9},{6,10},{7,11},{8,12},{9,13},{1... | collective-permute-start | bytes 344072 | tf_op jit(solution)/shard_map/ppermute | solution.py:242
  81.5 0.0 collective-permute-start.17
  81.5 7.4 %collective-permute-done.18.refs_1_ = f32[4,136,256]{2,1,0:T(8,128)S(1)} collective-permute-done((f32[4,136,256]{2,1,0:T(8,128)S(1)}, f32[4,136,256]{2,1,0:T(8,128)S(1)}, u32[]{:S(2)}, u32[]{:S(2)}) %collective-permute-start.18) | collective-permute-done | bytes 557088 | tf_op jit(solution)/shard_map/ppermute | solution.py:242
  88.9 0.0 collective-permute-start.19
  88.9 0.0 collective-permute-done.22
  88.9 1.2 %collective-permute-done.21 = f32[2,56,256]{2,1,0:T(8,128)S(1)} collective-permute-done((f32[2,56,256]{2,1,0:T(8,128)S(1)}, f32[2,56,256]{2,1,0:T(8,128)S(1)}, u32[]{:S(2)}, u32[]{:S(2)}) %collective-permute-start.21) | collective-permute-done | bytes 114720 | tf_op jit(solution)/shard_map/ppermute | solution.py:242
  90.1 0.0 collective-permute-done.20
  90.1 0.1 collective-permute-start.23
  90.2 1.7 %shard_map.70.refs_8_ = f32[192,512]{1,0:T(8,128)S(1)} custom-call(f32[4,136,256]{2,1,0:T(8,128)S(1)} %pad_maximum_fusion.1.refs_0_, f32[4,136,256]{2,1,0:T(8,128)S(1)} %collective-permute-done.18.refs_1_, f32[4,2,56,256]{3,2,1,0:T(8,128)S(1)} %pad_maximum_fusion.3.refs_2_, f32[4,136,256]{2,1,0:T(8,128)S(1)} %pad_maximum_fusion.refs_0_.refs_3_, ...), custom_call_target="tpu_custom_call" | custom-call | flops 1207959552 | bytes 1048576 | tf_op jit(solution)/shard_map/pallas_call | solution.py:218
  91.9 0.0 collective-permute-done.17.refs_0_
  91.9 0.1 collective-permute-done.23.refs_2_
  92.0 0.0 collective-permute-done.19.refs_1_
  92.0 2.3 %shard_map.71 = f32[192,256]{1,0:T(8,128)} custom-call(f32[4,136,256]{2,1,0:T(8,128)S(1)} %collective-permute-done.17.refs_0_, f32[4,136,256]{2,1,0:T(8,128)S(1)} %collective-permute-done.19.refs_1_, f32[4,2,56,256]{3,2,1,0:T(8,128)S(1)} %collective-permute-done.23.refs_2_, f32[4,136,256]{2,1,0:T(8,128)S(1)} %collective-permute-done.4.refs_0_.refs_3_, ...), custom_call_target="tpu_custom_call" | custom-call | flops 1207959552 | bytes 1048576 | tf_op jit(solution)/shard_map/pallas_call | solution.py:218
  (6 shorter events, 0.2 us)
Async XLA Ops:
  22.9 0.9 copy-start.2
  24.5 8.6 %collective-permute-start = (f32[56,256]{1,0:T(8,128)S(1)}, f32[56,256]{1,0:T(8,128)S(1)}, u32[]{:S(2)}, u32[]{:S(2)}) collective-permute-start(f32[56,256]{1,0:T(8,128)S(1)} %get-tuple-element.25), channel_id=1, source_target_pairs={{0,2},{1,3},{2,0},{3,1},{4,6},{5,7},{6,4},{7,5},{8,10},{9,11},{10,... | collective-permute-start | bytes 172040 | tf_op jit(solution)/shard_map/ppermute | solution.py:242
  25.0 8.2 %collective-permute-start.3 = (f32[136,256]{1,0:T(8,128)S(1)}, f32[136,256]{1,0:T(8,128)S(1)}, u32[]{:S(2)}, u32[]{:S(2)}) collective-permute-start(f32[136,256]{1,0:T(8,128)S(1)} %get-tuple-element.26), channel_id=1, source_target_pairs={{0,12},{1,13},{2,14},{3,15},{4,0},{5,1},{6,2},{7,3},{8,4},{9,5},{1... | collective-permute-start | bytes 417800 | tf_op jit(solution)/shard_map/ppermute | solution.py:242
  27.7 13.1 %collective-permute-start.2 = (f32[136,256]{1,0:T(8,128)S(1)}, f32[136,256]{1,0:T(8,128)S(1)}, u32[]{:S(2)}, u32[]{:S(2)}) collective-permute-start(f32[136,256]{1,0:T(8,128)S(1)} %get-tuple-element.26), channel_id=1, source_target_pairs={{0,8},{1,9},{2,10},{3,11},{4,12},{5,13},{6,14},{7,15},{8,0},{9,1},... | collective-permute-start | bytes 417800 | tf_op jit(solution)/shard_map/ppermute | solution.py:242
  28.2 12.5 %collective-permute-start.1 = (f32[136,256]{1,0:T(8,128)S(1)}, f32[136,256]{1,0:T(8,128)S(1)}, u32[]{:S(2)}, u32[]{:S(2)}) collective-permute-start(f32[136,256]{1,0:T(8,128)S(1)} %get-tuple-element.26), channel_id=1, source_target_pairs={{0,4},{1,5},{2,6},{3,7},{4,8},{5,9},{6,10},{7,11},{8,12},{9,13},{1... | collective-permute-start | bytes 417800 | tf_op jit(solution)/shard_map/ppermute | solution.py:242
  28.8 3.4 %copy-start = (f32[2,256,4096]{2,1,0:T(8,128)S(1)}, f32[2,256,4096]{2,1,0:T(8,128)}, u32[]{:S(2)}) copy-start(f32[2,256,4096]{2,1,0:T(8,128)} %matrix_ref) | copy-start | bytes 25165828
  32.2 13.7 %copy-start.1 = (f32[2,256,4096]{2,1,0:T(8,128)S(1)}, f32[2,256,4096]{2,1,0:T(8,128)}, u32[]{:S(2)}) copy-start(f32[2,256,4096]{2,1,0:T(8,128)} %matrix_ref.1) | copy-start | bytes 25165828
  40.8 13.8 %collective-permute-start.5 = (f32[4,136,256]{2,1,0:T(8,128)S(1)}, f32[4,136,256]{2,1,0:T(8,128)S(1)}, u32[]{:S(2)}, u32[]{:S(2)}) collective-permute-start(f32[4,136,256]{2,1,0:T(8,128)S(1)} %pad_maximum_fusion.refs_0_.refs_3_), channel_id=1, source_target_pairs={{0,2},{1,3},{2,0},{3,1},{4,6},{5,7},{6,4},{7,5},{8,10},{9,11},{10,... | collective-permute-start | bytes 1671176 | tf_op jit(solution)/shard_map/ppermute | solution.py:242
  42.0 5.4 %collective-permute-start.8 = (f32[2,56,256]{2,1,0:T(8,128)S(1)}, f32[2,56,256]{2,1,0:T(8,128)S(1)}, u32[]{:S(2)}, u32[]{:S(2)}) collective-permute-start(f32[2,56,256]{2,1,0:T(8,128)S(1)} %pad_maximum_fusion.4), channel_id=1, source_target_pairs={{0,12},{1,13},{2,14},{3,15},{4,0},{5,1},{6,2},{7,3},{8,4},{9,5},{1... | collective-permute-start | bytes 344072 | tf_op jit(solution)/shard_map/ppermute | solution.py:242
  42.0 12.1 %collective-permute-start.7 = (f32[2,56,256]{2,1,0:T(8,128)S(1)}, f32[2,56,256]{2,1,0:T(8,128)S(1)}, u32[]{:S(2)}, u32[]{:S(2)}) collective-permute-start(f32[2,56,256]{2,1,0:T(8,128)S(1)} %pad_maximum_fusion.4), channel_id=1, source_target_pairs={{0,8},{1,9},{2,10},{3,11},{4,12},{5,13},{6,14},{7,15},{8,0},{9,1},... | collective-permute-start | bytes 344072 | tf_op jit(solution)/shard_map/ppermute | solution.py:242
  43.8 10.4 %collective-permute-start.6 = (f32[2,56,256]{2,1,0:T(8,128)S(1)}, f32[2,56,256]{2,1,0:T(8,128)S(1)}, u32[]{:S(2)}, u32[]{:S(2)}) collective-permute-start(f32[2,56,256]{2,1,0:T(8,128)S(1)} %pad_maximum_fusion.4), channel_id=1, source_target_pairs={{0,4},{1,5},{2,6},{3,7},{4,8},{5,9},{6,10},{7,11},{8,12},{9,13},{1... | collective-permute-start | bytes 344072 | tf_op jit(solution)/shard_map/ppermute | solution.py:242
  45.8 11.0 %collective-permute-start.4 = (f32[4,136,256]{2,1,0:T(8,128)S(1)}, f32[4,136,256]{2,1,0:T(8,128)S(1)}, u32[]{:S(2)}, u32[]{:S(2)}) collective-permute-start(f32[4,136,256]{2,1,0:T(8,128)S(1)} %pad_maximum_fusion.refs_0_.refs_3_), channel_id=1, source_target_pairs={{0,1},{1,0},{2,3},{3,2},{4,5},{5,4},{6,7},{7,6},{8,9},{9,8},{10,11... | collective-permute-start | bytes 1671176 | tf_op jit(solution)/shard_map/ppermute | solution.py:242
  54.6 2.6 %collective-permute-start.9 = (f32[4,136,256]{2,1,0:T(8,128)S(1)}, f32[4,136,256]{2,1,0:T(8,128)S(1)}, u32[]{:S(2)}, u32[]{:S(2)}) collective-permute-start(f32[4,136,256]{2,1,0:T(8,128)S(1)} %collective-permute-done.5.refs_1_.refs_4_), channel_id=1, source_target_pairs={{0,1},{1,0},{2,3},{3,2},{4,5},{5,4},{6,7},{7,6},{8,9},{9,8},{10,11... | collective-permute-start | bytes 1671176 | tf_op jit(solution)/shard_map/ppermute | solution.py:242
  54.6 2.6 %collective-permute-start.10 = (f32[4,2,56,256]{3,2,1,0:T(8,128)S(1)}, f32[4,2,56,256]{3,2,1,0:T(8,128)S(1)}, u32[]{:S(2)}, u32[]{:S(2)}) collective-permute-start(f32[4,2,56,256]{3,2,1,0:T(8,128)S(1)} %pad_maximum_fusion.2.refs_2_.refs_5_), channel_id=1, source_target_pairs={{0,1},{1,0},{2,3},{3,2},{4,5},{5,4},{6,7},{7,6},{8,9},{9,8},{10,11... | collective-permute-start | bytes 1376264 | tf_op jit(solution)/shard_map/ppermute | solution.py:242
  58.8 7.6 %collective-permute-start.12 = (f32[56,256]{1,0:T(8,128)S(1)}, f32[56,256]{1,0:T(8,128)S(1)}, u32[]{:S(2)}, u32[]{:S(2)}) collective-permute-start(f32[56,256]{1,0:T(8,128)S(1)} %get-tuple-element.39), channel_id=1, source_target_pairs={{0,18},{1,19},{2,16},{3,17},{4,22},{5,23},{6,20},{7,21},{8,26},{9,... | collective-permute-start | bytes 172040 | tf_op jit(solution)/shard_map/ppermute | solution.py:244
  59.7 8.7 %collective-permute-start.11 = (f32[56,256]{1,0:T(8,128)S(1)}, f32[56,256]{1,0:T(8,128)S(1)}, u32[]{:S(2)}, u32[]{:S(2)}) collective-permute-start(f32[56,256]{1,0:T(8,128)S(1)} %get-tuple-element.39), channel_id=1, source_target_pairs={{0,16},{1,17},{2,18},{3,19},{4,20},{5,21},{6,22},{7,23},{8,24},{9,... | collective-permute-start | bytes 172040 | tf_op jit(solution)/shard_map/ppermute | solution.py:244
  61.8 7.4 %collective-permute-start.16 = (f32[136,256]{1,0:T(8,128)S(1)}, f32[136,256]{1,0:T(8,128)S(1)}, u32[]{:S(2)}, u32[]{:S(2)}) collective-permute-start(f32[136,256]{1,0:T(8,128)S(1)} %get-tuple-element.40), channel_id=1, source_target_pairs={{0,28},{1,29},{2,30},{3,31},{4,16},{5,17},{6,18},{7,19},{8,20},{9,... | collective-permute-start | bytes 417800 | tf_op jit(solution)/shard_map/ppermute | solution.py:244
  61.8 14.8 %collective-permute-start.15 = (f32[136,256]{1,0:T(8,128)S(1)}, f32[136,256]{1,0:T(8,128)S(1)}, u32[]{:S(2)}, u32[]{:S(2)}) collective-permute-start(f32[136,256]{1,0:T(8,128)S(1)} %get-tuple-element.40), channel_id=1, source_target_pairs={{0,24},{1,25},{2,26},{3,27},{4,28},{5,29},{6,30},{7,31},{8,16},{9,... | collective-permute-start | bytes 417800 | tf_op jit(solution)/shard_map/ppermute | solution.py:244
  64.5 12.2 %collective-permute-start.14 = (f32[136,256]{1,0:T(8,128)S(1)}, f32[136,256]{1,0:T(8,128)S(1)}, u32[]{:S(2)}, u32[]{:S(2)}) collective-permute-start(f32[136,256]{1,0:T(8,128)S(1)} %get-tuple-element.40), channel_id=1, source_target_pairs={{0,20},{1,21},{2,22},{3,23},{4,24},{5,25},{6,26},{7,27},{8,28},{9,... | collective-permute-start | bytes 417800 | tf_op jit(solution)/shard_map/ppermute | solution.py:244
  66.4 10.5 %collective-permute-start.13 = (f32[136,256]{1,0:T(8,128)S(1)}, f32[136,256]{1,0:T(8,128)S(1)}, u32[]{:S(2)}, u32[]{:S(2)}) collective-permute-start(f32[136,256]{1,0:T(8,128)S(1)} %get-tuple-element.40), channel_id=1, source_target_pairs={{0,16},{1,17},{2,18},{3,19},{4,20},{5,21},{6,22},{7,23},{8,24},{9,... | collective-permute-start | bytes 417800 | tf_op jit(solution)/shard_map/ppermute | solution.py:244
  77.0 11.9 %collective-permute-start.18 = (f32[4,136,256]{2,1,0:T(8,128)S(1)}, f32[4,136,256]{2,1,0:T(8,128)S(1)}, u32[]{:S(2)}, u32[]{:S(2)}) collective-permute-start(f32[4,136,256]{2,1,0:T(8,128)S(1)} %pad_maximum_fusion.1.refs_0_), channel_id=1, source_target_pairs={{0,2},{1,3},{2,0},{3,1},{4,6},{5,7},{6,4},{7,5},{8,10},{9,11},{10,... | collective-permute-start | bytes 1671176 | tf_op jit(solution)/shard_map/ppermute | solution.py:242
  77.6 11.3 %collective-permute-start.22 = (f32[2,56,256]{2,1,0:T(8,128)S(1)}, f32[2,56,256]{2,1,0:T(8,128)S(1)}, u32[]{:S(2)}, u32[]{:S(2)}) collective-permute-start(f32[2,56,256]{2,1,0:T(8,128)S(1)} %pad_maximum_fusion.5), channel_id=1, source_target_pairs={{0,12},{1,13},{2,14},{3,15},{4,0},{5,1},{6,2},{7,3},{8,4},{9,5},{1... | collective-permute-start | bytes 344072 | tf_op jit(solution)/shard_map/ppermute | solution.py:242
  79.6 10.5 %collective-permute-start.21 = (f32[2,56,256]{2,1,0:T(8,128)S(1)}, f32[2,56,256]{2,1,0:T(8,128)S(1)}, u32[]{:S(2)}, u32[]{:S(2)}) collective-permute-start(f32[2,56,256]{2,1,0:T(8,128)S(1)} %pad_maximum_fusion.5), channel_id=1, source_target_pairs={{0,8},{1,9},{2,10},{3,11},{4,12},{5,13},{6,14},{7,15},{8,0},{9,1},... | collective-permute-start | bytes 344072 | tf_op jit(solution)/shard_map/ppermute | solution.py:242
  79.9 10.2 %collective-permute-start.20 = (f32[2,56,256]{2,1,0:T(8,128)S(1)}, f32[2,56,256]{2,1,0:T(8,128)S(1)}, u32[]{:S(2)}, u32[]{:S(2)}) collective-permute-start(f32[2,56,256]{2,1,0:T(8,128)S(1)} %pad_maximum_fusion.5), channel_id=1, source_target_pairs={{0,4},{1,5},{2,6},{3,7},{4,8},{5,9},{6,10},{7,11},{8,12},{9,13},{1... | collective-permute-start | bytes 344072 | tf_op jit(solution)/shard_map/ppermute | solution.py:242
  81.5 10.4 %collective-permute-start.17 = (f32[4,136,256]{2,1,0:T(8,128)S(1)}, f32[4,136,256]{2,1,0:T(8,128)S(1)}, u32[]{:S(2)}, u32[]{:S(2)}) collective-permute-start(f32[4,136,256]{2,1,0:T(8,128)S(1)} %pad_maximum_fusion.1.refs_0_), channel_id=1, source_target_pairs={{0,1},{1,0},{2,3},{3,2},{4,5},{5,4},{6,7},{7,6},{8,9},{9,8},{10,11... | collective-permute-start | bytes 1671176 | tf_op jit(solution)/shard_map/ppermute | solution.py:242
  88.9 3.1 %collective-permute-start.19 = (f32[4,136,256]{2,1,0:T(8,128)S(1)}, f32[4,136,256]{2,1,0:T(8,128)S(1)}, u32[]{:S(2)}, u32[]{:S(2)}) collective-permute-start(f32[4,136,256]{2,1,0:T(8,128)S(1)} %collective-permute-done.18.refs_1_), channel_id=1, source_target_pairs={{0,1},{1,0},{2,3},{3,2},{4,5},{5,4},{6,7},{7,6},{8,9},{9,8},{10,11... | collective-permute-start | bytes 1671176 | tf_op jit(solution)/shard_map/ppermute | solution.py:242
  90.1 1.9 %collective-permute-start.23 = (f32[4,2,56,256]{3,2,1,0:T(8,128)S(1)}, f32[4,2,56,256]{3,2,1,0:T(8,128)S(1)}, u32[]{:S(2)}, u32[]{:S(2)}) collective-permute-start(f32[4,2,56,256]{3,2,1,0:T(8,128)S(1)} %pad_maximum_fusion.3.refs_2_), channel_id=1, source_target_pairs={{0,1},{1,0},{2,3},{3,2},{4,5},{5,4},{6,7},{7,6},{8,9},{9,8},{10,11... | collective-permute-start | bytes 1376264 | tf_op jit(solution)/shard_map/ppermute | solution.py:242

commit v13 on v11

--- a/solution.py
+++ b/solution.py
@@ -43,12 +43,15 @@
         live = live | ((entry >= start) & (entry < start + counts_ref[tile]))
     rows = rows_ref[...]
     owner = rows // own_rows
+    me = lax.axis_index("tile")
+    local_row = (rows - owner * own_rows).astype(f32)
+    if height > cap:
+        owner = owner ^ lax.rem(me, 2)
     lane_owner = jnp.broadcast_to(owner.astype(f32), (entries, entries))
     rank = jnp.sum(jnp.where(earlier & (lane_owner.T == lane_owner), 1, 0), axis=0, keepdims=True)
     slot = owner * cap + rank
     choose = jnp.where(lax.broadcasted_iota(jnp.int32, (slots, entries), 0) == slot, 1.0, 0.0).astype(bf16)
     data = jnp.where(live, updates_ref[...], 0.0)
-    local_row = (rows - owner * own_rows).astype(f32)
     folded = height > cap
     if not folded:
         tail = jnp.where(lax.broadcasted_iota(jnp.int32, (width - columns, entries), 0) == 0, local_row, 0.0)
@@ -63,28 +66,34 @@
     half = cap // 2
     packed_ref[:, :cap, :] = packed[:, :, :width]
     packed_ref[:, cap:cap + half, :] = jnp.concatenate([packed[:, :half, width:], packed[:, half:, width:]], axis=2)
-    first = lax.axis_index("tile") * cap
+    first = lax.div(me, 2) * cap
     by_owner = jnp.where(lax.broadcasted_iota(jnp.int32, (owners, entries), 0) == owner, local_row, 0.0).astype(bf16)
-    by_lane = jnp.where(lax.broadcasted_iota(jnp.int32, (width, entries), 0) == first % width + rank, 1.0, 0.0).astype(bf16)
+    by_lane = jnp.where(lax.broadcasted_iota(jnp.int32, (width, entries), 0) == lax.rem(first, width) + rank, 1.0, 0.0).astype(bf16)
     numbers = lax.dot_general(by_owner, by_lane, lanes_contract, preferred_element_type=f32)
     line = lax.broadcasted_iota(jnp.int32, (owners, 8, width), 1)
-    packed_ref[:, cap + half:, :] = jnp.where(line == first // width, numbers[:, None, :], 0.0)
-
-
-def reduce_kernel(cap, received_ref, right_hbm, *refs):
-    reduced_refs, right_ref, sem = refs[:-2], refs[-2], refs[-1]
+    other = lax.broadcasted_iota(jnp.int32, (owners, 8, width), 0) % 2
+    target = lax.div(first, width) + other * (owners // 2 * cap // width)
+    packed_ref[:, cap + half:, :] = jnp.where(line == target, numbers[:, None, :], 0.0)
+
+
+def reduce_kernel(cap, inputs, right_hbm, *refs):
+    received_refs, reduced_refs, right_ref, sem = refs[:inputs], refs[inputs:-2], refs[-2], refs[-1]
     move = pltpu.make_async_copy(right_hbm, right_ref, sem)
     move.start()
-    owners, height, width = received_ref.shape
-    slots = owners * cap
+    owners, height, width = received_refs[-1].shape
+    slots = owners * cap * inputs
     columns, own_rows = right_ref.shape
     if height > cap:
         half = cap // 2
-        numbers = jnp.sum(received_ref[:, cap + half:, :], axis=0)
+        numbers = sum(jnp.sum(ref[:, cap + half:height, :], axis=0) for ref in received_refs)
         numbers = jnp.concatenate([numbers[i:i + 1] for i in range(slots // width)], axis=1).astype(jnp.int32)
-        rest = received_ref[:, cap:cap + half, :]
-        rest = jnp.concatenate([rest[:, :, :width // 2], rest[:, :, width // 2:]], axis=1)
-        sets = [received_ref[:, :cap, :].reshape(slots, width), rest.reshape(slots, width // 2)]
+        wide, rest = [], []
+        for ref in received_refs:
+            wide.append(ref[:, :cap, :].reshape(owners * cap, width))
+            folds = ref[:, cap:cap + half, :]
+            folds = jnp.concatenate([folds[:, :, :width // 2], folds[:, :, width // 2:]], axis=1)
+            rest.append(folds.reshape(owners * cap, width // 2))
+        sets = [jnp.concatenate(wide, axis=0), jnp.concatenate(rest, axis=0)]
         place = jnp.where(lax.broadcasted_iota(jnp.int32, (own_rows, slots), 0) == numbers, 1.0, 0.0).astype(bf16)
         totals = []
         for value in sets:
@@ -94,7 +103,7 @@
             totals.append(total.T)
         total = jnp.concatenate(totals, axis=0)
     else:
-        received = received_ref[...].reshape(slots, width)
+        received = received_refs[0][...].reshape(slots, width)
         local_row = received[:, columns:columns + 1].astype(jnp.int32)
         place = jnp.where(lax.broadcasted_iota(jnp.int32, (slots, own_rows), 1) == local_row, 1.0, 0.0).astype(bf16)
         total = jnp.zeros((columns, own_rows), f32)
@@ -306,6 +315,7 @@
     vmem = pl.BlockSpec(memory_space=pltpu.VMEM)
     hbm = pl.BlockSpec(memory_space=pltpu.HBM)
     folded = cap % 16 == 0 and slots <= 1024 and columns == 192 and own_rows <= 256 and 128 % cap == 0
+    folded = folded and tile_size % 2 == 0 and tile_size // 2 * cap % 128 == 0
     width = 128 if folded else -(-(columns + 1) // 128) * 128
     height = cap + cap // 2 + 8 if folded else cap
     packed = pl.pallas_call(
@@ -321,18 +331,25 @@
         ],
         compiler_params=kernel_params(56),
     )(tile_counts, update_rows[None, :], updates.T)
-    received = lax.all_to_all(packed, "tile", 0, 0, tiled=False)
+    if folded:
+        chips = tile_size // 2
+        groups = [[2 * chip + core for chip in range(chips)] for core in range(2)]
+        packed = packed.reshape(chips, 2 * height, width)
+        arrived = lax.all_to_all(packed, "tile", 0, 0, tiled=False, axis_index_groups=groups)
+        received = [arrived, lax.ppermute(arrived[:, height:, :], "tile", [(t, t ^ 1) for t in range(tile_size)])]
+    else:
+        received = [lax.all_to_all(packed, "tile", 0, 0, tiled=False)]
     paired = own_rows % 128 == 0 and tile_size % 8 == 0 and batches > 1
     early = batches * 2 // 3 * halves * sources
     shares = [early, columns - early] if paired else [columns]
     reduced = pl.pallas_call(
-        functools.partial(reduce_kernel, cap),
-        in_specs=[vmem, hbm],
+        functools.partial(reduce_kernel, cap, len(received)),
+        in_specs=[hbm] + [vmem] * len(received),
         out_specs=[vmem] * len(shares),
         out_shape=[jax.ShapeDtypeStruct((rows, own_rows), f32) for rows in shares],
         scratch_shapes=[pltpu.VMEM((columns, own_rows), f32), pltpu.SemaphoreType.DMA(())],
         compiler_params=kernel_params(20),
-    )(received, right_side.reshape(columns, own_rows))
+    )(right_side.reshape(columns, own_rows), *received)
     solve = solve_paired if paired else solve_flat
     return solve(reduced, diag_inverse, coupling, sources).reshape(right_side.shape)
 

time: 95.4 us -> 96.5 us (1.012)
  waiting for transfers between devices: 35 us -> 36.4 us
    ppermute x0 -> x1, waiting for transfers between devices: none -> 1.48 us  [body(): lax.ppermute(arrived[:, height:, :], 'tile', [(t, t ^ 1) for t in range(t...]
  transfers between devices with their start and end apart: 24 -> 25, of which waited for: 10 -> 11; matrix products, arithmetic and copies ran while one was open for 0% -> 0% of each run, Pallas kernels for 6% -> 5%
where the time goes in v13:
time: 96.5 us; the launch traced here: 96.2 us
  waiting for transfers between devices  36.4 us (38%)
  starting transfers between devices  22.5 us (23%)
  blocking collectives  20.5 us (21%)
  Pallas kernels  12.1 us (13%)
  local copies, waits for them, and re-layouts  4.33 us (4%)
    ppermute x18, waiting for transfers between devices, send(): lax.ppermute(value, 'tile', [(t, target(t)) for t in range(tile_size)])  26.1 us
    all_to_all x1, blocking collectives, body(): lax.all_to_all(packed, 'tile', 0, 0, tiled=False, axis_index_groups=groups)  20.5 us
    ppermute x18, starting transfers between devices, send(): lax.ppermute(value, 'tile', [(t, target(t)) for t in range(tile_size)])  14.6 us
    ppermute x6, waiting for transfers between devices, send(): return lax.ppermute(value, ('chain', 'tile'), pairs)  8.78 us
    ppermute x6, starting transfers between devices, send(): return lax.ppermute(value, ('chain', 'tile'), pairs)  7.81 us
    pallas_call x4, Pallas kernels, product_part(): pl.pallas_call(functools.partial(product_kernel, sources, layout, len(blo...  7.21 us
    unnamed x6, local copies, waits for them, and re-layouts  4.31 us
    pallas_call x1, Pallas kernels, body(): pl.pallas_call(functools.partial(pack_kernel, own_rows, cap, tile_rows),...  2.21 us
  transfers between devices with their start and end apart: 25, of which 11 were waited for; matrix products, arithmetic and copies ran while one was open for 0% of the time, Pallas kernels for 5%

profile of v13, /device:TPU:0, one launch (start us, length us, event | category | flops | bytes accessed | tf_op | source)
XLA Modules:
  0.0 96.2 jit_solution(11197564615072160478)
XLA Ops:
  0.0 2.2 %shard_map.64 = f32[16,56,128]{2,1,0:T(8,128)} custom-call(s32[2]{0:T(128)} %counts_hbm.1, s32[1,256]{1,0:T(1,128)} %bitcast.48, f32[192,256]{1,0:T(8,128)} %bitcast.31), custom_call_target="tpu_custom_call" | custom-call | tf_op jit(solution)/shard_map/pallas_call | solution.py:321
  2.2 20.5 %all_to_all.5.refs_0_ = f32[8,112,128]{2,1,0:T(8,128)S(1)} all-to-all(f32[8,112,128]{2,1,0:T(8,128)} %bitcast.28), channel_id=1, replica_groups={{0,2,4,6,8,10,12,14},{1,3,5,7,9,11,13,15},{16,18,20,22,24,26,28,30},{17..., dimensions={0} | all-to-all | bytes 917504 | tf_op jit(solution)/shard_map/all_to_all | solution.py:338
  22.8 0.1 collective-permute-start
  22.8 1.5 %collective-permute-done.refs_1_ = f32[8,56,128]{2,1,0:T(8,128)S(1)} collective-permute-done((f32[8,56,128]{2,1,0:T(8,128)S(1)}, f32[8,56,128]{2,1,0:T(8,128)S(1)}, u32[]{:S(2)}, u32[]{:S(2)}) %collective-permute-start) | collective-permute-done | bytes 229408 | tf_op jit(solution)/shard_map/ppermute | solution.py:339
  24.3 0.0 copy-start.2
  24.3 0.9 copy-done.2
  25.2 0.7 shard_map.65
  26.0 1.4 %collective-permute-start.1 = (f32[64,256]{1,0:T(8,128)S(1)}, f32[64,256]{1,0:T(8,128)S(1)}, u32[]{:S(2)}, u32[]{:S(2)}) collective-permute-start(f32[64,256]{1,0:T(8,128)S(1)} %get-tuple-element.25), channel_id=1, source_target_pairs={{0,2},{1,3},{2,0},{3,1},{4,6},{5,7},{6,4},{7,5},{8,10},{9,11},{10,... | collective-permute-start | bytes 196616 | tf_op jit(solution)/shard_map/ppermute | solution.py:243
  27.4 1.4 %collective-permute-start.4 = (f32[128,256]{1,0:T(8,128)S(1)}, f32[128,256]{1,0:T(8,128)S(1)}, u32[]{:S(2)}, u32[]{:S(2)}) collective-permute-start(f32[128,256]{1,0:T(8,128)S(1)} %get-tuple-element.26), channel_id=1, source_target_pairs={{0,12},{1,13},{2,14},{3,15},{4,0},{5,1},{6,2},{7,3},{8,4},{9,5},{1... | collective-permute-start | bytes 393224 | tf_op jit(solution)/shard_map/ppermute | solution.py:243
  28.8 0.1 collective-permute-start.3
  28.9 0.5 collective-permute-start.2
  29.4 0.0 copy-start
  29.4 3.4 %copy-done = f32[2,256,4096]{2,1,0:T(8,128)S(1)} copy-done((f32[2,256,4096]{2,1,0:T(8,128)S(1)}, f32[2,256,4096]{2,1,0:T(8,128)}, u32[]{:S(2)}) %copy-start) | copy-done | bytes 8388632
  32.8 1.0 %shard_map.66 = (bf16[4,512,1024]{2,1,0:T(8,128)(2,1)S(1)}, bf16[4,512,1024]{2,1,0:T(8,128)(2,1)S(1)}) custom-call(f32[2,256,4096]{2,1,0:T(8,128)S(1)} %copy-done), custom_call_target="tpu_custom_call" | custom-call | flops 6291456 | bytes 16777216 | tf_op jit(solution)/shard_map/pallas_call | solution.py:141
  33.8 0.0 collective-permute-done.1
  33.8 0.0 collective-permute-done.4
  33.8 6.8 %collective-permute-done.3 = f32[128,256]{1,0:T(8,128)S(1)} collective-permute-done((f32[128,256]{1,0:T(8,128)S(1)}, f32[128,256]{1,0:T(8,128)S(1)}, u32[]{:S(2)}, u32[]{:S(2)}) %collective-permute-start.3) | collective-permute-done | bytes 131104 | tf_op jit(solution)/shard_map/ppermute | solution.py:243
  40.6 0.0 collective-permute-done.2
  40.7 1.7 %collective-permute-start.6 = (f32[4,128,256]{2,1,0:T(8,128)S(1)}, f32[4,128,256]{2,1,0:T(8,128)S(1)}, u32[]{:S(2)}, u32[]{:S(2)}) collective-permute-start(f32[4,128,256]{2,1,0:T(8,128)S(1)} %pad_maximum_fusion.refs_0_.refs_3_), channel_id=1, source_target_pairs={{0,2},{1,3},{2,0},{3,1},{4,6},{5,7},{6,4},{7,5},{8,10},{9,11},{10,... | collective-permute-start | bytes 1572872 | tf_op jit(solution)/shard_map/ppermute | solution.py:243
  42.4 0.0 collective-permute-start.9
  42.4 1.5 %collective-permute-start.8 = (f32[2,64,256]{2,1,0:T(8,128)S(1)}, f32[2,64,256]{2,1,0:T(8,128)S(1)}, u32[]{:S(2)}, u32[]{:S(2)}) collective-permute-start(f32[2,64,256]{2,1,0:T(8,128)S(1)} %pad_maximum_fusion.4), channel_id=1, source_target_pairs={{0,8},{1,9},{2,10},{3,11},{4,12},{5,13},{6,14},{7,15},{8,0},{9,1},... | collective-permute-start | bytes 393224 | tf_op jit(solution)/shard_map/ppermute | solution.py:243
  43.9 2.0 %collective-permute-start.7 = (f32[2,64,256]{2,1,0:T(8,128)S(1)}, f32[2,64,256]{2,1,0:T(8,128)S(1)}, u32[]{:S(2)}, u32[]{:S(2)}) collective-permute-start(f32[2,64,256]{2,1,0:T(8,128)S(1)} %pad_maximum_fusion.4), channel_id=1, source_target_pairs={{0,4},{1,5},{2,6},{3,7},{4,8},{5,9},{6,10},{7,11},{8,12},{9,13},{1... | collective-permute-start | bytes 393224 | tf_op jit(solution)/shard_map/ppermute | solution.py:243
  45.9 0.0 collective-permute-start.5
  45.9 0.0 copy-done.1
  45.9 1.0 %shard_map.67 = (bf16[4,512,1024]{2,1,0:T(8,128)(2,1)S(1)}, bf16[4,512,1024]{2,1,0:T(8,128)(2,1)S(1)}) custom-call(f32[2,256,4096]{2,1,0:T(8,128)S(1)} %copy-done.1), custom_call_target="tpu_custom_call" | custom-call | flops 6291456 | bytes 16777216 | tf_op jit(solution)/shard_map/pallas_call | solution.py:141
  46.9 1.1 %collective-permute-done.9 = f32[2,64,256]{2,1,0:T(8,128)S(1)} collective-permute-done((f32[2,64,256]{2,1,0:T(8,128)S(1)}, f32[2,64,256]{2,1,0:T(8,128)S(1)}, u32[]{:S(2)}, u32[]{:S(2)}) %collective-permute-start.9) | collective-permute-done | bytes 131104 | tf_op jit(solution)/shard_map/ppermute | solution.py:243
  48.0 7.7 %collective-permute-done.8 = f32[2,64,256]{2,1,0:T(8,128)S(1)} collective-permute-done((f32[2,64,256]{2,1,0:T(8,128)S(1)}, f32[2,64,256]{2,1,0:T(8,128)S(1)}, u32[]{:S(2)}, u32[]{:S(2)}) %collective-permute-start.8) | collective-permute-done | bytes 131104 | tf_op jit(solution)/shard_map/ppermute | solution.py:243
  55.7 0.0 collective-permute-done.7
  55.7 0.0 collective-permute-done.6.refs_1_.refs_4_
  55.7 0.1 collective-permute-start.10
  55.8 0.5 collective-permute-start.11
  56.3 1.7 %shard_map.68.refs_5_ = f32[192,512]{1,0:T(8,128)S(1)} custom-call(f32[4,128,256]{2,1,0:T(8,128)S(1)} %pad_maximum_fusion.refs_0_.refs_3_, f32[4,128,256]{2,1,0:T(8,128)S(1)} %collective-permute-done.6.refs_1_.refs_4_, f32[4,2,64,256]{3,2,1,0:T(8,128)S(1)} %pad_maximum_fusion.1.refs_2_.refs_5_, bf16[4,512,1024]{2,1,0:T(8,128)(2,1)S(1)} %get-tuple-element.37.refs_3_, ...), custom_call_target="tpu_custom_call" | custom-call | flops 1207959552 | bytes 1048576 | tf_op jit(solution)/shard_map/pallas_call | solution.py:219
  58.0 0.0 collective-permute-done.5.refs_0_.refs_3_
  58.0 0.0 collective-permute-done.10.refs_1_.refs_4_
  58.0 0.5 collective-permute-done.11.refs_2_.refs_5_
  58.5 1.6 %shard_map.69 = (f32[128,256]{1,0:T(8,128)S(1)}, f32[64,256]{1,0:T(8,128)S(1)}) custom-call(f32[4,128,256]{2,1,0:T(8,128)S(1)} %collective-permute-done.5.refs_0_.refs_3_, f32[4,128,256]{2,1,0:T(8,128)S(1)} %collective-permute-done.10.refs_1_.refs_4_, f32[4,2,64,256]{3,2,1,0:T(8,128)S(1)} %collective-permute-done.11.refs_2_.refs_5_, ...), custom_call_target="tpu_custom_call" | custom-call | flops 1207959552 | bytes 1048576 | tf_op jit(solution)/shard_map/pallas_call | solution.py:219
  60.1 0.1 collective-permute-start.13
  60.2 1.8 %collective-permute-start.12 = (f32[64,256]{1,0:T(8,128)S(1)}, f32[64,256]{1,0:T(8,128)S(1)}, u32[]{:S(2)}, u32[]{:S(2)}) collective-permute-start(f32[64,256]{1,0:T(8,128)S(1)} %get-tuple-element.39), channel_id=1, source_target_pairs={{0,16},{1,17},{2,18},{3,19},{4,20},{5,21},{6,22},{7,23},{8,24},{9,... | collective-permute-start | bytes 196616 | tf_op jit(solution)/shard_map/ppermute | solution.py:245
  62.0 0.0 collective-permute-start.17
  62.0 2.0 %collective-permute-start.16 = (f32[128,256]{1,0:T(8,128)S(1)}, f32[128,256]{1,0:T(8,128)S(1)}, u32[]{:S(2)}, u32[]{:S(2)}) collective-permute-start(f32[128,256]{1,0:T(8,128)S(1)} %get-tuple-element.40), channel_id=1, source_target_pairs={{0,24},{1,25},{2,26},{3,27},{4,28},{5,29},{6,30},{7,31},{8,16},{9,... | collective-permute-start | bytes 393224 | tf_op jit(solution)/shard_map/ppermute | solution.py:245
  64.0 1.9 %collective-permute-start.15 = (f32[128,256]{1,0:T(8,128)S(1)}, f32[128,256]{1,0:T(8,128)S(1)}, u32[]{:S(2)}, u32[]{:S(2)}) collective-permute-start(f32[128,256]{1,0:T(8,128)S(1)} %get-tuple-element.40), channel_id=1, source_target_pairs={{0,20},{1,21},{2,22},{3,23},{4,24},{5,25},{6,26},{7,27},{8,28},{9,... | collective-permute-start | bytes 393224 | tf_op jit(solution)/shard_map/ppermute | solution.py:245
  65.9 0.0 collective-permute-done.13
  65.9 2.0 %collective-permute-start.14 = (f32[128,256]{1,0:T(8,128)S(1)}, f32[128,256]{1,0:T(8,128)S(1)}, u32[]{:S(2)}, u32[]{:S(2)}) collective-permute-start(f32[128,256]{1,0:T(8,128)S(1)} %get-tuple-element.40), channel_id=1, source_target_pairs={{0,16},{1,17},{2,18},{3,19},{4,20},{5,21},{6,22},{7,23},{8,24},{9,... | collective-permute-start | bytes 393224 | tf_op jit(solution)/shard_map/ppermute | solution.py:245
  67.9 2.8 %collective-permute-done.12 = f32[64,256]{1,0:T(8,128)S(1)} collective-permute-done((f32[64,256]{1,0:T(8,128)S(1)}, f32[64,256]{1,0:T(8,128)S(1)}, u32[]{:S(2)}, u32[]{:S(2)}) %collective-permute-start.12) | collective-permute-done | bytes 65568 | tf_op jit(solution)/shard_map/ppermute | solution.py:245
  70.8 0.0 collective-permute-done.17
  70.8 4.7 %collective-permute-done.16 = f32[128,256]{1,0:T(8,128)S(1)} collective-permute-done((f32[128,256]{1,0:T(8,128)S(1)}, f32[128,256]{1,0:T(8,128)S(1)}, u32[]{:S(2)}, u32[]{:S(2)}) %collective-permute-start.16) | collective-permute-done | bytes 131104 | tf_op jit(solution)/shard_map/ppermute | solution.py:245
  75.4 0.0 collective-permute-done.15
  75.4 1.3 %collective-permute-done.14 = f32[128,256]{1,0:T(8,128)S(1)} collective-permute-done((f32[128,256]{1,0:T(8,128)S(1)}, f32[128,256]{1,0:T(8,128)S(1)}, u32[]{:S(2)}, u32[]{:S(2)}) %collective-permute-start.14) | collective-permute-done | bytes 131104 | tf_op jit(solution)/shard_map/ppermute | solution.py:245
  76.7 1.7 %collective-permute-start.19 = (f32[4,128,256]{2,1,0:T(8,128)S(1)}, f32[4,128,256]{2,1,0:T(8,128)S(1)}, u32[]{:S(2)}, u32[]{:S(2)}) collective-permute-start(f32[4,128,256]{2,1,0:T(8,128)S(1)} %pad_maximum_fusion.2.refs_0_), channel_id=1, source_target_pairs={{0,2},{1,3},{2,0},{3,1},{4,6},{5,7},{6,4},{7,5},{8,10},{9,11},{10,... | collective-permute-start | bytes 1572872 | tf_op jit(solution)/shard_map/ppermute | solution.py:243
  78.5 1.3 %collective-permute-start.23 = (f32[2,64,256]{2,1,0:T(8,128)S(1)}, f32[2,64,256]{2,1,0:T(8,128)S(1)}, u32[]{:S(2)}, u32[]{:S(2)}) collective-permute-start(f32[2,64,256]{2,1,0:T(8,128)S(1)} %pad_maximum_fusion.5), channel_id=1, source_target_pairs={{0,12},{1,13},{2,14},{3,15},{4,0},{5,1},{6,2},{7,3},{8,4},{9,5},{1... | collective-permute-start | bytes 393224 | tf_op jit(solution)/shard_map/ppermute | solution.py:243
  79.8 0.0 collective-permute-start.22
  79.8 1.8 %collective-permute-start.21 = (f32[2,64,256]{2,1,0:T(8,128)S(1)}, f32[2,64,256]{2,1,0:T(8,128)S(1)}, u32[]{:S(2)}, u32[]{:S(2)}) collective-permute-start(f32[2,64,256]{2,1,0:T(8,128)S(1)} %pad_maximum_fusion.5), channel_id=1, source_target_pairs={{0,4},{1,5},{2,6},{3,7},{4,8},{5,9},{6,10},{7,11},{8,12},{9,13},{1... | collective-permute-start | bytes 393224 | tf_op jit(solution)/shard_map/ppermute | solution.py:243
  81.5 0.0 collective-permute-start.18
  81.5 2.7 %collective-permute-done.23 = f32[2,64,256]{2,1,0:T(8,128)S(1)} collective-permute-done((f32[2,64,256]{2,1,0:T(8,128)S(1)}, f32[2,64,256]{2,1,0:T(8,128)S(1)}, u32[]{:S(2)}, u32[]{:S(2)}) %collective-permute-start.23) | collective-permute-done | bytes 131104 | tf_op jit(solution)/shard_map/ppermute | solution.py:243
  84.2 6.9 %collective-permute-done.22 = f32[2,64,256]{2,1,0:T(8,128)S(1)} collective-permute-done((f32[2,64,256]{2,1,0:T(8,128)S(1)}, f32[2,64,256]{2,1,0:T(8,128)S(1)}, u32[]{:S(2)}, u32[]{:S(2)}) %collective-permute-start.22) | collective-permute-done | bytes 131104 | tf_op jit(solution)/shard_map/ppermute | solution.py:243
  91.1 0.0 collective-permute-done.21
  91.2 0.1 collective-permute-start.24
  91.3 0.0 collective-permute-done.19.refs_1_
  91.3 0.5 collective-permute-start.20
  91.8 1.7 %shard_map.70.refs_8_ = f32[192,512]{1,0:T(8,128)S(1)} custom-call(f32[4,128,256]{2,1,0:T(8,128)S(1)} %pad_maximum_fusion.2.refs_0_, f32[4,128,256]{2,1,0:T(8,128)S(1)} %collective-permute-done.19.refs_1_, f32[4,2,64,256]{3,2,1,0:T(8,128)S(1)} %pad_maximum_fusion.3.refs_2_, f32[4,128,256]{2,1,0:T(8,128)S(1)} %pad_maximum_fusion.refs_0_.refs_3_, ...), custom_call_target="tpu_custom_call" | custom-call | flops 1207959552 | bytes 1048576 | tf_op jit(solution)/shard_map/pallas_call | solution.py:219
  93.4 0.0 collective-permute-done.18.refs_0_
  93.4 0.0 collective-permute-done.24.refs_2_
  93.4 0.5 collective-permute-done.20.refs_1_
  93.9 2.3 %shard_map.71 = f32[192,256]{1,0:T(8,128)} custom-call(f32[4,128,256]{2,1,0:T(8,128)S(1)} %collective-permute-done.18.refs_0_, f32[4,128,256]{2,1,0:T(8,128)S(1)} %collective-permute-done.20.refs_1_, f32[4,2,64,256]{3,2,1,0:T(8,128)S(1)} %collective-permute-done.24.refs_2_, f32[4,128,256]{2,1,0:T(8,128)S(1)} %collective-permute-done.5.refs_0_.refs_3_, ...), custom_call_target="tpu_custom_call" | custom-call | flops 1207959552 | bytes 1048576 | tf_op jit(solution)/shard_map/pallas_call | solution.py:219
  (8 shorter events, 0.2 us)
Async XLA Ops:
  22.8 1.6 %collective-permute-start = (f32[8,56,128]{2,1,0:T(8,128)S(1)}, f32[8,56,128]{2,1,0:T(8,128)S(1)}, u32[]{:S(2)}, u32[]{:S(2)}) collective-permute-start(f32[8,56,128]{2,1,0:T(8,128)S(1)} %slice.4), channel_id=1, source_target_pairs={{0,1},{1,0},{2,3},{3,2},{4,5},{5,4},{6,7},{7,6},{8,9},{9,8},{10,11... | collective-permute-start | bytes 688136 | tf_op jit(solution)/shard_map/ppermute | solution.py:339
  24.3 0.9 copy-start.2
  26.0 7.8 %collective-permute-start.1 = (f32[64,256]{1,0:T(8,128)S(1)}, f32[64,256]{1,0:T(8,128)S(1)}, u32[]{:S(2)}, u32[]{:S(2)}) collective-permute-start(f32[64,256]{1,0:T(8,128)S(1)} %get-tuple-element.25), channel_id=1, source_target_pairs={{0,2},{1,3},{2,0},{3,1},{4,6},{5,7},{6,4},{7,5},{8,10},{9,11},{10,... | collective-permute-start | bytes 196616 | tf_op jit(solution)/shard_map/ppermute | solution.py:243
  27.4 6.4 %collective-permute-start.4 = (f32[128,256]{1,0:T(8,128)S(1)}, f32[128,256]{1,0:T(8,128)S(1)}, u32[]{:S(2)}, u32[]{:S(2)}) collective-permute-start(f32[128,256]{1,0:T(8,128)S(1)} %get-tuple-element.26), channel_id=1, source_target_pairs={{0,12},{1,13},{2,14},{3,15},{4,0},{5,1},{6,2},{7,3},{8,4},{9,5},{1... | collective-permute-start | bytes 393224 | tf_op jit(solution)/shard_map/ppermute | solution.py:243
  28.8 11.8 %collective-permute-start.3 = (f32[128,256]{1,0:T(8,128)S(1)}, f32[128,256]{1,0:T(8,128)S(1)}, u32[]{:S(2)}, u32[]{:S(2)}) collective-permute-start(f32[128,256]{1,0:T(8,128)S(1)} %get-tuple-element.26), channel_id=1, source_target_pairs={{0,8},{1,9},{2,10},{3,11},{4,12},{5,13},{6,14},{7,15},{8,0},{9,1},... | collective-permute-start | bytes 393224 | tf_op jit(solution)/shard_map/ppermute | solution.py:243
  28.9 11.7 %collective-permute-start.2 = (f32[128,256]{1,0:T(8,128)S(1)}, f32[128,256]{1,0:T(8,128)S(1)}, u32[]{:S(2)}, u32[]{:S(2)}) collective-permute-start(f32[128,256]{1,0:T(8,128)S(1)} %get-tuple-element.26), channel_id=1, source_target_pairs={{0,4},{1,5},{2,6},{3,7},{4,8},{5,9},{6,10},{7,11},{8,12},{9,13},{1... | collective-permute-start | bytes 393224 | tf_op jit(solution)/shard_map/ppermute | solution.py:243
  29.4 3.4 %copy-start = (f32[2,256,4096]{2,1,0:T(8,128)S(1)}, f32[2,256,4096]{2,1,0:T(8,128)}, u32[]{:S(2)}) copy-start(f32[2,256,4096]{2,1,0:T(8,128)} %matrix_ref) | copy-start | bytes 25165828
  32.8 13.1 %copy-start.1 = (f32[2,256,4096]{2,1,0:T(8,128)S(1)}, f32[2,256,4096]{2,1,0:T(8,128)}, u32[]{:S(2)}) copy-start(f32[2,256,4096]{2,1,0:T(8,128)} %matrix_ref.1) | copy-start | bytes 25165828
  40.7 15.1 %collective-permute-start.6 = (f32[4,128,256]{2,1,0:T(8,128)S(1)}, f32[4,128,256]{2,1,0:T(8,128)S(1)}, u32[]{:S(2)}, u32[]{:S(2)}) collective-permute-start(f32[4,128,256]{2,1,0:T(8,128)S(1)} %pad_maximum_fusion.refs_0_.refs_3_), channel_id=1, source_target_pairs={{0,2},{1,3},{2,0},{3,1},{4,6},{5,7},{6,4},{7,5},{8,10},{9,11},{10,... | collective-permute-start | bytes 1572872 | tf_op jit(solution)/shard_map/ppermute | solution.py:243
  42.4 5.6 %collective-permute-start.9 = (f32[2,64,256]{2,1,0:T(8,128)S(1)}, f32[2,64,256]{2,1,0:T(8,128)S(1)}, u32[]{:S(2)}, u32[]{:S(2)}) collective-permute-start(f32[2,64,256]{2,1,0:T(8,128)S(1)} %pad_maximum_fusion.4), channel_id=1, source_target_pairs={{0,12},{1,13},{2,14},{3,15},{4,0},{5,1},{6,2},{7,3},{8,4},{9,5},{1... | collective-permute-start | bytes 393224 | tf_op jit(solution)/shard_map/ppermute | solution.py:243
  42.4 13.3 %collective-permute-start.8 = (f32[2,64,256]{2,1,0:T(8,128)S(1)}, f32[2,64,256]{2,1,0:T(8,128)S(1)}, u32[]{:S(2)}, u32[]{:S(2)}) collective-permute-start(f32[2,64,256]{2,1,0:T(8,128)S(1)} %pad_maximum_fusion.4), channel_id=1, source_target_pairs={{0,8},{1,9},{2,10},{3,11},{4,12},{5,13},{6,14},{7,15},{8,0},{9,1},... | collective-permute-start | bytes 393224 | tf_op jit(solution)/shard_map/ppermute | solution.py:243
  43.9 11.8 %collective-permute-start.7 = (f32[2,64,256]{2,1,0:T(8,128)S(1)}, f32[2,64,256]{2,1,0:T(8,128)S(1)}, u32[]{:S(2)}, u32[]{:S(2)}) collective-permute-start(f32[2,64,256]{2,1,0:T(8,128)S(1)} %pad_maximum_fusion.4), channel_id=1, source_target_pairs={{0,4},{1,5},{2,6},{3,7},{4,8},{5,9},{6,10},{7,11},{8,12},{9,13},{1... | collective-permute-start | bytes 393224 | tf_op jit(solution)/shard_map/ppermute | solution.py:243
  45.9 12.1 %collective-permute-start.5 = (f32[4,128,256]{2,1,0:T(8,128)S(1)}, f32[4,128,256]{2,1,0:T(8,128)S(1)}, u32[]{:S(2)}, u32[]{:S(2)}) collective-permute-start(f32[4,128,256]{2,1,0:T(8,128)S(1)} %pad_maximum_fusion.refs_0_.refs_3_), channel_id=1, source_target_pairs={{0,1},{1,0},{2,3},{3,2},{4,5},{5,4},{6,7},{7,6},{8,9},{9,8},{10,11... | collective-permute-start | bytes 1572872 | tf_op jit(solution)/shard_map/ppermute | solution.py:243
  55.7 2.3 %collective-permute-start.10 = (f32[4,128,256]{2,1,0:T(8,128)S(1)}, f32[4,128,256]{2,1,0:T(8,128)S(1)}, u32[]{:S(2)}, u32[]{:S(2)}) collective-permute-start(f32[4,128,256]{2,1,0:T(8,128)S(1)} %collective-permute-done.6.refs_1_.refs_4_), channel_id=1, source_target_pairs={{0,1},{1,0},{2,3},{3,2},{4,5},{5,4},{6,7},{7,6},{8,9},{9,8},{10,11... | collective-permute-start | bytes 1572872 | tf_op jit(solution)/shard_map/ppermute | solution.py:243
  55.8 2.6 %collective-permute-start.11 = (f32[4,2,64,256]{3,2,1,0:T(8,128)S(1)}, f32[4,2,64,256]{3,2,1,0:T(8,128)S(1)}, u32[]{:S(2)}, u32[]{:S(2)}) collective-permute-start(f32[4,2,64,256]{3,2,1,0:T(8,128)S(1)} %pad_maximum_fusion.1.refs_2_.refs_5_), channel_id=1, source_target_pairs={{0,1},{1,0},{2,3},{3,2},{4,5},{5,4},{6,7},{7,6},{8,9},{9,8},{10,11... | collective-permute-start | bytes 1572872 | tf_op jit(solution)/shard_map/ppermute | solution.py:243
  60.1 5.8 %collective-permute-start.13 = (f32[64,256]{1,0:T(8,128)S(1)}, f32[64,256]{1,0:T(8,128)S(1)}, u32[]{:S(2)}, u32[]{:S(2)}) collective-permute-start(f32[64,256]{1,0:T(8,128)S(1)} %get-tuple-element.39), channel_id=1, source_target_pairs={{0,18},{1,19},{2,16},{3,17},{4,22},{5,23},{6,20},{7,21},{8,26},{9,... | collective-permute-start | bytes 196616 | tf_op jit(solution)/shard_map/ppermute | solution.py:245
  60.2 10.6 %collective-permute-start.12 = (f32[64,256]{1,0:T(8,128)S(1)}, f32[64,256]{1,0:T(8,128)S(1)}, u32[]{:S(2)}, u32[]{:S(2)}) collective-permute-start(f32[64,256]{1,0:T(8,128)S(1)} %get-tuple-element.39), channel_id=1, source_target_pairs={{0,16},{1,17},{2,18},{3,19},{4,20},{5,21},{6,22},{7,23},{8,24},{9,... | collective-permute-start | bytes 196616 | tf_op jit(solution)/shard_map/ppermute | solution.py:245
  62.0 8.8 %collective-permute-start.17 = (f32[128,256]{1,0:T(8,128)S(1)}, f32[128,256]{1,0:T(8,128)S(1)}, u32[]{:S(2)}, u32[]{:S(2)}) collective-permute-start(f32[128,256]{1,0:T(8,128)S(1)} %get-tuple-element.40), channel_id=1, source_target_pairs={{0,28},{1,29},{2,30},{3,31},{4,16},{5,17},{6,18},{7,19},{8,20},{9,... | collective-permute-start | bytes 393224 | tf_op jit(solution)/shard_map/ppermute | solution.py:245
  62.0 13.5 %collective-permute-start.16 = (f32[128,256]{1,0:T(8,128)S(1)}, f32[128,256]{1,0:T(8,128)S(1)}, u32[]{:S(2)}, u32[]{:S(2)}) collective-permute-start(f32[128,256]{1,0:T(8,128)S(1)} %get-tuple-element.40), channel_id=1, source_target_pairs={{0,24},{1,25},{2,26},{3,27},{4,28},{5,29},{6,30},{7,31},{8,16},{9,... | collective-permute-start | bytes 393224 | tf_op jit(solution)/shard_map/ppermute | solution.py:245
  64.0 11.5 %collective-permute-start.15 = (f32[128,256]{1,0:T(8,128)S(1)}, f32[128,256]{1,0:T(8,128)S(1)}, u32[]{:S(2)}, u32[]{:S(2)}) collective-permute-start(f32[128,256]{1,0:T(8,128)S(1)} %get-tuple-element.40), channel_id=1, source_target_pairs={{0,20},{1,21},{2,22},{3,23},{4,24},{5,25},{6,26},{7,27},{8,28},{9,... | collective-permute-start | bytes 393224 | tf_op jit(solution)/shard_map/ppermute | solution.py:245
  65.9 10.8 %collective-permute-start.14 = (f32[128,256]{1,0:T(8,128)S(1)}, f32[128,256]{1,0:T(8,128)S(1)}, u32[]{:S(2)}, u32[]{:S(2)}) collective-permute-start(f32[128,256]{1,0:T(8,128)S(1)} %get-tuple-element.40), channel_id=1, source_target_pairs={{0,16},{1,17},{2,18},{3,19},{4,20},{5,21},{6,22},{7,23},{8,24},{9,... | collective-permute-start | bytes 393224 | tf_op jit(solution)/shard_map/ppermute | solution.py:245
  76.7 14.5 %collective-permute-start.19 = (f32[4,128,256]{2,1,0:T(8,128)S(1)}, f32[4,128,256]{2,1,0:T(8,128)S(1)}, u32[]{:S(2)}, u32[]{:S(2)}) collective-permute-start(f32[4,128,256]{2,1,0:T(8,128)S(1)} %pad_maximum_fusion.2.refs_0_), channel_id=1, source_target_pairs={{0,2},{1,3},{2,0},{3,1},{4,6},{5,7},{6,4},{7,5},{8,10},{9,11},{10,... | collective-permute-start | bytes 1572872 | tf_op jit(solution)/shard_map/ppermute | solution.py:243
  78.5 5.7 %collective-permute-start.23 = (f32[2,64,256]{2,1,0:T(8,128)S(1)}, f32[2,64,256]{2,1,0:T(8,128)S(1)}, u32[]{:S(2)}, u32[]{:S(2)}) collective-permute-start(f32[2,64,256]{2,1,0:T(8,128)S(1)} %pad_maximum_fusion.5), channel_id=1, source_target_pairs={{0,12},{1,13},{2,14},{3,15},{4,0},{5,1},{6,2},{7,3},{8,4},{9,5},{1... | collective-permute-start | bytes 393224 | tf_op jit(solution)/shard_map/ppermute | solution.py:243
  79.8 11.4 %collective-permute-start.22 = (f32[2,64,256]{2,1,0:T(8,128)S(1)}, f32[2,64,256]{2,1,0:T(8,128)S(1)}, u32[]{:S(2)}, u32[]{:S(2)}) collective-permute-start(f32[2,64,256]{2,1,0:T(8,128)S(1)} %pad_maximum_fusion.5), channel_id=1, source_target_pairs={{0,8},{1,9},{2,10},{3,11},{4,12},{5,13},{6,14},{7,15},{8,0},{9,1},... | collective-permute-start | bytes 393224 | tf_op jit(solution)/shard_map/ppermute | solution.py:243
  79.8 11.4 %collective-permute-start.21 = (f32[2,64,256]{2,1,0:T(8,128)S(1)}, f32[2,64,256]{2,1,0:T(8,128)S(1)}, u32[]{:S(2)}, u32[]{:S(2)}) collective-permute-start(f32[2,64,256]{2,1,0:T(8,128)S(1)} %pad_maximum_fusion.5), channel_id=1, source_target_pairs={{0,4},{1,5},{2,6},{3,7},{4,8},{5,9},{6,10},{7,11},{8,12},{9,13},{1... | collective-permute-start | bytes 393224 | tf_op jit(solution)/shard_map/ppermute | solution.py:243
  81.5 11.9 %collective-permute-start.18 = (f32[4,128,256]{2,1,0:T(8,128)S(1)}, f32[4,128,256]{2,1,0:T(8,128)S(1)}, u32[]{:S(2)}, u32[]{:S(2)}) collective-permute-start(f32[4,128,256]{2,1,0:T(8,128)S(1)} %pad_maximum_fusion.2.refs_0_), channel_id=1, source_target_pairs={{0,1},{1,0},{2,3},{3,2},{4,5},{5,4},{6,7},{7,6},{8,9},{9,8},{10,11... | collective-permute-start | bytes 1572872 | tf_op jit(solution)/shard_map/ppermute | solution.py:243
  91.2 2.3 %collective-permute-start.24 = (f32[4,2,64,256]{3,2,1,0:T(8,128)S(1)}, f32[4,2,64,256]{3,2,1,0:T(8,128)S(1)}, u32[]{:S(2)}, u32[]{:S(2)}) collective-permute-start(f32[4,2,64,256]{3,2,1,0:T(8,128)S(1)} %pad_maximum_fusion.3.refs_2_), channel_id=1, source_target_pairs={{0,1},{1,0},{2,3},{3,2},{4,5},{5,4},{6,7},{7,6},{8,9},{9,8},{10,11... | collective-permute-start | bytes 1572872 | tf_op jit(solution)/shard_map/ppermute | solution.py:243
  91.3 2.6 %collective-permute-start.20 = (f32[4,128,256]{2,1,0:T(8,128)S(1)}, f32[4,128,256]{2,1,0:T(8,128)S(1)}, u32[]{:S(2)}, u32[]{:S(2)}) collective-permute-start(f32[4,128,256]{2,1,0:T(8,128)S(1)} %collective-permute-done.19.refs_1_), channel_id=1, source_target_pairs={{0,1},{1,0},{2,3},{3,2},{4,5},{5,4},{6,7},{7,6},{8,9},{9,8},{10,11... | collective-permute-start | bytes 1572872 | tf_op jit(solution)/shard_map/ppermute | solution.py:243

commit v14 on v11

--- a/solution.py
+++ b/solution.py
@@ -151,7 +151,7 @@
     me = lax.axis_index("tile")
 
     def block_of(step, layer):
-        held = lax.rem(lax.div(me, 4) + (layers - layer), layers) if relative else layer
+        held = lax.div(me, 4) ^ layer if relative else layer
         pieces = []
         for group in layout:
             which, place = group(step, held)
@@ -237,12 +237,12 @@
 
     def first_stage(first, second, hop):
         pair = [second if across == 0 and not hop else send(second, hop, lambda t: t ^ (2 * across)) for across in range(2)]
-        line = [first if by == 0 and not hop else send(first, hop, lambda t: (t + 4 * by) % tile_size) for by in range(layers)]
+        line = [first if by == 0 and not hop else send(first, hop, lambda t: t ^ (4 * by)) for by in range(layers)]
         return jnp.stack(pair), jnp.stack(line)
 
     def second_stage(pair, line):
         far = send(line, False, lambda t: t ^ 2)
-        rest = [pair if by == 0 else send(pair, False, lambda t: (t + 4 * by) % tile_size) for by in range(layers)]
+        rest = [pair if by == 0 else send(pair, False, lambda t: t ^ (4 * by)) for by in range(layers)]
         return [line, far, jnp.stack(rest)]
 
     layout = [lambda step, held: (step % 2, (held,)), lambda step, held: (2, (held, step % 2))]
@@ -322,7 +322,7 @@
         compiler_params=kernel_params(56),
     )(tile_counts, update_rows[None, :], updates.T)
     received = lax.all_to_all(packed, "tile", 0, 0, tiled=False)
-    paired = own_rows % 128 == 0 and tile_size % 8 == 0 and batches > 1
+    paired = own_rows % 128 == 0 and tile_size >= 8 and tile_size & (tile_size - 1) == 0 and batches > 1
     early = batches * 2 // 3 * halves * sources
     shares = [early, columns - early] if paired else [columns]
     reduced = pl.pallas_call(

time: 95.4 us -> 95.1 us (level)
  waiting for transfers between devices: 35 us -> 31.6 us
  starting transfers between devices: 22.7 us -> 25.8 us
    ppermute x18, waiting for transfers between devices: 26.2 us -> 22.3 us  [send(): lax.ppermute(value, 'tile', [(t, target(t)) for t in range(tile_size)])]
    ppermute x6, starting transfers between devices: 7.81 us -> 9.78 us  [send(): return lax.ppermute(value, ('chain', 'tile'), pairs)]
    ppermute x18, starting transfers between devices: 14.9 us -> 16 us  [send(): lax.ppermute(value, 'tile', [(t, target(t)) for t in range(tile_size)])]
  transfers between devices with their start and end apart: 24 -> 24, of which waited for: 10 -> 12; matrix products, arithmetic and copies ran while one was open for 0% -> 0% of each run, Pallas kernels for 6% -> 6%
where the time goes in v14:
time: 95.1 us; the launch traced here: 94.8 us
  waiting for transfers between devices  31.6 us (33%)
  starting transfers between devices  25.8 us (27%)
  blocking collectives  20.6 us (22%)
  Pallas kernels  12.1 us (13%)
  local copies, waits for them, and re-layouts  4.31 us (5%)
    ppermute x18, waiting for transfers between devices, send(): lax.ppermute(value, 'tile', [(t, target(t)) for t in range(tile_size)])  22.3 us
    all_to_all x1, blocking collectives, body(): received = lax.all_to_all(packed, 'tile', 0, 0, tiled=False)  20.6 us
    ppermute x18, starting transfers between devices, send(): lax.ppermute(value, 'tile', [(t, target(t)) for t in range(tile_size)])  16 us
    ppermute x6, starting transfers between devices, send(): return lax.ppermute(value, ('chain', 'tile'), pairs)  9.78 us
    ppermute x6, waiting for transfers between devices, send(): return lax.ppermute(value, ('chain', 'tile'), pairs)  9.33 us
    pallas_call x4, Pallas kernels, product_part(): pl.pallas_call(functools.partial(product_kernel, sources, layout, len(blo...  7.19 us
    unnamed x6, local copies, waits for them, and re-layouts  4.31 us
    pallas_call x1, Pallas kernels, body(): pl.pallas_call(functools.partial(pack_kernel, own_rows, cap, tile_rows),...  2.19 us
  transfers between devices with their start and end apart: 24, of which 12 were waited for; matrix products, arithmetic and copies ran while one was open for 0% of the time, Pallas kernels for 6%

profile of v14, /device:TPU:0, one launch (start us, length us, event | category | flops | bytes accessed | tf_op | source)
XLA Modules:
  0.0 94.8 jit_solution(12323971535302996990)
XLA Ops:
  0.0 2.2 %shard_map.64 = f32[16,56,128]{2,1,0:T(8,128)} custom-call(s32[2]{0:T(128)} %counts_hbm.1, s32[1,256]{1,0:T(1,128)} %bitcast.46, f32[192,256]{1,0:T(8,128)} %bitcast.29), custom_call_target="tpu_custom_call" | custom-call | tf_op jit(solution)/shard_map/pallas_call | solution.py:311
  2.2 20.6 %all_to_all.5.received_ref = f32[16,56,128]{2,1,0:T(8,128)S(1)} all-to-all(f32[16,56,128]{2,1,0:T(8,128)} %shard_map.64), channel_id=1, replica_groups=mesh['chain'=2,'tile'=16] {'tile'}, dimensions={0} | all-to-all | bytes 917504 | tf_op jit(solution)/shard_map/all_to_all | solution.py:324
  22.9 0.0 copy-start.2
  22.9 0.9 copy-done.2
  23.8 0.8 shard_map.65
  24.5 0.4 collective-permute-start
  25.0 2.7 %collective-permute-start.3 = (f32[128,256]{1,0:T(8,128)S(1)}, f32[128,256]{1,0:T(8,128)S(1)}, u32[]{:S(2)}, u32[]{:S(2)}) collective-permute-start(f32[128,256]{1,0:T(8,128)S(1)} %get-tuple-element.26), channel_id=1, source_target_pairs={{0,12},{1,13},{2,14},{3,15},{4,8},{5,9},{6,10},{7,11},{8,4},{9,5},... | collective-permute-start | bytes 393224 | tf_op jit(solution)/shard_map/ppermute | solution.py:234
  27.7 0.5 collective-permute-start.2
  28.2 1.1 %collective-permute-start.1 = (f32[128,256]{1,0:T(8,128)S(1)}, f32[128,256]{1,0:T(8,128)S(1)}, u32[]{:S(2)}, u32[]{:S(2)}) collective-permute-start(f32[128,256]{1,0:T(8,128)S(1)} %get-tuple-element.26), channel_id=1, source_target_pairs={{0,4},{1,5},{2,6},{3,7},{4,0},{5,1},{6,2},{7,3},{8,12},{9,13},{10,... | collective-permute-start | bytes 393224 | tf_op jit(solution)/shard_map/ppermute | solution.py:234
  29.4 0.0 copy-start
  29.4 3.4 %copy-done = f32[2,256,4096]{2,1,0:T(8,128)S(1)} copy-done((f32[2,256,4096]{2,1,0:T(8,128)S(1)}, f32[2,256,4096]{2,1,0:T(8,128)}, u32[]{:S(2)}) %copy-start) | copy-done | bytes 8388632
  32.7 0.0 copy-start.1
  32.7 1.0 %shard_map.66 = (bf16[4,512,1024]{2,1,0:T(8,128)(2,1)S(1)}, bf16[4,512,1024]{2,1,0:T(8,128)(2,1)S(1)}) custom-call(f32[2,256,4096]{2,1,0:T(8,128)S(1)} %copy-done), custom_call_target="tpu_custom_call" | custom-call | flops 6291456 | bytes 16777216 | tf_op jit(solution)/shard_map/pallas_call | solution.py:132
  33.7 0.0 collective-permute-done
  33.8 0.0 collective-permute-done.3
  33.8 6.3 %collective-permute-done.2 = f32[128,256]{1,0:T(8,128)S(1)} collective-permute-done((f32[128,256]{1,0:T(8,128)S(1)}, f32[128,256]{1,0:T(8,128)S(1)}, u32[]{:S(2)}, u32[]{:S(2)}) %collective-permute-start.2) | collective-permute-done | bytes 131104 | tf_op jit(solution)/shard_map/ppermute | solution.py:234
  40.1 0.0 collective-permute-done.1
  40.1 1.2 %collective-permute-start.5 = (f32[4,128,256]{2,1,0:T(8,128)S(1)}, f32[4,128,256]{2,1,0:T(8,128)S(1)}, u32[]{:S(2)}, u32[]{:S(2)}) collective-permute-start(f32[4,128,256]{2,1,0:T(8,128)S(1)} %pad_maximum_fusion.refs_0_.refs_3_), channel_id=1, source_target_pairs={{0,2},{1,3},{2,0},{3,1},{4,6},{5,7},{6,4},{7,5},{8,10},{9,11},{10,... | collective-permute-start | bytes 1572872 | tf_op jit(solution)/shard_map/ppermute | solution.py:234
  41.3 1.4 %collective-permute-start.8 = (f32[2,64,256]{2,1,0:T(8,128)S(1)}, f32[2,64,256]{2,1,0:T(8,128)S(1)}, u32[]{:S(2)}, u32[]{:S(2)}) collective-permute-start(f32[2,64,256]{2,1,0:T(8,128)S(1)} %pad_maximum_fusion.4), channel_id=1, source_target_pairs={{0,12},{1,13},{2,14},{3,15},{4,8},{5,9},{6,10},{7,11},{8,4},{9,5},... | collective-permute-start | bytes 393224 | tf_op jit(solution)/shard_map/ppermute | solution.py:234
  42.7 0.0 collective-permute-start.7
  42.7 3.0 %collective-permute-start.6 = (f32[2,64,256]{2,1,0:T(8,128)S(1)}, f32[2,64,256]{2,1,0:T(8,128)S(1)}, u32[]{:S(2)}, u32[]{:S(2)}) collective-permute-start(f32[2,64,256]{2,1,0:T(8,128)S(1)} %pad_maximum_fusion.4), channel_id=1, source_target_pairs={{0,4},{1,5},{2,6},{3,7},{4,0},{5,1},{6,2},{7,3},{8,12},{9,13},{10,... | collective-permute-start | bytes 393224 | tf_op jit(solution)/shard_map/ppermute | solution.py:234
  45.7 0.0 collective-permute-start.4
  45.7 0.0 copy-done.1
  45.7 1.0 %shard_map.67 = (bf16[4,512,1024]{2,1,0:T(8,128)(2,1)S(1)}, bf16[4,512,1024]{2,1,0:T(8,128)(2,1)S(1)}) custom-call(f32[2,256,4096]{2,1,0:T(8,128)S(1)} %copy-done.1), custom_call_target="tpu_custom_call" | custom-call | flops 6291456 | bytes 16777216 | tf_op jit(solution)/shard_map/pallas_call | solution.py:132
  46.7 2.9 %collective-permute-done.8 = f32[2,64,256]{2,1,0:T(8,128)S(1)} collective-permute-done((f32[2,64,256]{2,1,0:T(8,128)S(1)}, f32[2,64,256]{2,1,0:T(8,128)S(1)}, u32[]{:S(2)}, u32[]{:S(2)}) %collective-permute-start.8) | collective-permute-done | bytes 131104 | tf_op jit(solution)/shard_map/ppermute | solution.py:234
  49.6 3.2 %collective-permute-done.7 = f32[2,64,256]{2,1,0:T(8,128)S(1)} collective-permute-done((f32[2,64,256]{2,1,0:T(8,128)S(1)}, f32[2,64,256]{2,1,0:T(8,128)S(1)}, u32[]{:S(2)}, u32[]{:S(2)}) %collective-permute-start.7) | collective-permute-done | bytes 131104 | tf_op jit(solution)/shard_map/ppermute | solution.py:234
  52.8 0.0 collective-permute-done.6
  52.8 0.4 collective-permute-done.5.refs_1_.refs_4_
  53.2 0.0 collective-permute-start.9
  53.2 0.5 collective-permute-start.10
  53.7 1.7 %shard_map.68.refs_5_ = f32[192,512]{1,0:T(8,128)S(1)} custom-call(f32[4,128,256]{2,1,0:T(8,128)S(1)} %pad_maximum_fusion.refs_0_.refs_3_, f32[4,128,256]{2,1,0:T(8,128)S(1)} %collective-permute-done.5.refs_1_.refs_4_, f32[4,2,64,256]{3,2,1,0:T(8,128)S(1)} %pad_maximum_fusion.1.refs_2_.refs_5_, bf16[4,512,1024]{2,1,0:T(8,128)(2,1)S(1)} %get-tuple-element.37.refs_3_, ...), custom_call_target="tpu_custom_call" | custom-call | flops 1207959552 | bytes 1048576 | tf_op jit(solution)/shard_map/pallas_call | solution.py:210
  55.3 0.0 collective-permute-done.4.refs_0_.refs_3_
  55.4 0.0 collective-permute-done.9.refs_1_.refs_4_
  55.4 0.5 collective-permute-done.10.refs_2_.refs_5_
  55.8 1.6 %shard_map.69 = (f32[128,256]{1,0:T(8,128)S(1)}, f32[64,256]{1,0:T(8,128)S(1)}) custom-call(f32[4,128,256]{2,1,0:T(8,128)S(1)} %collective-permute-done.4.refs_0_.refs_3_, f32[4,128,256]{2,1,0:T(8,128)S(1)} %collective-permute-done.9.refs_1_.refs_4_, f32[4,2,64,256]{3,2,1,0:T(8,128)S(1)} %collective-permute-done.10.refs_2_.refs_5_, ...), custom_call_target="tpu_custom_call" | custom-call | flops 1207959552 | bytes 1048576 | tf_op jit(solution)/shard_map/pallas_call | solution.py:210
  57.4 0.9 collective-permute-start.12
  58.3 2.1 %collective-permute-start.11 = (f32[64,256]{1,0:T(8,128)S(1)}, f32[64,256]{1,0:T(8,128)S(1)}, u32[]{:S(2)}, u32[]{:S(2)}) collective-permute-start(f32[64,256]{1,0:T(8,128)S(1)} %get-tuple-element.39), channel_id=1, source_target_pairs={{0,16},{1,17},{2,18},{3,19},{4,20},{5,21},{6,22},{7,23},{8,24},{9,... | collective-permute-start | bytes 196616 | tf_op jit(solution)/shard_map/ppermute | solution.py:236
  60.5 0.9 collective-permute-start.16
  61.4 0.6 collective-permute-start.15
  62.0 3.2 %collective-permute-start.14 = (f32[128,256]{1,0:T(8,128)S(1)}, f32[128,256]{1,0:T(8,128)S(1)}, u32[]{:S(2)}, u32[]{:S(2)}) collective-permute-start(f32[128,256]{1,0:T(8,128)S(1)} %get-tuple-element.40), channel_id=1, source_target_pairs={{0,20},{1,21},{2,22},{3,23},{4,16},{5,17},{6,18},{7,19},{8,28},{9,... | collective-permute-start | bytes 393224 | tf_op jit(solution)/shard_map/ppermute | solution.py:236
  65.2 0.0 collective-permute-done.12
  65.2 2.0 %collective-permute-start.13 = (f32[128,256]{1,0:T(8,128)S(1)}, f32[128,256]{1,0:T(8,128)S(1)}, u32[]{:S(2)}, u32[]{:S(2)}) collective-permute-start(f32[128,256]{1,0:T(8,128)S(1)} %get-tuple-element.40), channel_id=1, source_target_pairs={{0,16},{1,17},{2,18},{3,19},{4,20},{5,21},{6,22},{7,23},{8,24},{9,... | collective-permute-start | bytes 393224 | tf_op jit(solution)/shard_map/ppermute | solution.py:236
  67.2 0.0 collective-permute-done.11
  67.2 2.5 %collective-permute-done.16 = f32[128,256]{1,0:T(8,128)S(1)} collective-permute-done((f32[128,256]{1,0:T(8,128)S(1)}, f32[128,256]{1,0:T(8,128)S(1)}, u32[]{:S(2)}, u32[]{:S(2)}) %collective-permute-start.16) | collective-permute-done | bytes 131104 | tf_op jit(solution)/shard_map/ppermute | solution.py:236
  69.7 4.1 %collective-permute-done.15 = f32[128,256]{1,0:T(8,128)S(1)} collective-permute-done((f32[128,256]{1,0:T(8,128)S(1)}, f32[128,256]{1,0:T(8,128)S(1)}, u32[]{:S(2)}, u32[]{:S(2)}) %collective-permute-start.15) | collective-permute-done | bytes 131104 | tf_op jit(solution)/shard_map/ppermute | solution.py:236
  73.8 0.0 collective-permute-done.14
  73.9 2.7 %collective-permute-done.13 = f32[128,256]{1,0:T(8,128)S(1)} collective-permute-done((f32[128,256]{1,0:T(8,128)S(1)}, f32[128,256]{1,0:T(8,128)S(1)}, u32[]{:S(2)}, u32[]{:S(2)}) %collective-permute-start.13) | collective-permute-done | bytes 131104 | tf_op jit(solution)/shard_map/ppermute | solution.py:236
  76.6 0.6 collective-permute-start.18
  77.2 2.2 %collective-permute-start.22 = (f32[2,64,256]{2,1,0:T(8,128)S(1)}, f32[2,64,256]{2,1,0:T(8,128)S(1)}, u32[]{:S(2)}, u32[]{:S(2)}) collective-permute-start(f32[2,64,256]{2,1,0:T(8,128)S(1)} %pad_maximum_fusion.5), channel_id=1, source_target_pairs={{0,12},{1,13},{2,14},{3,15},{4,8},{5,9},{6,10},{7,11},{8,4},{9,5},... | collective-permute-start | bytes 393224 | tf_op jit(solution)/shard_map/ppermute | solution.py:234
  79.4 0.0 collective-permute-start.21
  79.4 2.2 %collective-permute-start.20 = (f32[2,64,256]{2,1,0:T(8,128)S(1)}, f32[2,64,256]{2,1,0:T(8,128)S(1)}, u32[]{:S(2)}, u32[]{:S(2)}) collective-permute-start(f32[2,64,256]{2,1,0:T(8,128)S(1)} %pad_maximum_fusion.5), channel_id=1, source_target_pairs={{0,4},{1,5},{2,6},{3,7},{4,0},{5,1},{6,2},{7,3},{8,12},{9,13},{10,... | collective-permute-start | bytes 393224 | tf_op jit(solution)/shard_map/ppermute | solution.py:234
  81.6 0.0 collective-permute-start.17
  81.6 3.9 %collective-permute-done.22 = f32[2,64,256]{2,1,0:T(8,128)S(1)} collective-permute-done((f32[2,64,256]{2,1,0:T(8,128)S(1)}, f32[2,64,256]{2,1,0:T(8,128)S(1)}, u32[]{:S(2)}, u32[]{:S(2)}) %collective-permute-start.22) | collective-permute-done | bytes 131104 | tf_op jit(solution)/shard_map/ppermute | solution.py:234
  85.5 4.3 %collective-permute-done.21 = f32[2,64,256]{2,1,0:T(8,128)S(1)} collective-permute-done((f32[2,64,256]{2,1,0:T(8,128)S(1)}, f32[2,64,256]{2,1,0:T(8,128)S(1)}, u32[]{:S(2)}, u32[]{:S(2)}) %collective-permute-start.21) | collective-permute-done | bytes 131104 | tf_op jit(solution)/shard_map/ppermute | solution.py:234
  89.8 0.0 collective-permute-done.20
  89.8 0.1 collective-permute-start.23
  89.9 0.6 collective-permute-done.18.refs_1_
  90.5 0.0 collective-permute-start.19
  90.5 1.7 %shard_map.70.refs_8_ = f32[192,512]{1,0:T(8,128)S(1)} custom-call(f32[4,128,256]{2,1,0:T(8,128)S(1)} %pad_maximum_fusion.2.refs_0_, f32[4,128,256]{2,1,0:T(8,128)S(1)} %collective-permute-done.18.refs_1_, f32[4,2,64,256]{3,2,1,0:T(8,128)S(1)} %pad_maximum_fusion.3.refs_2_, f32[4,128,256]{2,1,0:T(8,128)S(1)} %pad_maximum_fusion.refs_0_.refs_3_, ...), custom_call_target="tpu_custom_call" | custom-call | flops 1207959552 | bytes 1048576 | tf_op jit(solution)/shard_map/pallas_call | solution.py:210
  92.2 0.0 collective-permute-done.17.refs_0_
  92.2 0.0 collective-permute-done.23.refs_2_
  92.2 0.3 collective-permute-done.19.refs_1_
  92.5 2.3 %shard_map.71 = f32[192,256]{1,0:T(8,128)} custom-call(f32[4,128,256]{2,1,0:T(8,128)S(1)} %collective-permute-done.17.refs_0_, f32[4,128,256]{2,1,0:T(8,128)S(1)} %collective-permute-done.19.refs_1_, f32[4,2,64,256]{3,2,1,0:T(8,128)S(1)} %collective-permute-done.23.refs_2_, f32[4,128,256]{2,1,0:T(8,128)S(1)} %collective-permute-done.4.refs_0_.refs_3_, ...), custom_call_target="tpu_custom_call" | custom-call | flops 1207959552 | bytes 1048576 | tf_op jit(solution)/shard_map/pallas_call | solution.py:210
  (6 shorter events, 0.2 us)
Async XLA Ops:
  22.9 0.9 copy-start.2
  24.5 9.2 %collective-permute-start = (f32[64,256]{1,0:T(8,128)S(1)}, f32[64,256]{1,0:T(8,128)S(1)}, u32[]{:S(2)}, u32[]{:S(2)}) collective-permute-start(f32[64,256]{1,0:T(8,128)S(1)} %get-tuple-element.25), channel_id=1, source_target_pairs={{0,2},{1,3},{2,0},{3,1},{4,6},{5,7},{6,4},{7,5},{8,10},{9,11},{10,... | collective-permute-start | bytes 196616 | tf_op jit(solution)/shard_map/ppermute | solution.py:234
  25.0 8.8 %collective-permute-start.3 = (f32[128,256]{1,0:T(8,128)S(1)}, f32[128,256]{1,0:T(8,128)S(1)}, u32[]{:S(2)}, u32[]{:S(2)}) collective-permute-start(f32[128,256]{1,0:T(8,128)S(1)} %get-tuple-element.26), channel_id=1, source_target_pairs={{0,12},{1,13},{2,14},{3,15},{4,8},{5,9},{6,10},{7,11},{8,4},{9,5},... | collective-permute-start | bytes 393224 | tf_op jit(solution)/shard_map/ppermute | solution.py:234
  27.7 12.4 %collective-permute-start.2 = (f32[128,256]{1,0:T(8,128)S(1)}, f32[128,256]{1,0:T(8,128)S(1)}, u32[]{:S(2)}, u32[]{:S(2)}) collective-permute-start(f32[128,256]{1,0:T(8,128)S(1)} %get-tuple-element.26), channel_id=1, source_target_pairs={{0,8},{1,9},{2,10},{3,11},{4,12},{5,13},{6,14},{7,15},{8,0},{9,1},... | collective-permute-start | bytes 393224 | tf_op jit(solution)/shard_map/ppermute | solution.py:234
  28.2 11.8 %collective-permute-start.1 = (f32[128,256]{1,0:T(8,128)S(1)}, f32[128,256]{1,0:T(8,128)S(1)}, u32[]{:S(2)}, u32[]{:S(2)}) collective-permute-start(f32[128,256]{1,0:T(8,128)S(1)} %get-tuple-element.26), channel_id=1, source_target_pairs={{0,4},{1,5},{2,6},{3,7},{4,0},{5,1},{6,2},{7,3},{8,12},{9,13},{10,... | collective-permute-start | bytes 393224 | tf_op jit(solution)/shard_map/ppermute | solution.py:234
  29.4 3.4 %copy-start = (f32[2,256,4096]{2,1,0:T(8,128)S(1)}, f32[2,256,4096]{2,1,0:T(8,128)}, u32[]{:S(2)}) copy-start(f32[2,256,4096]{2,1,0:T(8,128)} %matrix_ref) | copy-start | bytes 25165828
  32.7 13.0 %copy-start.1 = (f32[2,256,4096]{2,1,0:T(8,128)S(1)}, f32[2,256,4096]{2,1,0:T(8,128)}, u32[]{:S(2)}) copy-start(f32[2,256,4096]{2,1,0:T(8,128)} %matrix_ref.1) | copy-start | bytes 25165828
  40.1 13.1 %collective-permute-start.5 = (f32[4,128,256]{2,1,0:T(8,128)S(1)}, f32[4,128,256]{2,1,0:T(8,128)S(1)}, u32[]{:S(2)}, u32[]{:S(2)}) collective-permute-start(f32[4,128,256]{2,1,0:T(8,128)S(1)} %pad_maximum_fusion.refs_0_.refs_3_), channel_id=1, source_target_pairs={{0,2},{1,3},{2,0},{3,1},{4,6},{5,7},{6,4},{7,5},{8,10},{9,11},{10,... | collective-permute-start | bytes 1572872 | tf_op jit(solution)/shard_map/ppermute | solution.py:234
  41.3 8.3 %collective-permute-start.8 = (f32[2,64,256]{2,1,0:T(8,128)S(1)}, f32[2,64,256]{2,1,0:T(8,128)S(1)}, u32[]{:S(2)}, u32[]{:S(2)}) collective-permute-start(f32[2,64,256]{2,1,0:T(8,128)S(1)} %pad_maximum_fusion.4), channel_id=1, source_target_pairs={{0,12},{1,13},{2,14},{3,15},{4,8},{5,9},{6,10},{7,11},{8,4},{9,5},... | collective-permute-start | bytes 393224 | tf_op jit(solution)/shard_map/ppermute | solution.py:234
  42.7 10.0 %collective-permute-start.7 = (f32[2,64,256]{2,1,0:T(8,128)S(1)}, f32[2,64,256]{2,1,0:T(8,128)S(1)}, u32[]{:S(2)}, u32[]{:S(2)}) collective-permute-start(f32[2,64,256]{2,1,0:T(8,128)S(1)} %pad_maximum_fusion.4), channel_id=1, source_target_pairs={{0,8},{1,9},{2,10},{3,11},{4,12},{5,13},{6,14},{7,15},{8,0},{9,1},... | collective-permute-start | bytes 393224 | tf_op jit(solution)/shard_map/ppermute | solution.py:234
  42.7 10.0 %collective-permute-start.6 = (f32[2,64,256]{2,1,0:T(8,128)S(1)}, f32[2,64,256]{2,1,0:T(8,128)S(1)}, u32[]{:S(2)}, u32[]{:S(2)}) collective-permute-start(f32[2,64,256]{2,1,0:T(8,128)S(1)} %pad_maximum_fusion.4), channel_id=1, source_target_pairs={{0,4},{1,5},{2,6},{3,7},{4,0},{5,1},{6,2},{7,3},{8,12},{9,13},{10,... | collective-permute-start | bytes 393224 | tf_op jit(solution)/shard_map/ppermute | solution.py:234
  45.7 9.6 %collective-permute-start.4 = (f32[4,128,256]{2,1,0:T(8,128)S(1)}, f32[4,128,256]{2,1,0:T(8,128)S(1)}, u32[]{:S(2)}, u32[]{:S(2)}) collective-permute-start(f32[4,128,256]{2,1,0:T(8,128)S(1)} %pad_maximum_fusion.refs_0_.refs_3_), channel_id=1, source_target_pairs={{0,1},{1,0},{2,3},{3,2},{4,5},{5,4},{6,7},{7,6},{8,9},{9,8},{10,11... | collective-permute-start | bytes 1572872 | tf_op jit(solution)/shard_map/ppermute | solution.py:234
  53.2 2.2 %collective-permute-start.9 = (f32[4,128,256]{2,1,0:T(8,128)S(1)}, f32[4,128,256]{2,1,0:T(8,128)S(1)}, u32[]{:S(2)}, u32[]{:S(2)}) collective-permute-start(f32[4,128,256]{2,1,0:T(8,128)S(1)} %collective-permute-done.5.refs_1_.refs_4_), channel_id=1, source_target_pairs={{0,1},{1,0},{2,3},{3,2},{4,5},{5,4},{6,7},{7,6},{8,9},{9,8},{10,11... | collective-permute-start | bytes 1572872 | tf_op jit(solution)/shard_map/ppermute | solution.py:234
  53.2 2.7 %collective-permute-start.10 = (f32[4,2,64,256]{3,2,1,0:T(8,128)S(1)}, f32[4,2,64,256]{3,2,1,0:T(8,128)S(1)}, u32[]{:S(2)}, u32[]{:S(2)}) collective-permute-start(f32[4,2,64,256]{3,2,1,0:T(8,128)S(1)} %pad_maximum_fusion.1.refs_2_.refs_5_), channel_id=1, source_target_pairs={{0,1},{1,0},{2,3},{3,2},{4,5},{5,4},{6,7},{7,6},{8,9},{9,8},{10,11... | collective-permute-start | bytes 1572872 | tf_op jit(solution)/shard_map/ppermute | solution.py:234
  57.4 7.8 %collective-permute-start.12 = (f32[64,256]{1,0:T(8,128)S(1)}, f32[64,256]{1,0:T(8,128)S(1)}, u32[]{:S(2)}, u32[]{:S(2)}) collective-permute-start(f32[64,256]{1,0:T(8,128)S(1)} %get-tuple-element.39), channel_id=1, source_target_pairs={{0,18},{1,19},{2,16},{3,17},{4,22},{5,23},{6,20},{7,21},{8,26},{9,... | collective-permute-start | bytes 196616 | tf_op jit(solution)/shard_map/ppermute | solution.py:236
  58.3 8.9 %collective-permute-start.11 = (f32[64,256]{1,0:T(8,128)S(1)}, f32[64,256]{1,0:T(8,128)S(1)}, u32[]{:S(2)}, u32[]{:S(2)}) collective-permute-start(f32[64,256]{1,0:T(8,128)S(1)} %get-tuple-element.39), channel_id=1, source_target_pairs={{0,16},{1,17},{2,18},{3,19},{4,20},{5,21},{6,22},{7,23},{8,24},{9,... | collective-permute-start | bytes 196616 | tf_op jit(solution)/shard_map/ppermute | solution.py:236
  60.5 9.2 %collective-permute-start.16 = (f32[128,256]{1,0:T(8,128)S(1)}, f32[128,256]{1,0:T(8,128)S(1)}, u32[]{:S(2)}, u32[]{:S(2)}) collective-permute-start(f32[128,256]{1,0:T(8,128)S(1)} %get-tuple-element.40), channel_id=1, source_target_pairs={{0,28},{1,29},{2,30},{3,31},{4,24},{5,25},{6,26},{7,27},{8,20},{9,... | collective-permute-start | bytes 393224 | tf_op jit(solution)/shard_map/ppermute | solution.py:236
  61.4 12.4 %collective-permute-start.15 = (f32[128,256]{1,0:T(8,128)S(1)}, f32[128,256]{1,0:T(8,128)S(1)}, u32[]{:S(2)}, u32[]{:S(2)}) collective-permute-start(f32[128,256]{1,0:T(8,128)S(1)} %get-tuple-element.40), channel_id=1, source_target_pairs={{0,24},{1,25},{2,26},{3,27},{4,28},{5,29},{6,30},{7,31},{8,16},{9,... | collective-permute-start | bytes 393224 | tf_op jit(solution)/shard_map/ppermute | solution.py:236
  62.0 11.9 %collective-permute-start.14 = (f32[128,256]{1,0:T(8,128)S(1)}, f32[128,256]{1,0:T(8,128)S(1)}, u32[]{:S(2)}, u32[]{:S(2)}) collective-permute-start(f32[128,256]{1,0:T(8,128)S(1)} %get-tuple-element.40), channel_id=1, source_target_pairs={{0,20},{1,21},{2,22},{3,23},{4,16},{5,17},{6,18},{7,19},{8,28},{9,... | collective-permute-start | bytes 393224 | tf_op jit(solution)/shard_map/ppermute | solution.py:236
  65.2 11.4 %collective-permute-start.13 = (f32[128,256]{1,0:T(8,128)S(1)}, f32[128,256]{1,0:T(8,128)S(1)}, u32[]{:S(2)}, u32[]{:S(2)}) collective-permute-start(f32[128,256]{1,0:T(8,128)S(1)} %get-tuple-element.40), channel_id=1, source_target_pairs={{0,16},{1,17},{2,18},{3,19},{4,20},{5,21},{6,22},{7,23},{8,24},{9,... | collective-permute-start | bytes 393224 | tf_op jit(solution)/shard_map/ppermute | solution.py:236
  76.6 13.9 %collective-permute-start.18 = (f32[4,128,256]{2,1,0:T(8,128)S(1)}, f32[4,128,256]{2,1,0:T(8,128)S(1)}, u32[]{:S(2)}, u32[]{:S(2)}) collective-permute-start(f32[4,128,256]{2,1,0:T(8,128)S(1)} %pad_maximum_fusion.2.refs_0_), channel_id=1, source_target_pairs={{0,2},{1,3},{2,0},{3,1},{4,6},{5,7},{6,4},{7,5},{8,10},{9,11},{10,... | collective-permute-start | bytes 1572872 | tf_op jit(solution)/shard_map/ppermute | solution.py:234
  77.2 8.3 %collective-permute-start.22 = (f32[2,64,256]{2,1,0:T(8,128)S(1)}, f32[2,64,256]{2,1,0:T(8,128)S(1)}, u32[]{:S(2)}, u32[]{:S(2)}) collective-permute-start(f32[2,64,256]{2,1,0:T(8,128)S(1)} %pad_maximum_fusion.5), channel_id=1, source_target_pairs={{0,12},{1,13},{2,14},{3,15},{4,8},{5,9},{6,10},{7,11},{8,4},{9,5},... | collective-permute-start | bytes 393224 | tf_op jit(solution)/shard_map/ppermute | solution.py:234
  79.4 10.4 %collective-permute-start.21 = (f32[2,64,256]{2,1,0:T(8,128)S(1)}, f32[2,64,256]{2,1,0:T(8,128)S(1)}, u32[]{:S(2)}, u32[]{:S(2)}) collective-permute-start(f32[2,64,256]{2,1,0:T(8,128)S(1)} %pad_maximum_fusion.5), channel_id=1, source_target_pairs={{0,8},{1,9},{2,10},{3,11},{4,12},{5,13},{6,14},{7,15},{8,0},{9,1},... | collective-permute-start | bytes 393224 | tf_op jit(solution)/shard_map/ppermute | solution.py:234
  79.4 10.4 %collective-permute-start.20 = (f32[2,64,256]{2,1,0:T(8,128)S(1)}, f32[2,64,256]{2,1,0:T(8,128)S(1)}, u32[]{:S(2)}, u32[]{:S(2)}) collective-permute-start(f32[2,64,256]{2,1,0:T(8,128)S(1)} %pad_maximum_fusion.5), channel_id=1, source_target_pairs={{0,4},{1,5},{2,6},{3,7},{4,0},{5,1},{6,2},{7,3},{8,12},{9,13},{10,... | collective-permute-start | bytes 393224 | tf_op jit(solution)/shard_map/ppermute | solution.py:234
  81.6 10.6 %collective-permute-start.17 = (f32[4,128,256]{2,1,0:T(8,128)S(1)}, f32[4,128,256]{2,1,0:T(8,128)S(1)}, u32[]{:S(2)}, u32[]{:S(2)}) collective-permute-start(f32[4,128,256]{2,1,0:T(8,128)S(1)} %pad_maximum_fusion.2.refs_0_), channel_id=1, source_target_pairs={{0,1},{1,0},{2,3},{3,2},{4,5},{5,4},{6,7},{7,6},{8,9},{9,8},{10,11... | collective-permute-start | bytes 1572872 | tf_op jit(solution)/shard_map/ppermute | solution.py:234
  89.8 2.4 %collective-permute-start.23 = (f32[4,2,64,256]{3,2,1,0:T(8,128)S(1)}, f32[4,2,64,256]{3,2,1,0:T(8,128)S(1)}, u32[]{:S(2)}, u32[]{:S(2)}) collective-permute-start(f32[4,2,64,256]{3,2,1,0:T(8,128)S(1)} %pad_maximum_fusion.3.refs_2_), channel_id=1, source_target_pairs={{0,1},{1,0},{2,3},{3,2},{4,5},{5,4},{6,7},{7,6},{8,9},{9,8},{10,11... | collective-permute-start | bytes 1572872 | tf_op jit(solution)/shard_map/ppermute | solution.py:234
  90.5 2.0 %collective-permute-start.19 = (f32[4,128,256]{2,1,0:T(8,128)S(1)}, f32[4,128,256]{2,1,0:T(8,128)S(1)}, u32[]{:S(2)}, u32[]{:S(2)}) collective-permute-start(f32[4,128,256]{2,1,0:T(8,128)S(1)} %collective-permute-done.18.refs_1_), channel_id=1, source_target_pairs={{0,1},{1,0},{2,3},{3,2},{4,5},{5,4},{6,7},{7,6},{8,9},{9,8},{10,11... | collective-permute-start | bytes 1572872 | tf_op jit(solution)/shard_map/ppermute | solution.py:234

commit v15 on v14

--- a/solution.py
+++ b/solution.py
@@ -152,11 +152,13 @@
 
     def block_of(step, layer):
         held = lax.div(me, 4) ^ layer if relative else layer
+        hopped = lax.rem(lax.div(me, 4) + (layers - layer), layers)
         pieces = []
         for group in layout:
-            which, place = group(step, held)
+            which, place = group(step, held, held if sets == 1 else hopped)
             value = refs[which][place]
             if sets == 2:
+                which, place = group(step, held, held)
                 own = refs[inputs + which][place]
                 value = jnp.where(lax.axis_index("chain") == 0, own, own - value)
             pieces.append(value)
@@ -237,7 +239,10 @@
 
     def first_stage(first, second, hop):
         pair = [second if across == 0 and not hop else send(second, hop, lambda t: t ^ (2 * across)) for across in range(2)]
-        line = [first if by == 0 and not hop else send(first, hop, lambda t: t ^ (4 * by)) for by in range(layers)]
+        if hop:
+            line = [send(first, True, lambda t: (t + 4 * by) % tile_size) for by in range(layers)]
+        else:
+            line = [first if by == 0 else send(first, False, lambda t: t ^ (4 * by)) for by in range(layers)]
         return jnp.stack(pair), jnp.stack(line)
 
     def second_stage(pair, line):
@@ -245,7 +250,7 @@
         rest = [pair if by == 0 else send(pair, False, lambda t: t ^ (4 * by)) for by in range(layers)]
         return [line, far, jnp.stack(rest)]
 
-    layout = [lambda step, held: (step % 2, (held,)), lambda step, held: (2, (held, step % 2))]
+    layout = [lambda step, held, line: (step % 2, (line,)), lambda step, held, line: (2, (held, step % 2))]
 
     def products(split, onward, held, own, shares):
         other = [send(each, False, lambda t: t ^ 1) for each in held]
@@ -278,7 +283,7 @@
     full_rows = diag_inverse.shape[2]
     block = min(256, full_rows)
     count = full_rows // block
-    layout = [lambda step, held: (0, (step * layers + held,))]
+    layout = [lambda step, held, line: (0, (step * layers + held,))]
     onward = [(i, i + 1) for i in range(chain_size - 1)]
     diag_split = split_blocks(diag_inverse, block, False)
     coupling_split = split_blocks(coupling, block, False)

time: 95.1 us -> 94.2 us (level)
  starting transfers between devices: 25.8 us -> 23.9 us
  waiting for transfers between devices: 31.6 us -> 32.7 us
    ppermute x6, starting transfers between devices: 9.78 us -> 7.37 us  [send(): return lax.ppermute(value, ('chain', 'tile'), pairs)]
    ppermute x6, waiting for transfers between devices: 9.33 us -> 10.4 us  [send(): return lax.ppermute(value, ('chain', 'tile'), pairs)]
  transfers between devices with their start and end apart: 24 -> 24, of which waited for: 12 -> 11; matrix products, arithmetic and copies ran while one was open for 0% -> 0% of each run, Pallas kernels for 6% -> 6%
where the time goes in v15:
time: 94.2 us; the launch traced here: 93.9 us
  waiting for transfers between devices  32.7 us (35%)
  starting transfers between devices  23.9 us (25%)
  blocking collectives  20.6 us (22%)
  Pallas kernels  12.1 us (13%)
  local copies, waits for them, and re-layouts  4.31 us (5%)
    ppermute x18, waiting for transfers between devices, send(): lax.ppermute(value, 'tile', [(t, target(t)) for t in range(tile_size)])  22.3 us
    all_to_all x1, blocking collectives, body(): received = lax.all_to_all(packed, 'tile', 0, 0, tiled=False)  20.6 us
    ppermute x18, starting transfers between devices, send(): lax.ppermute(value, 'tile', [(t, target(t)) for t in range(tile_size)])  16.5 us
    ppermute x6, waiting for transfers between devices, send(): return lax.ppermute(value, ('chain', 'tile'), pairs)  10.4 us
    ppermute x6, starting transfers between devices, send(): return lax.ppermute(value, ('chain', 'tile'), pairs)  7.37 us
    pallas_call x4, Pallas kernels, product_part(): pl.pallas_call(functools.partial(product_kernel, sources, layout, len(blo...  7.21 us
    unnamed x6, local copies, waits for them, and re-layouts  4.31 us
    pallas_call x1, Pallas kernels, body(): pl.pallas_call(functools.partial(pack_kernel, own_rows, cap, tile_rows),...  2.19 us
  transfers between devices with their start and end apart: 24, of which 11 were waited for; matrix products, arithmetic and copies ran while one was open for 0% of the time, Pallas kernels for 6%

profile of v15, /device:TPU:0, one launch (start us, length us, event | category | flops | bytes accessed | tf_op | source)
XLA Modules:
  0.0 93.9 jit_solution(15716451255701405661)
XLA Ops:
  0.0 2.2 %shard_map.64 = f32[16,56,128]{2,1,0:T(8,128)} custom-call(s32[2]{0:T(128)} %counts_hbm.1, s32[1,256]{1,0:T(1,128)} %bitcast.46, f32[192,256]{1,0:T(8,128)} %bitcast.29), custom_call_target="tpu_custom_call" | custom-call | tf_op jit(solution)/shard_map/pallas_call | solution.py:316
  2.2 20.6 %all_to_all.5.received_ref = f32[16,56,128]{2,1,0:T(8,128)S(1)} all-to-all(f32[16,56,128]{2,1,0:T(8,128)} %shard_map.64), channel_id=1, replica_groups=mesh['chain'=2,'tile'=16] {'tile'}, dimensions={0} | all-to-all | bytes 917504 | tf_op jit(solution)/shard_map/all_to_all | solution.py:329
  22.9 0.0 copy-start.2
  22.9 0.9 copy-done.2
  23.8 0.8 shard_map.65
  24.5 0.4 collective-permute-start
  25.0 2.7 %collective-permute-start.3 = (f32[128,256]{1,0:T(8,128)S(1)}, f32[128,256]{1,0:T(8,128)S(1)}, u32[]{:S(2)}, u32[]{:S(2)}) collective-permute-start(f32[128,256]{1,0:T(8,128)S(1)} %get-tuple-element.26), channel_id=1, source_target_pairs={{0,12},{1,13},{2,14},{3,15},{4,8},{5,9},{6,10},{7,11},{8,4},{9,5},... | collective-permute-start | bytes 393224 | tf_op jit(solution)/shard_map/ppermute | solution.py:236
  27.7 0.5 collective-permute-start.2
  28.2 1.1 %collective-permute-start.1 = (f32[128,256]{1,0:T(8,128)S(1)}, f32[128,256]{1,0:T(8,128)S(1)}, u32[]{:S(2)}, u32[]{:S(2)}) collective-permute-start(f32[128,256]{1,0:T(8,128)S(1)} %get-tuple-element.26), channel_id=1, source_target_pairs={{0,4},{1,5},{2,6},{3,7},{4,0},{5,1},{6,2},{7,3},{8,12},{9,13},{10,... | collective-permute-start | bytes 393224 | tf_op jit(solution)/shard_map/ppermute | solution.py:236
  29.4 0.0 copy-start
  29.4 3.4 %copy-done = f32[2,256,4096]{2,1,0:T(8,128)S(1)} copy-done((f32[2,256,4096]{2,1,0:T(8,128)S(1)}, f32[2,256,4096]{2,1,0:T(8,128)}, u32[]{:S(2)}) %copy-start) | copy-done | bytes 8388632
  32.7 0.0 copy-start.1
  32.7 1.0 %shard_map.66 = (bf16[4,512,1024]{2,1,0:T(8,128)(2,1)S(1)}, bf16[4,512,1024]{2,1,0:T(8,128)(2,1)S(1)}) custom-call(f32[2,256,4096]{2,1,0:T(8,128)S(1)} %copy-done), custom_call_target="tpu_custom_call" | custom-call | flops 6291456 | bytes 16777216 | tf_op jit(solution)/shard_map/pallas_call | solution.py:132
  33.7 0.0 collective-permute-done
  33.8 0.0 collective-permute-done.3
  33.8 6.3 %collective-permute-done.2 = f32[128,256]{1,0:T(8,128)S(1)} collective-permute-done((f32[128,256]{1,0:T(8,128)S(1)}, f32[128,256]{1,0:T(8,128)S(1)}, u32[]{:S(2)}, u32[]{:S(2)}) %collective-permute-start.2) | collective-permute-done | bytes 131104 | tf_op jit(solution)/shard_map/ppermute | solution.py:236
  40.1 0.0 collective-permute-done.1
  40.1 1.2 %collective-permute-start.5 = (f32[4,128,256]{2,1,0:T(8,128)S(1)}, f32[4,128,256]{2,1,0:T(8,128)S(1)}, u32[]{:S(2)}, u32[]{:S(2)}) collective-permute-start(f32[4,128,256]{2,1,0:T(8,128)S(1)} %pad_maximum_fusion.refs_0_.refs_3_), channel_id=1, source_target_pairs={{0,2},{1,3},{2,0},{3,1},{4,6},{5,7},{6,4},{7,5},{8,10},{9,11},{10,... | collective-permute-start | bytes 1572872 | tf_op jit(solution)/shard_map/ppermute | solution.py:236
  41.3 1.4 %collective-permute-start.8 = (f32[2,64,256]{2,1,0:T(8,128)S(1)}, f32[2,64,256]{2,1,0:T(8,128)S(1)}, u32[]{:S(2)}, u32[]{:S(2)}) collective-permute-start(f32[2,64,256]{2,1,0:T(8,128)S(1)} %pad_maximum_fusion.4), channel_id=1, source_target_pairs={{0,12},{1,13},{2,14},{3,15},{4,8},{5,9},{6,10},{7,11},{8,4},{9,5},... | collective-permute-start | bytes 393224 | tf_op jit(solution)/shard_map/ppermute | solution.py:236
  42.7 0.0 collective-permute-start.7
  42.7 3.0 %collective-permute-start.6 = (f32[2,64,256]{2,1,0:T(8,128)S(1)}, f32[2,64,256]{2,1,0:T(8,128)S(1)}, u32[]{:S(2)}, u32[]{:S(2)}) collective-permute-start(f32[2,64,256]{2,1,0:T(8,128)S(1)} %pad_maximum_fusion.4), channel_id=1, source_target_pairs={{0,4},{1,5},{2,6},{3,7},{4,0},{5,1},{6,2},{7,3},{8,12},{9,13},{10,... | collective-permute-start | bytes 393224 | tf_op jit(solution)/shard_map/ppermute | solution.py:236
  45.7 0.0 collective-permute-start.4
  45.7 0.0 copy-done.1
  45.7 1.0 %shard_map.67 = (bf16[4,512,1024]{2,1,0:T(8,128)(2,1)S(1)}, bf16[4,512,1024]{2,1,0:T(8,128)(2,1)S(1)}) custom-call(f32[2,256,4096]{2,1,0:T(8,128)S(1)} %copy-done.1), custom_call_target="tpu_custom_call" | custom-call | flops 6291456 | bytes 16777216 | tf_op jit(solution)/shard_map/pallas_call | solution.py:132
  46.7 2.9 %collective-permute-done.8 = f32[2,64,256]{2,1,0:T(8,128)S(1)} collective-permute-done((f32[2,64,256]{2,1,0:T(8,128)S(1)}, f32[2,64,256]{2,1,0:T(8,128)S(1)}, u32[]{:S(2)}, u32[]{:S(2)}) %collective-permute-start.8) | collective-permute-done | bytes 131104 | tf_op jit(solution)/shard_map/ppermute | solution.py:236
  49.6 3.2 %collective-permute-done.7 = f32[2,64,256]{2,1,0:T(8,128)S(1)} collective-permute-done((f32[2,64,256]{2,1,0:T(8,128)S(1)}, f32[2,64,256]{2,1,0:T(8,128)S(1)}, u32[]{:S(2)}, u32[]{:S(2)}) %collective-permute-start.7) | collective-permute-done | bytes 131104 | tf_op jit(solution)/shard_map/ppermute | solution.py:236
  52.8 0.0 collective-permute-done.6
  52.8 0.4 collective-permute-done.5.refs_1_.refs_4_
  53.2 0.0 collective-permute-start.9
  53.2 0.5 collective-permute-start.10
  53.7 1.7 %shard_map.68.refs_5_ = f32[192,512]{1,0:T(8,128)S(1)} custom-call(f32[4,128,256]{2,1,0:T(8,128)S(1)} %pad_maximum_fusion.refs_0_.refs_3_, f32[4,128,256]{2,1,0:T(8,128)S(1)} %collective-permute-done.5.refs_1_.refs_4_, f32[4,2,64,256]{3,2,1,0:T(8,128)S(1)} %pad_maximum_fusion.1.refs_2_.refs_5_, bf16[4,512,1024]{2,1,0:T(8,128)(2,1)S(1)} %get-tuple-element.37.refs_3_, ...), custom_call_target="tpu_custom_call" | custom-call | flops 1207959552 | bytes 1048576 | tf_op jit(solution)/shard_map/pallas_call | solution.py:212
  55.3 0.0 collective-permute-done.4.refs_0_.refs_3_
  55.4 0.0 collective-permute-done.9.refs_1_.refs_4_
  55.4 0.5 collective-permute-done.10.refs_2_.refs_5_
  55.8 1.6 %shard_map.69 = (f32[128,256]{1,0:T(8,128)S(1)}, f32[64,256]{1,0:T(8,128)S(1)}) custom-call(f32[4,128,256]{2,1,0:T(8,128)S(1)} %collective-permute-done.4.refs_0_.refs_3_, f32[4,128,256]{2,1,0:T(8,128)S(1)} %collective-permute-done.9.refs_1_.refs_4_, f32[4,2,64,256]{3,2,1,0:T(8,128)S(1)} %collective-permute-done.10.refs_2_.refs_5_, ...), custom_call_target="tpu_custom_call" | custom-call | flops 1207959552 | bytes 1048576 | tf_op jit(solution)/shard_map/pallas_call | solution.py:212
  57.4 0.9 collective-permute-start.12
  58.3 2.1 %collective-permute-start.11 = (f32[64,256]{1,0:T(8,128)S(1)}, f32[64,256]{1,0:T(8,128)S(1)}, u32[]{:S(2)}, u32[]{:S(2)}) collective-permute-start(f32[64,256]{1,0:T(8,128)S(1)} %get-tuple-element.39), channel_id=1, source_target_pairs={{0,16},{1,17},{2,18},{3,19},{4,20},{5,21},{6,22},{7,23},{8,24},{9,... | collective-permute-start | bytes 196616 | tf_op jit(solution)/shard_map/ppermute | solution.py:238
  60.5 0.9 collective-permute-start.16
  61.4 0.6 collective-permute-start.15
  62.0 1.4 %collective-permute-start.14 = (f32[128,256]{1,0:T(8,128)S(1)}, f32[128,256]{1,0:T(8,128)S(1)}, u32[]{:S(2)}, u32[]{:S(2)}) collective-permute-start(f32[128,256]{1,0:T(8,128)S(1)} %get-tuple-element.40), channel_id=1, source_target_pairs={{0,20},{1,21},{2,22},{3,23},{4,24},{5,25},{6,26},{7,27},{8,28},{9,... | collective-permute-start | bytes 393224 | tf_op jit(solution)/shard_map/ppermute | solution.py:238
  63.4 0.0 collective-permute-done.12
  63.4 1.4 %collective-permute-start.13 = (f32[128,256]{1,0:T(8,128)S(1)}, f32[128,256]{1,0:T(8,128)S(1)}, u32[]{:S(2)}, u32[]{:S(2)}) collective-permute-start(f32[128,256]{1,0:T(8,128)S(1)} %get-tuple-element.40), channel_id=1, source_target_pairs={{0,16},{1,17},{2,18},{3,19},{4,20},{5,21},{6,22},{7,23},{8,24},{9,... | collective-permute-start | bytes 393224 | tf_op jit(solution)/shard_map/ppermute | solution.py:238
  64.8 2.8 %collective-permute-done.11 = f32[64,256]{1,0:T(8,128)S(1)} collective-permute-done((f32[64,256]{1,0:T(8,128)S(1)}, f32[64,256]{1,0:T(8,128)S(1)}, u32[]{:S(2)}, u32[]{:S(2)}) %collective-permute-start.11) | collective-permute-done | bytes 65568 | tf_op jit(solution)/shard_map/ppermute | solution.py:238
  67.6 0.0 collective-permute-done.16
  67.6 6.3 %collective-permute-done.15 = f32[128,256]{1,0:T(8,128)S(1)} collective-permute-done((f32[128,256]{1,0:T(8,128)S(1)}, f32[128,256]{1,0:T(8,128)S(1)}, u32[]{:S(2)}, u32[]{:S(2)}) %collective-permute-start.15) | collective-permute-done | bytes 131104 | tf_op jit(solution)/shard_map/ppermute | solution.py:238
  73.9 0.0 collective-permute-done.14
  73.9 1.3 %collective-permute-done.13 = f32[128,256]{1,0:T(8,128)S(1)} collective-permute-done((f32[128,256]{1,0:T(8,128)S(1)}, f32[128,256]{1,0:T(8,128)S(1)}, u32[]{:S(2)}, u32[]{:S(2)}) %collective-permute-start.13) | collective-permute-done | bytes 131104 | tf_op jit(solution)/shard_map/ppermute | solution.py:238
  75.2 0.6 collective-permute-start.18
  75.8 2.6 %collective-permute-start.22 = (f32[2,64,256]{2,1,0:T(8,128)S(1)}, f32[2,64,256]{2,1,0:T(8,128)S(1)}, u32[]{:S(2)}, u32[]{:S(2)}) collective-permute-start(f32[2,64,256]{2,1,0:T(8,128)S(1)} %pad_maximum_fusion.5), channel_id=1, source_target_pairs={{0,12},{1,13},{2,14},{3,15},{4,8},{5,9},{6,10},{7,11},{8,4},{9,5},... | collective-permute-start | bytes 393224 | tf_op jit(solution)/shard_map/ppermute | solution.py:236
  78.4 0.0 collective-permute-start.21
  78.4 1.8 %collective-permute-start.20 = (f32[2,64,256]{2,1,0:T(8,128)S(1)}, f32[2,64,256]{2,1,0:T(8,128)S(1)}, u32[]{:S(2)}, u32[]{:S(2)}) collective-permute-start(f32[2,64,256]{2,1,0:T(8,128)S(1)} %pad_maximum_fusion.5), channel_id=1, source_target_pairs={{0,4},{1,5},{2,6},{3,7},{4,0},{5,1},{6,2},{7,3},{8,12},{9,13},{10,... | collective-permute-start | bytes 393224 | tf_op jit(solution)/shard_map/ppermute | solution.py:236
  80.2 0.0 collective-permute-start.17
  80.2 3.9 %collective-permute-done.22 = f32[2,64,256]{2,1,0:T(8,128)S(1)} collective-permute-done((f32[2,64,256]{2,1,0:T(8,128)S(1)}, f32[2,64,256]{2,1,0:T(8,128)S(1)}, u32[]{:S(2)}, u32[]{:S(2)}) %collective-permute-start.22) | collective-permute-done | bytes 131104 | tf_op jit(solution)/shard_map/ppermute | solution.py:236
  84.1 4.8 %collective-permute-done.21 = f32[2,64,256]{2,1,0:T(8,128)S(1)} collective-permute-done((f32[2,64,256]{2,1,0:T(8,128)S(1)}, f32[2,64,256]{2,1,0:T(8,128)S(1)}, u32[]{:S(2)}, u32[]{:S(2)}) %collective-permute-start.21) | collective-permute-done | bytes 131104 | tf_op jit(solution)/shard_map/ppermute | solution.py:236
  88.9 0.0 collective-permute-done.20
  88.9 0.1 collective-permute-start.23
  89.0 0.0 collective-permute-done.18.refs_1_
  89.0 0.5 collective-permute-start.19
  89.5 1.7 %shard_map.70.refs_8_ = f32[192,512]{1,0:T(8,128)S(1)} custom-call(f32[4,128,256]{2,1,0:T(8,128)S(1)} %pad_maximum_fusion.2.refs_0_, f32[4,128,256]{2,1,0:T(8,128)S(1)} %collective-permute-done.18.refs_1_, f32[4,2,64,256]{3,2,1,0:T(8,128)S(1)} %pad_maximum_fusion.3.refs_2_, f32[4,128,256]{2,1,0:T(8,128)S(1)} %pad_maximum_fusion.refs_0_.refs_3_, ...), custom_call_target="tpu_custom_call" | custom-call | flops 1207959552 | bytes 1048576 | tf_op jit(solution)/shard_map/pallas_call | solution.py:212
  91.2 0.0 collective-permute-done.17.refs_0_
  91.2 0.0 collective-permute-done.23.refs_2_
  91.2 0.5 collective-permute-done.19.refs_1_
  91.7 2.3 %shard_map.71 = f32[192,256]{1,0:T(8,128)} custom-call(f32[4,128,256]{2,1,0:T(8,128)S(1)} %collective-permute-done.17.refs_0_, f32[4,128,256]{2,1,0:T(8,128)S(1)} %collective-permute-done.19.refs_1_, f32[4,2,64,256]{3,2,1,0:T(8,128)S(1)} %collective-permute-done.23.refs_2_, f32[4,128,256]{2,1,0:T(8,128)S(1)} %collective-permute-done.4.refs_0_.refs_3_, ...), custom_call_target="tpu_custom_call" | custom-call | flops 1207959552 | bytes 1048576 | tf_op jit(solution)/shard_map/pallas_call | solution.py:212
  (6 shorter events, 0.2 us)
Async XLA Ops:
  22.9 0.9 copy-start.2
  24.5 9.2 %collective-permute-start = (f32[64,256]{1,0:T(8,128)S(1)}, f32[64,256]{1,0:T(8,128)S(1)}, u32[]{:S(2)}, u32[]{:S(2)}) collective-permute-start(f32[64,256]{1,0:T(8,128)S(1)} %get-tuple-element.25), channel_id=1, source_target_pairs={{0,2},{1,3},{2,0},{3,1},{4,6},{5,7},{6,4},{7,5},{8,10},{9,11},{10,... | collective-permute-start | bytes 196616 | tf_op jit(solution)/shard_map/ppermute | solution.py:236
  25.0 8.8 %collective-permute-start.3 = (f32[128,256]{1,0:T(8,128)S(1)}, f32[128,256]{1,0:T(8,128)S(1)}, u32[]{:S(2)}, u32[]{:S(2)}) collective-permute-start(f32[128,256]{1,0:T(8,128)S(1)} %get-tuple-element.26), channel_id=1, source_target_pairs={{0,12},{1,13},{2,14},{3,15},{4,8},{5,9},{6,10},{7,11},{8,4},{9,5},... | collective-permute-start | bytes 393224 | tf_op jit(solution)/shard_map/ppermute | solution.py:236
  27.7 12.4 %collective-permute-start.2 = (f32[128,256]{1,0:T(8,128)S(1)}, f32[128,256]{1,0:T(8,128)S(1)}, u32[]{:S(2)}, u32[]{:S(2)}) collective-permute-start(f32[128,256]{1,0:T(8,128)S(1)} %get-tuple-element.26), channel_id=1, source_target_pairs={{0,8},{1,9},{2,10},{3,11},{4,12},{5,13},{6,14},{7,15},{8,0},{9,1},... | collective-permute-start | bytes 393224 | tf_op jit(solution)/shard_map/ppermute | solution.py:236
  28.2 11.8 %collective-permute-start.1 = (f32[128,256]{1,0:T(8,128)S(1)}, f32[128,256]{1,0:T(8,128)S(1)}, u32[]{:S(2)}, u32[]{:S(2)}) collective-permute-start(f32[128,256]{1,0:T(8,128)S(1)} %get-tuple-element.26), channel_id=1, source_target_pairs={{0,4},{1,5},{2,6},{3,7},{4,0},{5,1},{6,2},{7,3},{8,12},{9,13},{10,... | collective-permute-start | bytes 393224 | tf_op jit(solution)/shard_map/ppermute | solution.py:236
  29.4 3.4 %copy-start = (f32[2,256,4096]{2,1,0:T(8,128)S(1)}, f32[2,256,4096]{2,1,0:T(8,128)}, u32[]{:S(2)}) copy-start(f32[2,256,4096]{2,1,0:T(8,128)} %matrix_ref) | copy-start | bytes 25165828
  32.7 13.0 %copy-start.1 = (f32[2,256,4096]{2,1,0:T(8,128)S(1)}, f32[2,256,4096]{2,1,0:T(8,128)}, u32[]{:S(2)}) copy-start(f32[2,256,4096]{2,1,0:T(8,128)} %matrix_ref.1) | copy-start | bytes 25165828
  40.1 13.1 %collective-permute-start.5 = (f32[4,128,256]{2,1,0:T(8,128)S(1)}, f32[4,128,256]{2,1,0:T(8,128)S(1)}, u32[]{:S(2)}, u32[]{:S(2)}) collective-permute-start(f32[4,128,256]{2,1,0:T(8,128)S(1)} %pad_maximum_fusion.refs_0_.refs_3_), channel_id=1, source_target_pairs={{0,2},{1,3},{2,0},{3,1},{4,6},{5,7},{6,4},{7,5},{8,10},{9,11},{10,... | collective-permute-start | bytes 1572872 | tf_op jit(solution)/shard_map/ppermute | solution.py:236
  41.3 8.3 %collective-permute-start.8 = (f32[2,64,256]{2,1,0:T(8,128)S(1)}, f32[2,64,256]{2,1,0:T(8,128)S(1)}, u32[]{:S(2)}, u32[]{:S(2)}) collective-permute-start(f32[2,64,256]{2,1,0:T(8,128)S(1)} %pad_maximum_fusion.4), channel_id=1, source_target_pairs={{0,12},{1,13},{2,14},{3,15},{4,8},{5,9},{6,10},{7,11},{8,4},{9,5},... | collective-permute-start | bytes 393224 | tf_op jit(solution)/shard_map/ppermute | solution.py:236
  42.7 10.0 %collective-permute-start.7 = (f32[2,64,256]{2,1,0:T(8,128)S(1)}, f32[2,64,256]{2,1,0:T(8,128)S(1)}, u32[]{:S(2)}, u32[]{:S(2)}) collective-permute-start(f32[2,64,256]{2,1,0:T(8,128)S(1)} %pad_maximum_fusion.4), channel_id=1, source_target_pairs={{0,8},{1,9},{2,10},{3,11},{4,12},{5,13},{6,14},{7,15},{8,0},{9,1},... | collective-permute-start | bytes 393224 | tf_op jit(solution)/shard_map/ppermute | solution.py:236
  42.7 10.0 %collective-permute-start.6 = (f32[2,64,256]{2,1,0:T(8,128)S(1)}, f32[2,64,256]{2,1,0:T(8,128)S(1)}, u32[]{:S(2)}, u32[]{:S(2)}) collective-permute-start(f32[2,64,256]{2,1,0:T(8,128)S(1)} %pad_maximum_fusion.4), channel_id=1, source_target_pairs={{0,4},{1,5},{2,6},{3,7},{4,0},{5,1},{6,2},{7,3},{8,12},{9,13},{10,... | collective-permute-start | bytes 393224 | tf_op jit(solution)/shard_map/ppermute | solution.py:236
  45.7 9.6 %collective-permute-start.4 = (f32[4,128,256]{2,1,0:T(8,128)S(1)}, f32[4,128,256]{2,1,0:T(8,128)S(1)}, u32[]{:S(2)}, u32[]{:S(2)}) collective-permute-start(f32[4,128,256]{2,1,0:T(8,128)S(1)} %pad_maximum_fusion.refs_0_.refs_3_), channel_id=1, source_target_pairs={{0,1},{1,0},{2,3},{3,2},{4,5},{5,4},{6,7},{7,6},{8,9},{9,8},{10,11... | collective-permute-start | bytes 1572872 | tf_op jit(solution)/shard_map/ppermute | solution.py:236
  53.2 2.2 %collective-permute-start.9 = (f32[4,128,256]{2,1,0:T(8,128)S(1)}, f32[4,128,256]{2,1,0:T(8,128)S(1)}, u32[]{:S(2)}, u32[]{:S(2)}) collective-permute-start(f32[4,128,256]{2,1,0:T(8,128)S(1)} %collective-permute-done.5.refs_1_.refs_4_), channel_id=1, source_target_pairs={{0,1},{1,0},{2,3},{3,2},{4,5},{5,4},{6,7},{7,6},{8,9},{9,8},{10,11... | collective-permute-start | bytes 1572872 | tf_op jit(solution)/shard_map/ppermute | solution.py:236
  53.2 2.7 %collective-permute-start.10 = (f32[4,2,64,256]{3,2,1,0:T(8,128)S(1)}, f32[4,2,64,256]{3,2,1,0:T(8,128)S(1)}, u32[]{:S(2)}, u32[]{:S(2)}) collective-permute-start(f32[4,2,64,256]{3,2,1,0:T(8,128)S(1)} %pad_maximum_fusion.1.refs_2_.refs_5_), channel_id=1, source_target_pairs={{0,1},{1,0},{2,3},{3,2},{4,5},{5,4},{6,7},{7,6},{8,9},{9,8},{10,11... | collective-permute-start | bytes 1572872 | tf_op jit(solution)/shard_map/ppermute | solution.py:236
  57.4 6.0 %collective-permute-start.12 = (f32[64,256]{1,0:T(8,128)S(1)}, f32[64,256]{1,0:T(8,128)S(1)}, u32[]{:S(2)}, u32[]{:S(2)}) collective-permute-start(f32[64,256]{1,0:T(8,128)S(1)} %get-tuple-element.39), channel_id=1, source_target_pairs={{0,18},{1,19},{2,16},{3,17},{4,22},{5,23},{6,20},{7,21},{8,26},{9,... | collective-permute-start | bytes 196616 | tf_op jit(solution)/shard_map/ppermute | solution.py:238
  58.3 9.3 %collective-permute-start.11 = (f32[64,256]{1,0:T(8,128)S(1)}, f32[64,256]{1,0:T(8,128)S(1)}, u32[]{:S(2)}, u32[]{:S(2)}) collective-permute-start(f32[64,256]{1,0:T(8,128)S(1)} %get-tuple-element.39), channel_id=1, source_target_pairs={{0,16},{1,17},{2,18},{3,19},{4,20},{5,21},{6,22},{7,23},{8,24},{9,... | collective-permute-start | bytes 196616 | tf_op jit(solution)/shard_map/ppermute | solution.py:238
  60.5 7.1 %collective-permute-start.16 = (f32[128,256]{1,0:T(8,128)S(1)}, f32[128,256]{1,0:T(8,128)S(1)}, u32[]{:S(2)}, u32[]{:S(2)}) collective-permute-start(f32[128,256]{1,0:T(8,128)S(1)} %get-tuple-element.40), channel_id=1, source_target_pairs={{0,28},{1,29},{2,30},{3,31},{4,16},{5,17},{6,18},{7,19},{8,20},{9,... | collective-permute-start | bytes 393224 | tf_op jit(solution)/shard_map/ppermute | solution.py:238
  61.4 12.5 %collective-permute-start.15 = (f32[128,256]{1,0:T(8,128)S(1)}, f32[128,256]{1,0:T(8,128)S(1)}, u32[]{:S(2)}, u32[]{:S(2)}) collective-permute-start(f32[128,256]{1,0:T(8,128)S(1)} %get-tuple-element.40), channel_id=1, source_target_pairs={{0,24},{1,25},{2,26},{3,27},{4,28},{5,29},{6,30},{7,31},{8,16},{9,... | collective-permute-start | bytes 393224 | tf_op jit(solution)/shard_map/ppermute | solution.py:238
  62.0 11.9 %collective-permute-start.14 = (f32[128,256]{1,0:T(8,128)S(1)}, f32[128,256]{1,0:T(8,128)S(1)}, u32[]{:S(2)}, u32[]{:S(2)}) collective-permute-start(f32[128,256]{1,0:T(8,128)S(1)} %get-tuple-element.40), channel_id=1, source_target_pairs={{0,20},{1,21},{2,22},{3,23},{4,24},{5,25},{6,26},{7,27},{8,28},{9,... | collective-permute-start | bytes 393224 | tf_op jit(solution)/shard_map/ppermute | solution.py:238
  63.4 11.8 %collective-permute-start.13 = (f32[128,256]{1,0:T(8,128)S(1)}, f32[128,256]{1,0:T(8,128)S(1)}, u32[]{:S(2)}, u32[]{:S(2)}) collective-permute-start(f32[128,256]{1,0:T(8,128)S(1)} %get-tuple-element.40), channel_id=1, source_target_pairs={{0,16},{1,17},{2,18},{3,19},{4,20},{5,21},{6,22},{7,23},{8,24},{9,... | collective-permute-start | bytes 393224 | tf_op jit(solution)/shard_map/ppermute | solution.py:238
  75.2 13.8 %collective-permute-start.18 = (f32[4,128,256]{2,1,0:T(8,128)S(1)}, f32[4,128,256]{2,1,0:T(8,128)S(1)}, u32[]{:S(2)}, u32[]{:S(2)}) collective-permute-start(f32[4,128,256]{2,1,0:T(8,128)S(1)} %pad_maximum_fusion.2.refs_0_), channel_id=1, source_target_pairs={{0,2},{1,3},{2,0},{3,1},{4,6},{5,7},{6,4},{7,5},{8,10},{9,11},{10,... | collective-permute-start | bytes 1572872 | tf_op jit(solution)/shard_map/ppermute | solution.py:236
  75.8 8.3 %collective-permute-start.22 = (f32[2,64,256]{2,1,0:T(8,128)S(1)}, f32[2,64,256]{2,1,0:T(8,128)S(1)}, u32[]{:S(2)}, u32[]{:S(2)}) collective-permute-start(f32[2,64,256]{2,1,0:T(8,128)S(1)} %pad_maximum_fusion.5), channel_id=1, source_target_pairs={{0,12},{1,13},{2,14},{3,15},{4,8},{5,9},{6,10},{7,11},{8,4},{9,5},... | collective-permute-start | bytes 393224 | tf_op jit(solution)/shard_map/ppermute | solution.py:236
  78.4 10.5 %collective-permute-start.21 = (f32[2,64,256]{2,1,0:T(8,128)S(1)}, f32[2,64,256]{2,1,0:T(8,128)S(1)}, u32[]{:S(2)}, u32[]{:S(2)}) collective-permute-start(f32[2,64,256]{2,1,0:T(8,128)S(1)} %pad_maximum_fusion.5), channel_id=1, source_target_pairs={{0,8},{1,9},{2,10},{3,11},{4,12},{5,13},{6,14},{7,15},{8,0},{9,1},... | collective-permute-start | bytes 393224 | tf_op jit(solution)/shard_map/ppermute | solution.py:236
  78.4 10.5 %collective-permute-start.20 = (f32[2,64,256]{2,1,0:T(8,128)S(1)}, f32[2,64,256]{2,1,0:T(8,128)S(1)}, u32[]{:S(2)}, u32[]{:S(2)}) collective-permute-start(f32[2,64,256]{2,1,0:T(8,128)S(1)} %pad_maximum_fusion.5), channel_id=1, source_target_pairs={{0,4},{1,5},{2,6},{3,7},{4,0},{5,1},{6,2},{7,3},{8,12},{9,13},{10,... | collective-permute-start | bytes 393224 | tf_op jit(solution)/shard_map/ppermute | solution.py:236
  80.2 11.0 %collective-permute-start.17 = (f32[4,128,256]{2,1,0:T(8,128)S(1)}, f32[4,128,256]{2,1,0:T(8,128)S(1)}, u32[]{:S(2)}, u32[]{:S(2)}) collective-permute-start(f32[4,128,256]{2,1,0:T(8,128)S(1)} %pad_maximum_fusion.2.refs_0_), channel_id=1, source_target_pairs={{0,1},{1,0},{2,3},{3,2},{4,5},{5,4},{6,7},{7,6},{8,9},{9,8},{10,11... | collective-permute-start | bytes 1572872 | tf_op jit(solution)/shard_map/ppermute | solution.py:236
  88.9 2.3 %collective-permute-start.23 = (f32[4,2,64,256]{3,2,1,0:T(8,128)S(1)}, f32[4,2,64,256]{3,2,1,0:T(8,128)S(1)}, u32[]{:S(2)}, u32[]{:S(2)}) collective-permute-start(f32[4,2,64,256]{3,2,1,0:T(8,128)S(1)} %pad_maximum_fusion.3.refs_2_), channel_id=1, source_target_pairs={{0,1},{1,0},{2,3},{3,2},{4,5},{5,4},{6,7},{7,6},{8,9},{9,8},{10,11... | collective-permute-start | bytes 1572872 | tf_op jit(solution)/shard_map/ppermute | solution.py:236
  89.0 2.6 %collective-permute-start.19 = (f32[4,128,256]{2,1,0:T(8,128)S(1)}, f32[4,128,256]{2,1,0:T(8,128)S(1)}, u32[]{:S(2)}, u32[]{:S(2)}) collective-permute-start(f32[4,128,256]{2,1,0:T(8,128)S(1)} %collective-permute-done.18.refs_1_), channel_id=1, source_target_pairs={{0,1},{1,0},{2,3},{3,2},{4,5},{5,4},{6,7},{7,6},{8,9},{9,8},{10,11... | collective-permute-start | bytes 1572872 | tf_op jit(solution)/shard_map/ppermute | solution.py:236

commit v16 on v15

--- a/solution.py
+++ b/solution.py
@@ -243,6 +243,8 @@
             line = [send(first, True, lambda t: (t + 4 * by) % tile_size) for by in range(layers)]
         else:
             line = [first if by == 0 else send(first, False, lambda t: t ^ (4 * by)) for by in range(layers)]
+        if hop:
+            *pair, line[-1] = lax.optimization_barrier((*pair, line[-1]))
         return jnp.stack(pair), jnp.stack(line)
 
     def second_stage(pair, line):

time: 94.2 us -> 94.3 us (level)
  starting transfers between devices: 23.9 us -> 22.6 us
  waiting for transfers between devices: 32.7 us -> 34 us
    ppermute x6, waiting for transfers between devices: 10.4 us -> 12.2 us  [send(): return lax.ppermute(value, ('chain', 'tile'), pairs)]
  transfers between devices with their start and end apart: 24 -> 24, of which waited for: 11 -> 12; matrix products, arithmetic and copies ran while one was open for 0% -> 0% of each run, Pallas kernels for 6% -> 6%
where the time goes in v16:
time: 94.3 us; the launch traced here: 94 us
  waiting for transfers between devices  34 us (36%)
  starting transfers between devices  22.6 us (24%)
  blocking collectives  20.6 us (22%)
  Pallas kernels  12.1 us (13%)
  local copies, waits for them, and re-layouts  4.31 us (5%)
    ppermute x18, waiting for transfers between devices, send(): lax.ppermute(value, 'tile', [(t, target(t)) for t in range(tile_size)])  21.8 us
    all_to_all x1, blocking collectives, body(): received = lax.all_to_all(packed, 'tile', 0, 0, tiled=False)  20.6 us
    ppermute x18, starting transfers between devices, send(): lax.ppermute(value, 'tile', [(t, target(t)) for t in range(tile_size)])  16.1 us
    ppermute x6, waiting for transfers between devices, send(): return lax.ppermute(value, ('chain', 'tile'), pairs)  12.2 us
    pallas_call x4, Pallas kernels, product_part(): pl.pallas_call(functools.partial(product_kernel, sources, layout, len(blo...  7.21 us
    ppermute x6, starting transfers between devices, send(): return lax.ppermute(value, ('chain', 'tile'), pairs)  6.5 us
    unnamed x6, local copies, waits for them, and re-layouts  4.31 us
    pallas_call x1, Pallas kernels, body(): pl.pallas_call(functools.partial(pack_kernel, own_rows, cap, tile_rows),...  2.19 us
  transfers between devices with their start and end apart: 24, of which 12 were waited for; matrix products, arithmetic and copies ran while one was open for 0% of the time, Pallas kernels for 6%

profile of v16, /device:TPU:0, one launch (start us, length us, event | category | flops | bytes accessed | tf_op | source)
XLA Modules:
  0.0 94.0 jit_solution(13158498418080381744)
XLA Ops:
  0.0 2.2 %shard_map.64 = f32[16,56,128]{2,1,0:T(8,128)} custom-call(s32[2]{0:T(128)} %counts_hbm.1, s32[1,256]{1,0:T(1,128)} %bitcast.46, f32[192,256]{1,0:T(8,128)} %bitcast.29), custom_call_target="tpu_custom_call" | custom-call | tf_op jit(solution)/shard_map/pallas_call | solution.py:318
  2.2 20.6 %all_to_all.5.received_ref = f32[16,56,128]{2,1,0:T(8,128)S(1)} all-to-all(f32[16,56,128]{2,1,0:T(8,128)} %shard_map.64), channel_id=1, replica_groups=mesh['chain'=2,'tile'=16] {'tile'}, dimensions={0} | all-to-all | bytes 917504 | tf_op jit(solution)/shard_map/all_to_all | solution.py:331
  22.9 0.0 copy-start.2
  22.9 0.9 copy-done.2
  23.8 0.8 shard_map.65
  24.5 0.4 collective-permute-start
  25.0 2.7 %collective-permute-start.3 = (f32[128,256]{1,0:T(8,128)S(1)}, f32[128,256]{1,0:T(8,128)S(1)}, u32[]{:S(2)}, u32[]{:S(2)}) collective-permute-start(f32[128,256]{1,0:T(8,128)S(1)} %get-tuple-element.29), channel_id=1, source_target_pairs={{0,12},{1,13},{2,14},{3,15},{4,8},{5,9},{6,10},{7,11},{8,4},{9,5},... | collective-permute-start | bytes 393224 | tf_op jit(solution)/shard_map/ppermute | solution.py:236
  27.7 0.5 collective-permute-start.2
  28.2 1.1 %collective-permute-start.1 = (f32[128,256]{1,0:T(8,128)S(1)}, f32[128,256]{1,0:T(8,128)S(1)}, u32[]{:S(2)}, u32[]{:S(2)}) collective-permute-start(f32[128,256]{1,0:T(8,128)S(1)} %get-tuple-element.29), channel_id=1, source_target_pairs={{0,4},{1,5},{2,6},{3,7},{4,0},{5,1},{6,2},{7,3},{8,12},{9,13},{10,... | collective-permute-start | bytes 393224 | tf_op jit(solution)/shard_map/ppermute | solution.py:236
  29.4 0.0 copy-start
  29.4 3.4 %copy-done = f32[2,256,4096]{2,1,0:T(8,128)S(1)} copy-done((f32[2,256,4096]{2,1,0:T(8,128)S(1)}, f32[2,256,4096]{2,1,0:T(8,128)}, u32[]{:S(2)}) %copy-start) | copy-done | bytes 8388632
  32.7 0.0 copy-start.1
  32.7 1.0 %shard_map.66 = (bf16[4,512,1024]{2,1,0:T(8,128)(2,1)S(1)}, bf16[4,512,1024]{2,1,0:T(8,128)(2,1)S(1)}) custom-call(f32[2,256,4096]{2,1,0:T(8,128)S(1)} %copy-done), custom_call_target="tpu_custom_call" | custom-call | flops 6291456 | bytes 16777216 | tf_op jit(solution)/shard_map/pallas_call | solution.py:132
  33.7 0.0 collective-permute-done
  33.8 0.0 collective-permute-done.3
  33.8 6.3 %collective-permute-done.2 = f32[128,256]{1,0:T(8,128)S(1)} collective-permute-done((f32[128,256]{1,0:T(8,128)S(1)}, f32[128,256]{1,0:T(8,128)S(1)}, u32[]{:S(2)}, u32[]{:S(2)}) %collective-permute-start.2) | collective-permute-done | bytes 131104 | tf_op jit(solution)/shard_map/ppermute | solution.py:236
  40.1 0.0 collective-permute-done.1
  40.1 1.2 %collective-permute-start.5 = (f32[4,128,256]{2,1,0:T(8,128)S(1)}, f32[4,128,256]{2,1,0:T(8,128)S(1)}, u32[]{:S(2)}, u32[]{:S(2)}) collective-permute-start(f32[4,128,256]{2,1,0:T(8,128)S(1)} %pad_maximum_fusion.refs_0_.refs_3_), channel_id=1, source_target_pairs={{0,2},{1,3},{2,0},{3,1},{4,6},{5,7},{6,4},{7,5},{8,10},{9,11},{10,... | collective-permute-start | bytes 1572872 | tf_op jit(solution)/shard_map/ppermute | solution.py:236
  41.3 1.4 %collective-permute-start.8 = (f32[2,64,256]{2,1,0:T(8,128)S(1)}, f32[2,64,256]{2,1,0:T(8,128)S(1)}, u32[]{:S(2)}, u32[]{:S(2)}) collective-permute-start(f32[2,64,256]{2,1,0:T(8,128)S(1)} %pad_maximum_fusion.4), channel_id=1, source_target_pairs={{0,12},{1,13},{2,14},{3,15},{4,8},{5,9},{6,10},{7,11},{8,4},{9,5},... | collective-permute-start | bytes 393224 | tf_op jit(solution)/shard_map/ppermute | solution.py:236
  42.7 0.0 collective-permute-start.7
  42.7 3.0 %collective-permute-start.6 = (f32[2,64,256]{2,1,0:T(8,128)S(1)}, f32[2,64,256]{2,1,0:T(8,128)S(1)}, u32[]{:S(2)}, u32[]{:S(2)}) collective-permute-start(f32[2,64,256]{2,1,0:T(8,128)S(1)} %pad_maximum_fusion.4), channel_id=1, source_target_pairs={{0,4},{1,5},{2,6},{3,7},{4,0},{5,1},{6,2},{7,3},{8,12},{9,13},{10,... | collective-permute-start | bytes 393224 | tf_op jit(solution)/shard_map/ppermute | solution.py:236
  45.7 0.0 collective-permute-start.4
  45.7 0.0 copy-done.1
  45.7 1.0 %shard_map.67 = (bf16[4,512,1024]{2,1,0:T(8,128)(2,1)S(1)}, bf16[4,512,1024]{2,1,0:T(8,128)(2,1)S(1)}) custom-call(f32[2,256,4096]{2,1,0:T(8,128)S(1)} %copy-done.1), custom_call_target="tpu_custom_call" | custom-call | flops 6291456 | bytes 16777216 | tf_op jit(solution)/shard_map/pallas_call | solution.py:132
  46.7 2.9 %collective-permute-done.8 = f32[2,64,256]{2,1,0:T(8,128)S(1)} collective-permute-done((f32[2,64,256]{2,1,0:T(8,128)S(1)}, f32[2,64,256]{2,1,0:T(8,128)S(1)}, u32[]{:S(2)}, u32[]{:S(2)}) %collective-permute-start.8) | collective-permute-done | bytes 131104 | tf_op jit(solution)/shard_map/ppermute | solution.py:236
  49.6 3.2 %collective-permute-done.7 = f32[2,64,256]{2,1,0:T(8,128)S(1)} collective-permute-done((f32[2,64,256]{2,1,0:T(8,128)S(1)}, f32[2,64,256]{2,1,0:T(8,128)S(1)}, u32[]{:S(2)}, u32[]{:S(2)}) %collective-permute-start.7) | collective-permute-done | bytes 131104 | tf_op jit(solution)/shard_map/ppermute | solution.py:236
  52.8 0.0 collective-permute-done.6
  52.8 0.4 collective-permute-done.5.refs_1_.refs_4_
  53.2 0.0 collective-permute-start.9
  53.2 0.5 collective-permute-start.10
  53.7 1.7 %shard_map.68.refs_5_ = f32[192,512]{1,0:T(8,128)S(1)} custom-call(f32[4,128,256]{2,1,0:T(8,128)S(1)} %pad_maximum_fusion.refs_0_.refs_3_, f32[4,128,256]{2,1,0:T(8,128)S(1)} %collective-permute-done.5.refs_1_.refs_4_, f32[4,2,64,256]{3,2,1,0:T(8,128)S(1)} %pad_maximum_fusion.1.refs_2_.refs_5_, bf16[4,512,1024]{2,1,0:T(8,128)(2,1)S(1)} %get-tuple-element.40.refs_3_, ...), custom_call_target="tpu_custom_call" | custom-call | flops 1207959552 | bytes 1048576 | tf_op jit(solution)/shard_map/pallas_call | solution.py:212
  55.3 0.0 collective-permute-done.4.refs_0_.refs_3_
  55.4 0.0 collective-permute-done.9.refs_1_.refs_4_
  55.4 0.5 collective-permute-done.10.refs_2_.refs_5_
  55.8 1.6 %shard_map.69 = (f32[128,256]{1,0:T(8,128)S(1)}, f32[64,256]{1,0:T(8,128)S(1)}) custom-call(f32[4,128,256]{2,1,0:T(8,128)S(1)} %collective-permute-done.4.refs_0_.refs_3_, f32[4,128,256]{2,1,0:T(8,128)S(1)} %collective-permute-done.9.refs_1_.refs_4_, f32[4,2,64,256]{3,2,1,0:T(8,128)S(1)} %collective-permute-done.10.refs_2_.refs_5_, ...), custom_call_target="tpu_custom_call" | custom-call | flops 1207959552 | bytes 1048576 | tf_op jit(solution)/shard_map/pallas_call | solution.py:212
  57.4 1.5 %collective-permute-start.13 = (f32[128,256]{1,0:T(8,128)S(1)}, f32[128,256]{1,0:T(8,128)S(1)}, u32[]{:S(2)}, u32[]{:S(2)}) collective-permute-start(f32[128,256]{1,0:T(8,128)S(1)} %get-tuple-element.43), channel_id=1, source_target_pairs={{0,28},{1,29},{2,30},{3,31},{4,16},{5,17},{6,18},{7,19},{8,20},{9,... | collective-permute-start | bytes 393224 | tf_op jit(solution)/shard_map/ppermute | solution.py:238
  58.9 2.4 %collective-permute-start.12 = (f32[64,256]{1,0:T(8,128)S(1)}, f32[64,256]{1,0:T(8,128)S(1)}, u32[]{:S(2)}, u32[]{:S(2)}) collective-permute-start(f32[64,256]{1,0:T(8,128)S(1)} %get-tuple-element.42), channel_id=1, source_target_pairs={{0,18},{1,19},{2,16},{3,17},{4,22},{5,23},{6,20},{7,21},{8,26},{9,... | collective-permute-start | bytes 196616 | tf_op jit(solution)/shard_map/ppermute | solution.py:238
  61.4 0.0 collective-permute-start.11
  61.4 0.6 collective-permute-start.16
  62.0 1.5 %collective-permute-start.15 = (f32[128,256]{1,0:T(8,128)S(1)}, f32[128,256]{1,0:T(8,128)S(1)}, u32[]{:S(2)}, u32[]{:S(2)}) collective-permute-start(f32[128,256]{1,0:T(8,128)S(1)} %get-tuple-element.43), channel_id=1, source_target_pairs={{0,20},{1,21},{2,22},{3,23},{4,24},{5,25},{6,26},{7,27},{8,28},{9,... | collective-permute-start | bytes 393224 | tf_op jit(solution)/shard_map/ppermute | solution.py:238
  63.5 2.9 %collective-permute-done.12 = f32[64,256]{1,0:T(8,128)S(1)} collective-permute-done((f32[64,256]{1,0:T(8,128)S(1)}, f32[64,256]{1,0:T(8,128)S(1)}, u32[]{:S(2)}, u32[]{:S(2)}) %collective-permute-start.12) | collective-permute-done | bytes 65568 | tf_op jit(solution)/shard_map/ppermute | solution.py:238
  66.4 0.5 collective-permute-start.14
  66.9 0.0 collective-permute-done.11
  66.9 0.0 collective-permute-done.13
  66.9 6.9 %collective-permute-done.16 = f32[128,256]{1,0:T(8,128)S(1)} collective-permute-done((f32[128,256]{1,0:T(8,128)S(1)}, f32[128,256]{1,0:T(8,128)S(1)}, u32[]{:S(2)}, u32[]{:S(2)}) %collective-permute-start.16) | collective-permute-done | bytes 131104 | tf_op jit(solution)/shard_map/ppermute | solution.py:238
  73.8 0.0 collective-permute-done.15
  73.8 2.4 %collective-permute-done.14 = f32[128,256]{1,0:T(8,128)S(1)} collective-permute-done((f32[128,256]{1,0:T(8,128)S(1)}, f32[128,256]{1,0:T(8,128)S(1)}, u32[]{:S(2)}, u32[]{:S(2)}) %collective-permute-start.14) | collective-permute-done | bytes 131104 | tf_op jit(solution)/shard_map/ppermute | solution.py:238
  76.2 0.7 collective-permute-start.18
  76.9 2.1 %collective-permute-start.22 = (f32[2,64,256]{2,1,0:T(8,128)S(1)}, f32[2,64,256]{2,1,0:T(8,128)S(1)}, u32[]{:S(2)}, u32[]{:S(2)}) collective-permute-start(f32[2,64,256]{2,1,0:T(8,128)S(1)} %pad_maximum_fusion.5), channel_id=1, source_target_pairs={{0,12},{1,13},{2,14},{3,15},{4,8},{5,9},{6,10},{7,11},{8,4},{9,5},... | collective-permute-start | bytes 393224 | tf_op jit(solution)/shard_map/ppermute | solution.py:236
  78.9 0.0 collective-permute-start.21
  79.0 2.3 %collective-permute-start.20 = (f32[2,64,256]{2,1,0:T(8,128)S(1)}, f32[2,64,256]{2,1,0:T(8,128)S(1)}, u32[]{:S(2)}, u32[]{:S(2)}) collective-permute-start(f32[2,64,256]{2,1,0:T(8,128)S(1)} %pad_maximum_fusion.5), channel_id=1, source_target_pairs={{0,4},{1,5},{2,6},{3,7},{4,0},{5,1},{6,2},{7,3},{8,12},{9,13},{10,... | collective-permute-start | bytes 393224 | tf_op jit(solution)/shard_map/ppermute | solution.py:236
  81.3 0.0 collective-permute-start.17
  81.3 3.8 %collective-permute-done.22 = f32[2,64,256]{2,1,0:T(8,128)S(1)} collective-permute-done((f32[2,64,256]{2,1,0:T(8,128)S(1)}, f32[2,64,256]{2,1,0:T(8,128)S(1)}, u32[]{:S(2)}, u32[]{:S(2)}) %collective-permute-start.22) | collective-permute-done | bytes 131104 | tf_op jit(solution)/shard_map/ppermute | solution.py:236
  85.1 3.8 %collective-permute-done.21 = f32[2,64,256]{2,1,0:T(8,128)S(1)} collective-permute-done((f32[2,64,256]{2,1,0:T(8,128)S(1)}, f32[2,64,256]{2,1,0:T(8,128)S(1)}, u32[]{:S(2)}, u32[]{:S(2)}) %collective-permute-start.21) | collective-permute-done | bytes 131104 | tf_op jit(solution)/shard_map/ppermute | solution.py:236
  88.9 0.0 collective-permute-done.20
  89.0 0.1 collective-permute-start.23
  89.0 0.7 collective-permute-done.18.refs_1_
  89.8 0.0 collective-permute-start.19
  89.8 1.7 %shard_map.70.refs_8_ = f32[192,512]{1,0:T(8,128)S(1)} custom-call(f32[4,128,256]{2,1,0:T(8,128)S(1)} %pad_maximum_fusion.2.refs_0_, f32[4,128,256]{2,1,0:T(8,128)S(1)} %collective-permute-done.18.refs_1_, f32[4,2,64,256]{3,2,1,0:T(8,128)S(1)} %pad_maximum_fusion.3.refs_2_, f32[4,128,256]{2,1,0:T(8,128)S(1)} %pad_maximum_fusion.refs_0_.refs_3_, ...), custom_call_target="tpu_custom_call" | custom-call | flops 1207959552 | bytes 1048576 | tf_op jit(solution)/shard_map/pallas_call | solution.py:212
  91.5 0.0 collective-permute-done.17.refs_0_
  91.5 0.0 collective-permute-done.23.refs_2_
  91.5 0.2 collective-permute-done.19.refs_1_
  91.7 2.3 %shard_map.71 = f32[192,256]{1,0:T(8,128)} custom-call(f32[4,128,256]{2,1,0:T(8,128)S(1)} %collective-permute-done.17.refs_0_, f32[4,128,256]{2,1,0:T(8,128)S(1)} %collective-permute-done.19.refs_1_, f32[4,2,64,256]{3,2,1,0:T(8,128)S(1)} %collective-permute-done.23.refs_2_, f32[4,128,256]{2,1,0:T(8,128)S(1)} %collective-permute-done.4.refs_0_.refs_3_, ...), custom_call_target="tpu_custom_call" | custom-call | flops 1207959552 | bytes 1048576 | tf_op jit(solution)/shard_map/pallas_call | solution.py:212
  (6 shorter events, 0.2 us)
Async XLA Ops:
  22.9 0.9 copy-start.2
  24.5 9.2 %collective-permute-start = (f32[64,256]{1,0:T(8,128)S(1)}, f32[64,256]{1,0:T(8,128)S(1)}, u32[]{:S(2)}, u32[]{:S(2)}) collective-permute-start(f32[64,256]{1,0:T(8,128)S(1)} %get-tuple-element.28), channel_id=1, source_target_pairs={{0,2},{1,3},{2,0},{3,1},{4,6},{5,7},{6,4},{7,5},{8,10},{9,11},{10,... | collective-permute-start | bytes 196616 | tf_op jit(solution)/shard_map/ppermute | solution.py:236
  25.0 8.8 %collective-permute-start.3 = (f32[128,256]{1,0:T(8,128)S(1)}, f32[128,256]{1,0:T(8,128)S(1)}, u32[]{:S(2)}, u32[]{:S(2)}) collective-permute-start(f32[128,256]{1,0:T(8,128)S(1)} %get-tuple-element.29), channel_id=1, source_target_pairs={{0,12},{1,13},{2,14},{3,15},{4,8},{5,9},{6,10},{7,11},{8,4},{9,5},... | collective-permute-start | bytes 393224 | tf_op jit(solution)/shard_map/ppermute | solution.py:236
  27.7 12.4 %collective-permute-start.2 = (f32[128,256]{1,0:T(8,128)S(1)}, f32[128,256]{1,0:T(8,128)S(1)}, u32[]{:S(2)}, u32[]{:S(2)}) collective-permute-start(f32[128,256]{1,0:T(8,128)S(1)} %get-tuple-element.29), channel_id=1, source_target_pairs={{0,8},{1,9},{2,10},{3,11},{4,12},{5,13},{6,14},{7,15},{8,0},{9,1},... | collective-permute-start | bytes 393224 | tf_op jit(solution)/shard_map/ppermute | solution.py:236
  28.2 11.8 %collective-permute-start.1 = (f32[128,256]{1,0:T(8,128)S(1)}, f32[128,256]{1,0:T(8,128)S(1)}, u32[]{:S(2)}, u32[]{:S(2)}) collective-permute-start(f32[128,256]{1,0:T(8,128)S(1)} %get-tuple-element.29), channel_id=1, source_target_pairs={{0,4},{1,5},{2,6},{3,7},{4,0},{5,1},{6,2},{7,3},{8,12},{9,13},{10,... | collective-permute-start | bytes 393224 | tf_op jit(solution)/shard_map/ppermute | solution.py:236
  29.4 3.4 %copy-start = (f32[2,256,4096]{2,1,0:T(8,128)S(1)}, f32[2,256,4096]{2,1,0:T(8,128)}, u32[]{:S(2)}) copy-start(f32[2,256,4096]{2,1,0:T(8,128)} %matrix_ref) | copy-start | bytes 25165828
  32.7 13.0 %copy-start.1 = (f32[2,256,4096]{2,1,0:T(8,128)S(1)}, f32[2,256,4096]{2,1,0:T(8,128)}, u32[]{:S(2)}) copy-start(f32[2,256,4096]{2,1,0:T(8,128)} %matrix_ref.1) | copy-start | bytes 25165828
  40.1 13.1 %collective-permute-start.5 = (f32[4,128,256]{2,1,0:T(8,128)S(1)}, f32[4,128,256]{2,1,0:T(8,128)S(1)}, u32[]{:S(2)}, u32[]{:S(2)}) collective-permute-start(f32[4,128,256]{2,1,0:T(8,128)S(1)} %pad_maximum_fusion.refs_0_.refs_3_), channel_id=1, source_target_pairs={{0,2},{1,3},{2,0},{3,1},{4,6},{5,7},{6,4},{7,5},{8,10},{9,11},{10,... | collective-permute-start | bytes 1572872 | tf_op jit(solution)/shard_map/ppermute | solution.py:236
  41.3 8.3 %collective-permute-start.8 = (f32[2,64,256]{2,1,0:T(8,128)S(1)}, f32[2,64,256]{2,1,0:T(8,128)S(1)}, u32[]{:S(2)}, u32[]{:S(2)}) collective-permute-start(f32[2,64,256]{2,1,0:T(8,128)S(1)} %pad_maximum_fusion.4), channel_id=1, source_target_pairs={{0,12},{1,13},{2,14},{3,15},{4,8},{5,9},{6,10},{7,11},{8,4},{9,5},... | collective-permute-start | bytes 393224 | tf_op jit(solution)/shard_map/ppermute | solution.py:236
  42.7 10.0 %collective-permute-start.7 = (f32[2,64,256]{2,1,0:T(8,128)S(1)}, f32[2,64,256]{2,1,0:T(8,128)S(1)}, u32[]{:S(2)}, u32[]{:S(2)}) collective-permute-start(f32[2,64,256]{2,1,0:T(8,128)S(1)} %pad_maximum_fusion.4), channel_id=1, source_target_pairs={{0,8},{1,9},{2,10},{3,11},{4,12},{5,13},{6,14},{7,15},{8,0},{9,1},... | collective-permute-start | bytes 393224 | tf_op jit(solution)/shard_map/ppermute | solution.py:236
  42.7 10.0 %collective-permute-start.6 = (f32[2,64,256]{2,1,0:T(8,128)S(1)}, f32[2,64,256]{2,1,0:T(8,128)S(1)}, u32[]{:S(2)}, u32[]{:S(2)}) collective-permute-start(f32[2,64,256]{2,1,0:T(8,128)S(1)} %pad_maximum_fusion.4), channel_id=1, source_target_pairs={{0,4},{1,5},{2,6},{3,7},{4,0},{5,1},{6,2},{7,3},{8,12},{9,13},{10,... | collective-permute-start | bytes 393224 | tf_op jit(solution)/shard_map/ppermute | solution.py:236
  45.7 9.6 %collective-permute-start.4 = (f32[4,128,256]{2,1,0:T(8,128)S(1)}, f32[4,128,256]{2,1,0:T(8,128)S(1)}, u32[]{:S(2)}, u32[]{:S(2)}) collective-permute-start(f32[4,128,256]{2,1,0:T(8,128)S(1)} %pad_maximum_fusion.refs_0_.refs_3_), channel_id=1, source_target_pairs={{0,1},{1,0},{2,3},{3,2},{4,5},{5,4},{6,7},{7,6},{8,9},{9,8},{10,11... | collective-permute-start | bytes 1572872 | tf_op jit(solution)/shard_map/ppermute | solution.py:236
  53.2 2.2 %collective-permute-start.9 = (f32[4,128,256]{2,1,0:T(8,128)S(1)}, f32[4,128,256]{2,1,0:T(8,128)S(1)}, u32[]{:S(2)}, u32[]{:S(2)}) collective-permute-start(f32[4,128,256]{2,1,0:T(8,128)S(1)} %collective-permute-done.5.refs_1_.refs_4_), channel_id=1, source_target_pairs={{0,1},{1,0},{2,3},{3,2},{4,5},{5,4},{6,7},{7,6},{8,9},{9,8},{10,11... | collective-permute-start | bytes 1572872 | tf_op jit(solution)/shard_map/ppermute | solution.py:236
  53.2 2.7 %collective-permute-start.10 = (f32[4,2,64,256]{3,2,1,0:T(8,128)S(1)}, f32[4,2,64,256]{3,2,1,0:T(8,128)S(1)}, u32[]{:S(2)}, u32[]{:S(2)}) collective-permute-start(f32[4,2,64,256]{3,2,1,0:T(8,128)S(1)} %pad_maximum_fusion.1.refs_2_.refs_5_), channel_id=1, source_target_pairs={{0,1},{1,0},{2,3},{3,2},{4,5},{5,4},{6,7},{7,6},{8,9},{9,8},{10,11... | collective-permute-start | bytes 1572872 | tf_op jit(solution)/shard_map/ppermute | solution.py:236
  57.4 9.4 %collective-permute-start.13 = (f32[128,256]{1,0:T(8,128)S(1)}, f32[128,256]{1,0:T(8,128)S(1)}, u32[]{:S(2)}, u32[]{:S(2)}) collective-permute-start(f32[128,256]{1,0:T(8,128)S(1)} %get-tuple-element.43), channel_id=1, source_target_pairs={{0,28},{1,29},{2,30},{3,31},{4,16},{5,17},{6,18},{7,19},{8,20},{9,... | collective-permute-start | bytes 393224 | tf_op jit(solution)/shard_map/ppermute | solution.py:238
  58.9 7.5 %collective-permute-start.12 = (f32[64,256]{1,0:T(8,128)S(1)}, f32[64,256]{1,0:T(8,128)S(1)}, u32[]{:S(2)}, u32[]{:S(2)}) collective-permute-start(f32[64,256]{1,0:T(8,128)S(1)} %get-tuple-element.42), channel_id=1, source_target_pairs={{0,18},{1,19},{2,16},{3,17},{4,22},{5,23},{6,20},{7,21},{8,26},{9,... | collective-permute-start | bytes 196616 | tf_op jit(solution)/shard_map/ppermute | solution.py:238
  61.4 5.5 %collective-permute-start.11 = (f32[64,256]{1,0:T(8,128)S(1)}, f32[64,256]{1,0:T(8,128)S(1)}, u32[]{:S(2)}, u32[]{:S(2)}) collective-permute-start(f32[64,256]{1,0:T(8,128)S(1)} %get-tuple-element.42), channel_id=1, source_target_pairs={{0,16},{1,17},{2,18},{3,19},{4,20},{5,21},{6,22},{7,23},{8,24},{9,... | collective-permute-start | bytes 196616 | tf_op jit(solution)/shard_map/ppermute | solution.py:238
  61.4 12.4 %collective-permute-start.16 = (f32[128,256]{1,0:T(8,128)S(1)}, f32[128,256]{1,0:T(8,128)S(1)}, u32[]{:S(2)}, u32[]{:S(2)}) collective-permute-start(f32[128,256]{1,0:T(8,128)S(1)} %get-tuple-element.43), channel_id=1, source_target_pairs={{0,24},{1,25},{2,26},{3,27},{4,28},{5,29},{6,30},{7,31},{8,16},{9,... | collective-permute-start | bytes 393224 | tf_op jit(solution)/shard_map/ppermute | solution.py:238
  62.0 11.9 %collective-permute-start.15 = (f32[128,256]{1,0:T(8,128)S(1)}, f32[128,256]{1,0:T(8,128)S(1)}, u32[]{:S(2)}, u32[]{:S(2)}) collective-permute-start(f32[128,256]{1,0:T(8,128)S(1)} %get-tuple-element.43), channel_id=1, source_target_pairs={{0,20},{1,21},{2,22},{3,23},{4,24},{5,25},{6,26},{7,27},{8,28},{9,... | collective-permute-start | bytes 393224 | tf_op jit(solution)/shard_map/ppermute | solution.py:238
  66.4 9.8 %collective-permute-start.14 = (f32[128,256]{1,0:T(8,128)S(1)}, f32[128,256]{1,0:T(8,128)S(1)}, u32[]{:S(2)}, u32[]{:S(2)}) collective-permute-start(f32[128,256]{1,0:T(8,128)S(1)} %get-tuple-element.43), channel_id=1, source_target_pairs={{0,16},{1,17},{2,18},{3,19},{4,20},{5,21},{6,22},{7,23},{8,24},{9,... | collective-permute-start | bytes 393224 | tf_op jit(solution)/shard_map/ppermute | solution.py:238
  76.2 13.6 %collective-permute-start.18 = (f32[4,128,256]{2,1,0:T(8,128)S(1)}, f32[4,128,256]{2,1,0:T(8,128)S(1)}, u32[]{:S(2)}, u32[]{:S(2)}) collective-permute-start(f32[4,128,256]{2,1,0:T(8,128)S(1)} %pad_maximum_fusion.2.refs_0_), channel_id=1, source_target_pairs={{0,2},{1,3},{2,0},{3,1},{4,6},{5,7},{6,4},{7,5},{8,10},{9,11},{10,... | collective-permute-start | bytes 1572872 | tf_op jit(solution)/shard_map/ppermute | solution.py:236
  76.9 8.2 %collective-permute-start.22 = (f32[2,64,256]{2,1,0:T(8,128)S(1)}, f32[2,64,256]{2,1,0:T(8,128)S(1)}, u32[]{:S(2)}, u32[]{:S(2)}) collective-permute-start(f32[2,64,256]{2,1,0:T(8,128)S(1)} %pad_maximum_fusion.5), channel_id=1, source_target_pairs={{0,12},{1,13},{2,14},{3,15},{4,8},{5,9},{6,10},{7,11},{8,4},{9,5},... | collective-permute-start | bytes 393224 | tf_op jit(solution)/shard_map/ppermute | solution.py:236
  78.9 10.0 %collective-permute-start.21 = (f32[2,64,256]{2,1,0:T(8,128)S(1)}, f32[2,64,256]{2,1,0:T(8,128)S(1)}, u32[]{:S(2)}, u32[]{:S(2)}) collective-permute-start(f32[2,64,256]{2,1,0:T(8,128)S(1)} %pad_maximum_fusion.5), channel_id=1, source_target_pairs={{0,8},{1,9},{2,10},{3,11},{4,12},{5,13},{6,14},{7,15},{8,0},{9,1},... | collective-permute-start | bytes 393224 | tf_op jit(solution)/shard_map/ppermute | solution.py:236
  79.0 10.0 %collective-permute-start.20 = (f32[2,64,256]{2,1,0:T(8,128)S(1)}, f32[2,64,256]{2,1,0:T(8,128)S(1)}, u32[]{:S(2)}, u32[]{:S(2)}) collective-permute-start(f32[2,64,256]{2,1,0:T(8,128)S(1)} %pad_maximum_fusion.5), channel_id=1, source_target_pairs={{0,4},{1,5},{2,6},{3,7},{4,0},{5,1},{6,2},{7,3},{8,12},{9,13},{10,... | collective-permute-start | bytes 393224 | tf_op jit(solution)/shard_map/ppermute | solution.py:236
  81.3 10.2 %collective-permute-start.17 = (f32[4,128,256]{2,1,0:T(8,128)S(1)}, f32[4,128,256]{2,1,0:T(8,128)S(1)}, u32[]{:S(2)}, u32[]{:S(2)}) collective-permute-start(f32[4,128,256]{2,1,0:T(8,128)S(1)} %pad_maximum_fusion.2.refs_0_), channel_id=1, source_target_pairs={{0,1},{1,0},{2,3},{3,2},{4,5},{5,4},{6,7},{7,6},{8,9},{9,8},{10,11... | collective-permute-start | bytes 1572872 | tf_op jit(solution)/shard_map/ppermute | solution.py:236
  89.0 2.5 %collective-permute-start.23 = (f32[4,2,64,256]{3,2,1,0:T(8,128)S(1)}, f32[4,2,64,256]{3,2,1,0:T(8,128)S(1)}, u32[]{:S(2)}, u32[]{:S(2)}) collective-permute-start(f32[4,2,64,256]{3,2,1,0:T(8,128)S(1)} %pad_maximum_fusion.3.refs_2_), channel_id=1, source_target_pairs={{0,1},{1,0},{2,3},{3,2},{4,5},{5,4},{6,7},{7,6},{8,9},{9,8},{10,11... | collective-permute-start | bytes 1572872 | tf_op jit(solution)/shard_map/ppermute | solution.py:236
  89.8 1.9 %collective-permute-start.19 = (f32[4,128,256]{2,1,0:T(8,128)S(1)}, f32[4,128,256]{2,1,0:T(8,128)S(1)}, u32[]{:S(2)}, u32[]{:S(2)}) collective-permute-start(f32[4,128,256]{2,1,0:T(8,128)S(1)} %collective-permute-done.18.refs_1_), channel_id=1, source_target_pairs={{0,1},{1,0},{2,3},{3,2},{4,5},{5,4},{6,7},{7,6},{8,9},{9,8},{10,11... | collective-permute-start | bytes 1572872 | tf_op jit(solution)/shard_map/ppermute | solution.py:236

commit v17 on v16

--- a/solution.py
+++ b/solution.py
@@ -8,6 +8,7 @@
 from jax.sharding import PartitionSpec as P
 
 MIB = 1 << 20
+STORE = 24
 f32 = jnp.float32
 bf16 = jnp.bfloat16
 lanes_contract = (((1,), (1,)), ((), ()))
@@ -22,7 +23,9 @@
     return pltpu.CompilerParams(vmem_limit_bytes=int(size * MIB))
 
 
-def pack_kernel(own_rows, cap, tile_rows, counts_hbm, rows_hbm, updates_hbm, packed_ref, counts_ref, rows_ref, updates_ref, sems):
+def pack_kernel(own_rows, cap, tile_rows, counts_hbm, rows_hbm, updates_hbm, right_hbm, packed_ref, store_hbm, *scratch):
+    counts_ref, rows_ref, updates_ref, sems = scratch
+    keep = pltpu.make_async_copy(right_hbm, store_hbm.at[0], sems.at[3])
     moves = [
         pltpu.make_async_copy(counts_hbm, counts_ref, sems.at[0]),
         pltpu.make_async_copy(rows_hbm, rows_ref, sems.at[1]),
@@ -30,6 +33,7 @@
     ]
     for move in moves:
         move.start()
+    keep.start()
     columns, entries = updates_ref.shape
     owners, height, width = packed_ref.shape
     slots = owners * cap
@@ -57,6 +61,7 @@
     for piece in halves_of(data):
         packed += lax.dot_general(choose, piece, lanes_contract, preferred_element_type=f32)
     packed = packed.reshape(owners, cap, data.shape[0])
+    keep.wait()
     if not folded:
         packed_ref[...] = packed
         return
@@ -73,7 +78,7 @@
 
 def reduce_kernel(cap, received_ref, right_hbm, *refs):
     reduced_refs, right_ref, sem = refs[:-2], refs[-2], refs[-1]
-    move = pltpu.make_async_copy(right_hbm, right_ref, sem)
+    move = pltpu.make_async_copy(right_hbm.at[0], right_ref, sem)
     move.start()
     owners, height, width = received_ref.shape
     slots = owners * cap
@@ -315,19 +320,22 @@
     folded = cap % 16 == 0 and slots <= 1024 and columns == 192 and own_rows <= 256 and 128 % cap == 0
     width = 128 if folded else -(-(columns + 1) // 128) * 128
     height = cap + cap // 2 + 8 if folded else cap
-    packed = pl.pallas_call(
+    packed, stored = pl.pallas_call(
         functools.partial(pack_kernel, own_rows, cap, tile_rows),
-        in_specs=[hbm, hbm, hbm],
-        out_specs=vmem,
-        out_shape=jax.ShapeDtypeStruct((tile_size, height, width), f32),
+        in_specs=[hbm, hbm, hbm, hbm],
+        out_specs=[vmem, hbm],
+        out_shape=[
+            jax.ShapeDtypeStruct((tile_size, height, width), f32),
+            jax.ShapeDtypeStruct((STORE, columns, own_rows), f32),
+        ],
         scratch_shapes=[
             pltpu.SMEM(tile_counts.shape, jnp.int32),
             pltpu.VMEM((1, entries), jnp.int32),
             pltpu.VMEM((columns, entries), f32),
-            pltpu.SemaphoreType.DMA((3,)),
+            pltpu.SemaphoreType.DMA((4,)),
         ],
         compiler_params=kernel_params(56),
-    )(tile_counts, update_rows[None, :], updates.T)
+    )(tile_counts, update_rows[None, :], updates.T, right_side.reshape(columns, own_rows))
     received = lax.all_to_all(packed, "tile", 0, 0, tiled=False)
     paired = own_rows % 128 == 0 and tile_size >= 8 and tile_size & (tile_size - 1) == 0 and batches > 1
     early = batches * 2 // 3 * halves * sources
@@ -338,8 +346,8 @@
         out_specs=[vmem] * len(shares),
         out_shape=[jax.ShapeDtypeStruct((rows, own_rows), f32) for rows in shares],
         scratch_shapes=[pltpu.VMEM((columns, own_rows), f32), pltpu.SemaphoreType.DMA(())],
-        compiler_params=kernel_params(20),
-    )(received, right_side.reshape(columns, own_rows))
+        compiler_params=kernel_params(50),
+    )(received, stored)
     solve = solve_paired if paired else solve_flat
     return solve(reduced, diag_inverse, coupling, sources).reshape(right_side.shape)
 

time: 94.3 us -> 99.5 us (1.055)
  Pallas kernels: 12.1 us -> 18.3 us
    pallas_call x1, Pallas kernels: 2.19 us -> 8.05 us  [body(): pl.pallas_call(functools.partial(pack_kernel, own_rows, cap, tile_rows),...]
    unnamed x6 -> x4, local copies, waits for them, and re-layouts: 4.31 us -> 3.38 us
  transfers between devices with their start and end apart: 24 -> 24, of which waited for: 12 -> 12; matrix products, arithmetic and copies ran while one was open for 0% -> 0% of each run, Pallas kernels for 6% -> 5%
where the time goes in v17:
time: 99.5 us; the launch traced here: 99.2 us
  waiting for transfers between devices  34 us (34%)
  starting transfers between devices  22.6 us (23%)
  blocking collectives  20.6 us (21%)
  Pallas kernels  18.3 us (18%)
  local copies, waits for them, and re-layouts  3.38 us (3%)
    ppermute x18, waiting for transfers between devices, send(): lax.ppermute(value, 'tile', [(t, target(t)) for t in range(tile_size)])  21.8 us
    all_to_all x1, blocking collectives, body(): received = lax.all_to_all(packed, 'tile', 0, 0, tiled=False)  20.6 us
    ppermute x18, starting transfers between devices, send(): lax.ppermute(value, 'tile', [(t, target(t)) for t in range(tile_size)])  16.1 us
    ppermute x6, waiting for transfers between devices, send(): return lax.ppermute(value, ('chain', 'tile'), pairs)  12.2 us
    pallas_call x1, Pallas kernels, body(): pl.pallas_call(functools.partial(pack_kernel, own_rows, cap, tile_rows),...  8.05 us
    pallas_call x4, Pallas kernels, product_part(): pl.pallas_call(functools.partial(product_kernel, sources, layout, len(blo...  7.21 us
    ppermute x6, starting transfers between devices, send(): return lax.ppermute(value, ('chain', 'tile'), pairs)  6.5 us
    unnamed x4, local copies, waits for them, and re-layouts  3.38 us
  transfers between devices with their start and end apart: 24, of which 12 were waited for; matrix products, arithmetic and copies ran while one was open for 0% of the time, Pallas kernels for 5%

profile of v17, /device:TPU:0, one launch (start us, length us, event | category | flops | bytes accessed | tf_op | source)
XLA Modules:
  0.0 99.2 jit_solution(14949802418055005084)
XLA Ops:
  0.0 8.1 %shard_map.64 = (f32[16,56,128]{2,1,0:T(8,128)}, f32[24,192,256]{2,1,0:T(8,128)}) custom-call(s32[2]{0:T(128)} %counts_hbm.1, s32[1,256]{1,0:T(1,128)} %bitcast.46, f32[192,256]{1,0:T(8,128)} %bitcast.28, f32[192,256]{1,0:T(8,128)} %bitcast.29), custom_call_target="tpu_custom_call" | custom-call | tf_op jit(solution)/shard_map/pallas_call | solution.py:323
  8.1 20.6 %all_to_all.5.received_ref = f32[16,56,128]{2,1,0:T(8,128)S(1)} all-to-all(f32[16,56,128]{2,1,0:T(8,128)} %get-tuple-element.30), channel_id=1, replica_groups=mesh['chain'=2,'tile'=16] {'tile'}, dimensions={0} | all-to-all | bytes 917504 | tf_op jit(solution)/shard_map/all_to_all | solution.py:339
  28.7 1.1 %shard_map.65 = (f32[128,256]{1,0:T(8,128)S(1)}, f32[64,256]{1,0:T(8,128)S(1)}) custom-call(f32[16,56,128]{2,1,0:T(8,128)S(1)} %all_to_all.5.received_ref, f32[24,192,256]{2,1,0:T(8,128)} %get-tuple-element.31.right_hbm), custom_call_target="tpu_custom_call" | custom-call | tf_op jit(solution)/shard_map/pallas_call | solution.py:343
  29.8 0.4 collective-permute-start
  30.2 2.7 %collective-permute-start.3 = (f32[128,256]{1,0:T(8,128)S(1)}, f32[128,256]{1,0:T(8,128)S(1)}, u32[]{:S(2)}, u32[]{:S(2)}) collective-permute-start(f32[128,256]{1,0:T(8,128)S(1)} %get-tuple-element.33), channel_id=1, source_target_pairs={{0,12},{1,13},{2,14},{3,15},{4,8},{5,9},{6,10},{7,11},{8,4},{9,5},... | collective-permute-start | bytes 393224 | tf_op jit(solution)/shard_map/ppermute | solution.py:241
  33.0 0.5 collective-permute-start.2
  33.5 1.1 %collective-permute-start.1 = (f32[128,256]{1,0:T(8,128)S(1)}, f32[128,256]{1,0:T(8,128)S(1)}, u32[]{:S(2)}, u32[]{:S(2)}) collective-permute-start(f32[128,256]{1,0:T(8,128)S(1)} %get-tuple-element.33), channel_id=1, source_target_pairs={{0,4},{1,5},{2,6},{3,7},{4,0},{5,1},{6,2},{7,3},{8,12},{9,13},{10,... | collective-permute-start | bytes 393224 | tf_op jit(solution)/shard_map/ppermute | solution.py:241
  34.6 0.0 copy-start
  34.6 3.4 %copy-done = f32[2,256,4096]{2,1,0:T(8,128)S(1)} copy-done((f32[2,256,4096]{2,1,0:T(8,128)S(1)}, f32[2,256,4096]{2,1,0:T(8,128)}, u32[]{:S(2)}) %copy-start) | copy-done | bytes 8388632
  38.0 0.0 copy-start.1
  38.0 1.0 shard_map.66
  39.0 0.0 collective-permute-done
  39.0 0.0 collective-permute-done.3
  39.0 6.3 %collective-permute-done.2 = f32[128,256]{1,0:T(8,128)S(1)} collective-permute-done((f32[128,256]{1,0:T(8,128)S(1)}, f32[128,256]{1,0:T(8,128)S(1)}, u32[]{:S(2)}, u32[]{:S(2)}) %collective-permute-start.2) | collective-permute-done | bytes 131104 | tf_op jit(solution)/shard_map/ppermute | solution.py:241
  45.3 0.0 collective-permute-done.1
  45.4 1.2 %collective-permute-start.5 = (f32[4,128,256]{2,1,0:T(8,128)S(1)}, f32[4,128,256]{2,1,0:T(8,128)S(1)}, u32[]{:S(2)}, u32[]{:S(2)}) collective-permute-start(f32[4,128,256]{2,1,0:T(8,128)S(1)} %pad_maximum_fusion.refs_0_.refs_3_), channel_id=1, source_target_pairs={{0,2},{1,3},{2,0},{3,1},{4,6},{5,7},{6,4},{7,5},{8,10},{9,11},{10,... | collective-permute-start | bytes 1572872 | tf_op jit(solution)/shard_map/ppermute | solution.py:241
  46.6 1.4 %collective-permute-start.8 = (f32[2,64,256]{2,1,0:T(8,128)S(1)}, f32[2,64,256]{2,1,0:T(8,128)S(1)}, u32[]{:S(2)}, u32[]{:S(2)}) collective-permute-start(f32[2,64,256]{2,1,0:T(8,128)S(1)} %pad_maximum_fusion.4), channel_id=1, source_target_pairs={{0,12},{1,13},{2,14},{3,15},{4,8},{5,9},{6,10},{7,11},{8,4},{9,5},... | collective-permute-start | bytes 393224 | tf_op jit(solution)/shard_map/ppermute | solution.py:241
  48.0 0.0 collective-permute-start.7
  48.0 3.0 %collective-permute-start.6 = (f32[2,64,256]{2,1,0:T(8,128)S(1)}, f32[2,64,256]{2,1,0:T(8,128)S(1)}, u32[]{:S(2)}, u32[]{:S(2)}) collective-permute-start(f32[2,64,256]{2,1,0:T(8,128)S(1)} %pad_maximum_fusion.4), channel_id=1, source_target_pairs={{0,4},{1,5},{2,6},{3,7},{4,0},{5,1},{6,2},{7,3},{8,12},{9,13},{10,... | collective-permute-start | bytes 393224 | tf_op jit(solution)/shard_map/ppermute | solution.py:241
  51.0 0.0 collective-permute-start.4
  51.0 0.0 copy-done.1
  51.0 1.0 shard_map.67
  52.0 2.9 %collective-permute-done.8 = f32[2,64,256]{2,1,0:T(8,128)S(1)} collective-permute-done((f32[2,64,256]{2,1,0:T(8,128)S(1)}, f32[2,64,256]{2,1,0:T(8,128)S(1)}, u32[]{:S(2)}, u32[]{:S(2)}) %collective-permute-start.8) | collective-permute-done | bytes 131104 | tf_op jit(solution)/shard_map/ppermute | solution.py:241
  54.9 3.1 %collective-permute-done.7 = f32[2,64,256]{2,1,0:T(8,128)S(1)} collective-permute-done((f32[2,64,256]{2,1,0:T(8,128)S(1)}, f32[2,64,256]{2,1,0:T(8,128)S(1)}, u32[]{:S(2)}, u32[]{:S(2)}) %collective-permute-start.7) | collective-permute-done | bytes 131104 | tf_op jit(solution)/shard_map/ppermute | solution.py:241
  58.0 0.0 collective-permute-done.6
  58.1 0.4 collective-permute-done.5.refs_1_.refs_4_
  58.4 0.0 collective-permute-start.9
  58.4 0.5 collective-permute-start.10
  58.9 1.7 %shard_map.68.refs_5_ = f32[192,512]{1,0:T(8,128)S(1)} custom-call(f32[4,128,256]{2,1,0:T(8,128)S(1)} %pad_maximum_fusion.refs_0_.refs_3_, f32[4,128,256]{2,1,0:T(8,128)S(1)} %collective-permute-done.5.refs_1_.refs_4_, f32[4,2,64,256]{3,2,1,0:T(8,128)S(1)} %pad_maximum_fusion.1.refs_2_.refs_5_, bf16[4,512,1024]{2,1,0:T(8,128)(2,1)S(1)} %get-tuple-element.44.refs_3_, ...), custom_call_target="tpu_custom_call" | custom-call | flops 1207959552 | bytes 1048576 | tf_op jit(solution)/shard_map/pallas_call | solution.py:217
  60.6 0.0 collective-permute-done.4.refs_0_.refs_3_
  60.6 0.0 collective-permute-done.9.refs_1_.refs_4_
  60.6 0.5 collective-permute-done.10.refs_2_.refs_5_
  61.1 1.6 %shard_map.69 = (f32[128,256]{1,0:T(8,128)S(1)}, f32[64,256]{1,0:T(8,128)S(1)}) custom-call(f32[4,128,256]{2,1,0:T(8,128)S(1)} %collective-permute-done.4.refs_0_.refs_3_, f32[4,128,256]{2,1,0:T(8,128)S(1)} %collective-permute-done.9.refs_1_.refs_4_, f32[4,2,64,256]{3,2,1,0:T(8,128)S(1)} %collective-permute-done.10.refs_2_.refs_5_, ...), custom_call_target="tpu_custom_call" | custom-call | flops 1207959552 | bytes 1048576 | tf_op jit(solution)/shard_map/pallas_call | solution.py:217
  62.7 1.5 %collective-permute-start.13 = (f32[128,256]{1,0:T(8,128)S(1)}, f32[128,256]{1,0:T(8,128)S(1)}, u32[]{:S(2)}, u32[]{:S(2)}) collective-permute-start(f32[128,256]{1,0:T(8,128)S(1)} %get-tuple-element.47), channel_id=1, source_target_pairs={{0,28},{1,29},{2,30},{3,31},{4,16},{5,17},{6,18},{7,19},{8,20},{9,... | collective-permute-start | bytes 393224 | tf_op jit(solution)/shard_map/ppermute | solution.py:243
  64.2 2.4 %collective-permute-start.12 = (f32[64,256]{1,0:T(8,128)S(1)}, f32[64,256]{1,0:T(8,128)S(1)}, u32[]{:S(2)}, u32[]{:S(2)}) collective-permute-start(f32[64,256]{1,0:T(8,128)S(1)} %get-tuple-element.46), channel_id=1, source_target_pairs={{0,18},{1,19},{2,16},{3,17},{4,22},{5,23},{6,20},{7,21},{8,26},{9,... | collective-permute-start | bytes 196616 | tf_op jit(solution)/shard_map/ppermute | solution.py:243
  66.6 0.0 collective-permute-start.11
  66.6 0.6 collective-permute-start.16
  67.2 1.5 %collective-permute-start.15 = (f32[128,256]{1,0:T(8,128)S(1)}, f32[128,256]{1,0:T(8,128)S(1)}, u32[]{:S(2)}, u32[]{:S(2)}) collective-permute-start(f32[128,256]{1,0:T(8,128)S(1)} %get-tuple-element.47), channel_id=1, source_target_pairs={{0,20},{1,21},{2,22},{3,23},{4,24},{5,25},{6,26},{7,27},{8,28},{9,... | collective-permute-start | bytes 393224 | tf_op jit(solution)/shard_map/ppermute | solution.py:243
  68.7 2.9 %collective-permute-done.12 = f32[64,256]{1,0:T(8,128)S(1)} collective-permute-done((f32[64,256]{1,0:T(8,128)S(1)}, f32[64,256]{1,0:T(8,128)S(1)}, u32[]{:S(2)}, u32[]{:S(2)}) %collective-permute-start.12) | collective-permute-done | bytes 65568 | tf_op jit(solution)/shard_map/ppermute | solution.py:243
  71.7 0.5 collective-permute-start.14
  72.1 0.0 collective-permute-done.11
  72.1 0.0 collective-permute-done.13
  72.2 7.0 %collective-permute-done.16 = f32[128,256]{1,0:T(8,128)S(1)} collective-permute-done((f32[128,256]{1,0:T(8,128)S(1)}, f32[128,256]{1,0:T(8,128)S(1)}, u32[]{:S(2)}, u32[]{:S(2)}) %collective-permute-start.16) | collective-permute-done | bytes 131104 | tf_op jit(solution)/shard_map/ppermute | solution.py:243
  79.1 0.0 collective-permute-done.15
  79.1 2.3 %collective-permute-done.14 = f32[128,256]{1,0:T(8,128)S(1)} collective-permute-done((f32[128,256]{1,0:T(8,128)S(1)}, f32[128,256]{1,0:T(8,128)S(1)}, u32[]{:S(2)}, u32[]{:S(2)}) %collective-permute-start.14) | collective-permute-done | bytes 131104 | tf_op jit(solution)/shard_map/ppermute | solution.py:243
  81.5 0.7 collective-permute-start.18
  82.1 2.1 %collective-permute-start.22 = (f32[2,64,256]{2,1,0:T(8,128)S(1)}, f32[2,64,256]{2,1,0:T(8,128)S(1)}, u32[]{:S(2)}, u32[]{:S(2)}) collective-permute-start(f32[2,64,256]{2,1,0:T(8,128)S(1)} %pad_maximum_fusion.5), channel_id=1, source_target_pairs={{0,12},{1,13},{2,14},{3,15},{4,8},{5,9},{6,10},{7,11},{8,4},{9,5},... | collective-permute-start | bytes 393224 | tf_op jit(solution)/shard_map/ppermute | solution.py:241
  84.2 0.0 collective-permute-start.21
  84.2 2.3 %collective-permute-start.20 = (f32[2,64,256]{2,1,0:T(8,128)S(1)}, f32[2,64,256]{2,1,0:T(8,128)S(1)}, u32[]{:S(2)}, u32[]{:S(2)}) collective-permute-start(f32[2,64,256]{2,1,0:T(8,128)S(1)} %pad_maximum_fusion.5), channel_id=1, source_target_pairs={{0,4},{1,5},{2,6},{3,7},{4,0},{5,1},{6,2},{7,3},{8,12},{9,13},{10,... | collective-permute-start | bytes 393224 | tf_op jit(solution)/shard_map/ppermute | solution.py:241
  86.5 0.0 collective-permute-start.17
  86.5 3.8 %collective-permute-done.22 = f32[2,64,256]{2,1,0:T(8,128)S(1)} collective-permute-done((f32[2,64,256]{2,1,0:T(8,128)S(1)}, f32[2,64,256]{2,1,0:T(8,128)S(1)}, u32[]{:S(2)}, u32[]{:S(2)}) %collective-permute-start.22) | collective-permute-done | bytes 131104 | tf_op jit(solution)/shard_map/ppermute | solution.py:241
  90.4 3.8 %collective-permute-done.21 = f32[2,64,256]{2,1,0:T(8,128)S(1)} collective-permute-done((f32[2,64,256]{2,1,0:T(8,128)S(1)}, f32[2,64,256]{2,1,0:T(8,128)S(1)}, u32[]{:S(2)}, u32[]{:S(2)}) %collective-permute-start.21) | collective-permute-done | bytes 131104 | tf_op jit(solution)/shard_map/ppermute | solution.py:241
  94.2 0.0 collective-permute-done.20
  94.2 0.1 collective-permute-start.23
  94.3 0.7 collective-permute-done.18.refs_1_
  95.0 0.0 collective-permute-start.19
  95.0 1.7 %shard_map.70.refs_8_ = f32[192,512]{1,0:T(8,128)S(1)} custom-call(f32[4,128,256]{2,1,0:T(8,128)S(1)} %pad_maximum_fusion.2.refs_0_, f32[4,128,256]{2,1,0:T(8,128)S(1)} %collective-permute-done.18.refs_1_, f32[4,2,64,256]{3,2,1,0:T(8,128)S(1)} %pad_maximum_fusion.3.refs_2_, f32[4,128,256]{2,1,0:T(8,128)S(1)} %pad_maximum_fusion.refs_0_.refs_3_, ...), custom_call_target="tpu_custom_call" | custom-call | flops 1207959552 | bytes 1048576 | tf_op jit(solution)/shard_map/pallas_call | solution.py:217
  96.7 0.0 collective-permute-done.17.refs_0_
  96.7 0.0 collective-permute-done.23.refs_2_
  96.7 0.3 collective-permute-done.19.refs_1_
  97.0 2.3 %shard_map.71 = f32[192,256]{1,0:T(8,128)} custom-call(f32[4,128,256]{2,1,0:T(8,128)S(1)} %collective-permute-done.17.refs_0_, f32[4,128,256]{2,1,0:T(8,128)S(1)} %collective-permute-done.19.refs_1_, f32[4,2,64,256]{3,2,1,0:T(8,128)S(1)} %collective-permute-done.23.refs_2_, f32[4,128,256]{2,1,0:T(8,128)S(1)} %collective-permute-done.4.refs_0_.refs_3_, ...), custom_call_target="tpu_custom_call" | custom-call | flops 1207959552 | bytes 1048576 | tf_op jit(solution)/shard_map/pallas_call | solution.py:217
  (6 shorter events, 0.2 us)
Async XLA Ops:
  29.8 9.2 %collective-permute-start = (f32[64,256]{1,0:T(8,128)S(1)}, f32[64,256]{1,0:T(8,128)S(1)}, u32[]{:S(2)}, u32[]{:S(2)}) collective-permute-start(f32[64,256]{1,0:T(8,128)S(1)} %get-tuple-element.32), channel_id=1, source_target_pairs={{0,2},{1,3},{2,0},{3,1},{4,6},{5,7},{6,4},{7,5},{8,10},{9,11},{10,... | collective-permute-start | bytes 196616 | tf_op jit(solution)/shard_map/ppermute | solution.py:241
  30.2 8.8 %collective-permute-start.3 = (f32[128,256]{1,0:T(8,128)S(1)}, f32[128,256]{1,0:T(8,128)S(1)}, u32[]{:S(2)}, u32[]{:S(2)}) collective-permute-start(f32[128,256]{1,0:T(8,128)S(1)} %get-tuple-element.33), channel_id=1, source_target_pairs={{0,12},{1,13},{2,14},{3,15},{4,8},{5,9},{6,10},{7,11},{8,4},{9,5},... | collective-permute-start | bytes 393224 | tf_op jit(solution)/shard_map/ppermute | solution.py:241
  33.0 12.4 %collective-permute-start.2 = (f32[128,256]{1,0:T(8,128)S(1)}, f32[128,256]{1,0:T(8,128)S(1)}, u32[]{:S(2)}, u32[]{:S(2)}) collective-permute-start(f32[128,256]{1,0:T(8,128)S(1)} %get-tuple-element.33), channel_id=1, source_target_pairs={{0,8},{1,9},{2,10},{3,11},{4,12},{5,13},{6,14},{7,15},{8,0},{9,1},... | collective-permute-start | bytes 393224 | tf_op jit(solution)/shard_map/ppermute | solution.py:241
  33.5 11.8 %collective-permute-start.1 = (f32[128,256]{1,0:T(8,128)S(1)}, f32[128,256]{1,0:T(8,128)S(1)}, u32[]{:S(2)}, u32[]{:S(2)}) collective-permute-start(f32[128,256]{1,0:T(8,128)S(1)} %get-tuple-element.33), channel_id=1, source_target_pairs={{0,4},{1,5},{2,6},{3,7},{4,0},{5,1},{6,2},{7,3},{8,12},{9,13},{10,... | collective-permute-start | bytes 393224 | tf_op jit(solution)/shard_map/ppermute | solution.py:241
  34.6 3.4 %copy-start = (f32[2,256,4096]{2,1,0:T(8,128)S(1)}, f32[2,256,4096]{2,1,0:T(8,128)}, u32[]{:S(2)}) copy-start(f32[2,256,4096]{2,1,0:T(8,128)} %matrix_ref) | copy-start | bytes 25165828
  38.0 13.0 %copy-start.1 = (f32[2,256,4096]{2,1,0:T(8,128)S(1)}, f32[2,256,4096]{2,1,0:T(8,128)}, u32[]{:S(2)}) copy-start(f32[2,256,4096]{2,1,0:T(8,128)} %matrix_ref.1) | copy-start | bytes 25165828
  45.4 13.1 %collective-permute-start.5 = (f32[4,128,256]{2,1,0:T(8,128)S(1)}, f32[4,128,256]{2,1,0:T(8,128)S(1)}, u32[]{:S(2)}, u32[]{:S(2)}) collective-permute-start(f32[4,128,256]{2,1,0:T(8,128)S(1)} %pad_maximum_fusion.refs_0_.refs_3_), channel_id=1, source_target_pairs={{0,2},{1,3},{2,0},{3,1},{4,6},{5,7},{6,4},{7,5},{8,10},{9,11},{10,... | collective-permute-start | bytes 1572872 | tf_op jit(solution)/shard_map/ppermute | solution.py:241
  46.6 8.3 %collective-permute-start.8 = (f32[2,64,256]{2,1,0:T(8,128)S(1)}, f32[2,64,256]{2,1,0:T(8,128)S(1)}, u32[]{:S(2)}, u32[]{:S(2)}) collective-permute-start(f32[2,64,256]{2,1,0:T(8,128)S(1)} %pad_maximum_fusion.4), channel_id=1, source_target_pairs={{0,12},{1,13},{2,14},{3,15},{4,8},{5,9},{6,10},{7,11},{8,4},{9,5},... | collective-permute-start | bytes 393224 | tf_op jit(solution)/shard_map/ppermute | solution.py:241
  48.0 10.0 %collective-permute-start.7 = (f32[2,64,256]{2,1,0:T(8,128)S(1)}, f32[2,64,256]{2,1,0:T(8,128)S(1)}, u32[]{:S(2)}, u32[]{:S(2)}) collective-permute-start(f32[2,64,256]{2,1,0:T(8,128)S(1)} %pad_maximum_fusion.4), channel_id=1, source_target_pairs={{0,8},{1,9},{2,10},{3,11},{4,12},{5,13},{6,14},{7,15},{8,0},{9,1},... | collective-permute-start | bytes 393224 | tf_op jit(solution)/shard_map/ppermute | solution.py:241
  48.0 10.0 %collective-permute-start.6 = (f32[2,64,256]{2,1,0:T(8,128)S(1)}, f32[2,64,256]{2,1,0:T(8,128)S(1)}, u32[]{:S(2)}, u32[]{:S(2)}) collective-permute-start(f32[2,64,256]{2,1,0:T(8,128)S(1)} %pad_maximum_fusion.4), channel_id=1, source_target_pairs={{0,4},{1,5},{2,6},{3,7},{4,0},{5,1},{6,2},{7,3},{8,12},{9,13},{10,... | collective-permute-start | bytes 393224 | tf_op jit(solution)/shard_map/ppermute | solution.py:241
  51.0 9.6 %collective-permute-start.4 = (f32[4,128,256]{2,1,0:T(8,128)S(1)}, f32[4,128,256]{2,1,0:T(8,128)S(1)}, u32[]{:S(2)}, u32[]{:S(2)}) collective-permute-start(f32[4,128,256]{2,1,0:T(8,128)S(1)} %pad_maximum_fusion.refs_0_.refs_3_), channel_id=1, source_target_pairs={{0,1},{1,0},{2,3},{3,2},{4,5},{5,4},{6,7},{7,6},{8,9},{9,8},{10,11... | collective-permute-start | bytes 1572872 | tf_op jit(solution)/shard_map/ppermute | solution.py:241
  58.4 2.2 %collective-permute-start.9 = (f32[4,128,256]{2,1,0:T(8,128)S(1)}, f32[4,128,256]{2,1,0:T(8,128)S(1)}, u32[]{:S(2)}, u32[]{:S(2)}) collective-permute-start(f32[4,128,256]{2,1,0:T(8,128)S(1)} %collective-permute-done.5.refs_1_.refs_4_), channel_id=1, source_target_pairs={{0,1},{1,0},{2,3},{3,2},{4,5},{5,4},{6,7},{7,6},{8,9},{9,8},{10,11... | collective-permute-start | bytes 1572872 | tf_op jit(solution)/shard_map/ppermute | solution.py:241
  58.4 2.7 %collective-permute-start.10 = (f32[4,2,64,256]{3,2,1,0:T(8,128)S(1)}, f32[4,2,64,256]{3,2,1,0:T(8,128)S(1)}, u32[]{:S(2)}, u32[]{:S(2)}) collective-permute-start(f32[4,2,64,256]{3,2,1,0:T(8,128)S(1)} %pad_maximum_fusion.1.refs_2_.refs_5_), channel_id=1, source_target_pairs={{0,1},{1,0},{2,3},{3,2},{4,5},{5,4},{6,7},{7,6},{8,9},{9,8},{10,11... | collective-permute-start | bytes 1572872 | tf_op jit(solution)/shard_map/ppermute | solution.py:241
  62.7 9.5 %collective-permute-start.13 = (f32[128,256]{1,0:T(8,128)S(1)}, f32[128,256]{1,0:T(8,128)S(1)}, u32[]{:S(2)}, u32[]{:S(2)}) collective-permute-start(f32[128,256]{1,0:T(8,128)S(1)} %get-tuple-element.47), channel_id=1, source_target_pairs={{0,28},{1,29},{2,30},{3,31},{4,16},{5,17},{6,18},{7,19},{8,20},{9,... | collective-permute-start | bytes 393224 | tf_op jit(solution)/shard_map/ppermute | solution.py:243
  64.2 7.5 %collective-permute-start.12 = (f32[64,256]{1,0:T(8,128)S(1)}, f32[64,256]{1,0:T(8,128)S(1)}, u32[]{:S(2)}, u32[]{:S(2)}) collective-permute-start(f32[64,256]{1,0:T(8,128)S(1)} %get-tuple-element.46), channel_id=1, source_target_pairs={{0,18},{1,19},{2,16},{3,17},{4,22},{5,23},{6,20},{7,21},{8,26},{9,... | collective-permute-start | bytes 196616 | tf_op jit(solution)/shard_map/ppermute | solution.py:243
  66.6 5.5 %collective-permute-start.11 = (f32[64,256]{1,0:T(8,128)S(1)}, f32[64,256]{1,0:T(8,128)S(1)}, u32[]{:S(2)}, u32[]{:S(2)}) collective-permute-start(f32[64,256]{1,0:T(8,128)S(1)} %get-tuple-element.46), channel_id=1, source_target_pairs={{0,16},{1,17},{2,18},{3,19},{4,20},{5,21},{6,22},{7,23},{8,24},{9,... | collective-permute-start | bytes 196616 | tf_op jit(solution)/shard_map/ppermute | solution.py:243
  66.6 12.5 %collective-permute-start.16 = (f32[128,256]{1,0:T(8,128)S(1)}, f32[128,256]{1,0:T(8,128)S(1)}, u32[]{:S(2)}, u32[]{:S(2)}) collective-permute-start(f32[128,256]{1,0:T(8,128)S(1)} %get-tuple-element.47), channel_id=1, source_target_pairs={{0,24},{1,25},{2,26},{3,27},{4,28},{5,29},{6,30},{7,31},{8,16},{9,... | collective-permute-start | bytes 393224 | tf_op jit(solution)/shard_map/ppermute | solution.py:243
  67.2 11.9 %collective-permute-start.15 = (f32[128,256]{1,0:T(8,128)S(1)}, f32[128,256]{1,0:T(8,128)S(1)}, u32[]{:S(2)}, u32[]{:S(2)}) collective-permute-start(f32[128,256]{1,0:T(8,128)S(1)} %get-tuple-element.47), channel_id=1, source_target_pairs={{0,20},{1,21},{2,22},{3,23},{4,24},{5,25},{6,26},{7,27},{8,28},{9,... | collective-permute-start | bytes 393224 | tf_op jit(solution)/shard_map/ppermute | solution.py:243
  71.7 9.8 %collective-permute-start.14 = (f32[128,256]{1,0:T(8,128)S(1)}, f32[128,256]{1,0:T(8,128)S(1)}, u32[]{:S(2)}, u32[]{:S(2)}) collective-permute-start(f32[128,256]{1,0:T(8,128)S(1)} %get-tuple-element.47), channel_id=1, source_target_pairs={{0,16},{1,17},{2,18},{3,19},{4,20},{5,21},{6,22},{7,23},{8,24},{9,... | collective-permute-start | bytes 393224 | tf_op jit(solution)/shard_map/ppermute | solution.py:243
  81.5 13.5 %collective-permute-start.18 = (f32[4,128,256]{2,1,0:T(8,128)S(1)}, f32[4,128,256]{2,1,0:T(8,128)S(1)}, u32[]{:S(2)}, u32[]{:S(2)}) collective-permute-start(f32[4,128,256]{2,1,0:T(8,128)S(1)} %pad_maximum_fusion.2.refs_0_), channel_id=1, source_target_pairs={{0,2},{1,3},{2,0},{3,1},{4,6},{5,7},{6,4},{7,5},{8,10},{9,11},{10,... | collective-permute-start | bytes 1572872 | tf_op jit(solution)/shard_map/ppermute | solution.py:241
  82.1 8.2 %collective-permute-start.22 = (f32[2,64,256]{2,1,0:T(8,128)S(1)}, f32[2,64,256]{2,1,0:T(8,128)S(1)}, u32[]{:S(2)}, u32[]{:S(2)}) collective-permute-start(f32[2,64,256]{2,1,0:T(8,128)S(1)} %pad_maximum_fusion.5), channel_id=1, source_target_pairs={{0,12},{1,13},{2,14},{3,15},{4,8},{5,9},{6,10},{7,11},{8,4},{9,5},... | collective-permute-start | bytes 393224 | tf_op jit(solution)/shard_map/ppermute | solution.py:241
  84.2 10.0 %collective-permute-start.21 = (f32[2,64,256]{2,1,0:T(8,128)S(1)}, f32[2,64,256]{2,1,0:T(8,128)S(1)}, u32[]{:S(2)}, u32[]{:S(2)}) collective-permute-start(f32[2,64,256]{2,1,0:T(8,128)S(1)} %pad_maximum_fusion.5), channel_id=1, source_target_pairs={{0,8},{1,9},{2,10},{3,11},{4,12},{5,13},{6,14},{7,15},{8,0},{9,1},... | collective-permute-start | bytes 393224 | tf_op jit(solution)/shard_map/ppermute | solution.py:241
  84.2 10.0 %collective-permute-start.20 = (f32[2,64,256]{2,1,0:T(8,128)S(1)}, f32[2,64,256]{2,1,0:T(8,128)S(1)}, u32[]{:S(2)}, u32[]{:S(2)}) collective-permute-start(f32[2,64,256]{2,1,0:T(8,128)S(1)} %pad_maximum_fusion.5), channel_id=1, source_target_pairs={{0,4},{1,5},{2,6},{3,7},{4,0},{5,1},{6,2},{7,3},{8,12},{9,13},{10,... | collective-permute-start | bytes 393224 | tf_op jit(solution)/shard_map/ppermute | solution.py:241
  86.5 10.1 %collective-permute-start.17 = (f32[4,128,256]{2,1,0:T(8,128)S(1)}, f32[4,128,256]{2,1,0:T(8,128)S(1)}, u32[]{:S(2)}, u32[]{:S(2)}) collective-permute-start(f32[4,128,256]{2,1,0:T(8,128)S(1)} %pad_maximum_fusion.2.refs_0_), channel_id=1, source_target_pairs={{0,1},{1,0},{2,3},{3,2},{4,5},{5,4},{6,7},{7,6},{8,9},{9,8},{10,11... | collective-permute-start | bytes 1572872 | tf_op jit(solution)/shard_map/ppermute | solution.py:241
  94.2 2.4 %collective-permute-start.23 = (f32[4,2,64,256]{3,2,1,0:T(8,128)S(1)}, f32[4,2,64,256]{3,2,1,0:T(8,128)S(1)}, u32[]{:S(2)}, u32[]{:S(2)}) collective-permute-start(f32[4,2,64,256]{3,2,1,0:T(8,128)S(1)} %pad_maximum_fusion.3.refs_2_), channel_id=1, source_target_pairs={{0,1},{1,0},{2,3},{3,2},{4,5},{5,4},{6,7},{7,6},{8,9},{9,8},{10,11... | collective-permute-start | bytes 1572872 | tf_op jit(solution)/shard_map/ppermute | solution.py:241
  95.0 2.0 %collective-permute-start.19 = (f32[4,128,256]{2,1,0:T(8,128)S(1)}, f32[4,128,256]{2,1,0:T(8,128)S(1)}, u32[]{:S(2)}, u32[]{:S(2)}) collective-permute-start(f32[4,128,256]{2,1,0:T(8,128)S(1)} %collective-permute-done.18.refs_1_), channel_id=1, source_target_pairs={{0,1},{1,0},{2,3},{3,2},{4,5},{5,4},{6,7},{7,6},{8,9},{9,8},{10,11... | collective-permute-start | bytes 1572872 | tf_op jit(solution)/shard_map/ppermute | solution.py:241

commit v18 on v17

--- a/solution.py
+++ b/solution.py
@@ -24,8 +24,9 @@
 
 
 def pack_kernel(own_rows, cap, tile_rows, counts_hbm, rows_hbm, updates_hbm, right_hbm, packed_ref, store_hbm, *scratch):
-    counts_ref, rows_ref, updates_ref, sems = scratch
-    keep = pltpu.make_async_copy(right_hbm, store_hbm.at[0], sems.at[3])
+    counts_ref, rows_ref, updates_ref, right_ref, sems = scratch
+    fetch = pltpu.make_async_copy(right_hbm, right_ref, sems.at[3])
+    keep = pltpu.make_async_copy(right_ref, store_hbm.at[0], sems.at[4])
     moves = [
         pltpu.make_async_copy(counts_hbm, counts_ref, sems.at[0]),
         pltpu.make_async_copy(rows_hbm, rows_ref, sems.at[1]),
@@ -33,7 +34,7 @@
     ]
     for move in moves:
         move.start()
-    keep.start()
+    fetch.start()
     columns, entries = updates_ref.shape
     owners, height, width = packed_ref.shape
     slots = owners * cap
@@ -41,6 +42,8 @@
     earlier = lax.broadcasted_iota(jnp.int32, (entries, entries), 0) < lax.broadcasted_iota(jnp.int32, (entries, entries), 1)
     for move in moves:
         move.wait()
+    fetch.wait()
+    keep.start()
     live = jnp.zeros((1, entries), jnp.bool_)
     for tile in range(entries // tile_rows):
         start = tile * tile_rows
@@ -332,7 +335,8 @@
             pltpu.SMEM(tile_counts.shape, jnp.int32),
             pltpu.VMEM((1, entries), jnp.int32),
             pltpu.VMEM((columns, entries), f32),
-            pltpu.SemaphoreType.DMA((4,)),
+            pltpu.VMEM((columns, own_rows), f32),
+            pltpu.SemaphoreType.DMA((5,)),
         ],
         compiler_params=kernel_params(56),
     )(tile_counts, update_rows[None, :], updates.T, right_side.reshape(columns, own_rows))

time: 99.5 us -> 94.2 us (0.947)
  Pallas kernels: 18.3 us -> 13 us
    pallas_call x1, Pallas kernels: 8.05 us -> 2.72 us  [body(): pl.pallas_call(functools.partial(pack_kernel, own_rows, cap, tile_rows),...]
  transfers between devices with their start and end apart: 24 -> 24, of which waited for: 12 -> 12; matrix products, arithmetic and copies ran while one was open for 0% -> 0% of each run, Pallas kernels for 5% -> 6%
where the time goes in v18:
time: 94.2 us; the launch traced here: 93.9 us
  waiting for transfers between devices  34 us (36%)
  starting transfers between devices  22.6 us (24%)
  blocking collectives  20.6 us (22%)
  Pallas kernels  13 us (14%)
  local copies, waits for them, and re-layouts  3.38 us (4%)
    ppermute x18, waiting for transfers between devices, send(): lax.ppermute(value, 'tile', [(t, target(t)) for t in range(tile_size)])  21.8 us
    all_to_all x1, blocking collectives, body(): received = lax.all_to_all(packed, 'tile', 0, 0, tiled=False)  20.6 us
    ppermute x18, starting transfers between devices, send(): lax.ppermute(value, 'tile', [(t, target(t)) for t in range(tile_size)])  16.1 us
    ppermute x6, waiting for transfers between devices, send(): return lax.ppermute(value, ('chain', 'tile'), pairs)  12.2 us
    pallas_call x4, Pallas kernels, product_part(): pl.pallas_call(functools.partial(product_kernel, sources, layout, len(blo...  7.21 us
    ppermute x6, starting transfers between devices, send(): return lax.ppermute(value, ('chain', 'tile'), pairs)  6.5 us
    unnamed x4, local copies, waits for them, and re-layouts  3.38 us
    pallas_call x1, Pallas kernels, body(): pl.pallas_call(functools.partial(pack_kernel, own_rows, cap, tile_rows),...  2.72 us
  transfers between devices with their start and end apart: 24, of which 12 were waited for; matrix products, arithmetic and copies ran while one was open for 0% of the time, Pallas kernels for 6%

profile of v18, /device:TPU:0, one launch (start us, length us, event | category | flops | bytes accessed | tf_op | source)
XLA Modules:
  0.0 93.9 jit_solution(804196762319852596)
XLA Ops:
  0.0 2.7 %shard_map.64 = (f32[16,56,128]{2,1,0:T(8,128)}, f32[24,192,256]{2,1,0:T(8,128)}) custom-call(s32[2]{0:T(128)} %counts_hbm.1, s32[1,256]{1,0:T(1,128)} %bitcast.46, f32[192,256]{1,0:T(8,128)} %bitcast.28, f32[192,256]{1,0:T(8,128)} %bitcast.29), custom_call_target="tpu_custom_call" | custom-call | tf_op jit(solution)/shard_map/pallas_call | solution.py:326
  2.7 20.6 %all_to_all.5.received_ref = f32[16,56,128]{2,1,0:T(8,128)S(1)} all-to-all(f32[16,56,128]{2,1,0:T(8,128)} %get-tuple-element.30), channel_id=1, replica_groups=mesh['chain'=2,'tile'=16] {'tile'}, dimensions={0} | all-to-all | bytes 917504 | tf_op jit(solution)/shard_map/all_to_all | solution.py:343
  23.4 1.1 %shard_map.65 = (f32[128,256]{1,0:T(8,128)S(1)}, f32[64,256]{1,0:T(8,128)S(1)}) custom-call(f32[16,56,128]{2,1,0:T(8,128)S(1)} %all_to_all.5.received_ref, f32[24,192,256]{2,1,0:T(8,128)} %get-tuple-element.31.right_hbm), custom_call_target="tpu_custom_call" | custom-call | tf_op jit(solution)/shard_map/pallas_call | solution.py:347
  24.5 0.4 collective-permute-start
  24.9 2.7 %collective-permute-start.3 = (f32[128,256]{1,0:T(8,128)S(1)}, f32[128,256]{1,0:T(8,128)S(1)}, u32[]{:S(2)}, u32[]{:S(2)}) collective-permute-start(f32[128,256]{1,0:T(8,128)S(1)} %get-tuple-element.33), channel_id=1, source_target_pairs={{0,12},{1,13},{2,14},{3,15},{4,8},{5,9},{6,10},{7,11},{8,4},{9,5},... | collective-permute-start | bytes 393224 | tf_op jit(solution)/shard_map/ppermute | solution.py:244
  27.6 0.5 collective-permute-start.2
  28.2 1.1 %collective-permute-start.1 = (f32[128,256]{1,0:T(8,128)S(1)}, f32[128,256]{1,0:T(8,128)S(1)}, u32[]{:S(2)}, u32[]{:S(2)}) collective-permute-start(f32[128,256]{1,0:T(8,128)S(1)} %get-tuple-element.33), channel_id=1, source_target_pairs={{0,4},{1,5},{2,6},{3,7},{4,0},{5,1},{6,2},{7,3},{8,12},{9,13},{10,... | collective-permute-start | bytes 393224 | tf_op jit(solution)/shard_map/ppermute | solution.py:244
  29.3 0.0 copy-start
  29.3 3.4 %copy-done = f32[2,256,4096]{2,1,0:T(8,128)S(1)} copy-done((f32[2,256,4096]{2,1,0:T(8,128)S(1)}, f32[2,256,4096]{2,1,0:T(8,128)}, u32[]{:S(2)}) %copy-start) | copy-done | bytes 8388632
  32.7 0.0 copy-start.1
  32.7 1.0 %shard_map.66 = (bf16[4,512,1024]{2,1,0:T(8,128)(2,1)S(1)}, bf16[4,512,1024]{2,1,0:T(8,128)(2,1)S(1)}) custom-call(f32[2,256,4096]{2,1,0:T(8,128)S(1)} %copy-done), custom_call_target="tpu_custom_call" | custom-call | flops 6291456 | bytes 16777216 | tf_op jit(solution)/shard_map/pallas_call | solution.py:140
  33.7 0.0 collective-permute-done
  33.7 0.0 collective-permute-done.3
  33.7 6.3 %collective-permute-done.2 = f32[128,256]{1,0:T(8,128)S(1)} collective-permute-done((f32[128,256]{1,0:T(8,128)S(1)}, f32[128,256]{1,0:T(8,128)S(1)}, u32[]{:S(2)}, u32[]{:S(2)}) %collective-permute-start.2) | collective-permute-done | bytes 131104 | tf_op jit(solution)/shard_map/ppermute | solution.py:244
  40.0 0.0 collective-permute-done.1
  40.0 1.2 %collective-permute-start.5 = (f32[4,128,256]{2,1,0:T(8,128)S(1)}, f32[4,128,256]{2,1,0:T(8,128)S(1)}, u32[]{:S(2)}, u32[]{:S(2)}) collective-permute-start(f32[4,128,256]{2,1,0:T(8,128)S(1)} %pad_maximum_fusion.refs_0_.refs_3_), channel_id=1, source_target_pairs={{0,2},{1,3},{2,0},{3,1},{4,6},{5,7},{6,4},{7,5},{8,10},{9,11},{10,... | collective-permute-start | bytes 1572872 | tf_op jit(solution)/shard_map/ppermute | solution.py:244
  41.3 1.4 %collective-permute-start.8 = (f32[2,64,256]{2,1,0:T(8,128)S(1)}, f32[2,64,256]{2,1,0:T(8,128)S(1)}, u32[]{:S(2)}, u32[]{:S(2)}) collective-permute-start(f32[2,64,256]{2,1,0:T(8,128)S(1)} %pad_maximum_fusion.4), channel_id=1, source_target_pairs={{0,12},{1,13},{2,14},{3,15},{4,8},{5,9},{6,10},{7,11},{8,4},{9,5},... | collective-permute-start | bytes 393224 | tf_op jit(solution)/shard_map/ppermute | solution.py:244
  42.7 0.0 collective-permute-start.7
  42.7 3.0 %collective-permute-start.6 = (f32[2,64,256]{2,1,0:T(8,128)S(1)}, f32[2,64,256]{2,1,0:T(8,128)S(1)}, u32[]{:S(2)}, u32[]{:S(2)}) collective-permute-start(f32[2,64,256]{2,1,0:T(8,128)S(1)} %pad_maximum_fusion.4), channel_id=1, source_target_pairs={{0,4},{1,5},{2,6},{3,7},{4,0},{5,1},{6,2},{7,3},{8,12},{9,13},{10,... | collective-permute-start | bytes 393224 | tf_op jit(solution)/shard_map/ppermute | solution.py:244
  45.6 0.0 collective-permute-start.4
  45.6 0.0 copy-done.1
  45.6 1.0 %shard_map.67 = (bf16[4,512,1024]{2,1,0:T(8,128)(2,1)S(1)}, bf16[4,512,1024]{2,1,0:T(8,128)(2,1)S(1)}) custom-call(f32[2,256,4096]{2,1,0:T(8,128)S(1)} %copy-done.1), custom_call_target="tpu_custom_call" | custom-call | flops 6291456 | bytes 16777216 | tf_op jit(solution)/shard_map/pallas_call | solution.py:140
  46.6 2.9 %collective-permute-done.8 = f32[2,64,256]{2,1,0:T(8,128)S(1)} collective-permute-done((f32[2,64,256]{2,1,0:T(8,128)S(1)}, f32[2,64,256]{2,1,0:T(8,128)S(1)}, u32[]{:S(2)}, u32[]{:S(2)}) %collective-permute-start.8) | collective-permute-done | bytes 131104 | tf_op jit(solution)/shard_map/ppermute | solution.py:244
  49.5 3.1 %collective-permute-done.7 = f32[2,64,256]{2,1,0:T(8,128)S(1)} collective-permute-done((f32[2,64,256]{2,1,0:T(8,128)S(1)}, f32[2,64,256]{2,1,0:T(8,128)S(1)}, u32[]{:S(2)}, u32[]{:S(2)}) %collective-permute-start.7) | collective-permute-done | bytes 131104 | tf_op jit(solution)/shard_map/ppermute | solution.py:244
  52.7 0.0 collective-permute-done.6
  52.7 0.4 collective-permute-done.5.refs_1_.refs_4_
  53.1 0.0 collective-permute-start.9
  53.1 0.5 collective-permute-start.10
  53.6 1.7 %shard_map.68.refs_5_ = f32[192,512]{1,0:T(8,128)S(1)} custom-call(f32[4,128,256]{2,1,0:T(8,128)S(1)} %pad_maximum_fusion.refs_0_.refs_3_, f32[4,128,256]{2,1,0:T(8,128)S(1)} %collective-permute-done.5.refs_1_.refs_4_, f32[4,2,64,256]{3,2,1,0:T(8,128)S(1)} %pad_maximum_fusion.1.refs_2_.refs_5_, bf16[4,512,1024]{2,1,0:T(8,128)(2,1)S(1)} %get-tuple-element.44.refs_3_, ...), custom_call_target="tpu_custom_call" | custom-call | flops 1207959552 | bytes 1048576 | tf_op jit(solution)/shard_map/pallas_call | solution.py:220
  55.3 0.0 collective-permute-done.4.refs_0_.refs_3_
  55.3 0.0 collective-permute-done.9.refs_1_.refs_4_
  55.3 0.5 collective-permute-done.10.refs_2_.refs_5_
  55.8 1.6 %shard_map.69 = (f32[128,256]{1,0:T(8,128)S(1)}, f32[64,256]{1,0:T(8,128)S(1)}) custom-call(f32[4,128,256]{2,1,0:T(8,128)S(1)} %collective-permute-done.4.refs_0_.refs_3_, f32[4,128,256]{2,1,0:T(8,128)S(1)} %collective-permute-done.9.refs_1_.refs_4_, f32[4,2,64,256]{3,2,1,0:T(8,128)S(1)} %collective-permute-done.10.refs_2_.refs_5_, ...), custom_call_target="tpu_custom_call" | custom-call | flops 1207959552 | bytes 1048576 | tf_op jit(solution)/shard_map/pallas_call | solution.py:220
  57.4 1.5 %collective-permute-start.13 = (f32[128,256]{1,0:T(8,128)S(1)}, f32[128,256]{1,0:T(8,128)S(1)}, u32[]{:S(2)}, u32[]{:S(2)}) collective-permute-start(f32[128,256]{1,0:T(8,128)S(1)} %get-tuple-element.47), channel_id=1, source_target_pairs={{0,28},{1,29},{2,30},{3,31},{4,16},{5,17},{6,18},{7,19},{8,20},{9,... | collective-permute-start | bytes 393224 | tf_op jit(solution)/shard_map/ppermute | solution.py:246
  58.9 2.4 %collective-permute-start.12 = (f32[64,256]{1,0:T(8,128)S(1)}, f32[64,256]{1,0:T(8,128)S(1)}, u32[]{:S(2)}, u32[]{:S(2)}) collective-permute-start(f32[64,256]{1,0:T(8,128)S(1)} %get-tuple-element.46), channel_id=1, source_target_pairs={{0,18},{1,19},{2,16},{3,17},{4,22},{5,23},{6,20},{7,21},{8,26},{9,... | collective-permute-start | bytes 196616 | tf_op jit(solution)/shard_map/ppermute | solution.py:246
  61.3 0.0 collective-permute-start.11
  61.3 0.6 collective-permute-start.16
  61.9 1.5 %collective-permute-start.15 = (f32[128,256]{1,0:T(8,128)S(1)}, f32[128,256]{1,0:T(8,128)S(1)}, u32[]{:S(2)}, u32[]{:S(2)}) collective-permute-start(f32[128,256]{1,0:T(8,128)S(1)} %get-tuple-element.47), channel_id=1, source_target_pairs={{0,20},{1,21},{2,22},{3,23},{4,24},{5,25},{6,26},{7,27},{8,28},{9,... | collective-permute-start | bytes 393224 | tf_op jit(solution)/shard_map/ppermute | solution.py:246
  63.4 2.9 %collective-permute-done.12 = f32[64,256]{1,0:T(8,128)S(1)} collective-permute-done((f32[64,256]{1,0:T(8,128)S(1)}, f32[64,256]{1,0:T(8,128)S(1)}, u32[]{:S(2)}, u32[]{:S(2)}) %collective-permute-start.12) | collective-permute-done | bytes 65568 | tf_op jit(solution)/shard_map/ppermute | solution.py:246
  66.3 0.5 collective-permute-start.14
  66.8 0.0 collective-permute-done.11
  66.8 0.0 collective-permute-done.13
  66.8 7.0 %collective-permute-done.16 = f32[128,256]{1,0:T(8,128)S(1)} collective-permute-done((f32[128,256]{1,0:T(8,128)S(1)}, f32[128,256]{1,0:T(8,128)S(1)}, u32[]{:S(2)}, u32[]{:S(2)}) %collective-permute-start.16) | collective-permute-done | bytes 131104 | tf_op jit(solution)/shard_map/ppermute | solution.py:246
  73.8 0.0 collective-permute-done.15
  73.8 2.3 %collective-permute-done.14 = f32[128,256]{1,0:T(8,128)S(1)} collective-permute-done((f32[128,256]{1,0:T(8,128)S(1)}, f32[128,256]{1,0:T(8,128)S(1)}, u32[]{:S(2)}, u32[]{:S(2)}) %collective-permute-start.14) | collective-permute-done | bytes 131104 | tf_op jit(solution)/shard_map/ppermute | solution.py:246
  76.1 0.7 collective-permute-start.18
  76.8 2.1 %collective-permute-start.22 = (f32[2,64,256]{2,1,0:T(8,128)S(1)}, f32[2,64,256]{2,1,0:T(8,128)S(1)}, u32[]{:S(2)}, u32[]{:S(2)}) collective-permute-start(f32[2,64,256]{2,1,0:T(8,128)S(1)} %pad_maximum_fusion.5), channel_id=1, source_target_pairs={{0,12},{1,13},{2,14},{3,15},{4,8},{5,9},{6,10},{7,11},{8,4},{9,5},... | collective-permute-start | bytes 393224 | tf_op jit(solution)/shard_map/ppermute | solution.py:244
  78.9 0.0 collective-permute-start.21
  78.9 2.3 %collective-permute-start.20 = (f32[2,64,256]{2,1,0:T(8,128)S(1)}, f32[2,64,256]{2,1,0:T(8,128)S(1)}, u32[]{:S(2)}, u32[]{:S(2)}) collective-permute-start(f32[2,64,256]{2,1,0:T(8,128)S(1)} %pad_maximum_fusion.5), channel_id=1, source_target_pairs={{0,4},{1,5},{2,6},{3,7},{4,0},{5,1},{6,2},{7,3},{8,12},{9,13},{10,... | collective-permute-start | bytes 393224 | tf_op jit(solution)/shard_map/ppermute | solution.py:244
  81.2 0.0 collective-permute-start.17
  81.2 3.8 %collective-permute-done.22 = f32[2,64,256]{2,1,0:T(8,128)S(1)} collective-permute-done((f32[2,64,256]{2,1,0:T(8,128)S(1)}, f32[2,64,256]{2,1,0:T(8,128)S(1)}, u32[]{:S(2)}, u32[]{:S(2)}) %collective-permute-start.22) | collective-permute-done | bytes 131104 | tf_op jit(solution)/shard_map/ppermute | solution.py:244
  85.0 3.8 %collective-permute-done.21 = f32[2,64,256]{2,1,0:T(8,128)S(1)} collective-permute-done((f32[2,64,256]{2,1,0:T(8,128)S(1)}, f32[2,64,256]{2,1,0:T(8,128)S(1)}, u32[]{:S(2)}, u32[]{:S(2)}) %collective-permute-start.21) | collective-permute-done | bytes 131104 | tf_op jit(solution)/shard_map/ppermute | solution.py:244
  88.9 0.0 collective-permute-done.20
  88.9 0.1 collective-permute-start.23
  89.0 0.7 collective-permute-done.18.refs_1_
  89.7 0.0 collective-permute-start.19
  89.7 1.7 %shard_map.70.refs_8_ = f32[192,512]{1,0:T(8,128)S(1)} custom-call(f32[4,128,256]{2,1,0:T(8,128)S(1)} %pad_maximum_fusion.2.refs_0_, f32[4,128,256]{2,1,0:T(8,128)S(1)} %collective-permute-done.18.refs_1_, f32[4,2,64,256]{3,2,1,0:T(8,128)S(1)} %pad_maximum_fusion.3.refs_2_, f32[4,128,256]{2,1,0:T(8,128)S(1)} %pad_maximum_fusion.refs_0_.refs_3_, ...), custom_call_target="tpu_custom_call" | custom-call | flops 1207959552 | bytes 1048576 | tf_op jit(solution)/shard_map/pallas_call | solution.py:220
  91.3 0.0 collective-permute-done.17.refs_0_
  91.3 0.0 collective-permute-done.23.refs_2_
  91.4 0.3 collective-permute-done.19.refs_1_
  91.6 2.3 %shard_map.71 = f32[192,256]{1,0:T(8,128)} custom-call(f32[4,128,256]{2,1,0:T(8,128)S(1)} %collective-permute-done.17.refs_0_, f32[4,128,256]{2,1,0:T(8,128)S(1)} %collective-permute-done.19.refs_1_, f32[4,2,64,256]{3,2,1,0:T(8,128)S(1)} %collective-permute-done.23.refs_2_, f32[4,128,256]{2,1,0:T(8,128)S(1)} %collective-permute-done.4.refs_0_.refs_3_, ...), custom_call_target="tpu_custom_call" | custom-call | flops 1207959552 | bytes 1048576 | tf_op jit(solution)/shard_map/pallas_call | solution.py:220
  (6 shorter events, 0.2 us)
Async XLA Ops:
  24.5 9.2 %collective-permute-start = (f32[64,256]{1,0:T(8,128)S(1)}, f32[64,256]{1,0:T(8,128)S(1)}, u32[]{:S(2)}, u32[]{:S(2)}) collective-permute-start(f32[64,256]{1,0:T(8,128)S(1)} %get-tuple-element.32), channel_id=1, source_target_pairs={{0,2},{1,3},{2,0},{3,1},{4,6},{5,7},{6,4},{7,5},{8,10},{9,11},{10,... | collective-permute-start | bytes 196616 | tf_op jit(solution)/shard_map/ppermute | solution.py:244
  24.9 8.8 %collective-permute-start.3 = (f32[128,256]{1,0:T(8,128)S(1)}, f32[128,256]{1,0:T(8,128)S(1)}, u32[]{:S(2)}, u32[]{:S(2)}) collective-permute-start(f32[128,256]{1,0:T(8,128)S(1)} %get-tuple-element.33), channel_id=1, source_target_pairs={{0,12},{1,13},{2,14},{3,15},{4,8},{5,9},{6,10},{7,11},{8,4},{9,5},... | collective-permute-start | bytes 393224 | tf_op jit(solution)/shard_map/ppermute | solution.py:244
  27.6 12.4 %collective-permute-start.2 = (f32[128,256]{1,0:T(8,128)S(1)}, f32[128,256]{1,0:T(8,128)S(1)}, u32[]{:S(2)}, u32[]{:S(2)}) collective-permute-start(f32[128,256]{1,0:T(8,128)S(1)} %get-tuple-element.33), channel_id=1, source_target_pairs={{0,8},{1,9},{2,10},{3,11},{4,12},{5,13},{6,14},{7,15},{8,0},{9,1},... | collective-permute-start | bytes 393224 | tf_op jit(solution)/shard_map/ppermute | solution.py:244
  28.2 11.8 %collective-permute-start.1 = (f32[128,256]{1,0:T(8,128)S(1)}, f32[128,256]{1,0:T(8,128)S(1)}, u32[]{:S(2)}, u32[]{:S(2)}) collective-permute-start(f32[128,256]{1,0:T(8,128)S(1)} %get-tuple-element.33), channel_id=1, source_target_pairs={{0,4},{1,5},{2,6},{3,7},{4,0},{5,1},{6,2},{7,3},{8,12},{9,13},{10,... | collective-permute-start | bytes 393224 | tf_op jit(solution)/shard_map/ppermute | solution.py:244
  29.3 3.4 %copy-start = (f32[2,256,4096]{2,1,0:T(8,128)S(1)}, f32[2,256,4096]{2,1,0:T(8,128)}, u32[]{:S(2)}) copy-start(f32[2,256,4096]{2,1,0:T(8,128)} %matrix_ref) | copy-start | bytes 25165828
  32.7 13.0 %copy-start.1 = (f32[2,256,4096]{2,1,0:T(8,128)S(1)}, f32[2,256,4096]{2,1,0:T(8,128)}, u32[]{:S(2)}) copy-start(f32[2,256,4096]{2,1,0:T(8,128)} %matrix_ref.1) | copy-start | bytes 25165828
  40.0 13.1 %collective-permute-start.5 = (f32[4,128,256]{2,1,0:T(8,128)S(1)}, f32[4,128,256]{2,1,0:T(8,128)S(1)}, u32[]{:S(2)}, u32[]{:S(2)}) collective-permute-start(f32[4,128,256]{2,1,0:T(8,128)S(1)} %pad_maximum_fusion.refs_0_.refs_3_), channel_id=1, source_target_pairs={{0,2},{1,3},{2,0},{3,1},{4,6},{5,7},{6,4},{7,5},{8,10},{9,11},{10,... | collective-permute-start | bytes 1572872 | tf_op jit(solution)/shard_map/ppermute | solution.py:244
  41.3 8.3 %collective-permute-start.8 = (f32[2,64,256]{2,1,0:T(8,128)S(1)}, f32[2,64,256]{2,1,0:T(8,128)S(1)}, u32[]{:S(2)}, u32[]{:S(2)}) collective-permute-start(f32[2,64,256]{2,1,0:T(8,128)S(1)} %pad_maximum_fusion.4), channel_id=1, source_target_pairs={{0,12},{1,13},{2,14},{3,15},{4,8},{5,9},{6,10},{7,11},{8,4},{9,5},... | collective-permute-start | bytes 393224 | tf_op jit(solution)/shard_map/ppermute | solution.py:244
  42.7 10.0 %collective-permute-start.7 = (f32[2,64,256]{2,1,0:T(8,128)S(1)}, f32[2,64,256]{2,1,0:T(8,128)S(1)}, u32[]{:S(2)}, u32[]{:S(2)}) collective-permute-start(f32[2,64,256]{2,1,0:T(8,128)S(1)} %pad_maximum_fusion.4), channel_id=1, source_target_pairs={{0,8},{1,9},{2,10},{3,11},{4,12},{5,13},{6,14},{7,15},{8,0},{9,1},... | collective-permute-start | bytes 393224 | tf_op jit(solution)/shard_map/ppermute | solution.py:244
  42.7 10.0 %collective-permute-start.6 = (f32[2,64,256]{2,1,0:T(8,128)S(1)}, f32[2,64,256]{2,1,0:T(8,128)S(1)}, u32[]{:S(2)}, u32[]{:S(2)}) collective-permute-start(f32[2,64,256]{2,1,0:T(8,128)S(1)} %pad_maximum_fusion.4), channel_id=1, source_target_pairs={{0,4},{1,5},{2,6},{3,7},{4,0},{5,1},{6,2},{7,3},{8,12},{9,13},{10,... | collective-permute-start | bytes 393224 | tf_op jit(solution)/shard_map/ppermute | solution.py:244
  45.6 9.6 %collective-permute-start.4 = (f32[4,128,256]{2,1,0:T(8,128)S(1)}, f32[4,128,256]{2,1,0:T(8,128)S(1)}, u32[]{:S(2)}, u32[]{:S(2)}) collective-permute-start(f32[4,128,256]{2,1,0:T(8,128)S(1)} %pad_maximum_fusion.refs_0_.refs_3_), channel_id=1, source_target_pairs={{0,1},{1,0},{2,3},{3,2},{4,5},{5,4},{6,7},{7,6},{8,9},{9,8},{10,11... | collective-permute-start | bytes 1572872 | tf_op jit(solution)/shard_map/ppermute | solution.py:244
  53.1 2.2 %collective-permute-start.9 = (f32[4,128,256]{2,1,0:T(8,128)S(1)}, f32[4,128,256]{2,1,0:T(8,128)S(1)}, u32[]{:S(2)}, u32[]{:S(2)}) collective-permute-start(f32[4,128,256]{2,1,0:T(8,128)S(1)} %collective-permute-done.5.refs_1_.refs_4_), channel_id=1, source_target_pairs={{0,1},{1,0},{2,3},{3,2},{4,5},{5,4},{6,7},{7,6},{8,9},{9,8},{10,11... | collective-permute-start | bytes 1572872 | tf_op jit(solution)/shard_map/ppermute | solution.py:244
  53.1 2.7 %collective-permute-start.10 = (f32[4,2,64,256]{3,2,1,0:T(8,128)S(1)}, f32[4,2,64,256]{3,2,1,0:T(8,128)S(1)}, u32[]{:S(2)}, u32[]{:S(2)}) collective-permute-start(f32[4,2,64,256]{3,2,1,0:T(8,128)S(1)} %pad_maximum_fusion.1.refs_2_.refs_5_), channel_id=1, source_target_pairs={{0,1},{1,0},{2,3},{3,2},{4,5},{5,4},{6,7},{7,6},{8,9},{9,8},{10,11... | collective-permute-start | bytes 1572872 | tf_op jit(solution)/shard_map/ppermute | solution.py:244
  57.4 9.5 %collective-permute-start.13 = (f32[128,256]{1,0:T(8,128)S(1)}, f32[128,256]{1,0:T(8,128)S(1)}, u32[]{:S(2)}, u32[]{:S(2)}) collective-permute-start(f32[128,256]{1,0:T(8,128)S(1)} %get-tuple-element.47), channel_id=1, source_target_pairs={{0,28},{1,29},{2,30},{3,31},{4,16},{5,17},{6,18},{7,19},{8,20},{9,... | collective-permute-start | bytes 393224 | tf_op jit(solution)/shard_map/ppermute | solution.py:246
  58.9 7.5 %collective-permute-start.12 = (f32[64,256]{1,0:T(8,128)S(1)}, f32[64,256]{1,0:T(8,128)S(1)}, u32[]{:S(2)}, u32[]{:S(2)}) collective-permute-start(f32[64,256]{1,0:T(8,128)S(1)} %get-tuple-element.46), channel_id=1, source_target_pairs={{0,18},{1,19},{2,16},{3,17},{4,22},{5,23},{6,20},{7,21},{8,26},{9,... | collective-permute-start | bytes 196616 | tf_op jit(solution)/shard_map/ppermute | solution.py:246
  61.3 5.5 %collective-permute-start.11 = (f32[64,256]{1,0:T(8,128)S(1)}, f32[64,256]{1,0:T(8,128)S(1)}, u32[]{:S(2)}, u32[]{:S(2)}) collective-permute-start(f32[64,256]{1,0:T(8,128)S(1)} %get-tuple-element.46), channel_id=1, source_target_pairs={{0,16},{1,17},{2,18},{3,19},{4,20},{5,21},{6,22},{7,23},{8,24},{9,... | collective-permute-start | bytes 196616 | tf_op jit(solution)/shard_map/ppermute | solution.py:246
  61.3 12.5 %collective-permute-start.16 = (f32[128,256]{1,0:T(8,128)S(1)}, f32[128,256]{1,0:T(8,128)S(1)}, u32[]{:S(2)}, u32[]{:S(2)}) collective-permute-start(f32[128,256]{1,0:T(8,128)S(1)} %get-tuple-element.47), channel_id=1, source_target_pairs={{0,24},{1,25},{2,26},{3,27},{4,28},{5,29},{6,30},{7,31},{8,16},{9,... | collective-permute-start | bytes 393224 | tf_op jit(solution)/shard_map/ppermute | solution.py:246
  61.9 11.9 %collective-permute-start.15 = (f32[128,256]{1,0:T(8,128)S(1)}, f32[128,256]{1,0:T(8,128)S(1)}, u32[]{:S(2)}, u32[]{:S(2)}) collective-permute-start(f32[128,256]{1,0:T(8,128)S(1)} %get-tuple-element.47), channel_id=1, source_target_pairs={{0,20},{1,21},{2,22},{3,23},{4,24},{5,25},{6,26},{7,27},{8,28},{9,... | collective-permute-start | bytes 393224 | tf_op jit(solution)/shard_map/ppermute | solution.py:246
  66.3 9.8 %collective-permute-start.14 = (f32[128,256]{1,0:T(8,128)S(1)}, f32[128,256]{1,0:T(8,128)S(1)}, u32[]{:S(2)}, u32[]{:S(2)}) collective-permute-start(f32[128,256]{1,0:T(8,128)S(1)} %get-tuple-element.47), channel_id=1, source_target_pairs={{0,16},{1,17},{2,18},{3,19},{4,20},{5,21},{6,22},{7,23},{8,24},{9,... | collective-permute-start | bytes 393224 | tf_op jit(solution)/shard_map/ppermute | solution.py:246
  76.1 13.5 %collective-permute-start.18 = (f32[4,128,256]{2,1,0:T(8,128)S(1)}, f32[4,128,256]{2,1,0:T(8,128)S(1)}, u32[]{:S(2)}, u32[]{:S(2)}) collective-permute-start(f32[4,128,256]{2,1,0:T(8,128)S(1)} %pad_maximum_fusion.2.refs_0_), channel_id=1, source_target_pairs={{0,2},{1,3},{2,0},{3,1},{4,6},{5,7},{6,4},{7,5},{8,10},{9,11},{10,... | collective-permute-start | bytes 1572872 | tf_op jit(solution)/shard_map/ppermute | solution.py:244
  76.8 8.2 %collective-permute-start.22 = (f32[2,64,256]{2,1,0:T(8,128)S(1)}, f32[2,64,256]{2,1,0:T(8,128)S(1)}, u32[]{:S(2)}, u32[]{:S(2)}) collective-permute-start(f32[2,64,256]{2,1,0:T(8,128)S(1)} %pad_maximum_fusion.5), channel_id=1, source_target_pairs={{0,12},{1,13},{2,14},{3,15},{4,8},{5,9},{6,10},{7,11},{8,4},{9,5},... | collective-permute-start | bytes 393224 | tf_op jit(solution)/shard_map/ppermute | solution.py:244
  78.9 10.0 %collective-permute-start.21 = (f32[2,64,256]{2,1,0:T(8,128)S(1)}, f32[2,64,256]{2,1,0:T(8,128)S(1)}, u32[]{:S(2)}, u32[]{:S(2)}) collective-permute-start(f32[2,64,256]{2,1,0:T(8,128)S(1)} %pad_maximum_fusion.5), channel_id=1, source_target_pairs={{0,8},{1,9},{2,10},{3,11},{4,12},{5,13},{6,14},{7,15},{8,0},{9,1},... | collective-permute-start | bytes 393224 | tf_op jit(solution)/shard_map/ppermute | solution.py:244
  78.9 10.0 %collective-permute-start.20 = (f32[2,64,256]{2,1,0:T(8,128)S(1)}, f32[2,64,256]{2,1,0:T(8,128)S(1)}, u32[]{:S(2)}, u32[]{:S(2)}) collective-permute-start(f32[2,64,256]{2,1,0:T(8,128)S(1)} %pad_maximum_fusion.5), channel_id=1, source_target_pairs={{0,4},{1,5},{2,6},{3,7},{4,0},{5,1},{6,2},{7,3},{8,12},{9,13},{10,... | collective-permute-start | bytes 393224 | tf_op jit(solution)/shard_map/ppermute | solution.py:244
  81.2 10.1 %collective-permute-start.17 = (f32[4,128,256]{2,1,0:T(8,128)S(1)}, f32[4,128,256]{2,1,0:T(8,128)S(1)}, u32[]{:S(2)}, u32[]{:S(2)}) collective-permute-start(f32[4,128,256]{2,1,0:T(8,128)S(1)} %pad_maximum_fusion.2.refs_0_), channel_id=1, source_target_pairs={{0,1},{1,0},{2,3},{3,2},{4,5},{5,4},{6,7},{7,6},{8,9},{9,8},{10,11... | collective-permute-start | bytes 1572872 | tf_op jit(solution)/shard_map/ppermute | solution.py:244
  88.9 2.4 %collective-permute-start.23 = (f32[4,2,64,256]{3,2,1,0:T(8,128)S(1)}, f32[4,2,64,256]{3,2,1,0:T(8,128)S(1)}, u32[]{:S(2)}, u32[]{:S(2)}) collective-permute-start(f32[4,2,64,256]{3,2,1,0:T(8,128)S(1)} %pad_maximum_fusion.3.refs_2_), channel_id=1, source_target_pairs={{0,1},{1,0},{2,3},{3,2},{4,5},{5,4},{6,7},{7,6},{8,9},{9,8},{10,11... | collective-permute-start | bytes 1572872 | tf_op jit(solution)/shard_map/ppermute | solution.py:244
  89.7 2.0 %collective-permute-start.19 = (f32[4,128,256]{2,1,0:T(8,128)S(1)}, f32[4,128,256]{2,1,0:T(8,128)S(1)}, u32[]{:S(2)}, u32[]{:S(2)}) collective-permute-start(f32[4,128,256]{2,1,0:T(8,128)S(1)} %collective-permute-done.18.refs_1_), channel_id=1, source_target_pairs={{0,1},{1,0},{2,3},{3,2},{4,5},{5,4},{6,7},{7,6},{8,9},{9,8},{10,11... | collective-permute-start | bytes 1572872 | tf_op jit(solution)/shard_map/ppermute | solution.py:244

commit v19 on v18

--- a/solution.py
+++ b/solution.py
@@ -42,8 +42,6 @@
     earlier = lax.broadcasted_iota(jnp.int32, (entries, entries), 0) < lax.broadcasted_iota(jnp.int32, (entries, entries), 1)
     for move in moves:
         move.wait()
-    fetch.wait()
-    keep.start()
     live = jnp.zeros((1, entries), jnp.bool_)
     for tile in range(entries // tile_rows):
         start = tile * tile_rows
@@ -60,6 +58,8 @@
     if not folded:
         tail = jnp.where(lax.broadcasted_iota(jnp.int32, (width - columns, entries), 0) == 0, local_row, 0.0)
         data = jnp.concatenate([data, tail], axis=0)
+    fetch.wait()
+    keep.start()
     packed = jnp.zeros((slots, data.shape[0]), f32)
     for piece in halves_of(data):
         packed += lax.dot_general(choose, piece, lanes_contract, preferred_element_type=f32)

time: 94.2 us -> 94.3 us (level)
  no operation moved by 1% of the time
where the time goes in v19:
time: 94.3 us; the launch traced here: 94 us
  waiting for transfers between devices  34 us (36%)
  starting transfers between devices  22.6 us (24%)
  blocking collectives  20.6 us (22%)
  Pallas kernels  13.1 us (14%)
  local copies, waits for them, and re-layouts  3.38 us (4%)
    ppermute x18, waiting for transfers between devices, send(): lax.ppermute(value, 'tile', [(t, target(t)) for t in range(tile_size)])  21.8 us
    all_to_all x1, blocking collectives, body(): received = lax.all_to_all(packed, 'tile', 0, 0, tiled=False)  20.6 us
    ppermute x18, starting transfers between devices, send(): lax.ppermute(value, 'tile', [(t, target(t)) for t in range(tile_size)])  16.1 us
    ppermute x6, waiting for transfers between devices, send(): return lax.ppermute(value, ('chain', 'tile'), pairs)  12.2 us
    pallas_call x4, Pallas kernels, product_part(): pl.pallas_call(functools.partial(product_kernel, sources, layout, len(blo...  7.2 us
    ppermute x6, starting transfers between devices, send(): return lax.ppermute(value, ('chain', 'tile'), pairs)  6.51 us
    unnamed x4, local copies, waits for them, and re-layouts  3.38 us
    pallas_call x1, Pallas kernels, body(): pl.pallas_call(functools.partial(pack_kernel, own_rows, cap, tile_rows),...  2.84 us
  transfers between devices with their start and end apart: 24, of which 12 were waited for; matrix products, arithmetic and copies ran while one was open for 0% of the time, Pallas kernels for 6%

profile of v19, /device:TPU:0, one launch (start us, length us, event | category | flops | bytes accessed | tf_op | source)
XLA Modules:
  0.0 94.0 jit_solution(5111663463564293202)
XLA Ops:
  0.0 2.8 %shard_map.64 = (f32[16,56,128]{2,1,0:T(8,128)}, f32[24,192,256]{2,1,0:T(8,128)}) custom-call(s32[2]{0:T(128)} %counts_hbm.1, s32[1,256]{1,0:T(1,128)} %bitcast.46, f32[192,256]{1,0:T(8,128)} %bitcast.28, f32[192,256]{1,0:T(8,128)} %bitcast.29), custom_call_target="tpu_custom_call" | custom-call | tf_op jit(solution)/shard_map/pallas_call | solution.py:326
  2.9 20.6 %all_to_all.5.received_ref = f32[16,56,128]{2,1,0:T(8,128)S(1)} all-to-all(f32[16,56,128]{2,1,0:T(8,128)} %get-tuple-element.30), channel_id=1, replica_groups=mesh['chain'=2,'tile'=16] {'tile'}, dimensions={0} | all-to-all | bytes 917504 | tf_op jit(solution)/shard_map/all_to_all | solution.py:343
  23.5 1.1 %shard_map.65 = (f32[128,256]{1,0:T(8,128)S(1)}, f32[64,256]{1,0:T(8,128)S(1)}) custom-call(f32[16,56,128]{2,1,0:T(8,128)S(1)} %all_to_all.5.received_ref, f32[24,192,256]{2,1,0:T(8,128)} %get-tuple-element.31.right_hbm), custom_call_target="tpu_custom_call" | custom-call | tf_op jit(solution)/shard_map/pallas_call | solution.py:347
  24.6 0.4 collective-permute-start
  25.0 2.7 %collective-permute-start.3 = (f32[128,256]{1,0:T(8,128)S(1)}, f32[128,256]{1,0:T(8,128)S(1)}, u32[]{:S(2)}, u32[]{:S(2)}) collective-permute-start(f32[128,256]{1,0:T(8,128)S(1)} %get-tuple-element.33), channel_id=1, source_target_pairs={{0,12},{1,13},{2,14},{3,15},{4,8},{5,9},{6,10},{7,11},{8,4},{9,5},... | collective-permute-start | bytes 393224 | tf_op jit(solution)/shard_map/ppermute | solution.py:244
  27.7 0.5 collective-permute-start.2
  28.3 1.1 %collective-permute-start.1 = (f32[128,256]{1,0:T(8,128)S(1)}, f32[128,256]{1,0:T(8,128)S(1)}, u32[]{:S(2)}, u32[]{:S(2)}) collective-permute-start(f32[128,256]{1,0:T(8,128)S(1)} %get-tuple-element.33), channel_id=1, source_target_pairs={{0,4},{1,5},{2,6},{3,7},{4,0},{5,1},{6,2},{7,3},{8,12},{9,13},{10,... | collective-permute-start | bytes 393224 | tf_op jit(solution)/shard_map/ppermute | solution.py:244
  29.4 0.0 copy-start
  29.4 3.4 %copy-done = f32[2,256,4096]{2,1,0:T(8,128)S(1)} copy-done((f32[2,256,4096]{2,1,0:T(8,128)S(1)}, f32[2,256,4096]{2,1,0:T(8,128)}, u32[]{:S(2)}) %copy-start) | copy-done | bytes 8388632
  32.8 0.0 copy-start.1
  32.8 1.0 %shard_map.66 = (bf16[4,512,1024]{2,1,0:T(8,128)(2,1)S(1)}, bf16[4,512,1024]{2,1,0:T(8,128)(2,1)S(1)}) custom-call(f32[2,256,4096]{2,1,0:T(8,128)S(1)} %copy-done), custom_call_target="tpu_custom_call" | custom-call | flops 6291456 | bytes 16777216 | tf_op jit(solution)/shard_map/pallas_call | solution.py:140
  33.8 0.0 collective-permute-done
  33.8 0.0 collective-permute-done.3
  33.8 6.3 %collective-permute-done.2 = f32[128,256]{1,0:T(8,128)S(1)} collective-permute-done((f32[128,256]{1,0:T(8,128)S(1)}, f32[128,256]{1,0:T(8,128)S(1)}, u32[]{:S(2)}, u32[]{:S(2)}) %collective-permute-start.2) | collective-permute-done | bytes 131104 | tf_op jit(solution)/shard_map/ppermute | solution.py:244
  40.1 0.0 collective-permute-done.1
  40.2 1.2 %collective-permute-start.5 = (f32[4,128,256]{2,1,0:T(8,128)S(1)}, f32[4,128,256]{2,1,0:T(8,128)S(1)}, u32[]{:S(2)}, u32[]{:S(2)}) collective-permute-start(f32[4,128,256]{2,1,0:T(8,128)S(1)} %pad_maximum_fusion.refs_0_.refs_3_), channel_id=1, source_target_pairs={{0,2},{1,3},{2,0},{3,1},{4,6},{5,7},{6,4},{7,5},{8,10},{9,11},{10,... | collective-permute-start | bytes 1572872 | tf_op jit(solution)/shard_map/ppermute | solution.py:244
  41.4 1.4 %collective-permute-start.8 = (f32[2,64,256]{2,1,0:T(8,128)S(1)}, f32[2,64,256]{2,1,0:T(8,128)S(1)}, u32[]{:S(2)}, u32[]{:S(2)}) collective-permute-start(f32[2,64,256]{2,1,0:T(8,128)S(1)} %pad_maximum_fusion.4), channel_id=1, source_target_pairs={{0,12},{1,13},{2,14},{3,15},{4,8},{5,9},{6,10},{7,11},{8,4},{9,5},... | collective-permute-start | bytes 393224 | tf_op jit(solution)/shard_map/ppermute | solution.py:244
  42.8 0.0 collective-permute-start.7
  42.8 3.0 %collective-permute-start.6 = (f32[2,64,256]{2,1,0:T(8,128)S(1)}, f32[2,64,256]{2,1,0:T(8,128)S(1)}, u32[]{:S(2)}, u32[]{:S(2)}) collective-permute-start(f32[2,64,256]{2,1,0:T(8,128)S(1)} %pad_maximum_fusion.4), channel_id=1, source_target_pairs={{0,4},{1,5},{2,6},{3,7},{4,0},{5,1},{6,2},{7,3},{8,12},{9,13},{10,... | collective-permute-start | bytes 393224 | tf_op jit(solution)/shard_map/ppermute | solution.py:244
  45.8 0.0 collective-permute-start.4
  45.8 0.0 copy-done.1
  45.8 1.0 %shard_map.67 = (bf16[4,512,1024]{2,1,0:T(8,128)(2,1)S(1)}, bf16[4,512,1024]{2,1,0:T(8,128)(2,1)S(1)}) custom-call(f32[2,256,4096]{2,1,0:T(8,128)S(1)} %copy-done.1), custom_call_target="tpu_custom_call" | custom-call | flops 6291456 | bytes 16777216 | tf_op jit(solution)/shard_map/pallas_call | solution.py:140
  46.8 2.9 %collective-permute-done.8 = f32[2,64,256]{2,1,0:T(8,128)S(1)} collective-permute-done((f32[2,64,256]{2,1,0:T(8,128)S(1)}, f32[2,64,256]{2,1,0:T(8,128)S(1)}, u32[]{:S(2)}, u32[]{:S(2)}) %collective-permute-start.8) | collective-permute-done | bytes 131104 | tf_op jit(solution)/shard_map/ppermute | solution.py:244
  49.7 3.2 %collective-permute-done.7 = f32[2,64,256]{2,1,0:T(8,128)S(1)} collective-permute-done((f32[2,64,256]{2,1,0:T(8,128)S(1)}, f32[2,64,256]{2,1,0:T(8,128)S(1)}, u32[]{:S(2)}, u32[]{:S(2)}) %collective-permute-start.7) | collective-permute-done | bytes 131104 | tf_op jit(solution)/shard_map/ppermute | solution.py:244
  52.8 0.0 collective-permute-done.6
  52.9 0.4 collective-permute-done.5.refs_1_.refs_4_
  53.2 0.0 collective-permute-start.9
  53.2 0.5 collective-permute-start.10
  53.7 1.7 %shard_map.68.refs_5_ = f32[192,512]{1,0:T(8,128)S(1)} custom-call(f32[4,128,256]{2,1,0:T(8,128)S(1)} %pad_maximum_fusion.refs_0_.refs_3_, f32[4,128,256]{2,1,0:T(8,128)S(1)} %collective-permute-done.5.refs_1_.refs_4_, f32[4,2,64,256]{3,2,1,0:T(8,128)S(1)} %pad_maximum_fusion.1.refs_2_.refs_5_, bf16[4,512,1024]{2,1,0:T(8,128)(2,1)S(1)} %get-tuple-element.44.refs_3_, ...), custom_call_target="tpu_custom_call" | custom-call | flops 1207959552 | bytes 1048576 | tf_op jit(solution)/shard_map/pallas_call | solution.py:220
  55.4 0.0 collective-permute-done.4.refs_0_.refs_3_
  55.4 0.0 collective-permute-done.9.refs_1_.refs_4_
  55.4 0.5 collective-permute-done.10.refs_2_.refs_5_
  55.9 1.6 %shard_map.69 = (f32[128,256]{1,0:T(8,128)S(1)}, f32[64,256]{1,0:T(8,128)S(1)}) custom-call(f32[4,128,256]{2,1,0:T(8,128)S(1)} %collective-permute-done.4.refs_0_.refs_3_, f32[4,128,256]{2,1,0:T(8,128)S(1)} %collective-permute-done.9.refs_1_.refs_4_, f32[4,2,64,256]{3,2,1,0:T(8,128)S(1)} %collective-permute-done.10.refs_2_.refs_5_, ...), custom_call_target="tpu_custom_call" | custom-call | flops 1207959552 | bytes 1048576 | tf_op jit(solution)/shard_map/pallas_call | solution.py:220
  57.5 1.5 %collective-permute-start.13 = (f32[128,256]{1,0:T(8,128)S(1)}, f32[128,256]{1,0:T(8,128)S(1)}, u32[]{:S(2)}, u32[]{:S(2)}) collective-permute-start(f32[128,256]{1,0:T(8,128)S(1)} %get-tuple-element.47), channel_id=1, source_target_pairs={{0,28},{1,29},{2,30},{3,31},{4,16},{5,17},{6,18},{7,19},{8,20},{9,... | collective-permute-start | bytes 393224 | tf_op jit(solution)/shard_map/ppermute | solution.py:246
  59.0 2.4 %collective-permute-start.12 = (f32[64,256]{1,0:T(8,128)S(1)}, f32[64,256]{1,0:T(8,128)S(1)}, u32[]{:S(2)}, u32[]{:S(2)}) collective-permute-start(f32[64,256]{1,0:T(8,128)S(1)} %get-tuple-element.46), channel_id=1, source_target_pairs={{0,18},{1,19},{2,16},{3,17},{4,22},{5,23},{6,20},{7,21},{8,26},{9,... | collective-permute-start | bytes 196616 | tf_op jit(solution)/shard_map/ppermute | solution.py:246
  61.4 0.0 collective-permute-start.11
  61.4 0.6 collective-permute-start.16
  62.0 1.5 %collective-permute-start.15 = (f32[128,256]{1,0:T(8,128)S(1)}, f32[128,256]{1,0:T(8,128)S(1)}, u32[]{:S(2)}, u32[]{:S(2)}) collective-permute-start(f32[128,256]{1,0:T(8,128)S(1)} %get-tuple-element.47), channel_id=1, source_target_pairs={{0,20},{1,21},{2,22},{3,23},{4,24},{5,25},{6,26},{7,27},{8,28},{9,... | collective-permute-start | bytes 393224 | tf_op jit(solution)/shard_map/ppermute | solution.py:246
  63.5 2.9 %collective-permute-done.12 = f32[64,256]{1,0:T(8,128)S(1)} collective-permute-done((f32[64,256]{1,0:T(8,128)S(1)}, f32[64,256]{1,0:T(8,128)S(1)}, u32[]{:S(2)}, u32[]{:S(2)}) %collective-permute-start.12) | collective-permute-done | bytes 65568 | tf_op jit(solution)/shard_map/ppermute | solution.py:246
  66.5 0.5 collective-permute-start.14
  66.9 0.0 collective-permute-done.11
  66.9 0.0 collective-permute-done.13
  67.0 6.9 %collective-permute-done.16 = f32[128,256]{1,0:T(8,128)S(1)} collective-permute-done((f32[128,256]{1,0:T(8,128)S(1)}, f32[128,256]{1,0:T(8,128)S(1)}, u32[]{:S(2)}, u32[]{:S(2)}) %collective-permute-start.16) | collective-permute-done | bytes 131104 | tf_op jit(solution)/shard_map/ppermute | solution.py:246
  73.9 0.0 collective-permute-done.15
  73.9 2.4 %collective-permute-done.14 = f32[128,256]{1,0:T(8,128)S(1)} collective-permute-done((f32[128,256]{1,0:T(8,128)S(1)}, f32[128,256]{1,0:T(8,128)S(1)}, u32[]{:S(2)}, u32[]{:S(2)}) %collective-permute-start.14) | collective-permute-done | bytes 131104 | tf_op jit(solution)/shard_map/ppermute | solution.py:246
  76.3 0.7 collective-permute-start.18
  76.9 2.1 %collective-permute-start.22 = (f32[2,64,256]{2,1,0:T(8,128)S(1)}, f32[2,64,256]{2,1,0:T(8,128)S(1)}, u32[]{:S(2)}, u32[]{:S(2)}) collective-permute-start(f32[2,64,256]{2,1,0:T(8,128)S(1)} %pad_maximum_fusion.5), channel_id=1, source_target_pairs={{0,12},{1,13},{2,14},{3,15},{4,8},{5,9},{6,10},{7,11},{8,4},{9,5},... | collective-permute-start | bytes 393224 | tf_op jit(solution)/shard_map/ppermute | solution.py:244
  79.0 0.0 collective-permute-start.21
  79.0 2.3 %collective-permute-start.20 = (f32[2,64,256]{2,1,0:T(8,128)S(1)}, f32[2,64,256]{2,1,0:T(8,128)S(1)}, u32[]{:S(2)}, u32[]{:S(2)}) collective-permute-start(f32[2,64,256]{2,1,0:T(8,128)S(1)} %pad_maximum_fusion.5), channel_id=1, source_target_pairs={{0,4},{1,5},{2,6},{3,7},{4,0},{5,1},{6,2},{7,3},{8,12},{9,13},{10,... | collective-permute-start | bytes 393224 | tf_op jit(solution)/shard_map/ppermute | solution.py:244
  81.3 0.0 collective-permute-start.17
  81.3 3.8 %collective-permute-done.22 = f32[2,64,256]{2,1,0:T(8,128)S(1)} collective-permute-done((f32[2,64,256]{2,1,0:T(8,128)S(1)}, f32[2,64,256]{2,1,0:T(8,128)S(1)}, u32[]{:S(2)}, u32[]{:S(2)}) %collective-permute-start.22) | collective-permute-done | bytes 131104 | tf_op jit(solution)/shard_map/ppermute | solution.py:244
  85.2 3.8 %collective-permute-done.21 = f32[2,64,256]{2,1,0:T(8,128)S(1)} collective-permute-done((f32[2,64,256]{2,1,0:T(8,128)S(1)}, f32[2,64,256]{2,1,0:T(8,128)S(1)}, u32[]{:S(2)}, u32[]{:S(2)}) %collective-permute-start.21) | collective-permute-done | bytes 131104 | tf_op jit(solution)/shard_map/ppermute | solution.py:244
  89.0 0.0 collective-permute-done.20
  89.0 0.1 collective-permute-start.23
  89.1 0.7 collective-permute-done.18.refs_1_
  89.8 0.0 collective-permute-start.19
  89.8 1.7 %shard_map.70.refs_8_ = f32[192,512]{1,0:T(8,128)S(1)} custom-call(f32[4,128,256]{2,1,0:T(8,128)S(1)} %pad_maximum_fusion.2.refs_0_, f32[4,128,256]{2,1,0:T(8,128)S(1)} %collective-permute-done.18.refs_1_, f32[4,2,64,256]{3,2,1,0:T(8,128)S(1)} %pad_maximum_fusion.3.refs_2_, f32[4,128,256]{2,1,0:T(8,128)S(1)} %pad_maximum_fusion.refs_0_.refs_3_, ...), custom_call_target="tpu_custom_call" | custom-call | flops 1207959552 | bytes 1048576 | tf_op jit(solution)/shard_map/pallas_call | solution.py:220
  91.5 0.0 collective-permute-done.17.refs_0_
  91.5 0.0 collective-permute-done.23.refs_2_
  91.5 0.2 collective-permute-done.19.refs_1_
  91.8 2.3 %shard_map.71 = f32[192,256]{1,0:T(8,128)} custom-call(f32[4,128,256]{2,1,0:T(8,128)S(1)} %collective-permute-done.17.refs_0_, f32[4,128,256]{2,1,0:T(8,128)S(1)} %collective-permute-done.19.refs_1_, f32[4,2,64,256]{3,2,1,0:T(8,128)S(1)} %collective-permute-done.23.refs_2_, f32[4,128,256]{2,1,0:T(8,128)S(1)} %collective-permute-done.4.refs_0_.refs_3_, ...), custom_call_target="tpu_custom_call" | custom-call | flops 1207959552 | bytes 1048576 | tf_op jit(solution)/shard_map/pallas_call | solution.py:220
  (6 shorter events, 0.2 us)
Async XLA Ops:
  24.6 9.2 %collective-permute-start = (f32[64,256]{1,0:T(8,128)S(1)}, f32[64,256]{1,0:T(8,128)S(1)}, u32[]{:S(2)}, u32[]{:S(2)}) collective-permute-start(f32[64,256]{1,0:T(8,128)S(1)} %get-tuple-element.32), channel_id=1, source_target_pairs={{0,2},{1,3},{2,0},{3,1},{4,6},{5,7},{6,4},{7,5},{8,10},{9,11},{10,... | collective-permute-start | bytes 196616 | tf_op jit(solution)/shard_map/ppermute | solution.py:244
  25.0 8.8 %collective-permute-start.3 = (f32[128,256]{1,0:T(8,128)S(1)}, f32[128,256]{1,0:T(8,128)S(1)}, u32[]{:S(2)}, u32[]{:S(2)}) collective-permute-start(f32[128,256]{1,0:T(8,128)S(1)} %get-tuple-element.33), channel_id=1, source_target_pairs={{0,12},{1,13},{2,14},{3,15},{4,8},{5,9},{6,10},{7,11},{8,4},{9,5},... | collective-permute-start | bytes 393224 | tf_op jit(solution)/shard_map/ppermute | solution.py:244
  27.7 12.4 %collective-permute-start.2 = (f32[128,256]{1,0:T(8,128)S(1)}, f32[128,256]{1,0:T(8,128)S(1)}, u32[]{:S(2)}, u32[]{:S(2)}) collective-permute-start(f32[128,256]{1,0:T(8,128)S(1)} %get-tuple-element.33), channel_id=1, source_target_pairs={{0,8},{1,9},{2,10},{3,11},{4,12},{5,13},{6,14},{7,15},{8,0},{9,1},... | collective-permute-start | bytes 393224 | tf_op jit(solution)/shard_map/ppermute | solution.py:244
  28.3 11.8 %collective-permute-start.1 = (f32[128,256]{1,0:T(8,128)S(1)}, f32[128,256]{1,0:T(8,128)S(1)}, u32[]{:S(2)}, u32[]{:S(2)}) collective-permute-start(f32[128,256]{1,0:T(8,128)S(1)} %get-tuple-element.33), channel_id=1, source_target_pairs={{0,4},{1,5},{2,6},{3,7},{4,0},{5,1},{6,2},{7,3},{8,12},{9,13},{10,... | collective-permute-start | bytes 393224 | tf_op jit(solution)/shard_map/ppermute | solution.py:244
  29.4 3.4 %copy-start = (f32[2,256,4096]{2,1,0:T(8,128)S(1)}, f32[2,256,4096]{2,1,0:T(8,128)}, u32[]{:S(2)}) copy-start(f32[2,256,4096]{2,1,0:T(8,128)} %matrix_ref) | copy-start | bytes 25165828
  32.8 13.0 %copy-start.1 = (f32[2,256,4096]{2,1,0:T(8,128)S(1)}, f32[2,256,4096]{2,1,0:T(8,128)}, u32[]{:S(2)}) copy-start(f32[2,256,4096]{2,1,0:T(8,128)} %matrix_ref.1) | copy-start | bytes 25165828
  40.2 13.1 %collective-permute-start.5 = (f32[4,128,256]{2,1,0:T(8,128)S(1)}, f32[4,128,256]{2,1,0:T(8,128)S(1)}, u32[]{:S(2)}, u32[]{:S(2)}) collective-permute-start(f32[4,128,256]{2,1,0:T(8,128)S(1)} %pad_maximum_fusion.refs_0_.refs_3_), channel_id=1, source_target_pairs={{0,2},{1,3},{2,0},{3,1},{4,6},{5,7},{6,4},{7,5},{8,10},{9,11},{10,... | collective-permute-start | bytes 1572872 | tf_op jit(solution)/shard_map/ppermute | solution.py:244
  41.4 8.3 %collective-permute-start.8 = (f32[2,64,256]{2,1,0:T(8,128)S(1)}, f32[2,64,256]{2,1,0:T(8,128)S(1)}, u32[]{:S(2)}, u32[]{:S(2)}) collective-permute-start(f32[2,64,256]{2,1,0:T(8,128)S(1)} %pad_maximum_fusion.4), channel_id=1, source_target_pairs={{0,12},{1,13},{2,14},{3,15},{4,8},{5,9},{6,10},{7,11},{8,4},{9,5},... | collective-permute-start | bytes 393224 | tf_op jit(solution)/shard_map/ppermute | solution.py:244
  42.8 10.0 %collective-permute-start.7 = (f32[2,64,256]{2,1,0:T(8,128)S(1)}, f32[2,64,256]{2,1,0:T(8,128)S(1)}, u32[]{:S(2)}, u32[]{:S(2)}) collective-permute-start(f32[2,64,256]{2,1,0:T(8,128)S(1)} %pad_maximum_fusion.4), channel_id=1, source_target_pairs={{0,8},{1,9},{2,10},{3,11},{4,12},{5,13},{6,14},{7,15},{8,0},{9,1},... | collective-permute-start | bytes 393224 | tf_op jit(solution)/shard_map/ppermute | solution.py:244
  42.8 10.0 %collective-permute-start.6 = (f32[2,64,256]{2,1,0:T(8,128)S(1)}, f32[2,64,256]{2,1,0:T(8,128)S(1)}, u32[]{:S(2)}, u32[]{:S(2)}) collective-permute-start(f32[2,64,256]{2,1,0:T(8,128)S(1)} %pad_maximum_fusion.4), channel_id=1, source_target_pairs={{0,4},{1,5},{2,6},{3,7},{4,0},{5,1},{6,2},{7,3},{8,12},{9,13},{10,... | collective-permute-start | bytes 393224 | tf_op jit(solution)/shard_map/ppermute | solution.py:244
  45.8 9.6 %collective-permute-start.4 = (f32[4,128,256]{2,1,0:T(8,128)S(1)}, f32[4,128,256]{2,1,0:T(8,128)S(1)}, u32[]{:S(2)}, u32[]{:S(2)}) collective-permute-start(f32[4,128,256]{2,1,0:T(8,128)S(1)} %pad_maximum_fusion.refs_0_.refs_3_), channel_id=1, source_target_pairs={{0,1},{1,0},{2,3},{3,2},{4,5},{5,4},{6,7},{7,6},{8,9},{9,8},{10,11... | collective-permute-start | bytes 1572872 | tf_op jit(solution)/shard_map/ppermute | solution.py:244
  53.2 2.2 %collective-permute-start.9 = (f32[4,128,256]{2,1,0:T(8,128)S(1)}, f32[4,128,256]{2,1,0:T(8,128)S(1)}, u32[]{:S(2)}, u32[]{:S(2)}) collective-permute-start(f32[4,128,256]{2,1,0:T(8,128)S(1)} %collective-permute-done.5.refs_1_.refs_4_), channel_id=1, source_target_pairs={{0,1},{1,0},{2,3},{3,2},{4,5},{5,4},{6,7},{7,6},{8,9},{9,8},{10,11... | collective-permute-start | bytes 1572872 | tf_op jit(solution)/shard_map/ppermute | solution.py:244
  53.2 2.7 %collective-permute-start.10 = (f32[4,2,64,256]{3,2,1,0:T(8,128)S(1)}, f32[4,2,64,256]{3,2,1,0:T(8,128)S(1)}, u32[]{:S(2)}, u32[]{:S(2)}) collective-permute-start(f32[4,2,64,256]{3,2,1,0:T(8,128)S(1)} %pad_maximum_fusion.1.refs_2_.refs_5_), channel_id=1, source_target_pairs={{0,1},{1,0},{2,3},{3,2},{4,5},{5,4},{6,7},{7,6},{8,9},{9,8},{10,11... | collective-permute-start | bytes 1572872 | tf_op jit(solution)/shard_map/ppermute | solution.py:244
  57.5 9.5 %collective-permute-start.13 = (f32[128,256]{1,0:T(8,128)S(1)}, f32[128,256]{1,0:T(8,128)S(1)}, u32[]{:S(2)}, u32[]{:S(2)}) collective-permute-start(f32[128,256]{1,0:T(8,128)S(1)} %get-tuple-element.47), channel_id=1, source_target_pairs={{0,28},{1,29},{2,30},{3,31},{4,16},{5,17},{6,18},{7,19},{8,20},{9,... | collective-permute-start | bytes 393224 | tf_op jit(solution)/shard_map/ppermute | solution.py:246
  59.0 7.5 %collective-permute-start.12 = (f32[64,256]{1,0:T(8,128)S(1)}, f32[64,256]{1,0:T(8,128)S(1)}, u32[]{:S(2)}, u32[]{:S(2)}) collective-permute-start(f32[64,256]{1,0:T(8,128)S(1)} %get-tuple-element.46), channel_id=1, source_target_pairs={{0,18},{1,19},{2,16},{3,17},{4,22},{5,23},{6,20},{7,21},{8,26},{9,... | collective-permute-start | bytes 196616 | tf_op jit(solution)/shard_map/ppermute | solution.py:246
  61.4 5.5 %collective-permute-start.11 = (f32[64,256]{1,0:T(8,128)S(1)}, f32[64,256]{1,0:T(8,128)S(1)}, u32[]{:S(2)}, u32[]{:S(2)}) collective-permute-start(f32[64,256]{1,0:T(8,128)S(1)} %get-tuple-element.46), channel_id=1, source_target_pairs={{0,16},{1,17},{2,18},{3,19},{4,20},{5,21},{6,22},{7,23},{8,24},{9,... | collective-permute-start | bytes 196616 | tf_op jit(solution)/shard_map/ppermute | solution.py:246
  61.4 12.4 %collective-permute-start.16 = (f32[128,256]{1,0:T(8,128)S(1)}, f32[128,256]{1,0:T(8,128)S(1)}, u32[]{:S(2)}, u32[]{:S(2)}) collective-permute-start(f32[128,256]{1,0:T(8,128)S(1)} %get-tuple-element.47), channel_id=1, source_target_pairs={{0,24},{1,25},{2,26},{3,27},{4,28},{5,29},{6,30},{7,31},{8,16},{9,... | collective-permute-start | bytes 393224 | tf_op jit(solution)/shard_map/ppermute | solution.py:246
  62.0 11.8 %collective-permute-start.15 = (f32[128,256]{1,0:T(8,128)S(1)}, f32[128,256]{1,0:T(8,128)S(1)}, u32[]{:S(2)}, u32[]{:S(2)}) collective-permute-start(f32[128,256]{1,0:T(8,128)S(1)} %get-tuple-element.47), channel_id=1, source_target_pairs={{0,20},{1,21},{2,22},{3,23},{4,24},{5,25},{6,26},{7,27},{8,28},{9,... | collective-permute-start | bytes 393224 | tf_op jit(solution)/shard_map/ppermute | solution.py:246
  66.5 9.8 %collective-permute-start.14 = (f32[128,256]{1,0:T(8,128)S(1)}, f32[128,256]{1,0:T(8,128)S(1)}, u32[]{:S(2)}, u32[]{:S(2)}) collective-permute-start(f32[128,256]{1,0:T(8,128)S(1)} %get-tuple-element.47), channel_id=1, source_target_pairs={{0,16},{1,17},{2,18},{3,19},{4,20},{5,21},{6,22},{7,23},{8,24},{9,... | collective-permute-start | bytes 393224 | tf_op jit(solution)/shard_map/ppermute | solution.py:246
  76.3 13.6 %collective-permute-start.18 = (f32[4,128,256]{2,1,0:T(8,128)S(1)}, f32[4,128,256]{2,1,0:T(8,128)S(1)}, u32[]{:S(2)}, u32[]{:S(2)}) collective-permute-start(f32[4,128,256]{2,1,0:T(8,128)S(1)} %pad_maximum_fusion.2.refs_0_), channel_id=1, source_target_pairs={{0,2},{1,3},{2,0},{3,1},{4,6},{5,7},{6,4},{7,5},{8,10},{9,11},{10,... | collective-permute-start | bytes 1572872 | tf_op jit(solution)/shard_map/ppermute | solution.py:244
  76.9 8.2 %collective-permute-start.22 = (f32[2,64,256]{2,1,0:T(8,128)S(1)}, f32[2,64,256]{2,1,0:T(8,128)S(1)}, u32[]{:S(2)}, u32[]{:S(2)}) collective-permute-start(f32[2,64,256]{2,1,0:T(8,128)S(1)} %pad_maximum_fusion.5), channel_id=1, source_target_pairs={{0,12},{1,13},{2,14},{3,15},{4,8},{5,9},{6,10},{7,11},{8,4},{9,5},... | collective-permute-start | bytes 393224 | tf_op jit(solution)/shard_map/ppermute | solution.py:244
  79.0 10.0 %collective-permute-start.21 = (f32[2,64,256]{2,1,0:T(8,128)S(1)}, f32[2,64,256]{2,1,0:T(8,128)S(1)}, u32[]{:S(2)}, u32[]{:S(2)}) collective-permute-start(f32[2,64,256]{2,1,0:T(8,128)S(1)} %pad_maximum_fusion.5), channel_id=1, source_target_pairs={{0,8},{1,9},{2,10},{3,11},{4,12},{5,13},{6,14},{7,15},{8,0},{9,1},... | collective-permute-start | bytes 393224 | tf_op jit(solution)/shard_map/ppermute | solution.py:244
  79.0 10.0 %collective-permute-start.20 = (f32[2,64,256]{2,1,0:T(8,128)S(1)}, f32[2,64,256]{2,1,0:T(8,128)S(1)}, u32[]{:S(2)}, u32[]{:S(2)}) collective-permute-start(f32[2,64,256]{2,1,0:T(8,128)S(1)} %pad_maximum_fusion.5), channel_id=1, source_target_pairs={{0,4},{1,5},{2,6},{3,7},{4,0},{5,1},{6,2},{7,3},{8,12},{9,13},{10,... | collective-permute-start | bytes 393224 | tf_op jit(solution)/shard_map/ppermute | solution.py:244
  81.3 10.2 %collective-permute-start.17 = (f32[4,128,256]{2,1,0:T(8,128)S(1)}, f32[4,128,256]{2,1,0:T(8,128)S(1)}, u32[]{:S(2)}, u32[]{:S(2)}) collective-permute-start(f32[4,128,256]{2,1,0:T(8,128)S(1)} %pad_maximum_fusion.2.refs_0_), channel_id=1, source_target_pairs={{0,1},{1,0},{2,3},{3,2},{4,5},{5,4},{6,7},{7,6},{8,9},{9,8},{10,11... | collective-permute-start | bytes 1572872 | tf_op jit(solution)/shard_map/ppermute | solution.py:244
  89.0 2.5 %collective-permute-start.23 = (f32[4,2,64,256]{3,2,1,0:T(8,128)S(1)}, f32[4,2,64,256]{3,2,1,0:T(8,128)S(1)}, u32[]{:S(2)}, u32[]{:S(2)}) collective-permute-start(f32[4,2,64,256]{3,2,1,0:T(8,128)S(1)} %pad_maximum_fusion.3.refs_2_), channel_id=1, source_target_pairs={{0,1},{1,0},{2,3},{3,2},{4,5},{5,4},{6,7},{7,6},{8,9},{9,8},{10,11... | collective-permute-start | bytes 1572872 | tf_op jit(solution)/shard_map/ppermute | solution.py:244
  89.8 1.9 %collective-permute-start.19 = (f32[4,128,256]{2,1,0:T(8,128)S(1)}, f32[4,128,256]{2,1,0:T(8,128)S(1)}, u32[]{:S(2)}, u32[]{:S(2)}) collective-permute-start(f32[4,128,256]{2,1,0:T(8,128)S(1)} %collective-permute-done.18.refs_1_), channel_id=1, source_target_pairs={{0,1},{1,0},{2,3},{3,2},{4,5},{5,4},{6,7},{7,6},{8,9},{9,8},{10,11... | collective-permute-start | bytes 1572872 | tf_op jit(solution)/shard_map/ppermute | solution.py:244

commit v20 on v18

--- a/solution.py
+++ b/solution.py
@@ -198,6 +198,7 @@
                 total_ref[...] = start_ref[...] + part
         start = 0
         for out_ref in out_refs:
+            start = 0 if start == columns else start
             for first in range(0, out_ref.shape[0], 2 * sources):
                 real = pl.ds(start + first, sources)
                 imag = pl.ds(start + first + sources, sources)
@@ -211,7 +212,8 @@
     block = blocks[0].shape[-1]
     vmem = pl.BlockSpec(memory_space=pltpu.VMEM)
     finish = end == groups
-    whole = (sum(shares), both_rows)
+    columns = shares[-1] if len(shares) == 3 else sum(shares)
+    whole = (columns, both_rows)
     arrays = list(blocks) + list(own) + list(split) + ([] if started is None else [started])
     if finish:
         out_shape = [jax.ShapeDtypeStruct((rows, both_rows // 2), f32) for rows in shares]
@@ -224,7 +226,7 @@
         out_shape=out_shape,
         scratch_shapes=[pltpu.VMEM(whole, f32)] if finish else [],
         compiler_params=kernel_params(20),
-        cost_estimate=pl.CostEstimate(flops=6 * sum(shares) * both_rows * width * (end - begin), bytes_accessed=MIB, transcendentals=0),
+        cost_estimate=pl.CostEstimate(flops=6 * columns * both_rows * width * (end - begin), bytes_accessed=MIB, transcendentals=0),
     )(*arrays)
 
 
@@ -245,15 +247,16 @@
         pairs = [(c * tile_size + t, (c + 1) % chain_size * tile_size + target(t)) for c in range(chain_size) for t in range(tile_size)]
         return lax.ppermute(value, ("chain", "tile"), pairs)
 
-    def first_stage(first, second, hop):
-        pair = [second if across == 0 and not hop else send(second, hop, lambda t: t ^ (2 * across)) for across in range(2)]
-        if hop:
-            line = [send(first, True, lambda t: (t + 4 * by) % tile_size) for by in range(layers)]
-        else:
+    def first_stage(first, second, whole=None):
+        if whole is None:
             line = [first if by == 0 else send(first, False, lambda t: t ^ (4 * by)) for by in range(layers)]
-        if hop:
-            *pair, line[-1] = lax.optimization_barrier((*pair, line[-1]))
-        return jnp.stack(pair), jnp.stack(line)
+            pair = [second, send(second, False, lambda t: t ^ 2)]
+            return jnp.stack(pair), jnp.stack(line)
+        line = [send(first, True, lambda t: (t + 4 * by) % tile_size) for by in range(1, layers)]
+        pair = send(second, True, lambda t: t ^ 2)
+        straight = send(whole, True, lambda t: t)
+        early = first.shape[0]
+        return jnp.stack([straight[early:], pair]), jnp.stack([straight[:early], *line])
 
     def second_stage(pair, line):
         far = send(line, False, lambda t: t ^ 2)
@@ -269,7 +272,7 @@
         return product_part(split, onward, layout, other, theirs, 2, 4, started, sources, shares, True), other
 
     only = chain_size == 1
-    pair, line = first_stage(*reduced, False)
+    pair, line = first_stage(*reduced)
     split = split_blocks(tied(diag_inverse if only else coupling, reduced[0]), own_rows, True)
     pair, line, split = lax.optimization_barrier((pair, line, split))
     held = second_stage(pair, line)
@@ -277,12 +280,12 @@
         return products(split, False, held, None, [sum(shares)])[0][0]
     diag_split = split_blocks(tied(diag_inverse, line), own_rows, True)
     held[1], held[2], diag_split = lax.optimization_barrier((held[1], held[2], diag_split))
-    carried, other = products(split, True, held, None, shares)
+    carried, other = products(split, True, held, None, [*shares, sum(shares)])
     own = (held, other)
     for step in range(chain_size - 1):
-        held = second_stage(*lax.optimization_barrier(first_stage(*carried, True)))
+        held = second_stage(*lax.optimization_barrier(first_stage(*carried)))
         if step < chain_size - 2:
-            carried = products(split, True, held, own, shares)[0]
+            carried = products(split, True, held, own, [*shares, sum(shares)])[0]
     return products(diag_split, False, held, own, [sum(shares)])[0][0]
 
 

time: 94.2 us -> 93.5 us (level)
    ppermute x6 -> x5, starting transfers between devices: 6.5 us -> 5.97 us  [send(): return lax.ppermute(value, ('chain', 'tile'), pairs)]
    ppermute x6 -> x5, waiting for transfers between devices: 12.2 us -> 11.8 us  [send(): return lax.ppermute(value, ('chain', 'tile'), pairs)]
  transfers between devices with their start and end apart: 24 -> 23, of which waited for: 12 -> 10; matrix products, arithmetic and copies ran while one was open for 0% -> 0% of each run, Pallas kernels for 6% -> 6%
where the time goes in v20:
time: 93.5 us; the launch traced here: 93.2 us
  waiting for transfers between devices  33.4 us (36%)
  starting transfers between devices  22.4 us (24%)
  blocking collectives  20.6 us (22%)
  Pallas kernels  13 us (14%)
  local copies, waits for them, and re-layouts  3.4 us (4%)
    ppermute x18, waiting for transfers between devices, send(): lax.ppermute(value, 'tile', [(t, target(t)) for t in range(tile_size)])  21.6 us
    all_to_all x1, blocking collectives, body(): received = lax.all_to_all(packed, 'tile', 0, 0, tiled=False)  20.6 us
    ppermute x18, starting transfers between devices, send(): lax.ppermute(value, 'tile', [(t, target(t)) for t in range(tile_size)])  16.5 us
    ppermute x5, waiting for transfers between devices, send(): return lax.ppermute(value, ('chain', 'tile'), pairs)  11.8 us
    pallas_call x4, Pallas kernels, product_part(): pl.pallas_call(functools.partial(product_kernel, sources, layout, len(blo...  7.21 us
    ppermute x5, starting transfers between devices, send(): return lax.ppermute(value, ('chain', 'tile'), pairs)  5.97 us
    unnamed x4, local copies, waits for them, and re-layouts  3.38 us
    pallas_call x1, Pallas kernels, body(): pl.pallas_call(functools.partial(pack_kernel, own_rows, cap, tile_rows),...  2.72 us
  transfers between devices with their start and end apart: 23, of which 10 were waited for; matrix products, arithmetic and copies ran while one was open for 0% of the time, Pallas kernels for 6%

profile of v20, /device:TPU:0, one launch (start us, length us, event | category | flops | bytes accessed | tf_op | source)
XLA Modules:
  0.0 93.2 jit_solution(5851440590502966861)
XLA Ops:
  0.0 2.7 %shard_map.64 = (f32[16,56,128]{2,1,0:T(8,128)}, f32[24,192,256]{2,1,0:T(8,128)}) custom-call(s32[2]{0:T(128)} %counts_hbm.1, s32[1,256]{1,0:T(1,128)} %bitcast.46, f32[192,256]{1,0:T(8,128)} %bitcast.30, f32[192,256]{1,0:T(8,128)} %bitcast.31), custom_call_target="tpu_custom_call" | custom-call | tf_op jit(solution)/shard_map/pallas_call | solution.py:329
  2.7 20.6 %all_to_all.5.received_ref = f32[16,56,128]{2,1,0:T(8,128)S(1)} all-to-all(f32[16,56,128]{2,1,0:T(8,128)} %get-tuple-element.28), channel_id=1, replica_groups=mesh['chain'=2,'tile'=16] {'tile'}, dimensions={0} | all-to-all | bytes 917504 | tf_op jit(solution)/shard_map/all_to_all | solution.py:346
  23.4 1.1 %shard_map.65 = (f32[128,256]{1,0:T(8,128)S(1)}, f32[64,256]{1,0:T(8,128)S(1)}) custom-call(f32[16,56,128]{2,1,0:T(8,128)S(1)} %all_to_all.5.received_ref, f32[24,192,256]{2,1,0:T(8,128)} %get-tuple-element.29.right_hbm), custom_call_target="tpu_custom_call" | custom-call | tf_op jit(solution)/shard_map/pallas_call | solution.py:350
  24.5 0.4 collective-permute-start
  24.9 2.7 %collective-permute-start.3 = (f32[128,256]{1,0:T(8,128)S(1)}, f32[128,256]{1,0:T(8,128)S(1)}, u32[]{:S(2)}, u32[]{:S(2)}) collective-permute-start(f32[128,256]{1,0:T(8,128)S(1)} %get-tuple-element.31), channel_id=1, source_target_pairs={{0,12},{1,13},{2,14},{3,15},{4,8},{5,9},{6,10},{7,11},{8,4},{9,5},... | collective-permute-start | bytes 393224 | tf_op jit(solution)/shard_map/ppermute | solution.py:246
  27.6 0.5 collective-permute-start.2
  28.2 1.1 %collective-permute-start.1 = (f32[128,256]{1,0:T(8,128)S(1)}, f32[128,256]{1,0:T(8,128)S(1)}, u32[]{:S(2)}, u32[]{:S(2)}) collective-permute-start(f32[128,256]{1,0:T(8,128)S(1)} %get-tuple-element.31), channel_id=1, source_target_pairs={{0,4},{1,5},{2,6},{3,7},{4,0},{5,1},{6,2},{7,3},{8,12},{9,13},{10,... | collective-permute-start | bytes 393224 | tf_op jit(solution)/shard_map/ppermute | solution.py:246
  29.3 0.0 copy-start
  29.3 3.4 %copy-done = f32[2,256,4096]{2,1,0:T(8,128)S(1)} copy-done((f32[2,256,4096]{2,1,0:T(8,128)S(1)}, f32[2,256,4096]{2,1,0:T(8,128)}, u32[]{:S(2)}) %copy-start) | copy-done | bytes 8388632
  32.7 0.0 copy-start.1
  32.7 1.0 %shard_map.66 = (bf16[4,512,1024]{2,1,0:T(8,128)(2,1)S(1)}, bf16[4,512,1024]{2,1,0:T(8,128)(2,1)S(1)}) custom-call(f32[2,256,4096]{2,1,0:T(8,128)S(1)} %copy-done), custom_call_target="tpu_custom_call" | custom-call | flops 6291456 | bytes 16777216 | tf_op jit(solution)/shard_map/pallas_call | solution.py:140
  33.7 0.0 collective-permute-done
  33.7 0.0 collective-permute-done.3
  33.7 6.3 %collective-permute-done.2 = f32[128,256]{1,0:T(8,128)S(1)} collective-permute-done((f32[128,256]{1,0:T(8,128)S(1)}, f32[128,256]{1,0:T(8,128)S(1)}, u32[]{:S(2)}, u32[]{:S(2)}) %collective-permute-start.2) | collective-permute-done | bytes 131104 | tf_op jit(solution)/shard_map/ppermute | solution.py:246
  40.0 0.0 collective-permute-done.1
  40.0 1.2 %collective-permute-start.5 = (f32[4,128,256]{2,1,0:T(8,128)S(1)}, f32[4,128,256]{2,1,0:T(8,128)S(1)}, u32[]{:S(2)}, u32[]{:S(2)}) collective-permute-start(f32[4,128,256]{2,1,0:T(8,128)S(1)} %pad_maximum_fusion.refs_0_.refs_3_), channel_id=1, source_target_pairs={{0,2},{1,3},{2,0},{3,1},{4,6},{5,7},{6,4},{7,5},{8,10},{9,11},{10,... | collective-permute-start | bytes 1572872 | tf_op jit(solution)/shard_map/ppermute | solution.py:246
  41.2 1.4 %collective-permute-start.8 = (f32[2,64,256]{2,1,0:T(8,128)S(1)}, f32[2,64,256]{2,1,0:T(8,128)S(1)}, u32[]{:S(2)}, u32[]{:S(2)}) collective-permute-start(f32[2,64,256]{2,1,0:T(8,128)S(1)} %pad_maximum_fusion.4), channel_id=1, source_target_pairs={{0,12},{1,13},{2,14},{3,15},{4,8},{5,9},{6,10},{7,11},{8,4},{9,5},... | collective-permute-start | bytes 393224 | tf_op jit(solution)/shard_map/ppermute | solution.py:246
  42.7 0.0 collective-permute-start.7
  42.7 3.0 %collective-permute-start.6 = (f32[2,64,256]{2,1,0:T(8,128)S(1)}, f32[2,64,256]{2,1,0:T(8,128)S(1)}, u32[]{:S(2)}, u32[]{:S(2)}) collective-permute-start(f32[2,64,256]{2,1,0:T(8,128)S(1)} %pad_maximum_fusion.4), channel_id=1, source_target_pairs={{0,4},{1,5},{2,6},{3,7},{4,0},{5,1},{6,2},{7,3},{8,12},{9,13},{10,... | collective-permute-start | bytes 393224 | tf_op jit(solution)/shard_map/ppermute | solution.py:246
  45.6 0.0 collective-permute-start.4
  45.6 0.0 copy-done.1
  45.6 1.0 %shard_map.67 = (bf16[4,512,1024]{2,1,0:T(8,128)(2,1)S(1)}, bf16[4,512,1024]{2,1,0:T(8,128)(2,1)S(1)}) custom-call(f32[2,256,4096]{2,1,0:T(8,128)S(1)} %copy-done.1), custom_call_target="tpu_custom_call" | custom-call | flops 6291456 | bytes 16777216 | tf_op jit(solution)/shard_map/pallas_call | solution.py:140
  46.6 2.9 %collective-permute-done.8 = f32[2,64,256]{2,1,0:T(8,128)S(1)} collective-permute-done((f32[2,64,256]{2,1,0:T(8,128)S(1)}, f32[2,64,256]{2,1,0:T(8,128)S(1)}, u32[]{:S(2)}, u32[]{:S(2)}) %collective-permute-start.8) | collective-permute-done | bytes 131104 | tf_op jit(solution)/shard_map/ppermute | solution.py:246
  49.5 3.1 %collective-permute-done.7 = f32[2,64,256]{2,1,0:T(8,128)S(1)} collective-permute-done((f32[2,64,256]{2,1,0:T(8,128)S(1)}, f32[2,64,256]{2,1,0:T(8,128)S(1)}, u32[]{:S(2)}, u32[]{:S(2)}) %collective-permute-start.7) | collective-permute-done | bytes 131104 | tf_op jit(solution)/shard_map/ppermute | solution.py:246
  52.7 0.0 collective-permute-done.6
  52.7 0.4 collective-permute-done.5.refs_1_.refs_4_
  53.1 0.0 collective-permute-start.9
  53.1 0.5 collective-permute-start.10
  53.6 1.7 %shard_map.68.refs_5_ = f32[192,512]{1,0:T(8,128)S(1)} custom-call(f32[4,128,256]{2,1,0:T(8,128)S(1)} %pad_maximum_fusion.refs_0_.refs_3_, f32[4,128,256]{2,1,0:T(8,128)S(1)} %collective-permute-done.5.refs_1_.refs_4_, f32[4,2,64,256]{3,2,1,0:T(8,128)S(1)} %pad_maximum_fusion.1.refs_2_.refs_5_, bf16[4,512,1024]{2,1,0:T(8,128)(2,1)S(1)} %get-tuple-element.42.refs_3_, ...), custom_call_target="tpu_custom_call" | custom-call | flops 1207959552 | bytes 1048576 | tf_op jit(solution)/shard_map/pallas_call | solution.py:222
  55.3 0.0 collective-permute-done.4.refs_0_.refs_3_
  55.3 0.0 collective-permute-done.9.refs_1_.refs_4_
  55.3 0.4 collective-permute-done.10.refs_2_.refs_5_
  55.8 1.6 %shard_map.69 = (f32[128,256]{1,0:T(8,128)S(1)}, f32[64,256]{1,0:T(8,128)S(1)}, f32[192,256]{1,0:T(8,128)S(1)}) custom-call(f32[4,128,256]{2,1,0:T(8,128)S(1)} %collective-permute-done.4.refs_0_.refs_3_, f32[4,128,256]{2,1,0:T(8,128)S(1)} %collective-permute-done.9.refs_1_.refs_4_, f32[4,2,64,256]{3,2,1,0:T(8,128)S(1)} %collective-permute-done.10.refs_2_.refs_5_, ...), custom_call_target="tpu_custom_call" | custom-call | flops 1207959552 | bytes 1048576 | tf_op jit(solution)/shard_map/pallas_call | solution.py:222
  57.4 0.1 collective-permute-start.11
  57.4 3.6 %collective-permute-start.15 = (f32[128,256]{1,0:T(8,128)S(1)}, f32[128,256]{1,0:T(8,128)S(1)}, u32[]{:S(2)}, u32[]{:S(2)}) collective-permute-start(f32[128,256]{1,0:T(8,128)S(1)} %get-tuple-element.46), channel_id=1, source_target_pairs={{0,28},{1,29},{2,30},{3,31},{4,16},{5,17},{6,18},{7,19},{8,20},{9,... | collective-permute-start | bytes 393224 | tf_op jit(solution)/shard_map/ppermute | solution.py:248
  61.0 0.0 collective-permute-start.14
  61.0 1.7 %collective-permute-start.13 = (f32[128,256]{1,0:T(8,128)S(1)}, f32[128,256]{1,0:T(8,128)S(1)}, u32[]{:S(2)}, u32[]{:S(2)}) collective-permute-start(f32[128,256]{1,0:T(8,128)S(1)} %get-tuple-element.46), channel_id=1, source_target_pairs={{0,20},{1,21},{2,22},{3,23},{4,24},{5,25},{6,26},{7,27},{8,28},{9,... | collective-permute-start | bytes 393224 | tf_op jit(solution)/shard_map/ppermute | solution.py:248
  62.8 0.6 collective-permute-start.12
  63.3 10.2 %collective-permute-done.11 = f32[192,256]{1,0:T(8,128)S(1)} collective-permute-done((f32[192,256]{1,0:T(8,128)S(1)}, f32[192,256]{1,0:T(8,128)S(1)}, u32[]{:S(2)}, u32[]{:S(2)}) %collective-permute-start.11) | collective-permute-done | bytes 196640 | tf_op jit(solution)/shard_map/ppermute | solution.py:248
  73.5 1.6 %collective-permute-done.12 = f32[64,256]{1,0:T(8,128)S(1)} collective-permute-done((f32[64,256]{1,0:T(8,128)S(1)}, f32[64,256]{1,0:T(8,128)S(1)}, u32[]{:S(2)}, u32[]{:S(2)}) %collective-permute-start.12) | collective-permute-done | bytes 65568 | tf_op jit(solution)/shard_map/ppermute | solution.py:248
  75.2 0.0 collective-permute-done.15
  75.2 0.0 collective-permute-done.14
  75.2 0.0 collective-permute-done.13
  75.2 0.6 collective-permute-start.17
  75.8 2.1 %collective-permute-start.21 = (f32[2,64,256]{2,1,0:T(8,128)S(1)}, f32[2,64,256]{2,1,0:T(8,128)S(1)}, u32[]{:S(2)}, u32[]{:S(2)}) collective-permute-start(f32[2,64,256]{2,1,0:T(8,128)S(1)} %pad_maximum_fusion.5), channel_id=1, source_target_pairs={{0,12},{1,13},{2,14},{3,15},{4,8},{5,9},{6,10},{7,11},{8,4},{9,5},... | collective-permute-start | bytes 393224 | tf_op jit(solution)/shard_map/ppermute | solution.py:246
  77.9 0.0 collective-permute-start.20
  77.9 2.3 %collective-permute-start.19 = (f32[2,64,256]{2,1,0:T(8,128)S(1)}, f32[2,64,256]{2,1,0:T(8,128)S(1)}, u32[]{:S(2)}, u32[]{:S(2)}) collective-permute-start(f32[2,64,256]{2,1,0:T(8,128)S(1)} %pad_maximum_fusion.5), channel_id=1, source_target_pairs={{0,4},{1,5},{2,6},{3,7},{4,0},{5,1},{6,2},{7,3},{8,12},{9,13},{10,... | collective-permute-start | bytes 393224 | tf_op jit(solution)/shard_map/ppermute | solution.py:246
  80.2 0.0 collective-permute-start.16
  80.2 3.8 %collective-permute-done.21 = f32[2,64,256]{2,1,0:T(8,128)S(1)} collective-permute-done((f32[2,64,256]{2,1,0:T(8,128)S(1)}, f32[2,64,256]{2,1,0:T(8,128)S(1)}, u32[]{:S(2)}, u32[]{:S(2)}) %collective-permute-start.21) | collective-permute-done | bytes 131104 | tf_op jit(solution)/shard_map/ppermute | solution.py:246
  84.1 4.1 %collective-permute-done.20 = f32[2,64,256]{2,1,0:T(8,128)S(1)} collective-permute-done((f32[2,64,256]{2,1,0:T(8,128)S(1)}, f32[2,64,256]{2,1,0:T(8,128)S(1)}, u32[]{:S(2)}, u32[]{:S(2)}) %collective-permute-start.20) | collective-permute-done | bytes 131104 | tf_op jit(solution)/shard_map/ppermute | solution.py:246
  88.2 0.0 collective-permute-done.19
  88.2 0.1 collective-permute-start.22
  88.3 0.0 collective-permute-done.17.refs_1_
  88.3 0.5 collective-permute-start.18
  88.8 1.7 %shard_map.70.refs_8_ = f32[192,512]{1,0:T(8,128)S(1)} custom-call(f32[4,128,256]{2,1,0:T(8,128)S(1)} %pad_maximum_fusion.2.refs_0_, f32[4,128,256]{2,1,0:T(8,128)S(1)} %collective-permute-done.17.refs_1_, f32[4,2,64,256]{3,2,1,0:T(8,128)S(1)} %pad_maximum_fusion.3.refs_2_, f32[4,128,256]{2,1,0:T(8,128)S(1)} %pad_maximum_fusion.refs_0_.refs_3_, ...), custom_call_target="tpu_custom_call" | custom-call | flops 1207959552 | bytes 1048576 | tf_op jit(solution)/shard_map/pallas_call | solution.py:222
  90.5 0.0 collective-permute-done.16.refs_0_
  90.5 0.0 collective-permute-done.22.refs_2_
  90.5 0.5 collective-permute-done.18.refs_1_
  91.0 2.3 %shard_map.71 = f32[192,256]{1,0:T(8,128)} custom-call(f32[4,128,256]{2,1,0:T(8,128)S(1)} %collective-permute-done.16.refs_0_, f32[4,128,256]{2,1,0:T(8,128)S(1)} %collective-permute-done.18.refs_1_, f32[4,2,64,256]{3,2,1,0:T(8,128)S(1)} %collective-permute-done.22.refs_2_, f32[4,128,256]{2,1,0:T(8,128)S(1)} %collective-permute-done.4.refs_0_.refs_3_, ...), custom_call_target="tpu_custom_call" | custom-call | flops 1207959552 | bytes 1048576 | tf_op jit(solution)/shard_map/pallas_call | solution.py:222
  (8 shorter events, 0.2 us)
Async XLA Ops:
  24.5 9.2 %collective-permute-start = (f32[64,256]{1,0:T(8,128)S(1)}, f32[64,256]{1,0:T(8,128)S(1)}, u32[]{:S(2)}, u32[]{:S(2)}) collective-permute-start(f32[64,256]{1,0:T(8,128)S(1)} %get-tuple-element.30), channel_id=1, source_target_pairs={{0,2},{1,3},{2,0},{3,1},{4,6},{5,7},{6,4},{7,5},{8,10},{9,11},{10,... | collective-permute-start | bytes 196616 | tf_op jit(solution)/shard_map/ppermute | solution.py:246
  24.9 8.8 %collective-permute-start.3 = (f32[128,256]{1,0:T(8,128)S(1)}, f32[128,256]{1,0:T(8,128)S(1)}, u32[]{:S(2)}, u32[]{:S(2)}) collective-permute-start(f32[128,256]{1,0:T(8,128)S(1)} %get-tuple-element.31), channel_id=1, source_target_pairs={{0,12},{1,13},{2,14},{3,15},{4,8},{5,9},{6,10},{7,11},{8,4},{9,5},... | collective-permute-start | bytes 393224 | tf_op jit(solution)/shard_map/ppermute | solution.py:246
  27.6 12.4 %collective-permute-start.2 = (f32[128,256]{1,0:T(8,128)S(1)}, f32[128,256]{1,0:T(8,128)S(1)}, u32[]{:S(2)}, u32[]{:S(2)}) collective-permute-start(f32[128,256]{1,0:T(8,128)S(1)} %get-tuple-element.31), channel_id=1, source_target_pairs={{0,8},{1,9},{2,10},{3,11},{4,12},{5,13},{6,14},{7,15},{8,0},{9,1},... | collective-permute-start | bytes 393224 | tf_op jit(solution)/shard_map/ppermute | solution.py:246
  28.2 11.8 %collective-permute-start.1 = (f32[128,256]{1,0:T(8,128)S(1)}, f32[128,256]{1,0:T(8,128)S(1)}, u32[]{:S(2)}, u32[]{:S(2)}) collective-permute-start(f32[128,256]{1,0:T(8,128)S(1)} %get-tuple-element.31), channel_id=1, source_target_pairs={{0,4},{1,5},{2,6},{3,7},{4,0},{5,1},{6,2},{7,3},{8,12},{9,13},{10,... | collective-permute-start | bytes 393224 | tf_op jit(solution)/shard_map/ppermute | solution.py:246
  29.3 3.4 %copy-start = (f32[2,256,4096]{2,1,0:T(8,128)S(1)}, f32[2,256,4096]{2,1,0:T(8,128)}, u32[]{:S(2)}) copy-start(f32[2,256,4096]{2,1,0:T(8,128)} %matrix_ref) | copy-start | bytes 25165828
  32.7 13.0 %copy-start.1 = (f32[2,256,4096]{2,1,0:T(8,128)S(1)}, f32[2,256,4096]{2,1,0:T(8,128)}, u32[]{:S(2)}) copy-start(f32[2,256,4096]{2,1,0:T(8,128)} %matrix_ref.1) | copy-start | bytes 25165828
  40.0 13.1 %collective-permute-start.5 = (f32[4,128,256]{2,1,0:T(8,128)S(1)}, f32[4,128,256]{2,1,0:T(8,128)S(1)}, u32[]{:S(2)}, u32[]{:S(2)}) collective-permute-start(f32[4,128,256]{2,1,0:T(8,128)S(1)} %pad_maximum_fusion.refs_0_.refs_3_), channel_id=1, source_target_pairs={{0,2},{1,3},{2,0},{3,1},{4,6},{5,7},{6,4},{7,5},{8,10},{9,11},{10,... | collective-permute-start | bytes 1572872 | tf_op jit(solution)/shard_map/ppermute | solution.py:246
  41.2 8.3 %collective-permute-start.8 = (f32[2,64,256]{2,1,0:T(8,128)S(1)}, f32[2,64,256]{2,1,0:T(8,128)S(1)}, u32[]{:S(2)}, u32[]{:S(2)}) collective-permute-start(f32[2,64,256]{2,1,0:T(8,128)S(1)} %pad_maximum_fusion.4), channel_id=1, source_target_pairs={{0,12},{1,13},{2,14},{3,15},{4,8},{5,9},{6,10},{7,11},{8,4},{9,5},... | collective-permute-start | bytes 393224 | tf_op jit(solution)/shard_map/ppermute | solution.py:246
  42.7 10.0 %collective-permute-start.7 = (f32[2,64,256]{2,1,0:T(8,128)S(1)}, f32[2,64,256]{2,1,0:T(8,128)S(1)}, u32[]{:S(2)}, u32[]{:S(2)}) collective-permute-start(f32[2,64,256]{2,1,0:T(8,128)S(1)} %pad_maximum_fusion.4), channel_id=1, source_target_pairs={{0,8},{1,9},{2,10},{3,11},{4,12},{5,13},{6,14},{7,15},{8,0},{9,1},... | collective-permute-start | bytes 393224 | tf_op jit(solution)/shard_map/ppermute | solution.py:246
  42.7 10.0 %collective-permute-start.6 = (f32[2,64,256]{2,1,0:T(8,128)S(1)}, f32[2,64,256]{2,1,0:T(8,128)S(1)}, u32[]{:S(2)}, u32[]{:S(2)}) collective-permute-start(f32[2,64,256]{2,1,0:T(8,128)S(1)} %pad_maximum_fusion.4), channel_id=1, source_target_pairs={{0,4},{1,5},{2,6},{3,7},{4,0},{5,1},{6,2},{7,3},{8,12},{9,13},{10,... | collective-permute-start | bytes 393224 | tf_op jit(solution)/shard_map/ppermute | solution.py:246
  45.6 9.6 %collective-permute-start.4 = (f32[4,128,256]{2,1,0:T(8,128)S(1)}, f32[4,128,256]{2,1,0:T(8,128)S(1)}, u32[]{:S(2)}, u32[]{:S(2)}) collective-permute-start(f32[4,128,256]{2,1,0:T(8,128)S(1)} %pad_maximum_fusion.refs_0_.refs_3_), channel_id=1, source_target_pairs={{0,1},{1,0},{2,3},{3,2},{4,5},{5,4},{6,7},{7,6},{8,9},{9,8},{10,11... | collective-permute-start | bytes 1572872 | tf_op jit(solution)/shard_map/ppermute | solution.py:246
  53.1 2.2 %collective-permute-start.9 = (f32[4,128,256]{2,1,0:T(8,128)S(1)}, f32[4,128,256]{2,1,0:T(8,128)S(1)}, u32[]{:S(2)}, u32[]{:S(2)}) collective-permute-start(f32[4,128,256]{2,1,0:T(8,128)S(1)} %collective-permute-done.5.refs_1_.refs_4_), channel_id=1, source_target_pairs={{0,1},{1,0},{2,3},{3,2},{4,5},{5,4},{6,7},{7,6},{8,9},{9,8},{10,11... | collective-permute-start | bytes 1572872 | tf_op jit(solution)/shard_map/ppermute | solution.py:246
  53.1 2.7 %collective-permute-start.10 = (f32[4,2,64,256]{3,2,1,0:T(8,128)S(1)}, f32[4,2,64,256]{3,2,1,0:T(8,128)S(1)}, u32[]{:S(2)}, u32[]{:S(2)}) collective-permute-start(f32[4,2,64,256]{3,2,1,0:T(8,128)S(1)} %pad_maximum_fusion.1.refs_2_.refs_5_), channel_id=1, source_target_pairs={{0,1},{1,0},{2,3},{3,2},{4,5},{5,4},{6,7},{7,6},{8,9},{9,8},{10,11... | collective-permute-start | bytes 1572872 | tf_op jit(solution)/shard_map/ppermute | solution.py:246
  57.4 16.1 %collective-permute-start.11 = (f32[192,256]{1,0:T(8,128)S(1)}, f32[192,256]{1,0:T(8,128)S(1)}, u32[]{:S(2)}, u32[]{:S(2)}) collective-permute-start(f32[192,256]{1,0:T(8,128)S(1)} %get-tuple-element.44), channel_id=1, source_target_pairs={{0,16},{1,17},{2,18},{3,19},{4,20},{5,21},{6,22},{7,23},{8,24},{9,... | collective-permute-start | bytes 589832 | tf_op jit(solution)/shard_map/ppermute | solution.py:248
  57.4 17.7 %collective-permute-start.15 = (f32[128,256]{1,0:T(8,128)S(1)}, f32[128,256]{1,0:T(8,128)S(1)}, u32[]{:S(2)}, u32[]{:S(2)}) collective-permute-start(f32[128,256]{1,0:T(8,128)S(1)} %get-tuple-element.46), channel_id=1, source_target_pairs={{0,28},{1,29},{2,30},{3,31},{4,16},{5,17},{6,18},{7,19},{8,20},{9,... | collective-permute-start | bytes 393224 | tf_op jit(solution)/shard_map/ppermute | solution.py:248
  61.0 14.2 %collective-permute-start.14 = (f32[128,256]{1,0:T(8,128)S(1)}, f32[128,256]{1,0:T(8,128)S(1)}, u32[]{:S(2)}, u32[]{:S(2)}) collective-permute-start(f32[128,256]{1,0:T(8,128)S(1)} %get-tuple-element.46), channel_id=1, source_target_pairs={{0,24},{1,25},{2,26},{3,27},{4,28},{5,29},{6,30},{7,31},{8,16},{9,... | collective-permute-start | bytes 393224 | tf_op jit(solution)/shard_map/ppermute | solution.py:248
  61.0 14.2 %collective-permute-start.13 = (f32[128,256]{1,0:T(8,128)S(1)}, f32[128,256]{1,0:T(8,128)S(1)}, u32[]{:S(2)}, u32[]{:S(2)}) collective-permute-start(f32[128,256]{1,0:T(8,128)S(1)} %get-tuple-element.46), channel_id=1, source_target_pairs={{0,20},{1,21},{2,22},{3,23},{4,24},{5,25},{6,26},{7,27},{8,28},{9,... | collective-permute-start | bytes 393224 | tf_op jit(solution)/shard_map/ppermute | solution.py:248
  62.8 12.4 %collective-permute-start.12 = (f32[64,256]{1,0:T(8,128)S(1)}, f32[64,256]{1,0:T(8,128)S(1)}, u32[]{:S(2)}, u32[]{:S(2)}) collective-permute-start(f32[64,256]{1,0:T(8,128)S(1)} %get-tuple-element.45), channel_id=1, source_target_pairs={{0,18},{1,19},{2,16},{3,17},{4,22},{5,23},{6,20},{7,21},{8,26},{9,... | collective-permute-start | bytes 196616 | tf_op jit(solution)/shard_map/ppermute | solution.py:248
  75.2 13.1 %collective-permute-start.17 = (f32[4,128,256]{2,1,0:T(8,128)S(1)}, f32[4,128,256]{2,1,0:T(8,128)S(1)}, u32[]{:S(2)}, u32[]{:S(2)}) collective-permute-start(f32[4,128,256]{2,1,0:T(8,128)S(1)} %pad_maximum_fusion.2.refs_0_), channel_id=1, source_target_pairs={{0,2},{1,3},{2,0},{3,1},{4,6},{5,7},{6,4},{7,5},{8,10},{9,11},{10,... | collective-permute-start | bytes 1572872 | tf_op jit(solution)/shard_map/ppermute | solution.py:246
  75.8 8.2 %collective-permute-start.21 = (f32[2,64,256]{2,1,0:T(8,128)S(1)}, f32[2,64,256]{2,1,0:T(8,128)S(1)}, u32[]{:S(2)}, u32[]{:S(2)}) collective-permute-start(f32[2,64,256]{2,1,0:T(8,128)S(1)} %pad_maximum_fusion.5), channel_id=1, source_target_pairs={{0,12},{1,13},{2,14},{3,15},{4,8},{5,9},{6,10},{7,11},{8,4},{9,5},... | collective-permute-start | bytes 393224 | tf_op jit(solution)/shard_map/ppermute | solution.py:246
  77.9 10.3 %collective-permute-start.20 = (f32[2,64,256]{2,1,0:T(8,128)S(1)}, f32[2,64,256]{2,1,0:T(8,128)S(1)}, u32[]{:S(2)}, u32[]{:S(2)}) collective-permute-start(f32[2,64,256]{2,1,0:T(8,128)S(1)} %pad_maximum_fusion.5), channel_id=1, source_target_pairs={{0,8},{1,9},{2,10},{3,11},{4,12},{5,13},{6,14},{7,15},{8,0},{9,1},... | collective-permute-start | bytes 393224 | tf_op jit(solution)/shard_map/ppermute | solution.py:246
  77.9 10.3 %collective-permute-start.19 = (f32[2,64,256]{2,1,0:T(8,128)S(1)}, f32[2,64,256]{2,1,0:T(8,128)S(1)}, u32[]{:S(2)}, u32[]{:S(2)}) collective-permute-start(f32[2,64,256]{2,1,0:T(8,128)S(1)} %pad_maximum_fusion.5), channel_id=1, source_target_pairs={{0,4},{1,5},{2,6},{3,7},{4,0},{5,1},{6,2},{7,3},{8,12},{9,13},{10,... | collective-permute-start | bytes 393224 | tf_op jit(solution)/shard_map/ppermute | solution.py:246
  80.2 10.3 %collective-permute-start.16 = (f32[4,128,256]{2,1,0:T(8,128)S(1)}, f32[4,128,256]{2,1,0:T(8,128)S(1)}, u32[]{:S(2)}, u32[]{:S(2)}) collective-permute-start(f32[4,128,256]{2,1,0:T(8,128)S(1)} %pad_maximum_fusion.2.refs_0_), channel_id=1, source_target_pairs={{0,1},{1,0},{2,3},{3,2},{4,5},{5,4},{6,7},{7,6},{8,9},{9,8},{10,11... | collective-permute-start | bytes 1572872 | tf_op jit(solution)/shard_map/ppermute | solution.py:246
  88.2 2.3 %collective-permute-start.22 = (f32[4,2,64,256]{3,2,1,0:T(8,128)S(1)}, f32[4,2,64,256]{3,2,1,0:T(8,128)S(1)}, u32[]{:S(2)}, u32[]{:S(2)}) collective-permute-start(f32[4,2,64,256]{3,2,1,0:T(8,128)S(1)} %pad_maximum_fusion.3.refs_2_), channel_id=1, source_target_pairs={{0,1},{1,0},{2,3},{3,2},{4,5},{5,4},{6,7},{7,6},{8,9},{9,8},{10,11... | collective-permute-start | bytes 1572872 | tf_op jit(solution)/shard_map/ppermute | solution.py:246
  88.3 2.6 %collective-permute-start.18 = (f32[4,128,256]{2,1,0:T(8,128)S(1)}, f32[4,128,256]{2,1,0:T(8,128)S(1)}, u32[]{:S(2)}, u32[]{:S(2)}) collective-permute-start(f32[4,128,256]{2,1,0:T(8,128)S(1)} %collective-permute-done.17.refs_1_), channel_id=1, source_target_pairs={{0,1},{1,0},{2,3},{3,2},{4,5},{5,4},{6,7},{7,6},{8,9},{9,8},{10,11... | collective-permute-start | bytes 1572872 | tf_op jit(solution)/shard_map/ppermute | solution.py:246
